TPU v7x, 32 devices: a whole 2x2x4 slice. The times are simulated.
32 devices in a mesh: rep: 4 (over y, x), blk: 8 (over z, core).
Axes of the slice: x: 2, y: 2, z: 4, core: 2. Of those that a mesh axis runs over, the one named last changes fastest.
Arguments:
- features: bfloat16 [16384, 128], P(('rep', 'blk')), may hold values from -6 to 6
- degrees: int32 [16384], P(('rep', 'blk')), may hold values from 1 to 32
- tile_weights: bfloat16 [4, 8, 160, 128, 128], P('rep', 'blk'), may hold values from 0 to 0.049804688
- tile_rows: int32 [4, 8, 160], P('rep', 'blk'), may hold values from 0 to 31, as said below
- tile_cols: int32 [4, 8, 160], P('rep', 'blk'), may hold values from 0 to 15, as said below
- tile_counts: int32 [4, 8], P('rep', 'blk'), may hold values from 1 to 160, as said below
- weight: bfloat16 [128, 256], replicated, may hold values from -0.5 to 0.5
- layer_bias: float32 [256], replicated, may hold values from -3 to 3
- upstream: bfloat16 [16384, 256], P(('rep', 'blk')), may hold values from -6 to 6
Outputs:
- hidden: bfloat16 [16384, 256], P(('rep', 'blk'))
- feature_grad: bfloat16 [16384, 128], P(('rep', 'blk'))
- weight_grad: float32 [128, 256], replicated
- bias_grad: float32 [256], replicated
Inputs may be any that keep to these rules, and one draw needn't show every extreme that they name: `tile_rows`: the first tile_counts slots of a device hold distinct tiles, ordered by row and then by column; a used row h lies in node block r * 8 + h // 4, whose index h // 4 is within 3 steps of the device's blk index around the loop of 8; unused slots hold the device's own first tile row. `tile_cols`: unused slots hold 0. `tile_counts`: at most 40 used slots of one device lie in the rows of one node block; this and the largest count are both reached by some device in every draw.
All inputs are finite; a program needn't handle non-finite values.
Results may differ from a plain program's by a relative error of at most 0.015.
Values may be sent and summed in bfloat16 or wider, within the bound.
No kernel may reach another device: no remote copies, remote signals or barrier semaphores. Data moves between devices by JAX's collectives and lax.ppermute only.
A program may use at most 128 MiB of HBM per device.

v0:
```python
import jax
import jax.numpy as jnp
from jax import lax
from jax.sharding import PartitionSpec as P

REACH = 3


def shifted(value, axis, by):
    length = lax.axis_size(axis)
    return lax.ppermute(value, axis, [(i, (i + by) % length) for i in range(length)])


def node_scale(degrees):
    return 1.0 / jnp.sqrt(degrees.astype(jnp.float32) + 1.0)


def on_device(
    features, degrees, tile_weights, tile_rows, tile_cols, tile_counts, weight, layer_bias, upstream
):
    row_count, feat_width = features.shape
    tile_size = tile_weights.shape[-1]
    slot_total = tile_weights.shape[2]
    row_tiles = row_count // tile_size
    rep_count = lax.axis_size("rep")
    blk_count = lax.axis_size("blk")
    blk_index = lax.axis_index("blk")
    window_blocks = 2 * REACH + 1
    window_tiles = window_blocks * row_tiles
    column_tiles = rep_count * row_tiles
    slot_block = slot_total // (2 * (REACH + 1))
    weights_dev = tile_weights[0, 0]
    rows_dev = tile_rows[0, 0]
    cols_dev = tile_cols[0, 0]
    count_dev = tile_counts[0, 0]
    group_index = rows_dev // row_tiles
    distance = (group_index - blk_index) % blk_count
    distance = jnp.where(distance > blk_count // 2, distance - blk_count, distance)
    window_rows = (distance + REACH) * row_tiles + rows_dev % row_tiles
    slot_ids = jnp.arange(slot_total, dtype=jnp.int32)
    slot_valid = slot_ids < count_dev
    window_seg = jnp.where(slot_valid, window_rows, window_tiles)
    column_seg = jnp.where(slot_valid, cols_dev, column_tiles)
    block_limit = (count_dev + slot_block - 1) // slot_block

    def tile_pass(source_tiles, gather_index, segment_index, segment_total, pattern):

        def add_block(block_id, running):
            slot_first = block_id * slot_block
            weights_part = lax.dynamic_slice_in_dim(weights_dev, slot_first, slot_block, 0)
            gather_part = lax.dynamic_slice_in_dim(gather_index, slot_first, slot_block, 0)
            segment_part = lax.dynamic_slice_in_dim(segment_index, slot_first, slot_block, 0)
            products = jnp.einsum(
                pattern, weights_part, source_tiles[gather_part], preferred_element_type=jnp.float32
            )
            return (
                running
                + jax.ops.segment_sum(products, segment_part, segment_total + 1)[:segment_total]
            )

        zero_sum = jnp.zeros((segment_total, tile_size, feat_width), jnp.float32)
        return lax.fori_loop(0, block_limit, add_block, zero_sum)

    node_norm = node_scale(degrees)
    scaled = (node_norm[:, None] * features.astype(jnp.float32)).astype(jnp.bfloat16)
    source_rows = lax.all_gather(scaled, "rep", axis=0, tiled=True)
    source_tiles = source_rows.reshape(column_tiles, tile_size, feat_width)
    partial_value = tile_pass(source_tiles, cols_dev, window_seg, window_tiles, "tab,tbf->taf")
    partial_value = partial_value.reshape(window_blocks, row_count, feat_width)
    neighbor_sum = partial_value[REACH]
    for offset in range(-REACH, REACH + 1):
        if offset != 0:
            neighbor_sum = neighbor_sum + shifted(
                partial_value[offset + REACH].astype(jnp.bfloat16), "blk", offset
            ).astype(jnp.float32)
    aggregated = (node_norm[:, None] * (neighbor_sum + scaled.astype(jnp.float32))).astype(
        jnp.bfloat16
    )
    pre_act = jnp.dot(aggregated, weight, preferred_element_type=jnp.float32) + layer_bias
    hidden = jax.nn.silu(pre_act).astype(jnp.bfloat16)
    gate_sigmoid = jax.nn.sigmoid(pre_act)
    pre_grad = (
        upstream.astype(jnp.float32)
        * (gate_sigmoid + pre_act * gate_sigmoid * (1.0 - gate_sigmoid))
    ).astype(jnp.bfloat16)
    local_weight = jnp.dot(aggregated.T, pre_grad, preferred_element_type=jnp.float32)
    local_bias = jnp.sum(pre_grad.astype(jnp.float32), axis=0)
    weight_sum, bias_sum = lax.psum((local_weight, local_bias), ("rep", "blk"))
    grad_scale = (row_count * rep_count * blk_count) ** (-0.5)
    scaled_grad = (
        node_norm[:, None] * jnp.dot(pre_grad, weight.T, preferred_element_type=jnp.float32)
    ).astype(jnp.bfloat16)
    window_parts = [scaled_grad] * window_blocks
    for offset in range(-REACH, REACH + 1):
        if offset != 0:
            window_parts[offset + REACH] = shifted(scaled_grad, "blk", -offset)
    grad_tiles = jnp.stack(window_parts).reshape(window_tiles, tile_size, feat_width)
    column_part = tile_pass(grad_tiles, window_rows, column_seg, column_tiles, "tab,taf->tbf")
    column_sum = lax.psum_scatter(
        column_part.reshape(rep_count * row_count, feat_width).astype(jnp.bfloat16),
        "rep",
        scatter_dimension=0,
        tiled=True,
    ).astype(jnp.float32)
    feature_grad = (node_norm[:, None] * (column_sum + scaled_grad.astype(jnp.float32))).astype(
        jnp.bfloat16
    )
    return (hidden, feature_grad, weight_sum * grad_scale, bias_sum * grad_scale)


def solution(mesh):
    placed = (
        P(("rep", "blk"), None),
        P(("rep", "blk")),
        P("rep", "blk", None, None, None),
        P("rep", "blk", None),
        P("rep", "blk", None),
        P("rep", "blk"),
        P(),
        P(),
        P(("rep", "blk"), None),
    )
    return jax.shard_map(
        on_device,
        mesh=mesh,
        in_specs=placed,
        out_specs=(P(("rep", "blk"), None), P(("rep", "blk"), None), P(), P()),
        check_vma=False,
    )
```

profile of v0, /device:TPU:0, one launch (start us, length us, event | category | flops | bytes accessed | tf_op | source)
XLA Modules:
  0.0 260.6 jit_solution(15760169504381164581)
XLA Ops:
  10.5 12.2 %all_gather.3 = bf16[2048,128]{1,0:T(8,128)(2,1)} all-gather(bf16[512,128]{1,0:T(8,128)(2,1)S(1)} %multiply_convert_fusion.2), channel_id=1, replica_groups=mesh['rep'=4,'blk'=8] {'rep'}, dimensions={0}, use_global_device_ids=true | all-gather | bytes 655360 | tf_op jit(solution)/shard_map/all_gather | solution.py:66
  24.9 54.6 %while.20 = (s32[]{:T(128)}, f32[28,128,128]{2,1,0:T(8,128)}, s32[]{:T(128)}, s32[160]{0:T(256)S(1)}, bf16[160,128,128]{2,1,0:T(8,128)(2,1)}, /*index=5*/s32[160...) while((s32[]{:T(128)}, f32[28,128,128]{2,1,0:T(8,128)}, ...), condition=%wide.region_2.3_spmd, body=%wide.region_0.2_spmd.sunk | while | flops 84673600 | bytes 15274723 | solution.py:62
  31.0 3.0 %slice_add_fusion.4 = f32[28,128,128]{2,1,0:T(8,128)} fusion(f32[28,128,128]{2,1,0:T(8,128)} %get-tuple-element.229, f32[29,128,128]{2,1,0:T(8,128)S(1)} %scatter_fusion), kind=kLoop, calls=%fused_computation.4.clone.1 | loop fusion | flops 458752 | bytes 5505024 | tf_op jit(solution)/shard_map/while/body/add | solution.py:57
  37.5 2.6 %scatter_fusion = f32[29,128,128]{2,1,0:T(8,128)S(1)} fusion(f32[29,128,128]{2,1,0:T(8,128)S(1)} %broadcast.83, s32[20]{0:T(128)S(1)} %dynamic_slice.32, f32[20,128,128]{2,1,0:T(8,128)S(1)} %fusion.42), kind=kCustom, calls=%fused_computation.2.clone.1 | custom fusion | flops 327680 | bytes 3932240 | tf_op jit(solution)/shard_map/while/body/scatter-add | solution.py:58
  40.1 3.0 %slice_add_fusion.4 = f32[28,128,128]{2,1,0:T(8,128)} fusion(f32[28,128,128]{2,1,0:T(8,128)} %get-tuple-element.229, f32[29,128,128]{2,1,0:T(8,128)S(1)} %scatter_fusion), kind=kLoop, calls=%fused_computation.4.clone.1 | loop fusion | flops 458752 | bytes 5505024 | tf_op jit(solution)/shard_map/while/body/add | solution.py:57
  46.6 2.6 %scatter_fusion = f32[29,128,128]{2,1,0:T(8,128)S(1)} fusion(f32[29,128,128]{2,1,0:T(8,128)S(1)} %broadcast.83, s32[20]{0:T(128)S(1)} %dynamic_slice.32, f32[20,128,128]{2,1,0:T(8,128)S(1)} %fusion.42), kind=kCustom, calls=%fused_computation.2.clone.1 | custom fusion | flops 327680 | bytes 3932240 | tf_op jit(solution)/shard_map/while/body/scatter-add | solution.py:58
  49.2 3.0 %slice_add_fusion.4 = f32[28,128,128]{2,1,0:T(8,128)} fusion(f32[28,128,128]{2,1,0:T(8,128)} %get-tuple-element.229, f32[29,128,128]{2,1,0:T(8,128)S(1)} %scatter_fusion), kind=kLoop, calls=%fused_computation.4.clone.1 | loop fusion | flops 458752 | bytes 5505024 | tf_op jit(solution)/shard_map/while/body/add | solution.py:57
  55.7 2.6 %scatter_fusion = f32[29,128,128]{2,1,0:T(8,128)S(1)} fusion(f32[29,128,128]{2,1,0:T(8,128)S(1)} %broadcast.83, s32[20]{0:T(128)S(1)} %dynamic_slice.32, f32[20,128,128]{2,1,0:T(8,128)S(1)} %fusion.42), kind=kCustom, calls=%fused_computation.2.clone.1 | custom fusion | flops 327680 | bytes 3932240 | tf_op jit(solution)/shard_map/while/body/scatter-add | solution.py:58
  58.3 3.0 %slice_add_fusion.4 = f32[28,128,128]{2,1,0:T(8,128)} fusion(f32[28,128,128]{2,1,0:T(8,128)} %get-tuple-element.229, f32[29,128,128]{2,1,0:T(8,128)S(1)} %scatter_fusion), kind=kLoop, calls=%fused_computation.4.clone.1 | loop fusion | flops 458752 | bytes 5505024 | tf_op jit(solution)/shard_map/while/body/add | solution.py:57
  64.8 2.6 %scatter_fusion = f32[29,128,128]{2,1,0:T(8,128)S(1)} fusion(f32[29,128,128]{2,1,0:T(8,128)S(1)} %broadcast.83, s32[20]{0:T(128)S(1)} %dynamic_slice.32, f32[20,128,128]{2,1,0:T(8,128)S(1)} %fusion.42), kind=kCustom, calls=%fused_computation.2.clone.1 | custom fusion | flops 327680 | bytes 3932240 | tf_op jit(solution)/shard_map/while/body/scatter-add | solution.py:58
  67.4 3.0 %slice_add_fusion.4 = f32[28,128,128]{2,1,0:T(8,128)} fusion(f32[28,128,128]{2,1,0:T(8,128)} %get-tuple-element.229, f32[29,128,128]{2,1,0:T(8,128)S(1)} %scatter_fusion), kind=kLoop, calls=%fused_computation.4.clone.1 | loop fusion | flops 458752 | bytes 5505024 | tf_op jit(solution)/shard_map/while/body/add | solution.py:57
  73.9 2.6 %scatter_fusion = f32[29,128,128]{2,1,0:T(8,128)S(1)} fusion(f32[29,128,128]{2,1,0:T(8,128)S(1)} %broadcast.83, s32[20]{0:T(128)S(1)} %dynamic_slice.32, f32[20,128,128]{2,1,0:T(8,128)S(1)} %fusion.42), kind=kCustom, calls=%fused_computation.2.clone.1 | custom fusion | flops 327680 | bytes 3932240 | tf_op jit(solution)/shard_map/while/body/scatter-add | solution.py:58
  76.5 3.0 %slice_add_fusion.4 = f32[28,128,128]{2,1,0:T(8,128)} fusion(f32[28,128,128]{2,1,0:T(8,128)} %get-tuple-element.229, f32[29,128,128]{2,1,0:T(8,128)S(1)} %scatter_fusion), kind=kLoop, calls=%fused_computation.4.clone.1 | loop fusion | flops 458752 | bytes 5505024 | tf_op jit(solution)/shard_map/while/body/add | solution.py:57
  81.2 9.4 %collective-permute-start = (bf16[512,128]{1,0:T(8,128)(2,1)S(1)}, bf16[512,128]{1,0:T(8,128)(2,1)S(1)}, u32[]{:S(2)}, u32[]{:S(2)}) collective-permute-start(bf16[512,128]{1,0:T(8,128)(2,1)S(1)} %bitcast.70), channel_id=1, source_target_pairs={{0,5},{1,6},{2,7},{3,0},{4,1},{5,2},{6,3},{7,4},{8,13},{9,14},{10,... | collective-permute-start | bytes 393224 | tf_op jit(solution)/shard_map/ppermute | solution.py:11
  90.7 3.9 %collective-permute-start.4 = (bf16[512,128]{1,0:T(8,128)(2,1)S(1)}, bf16[512,128]{1,0:T(8,128)(2,1)S(1)}, u32[]{:S(2)}, u32[]{:S(2)}) collective-permute-start(bf16[512,128]{1,0:T(8,128)(2,1)S(1)} %bitcast.69), channel_id=1, source_target_pairs={{0,2},{1,3},{2,4},{3,5},{4,6},{5,7},{6,0},{7,1},{8,10},{9,11},{10,... | collective-permute-start | bytes 393224 | tf_op jit(solution)/shard_map/ppermute | solution.py:11
  94.5 8.9 %collective-permute-start.3 = (bf16[512,128]{1,0:T(8,128)(2,1)S(1)}, bf16[512,128]{1,0:T(8,128)(2,1)S(1)}, u32[]{:S(2)}, u32[]{:S(2)}) collective-permute-start(bf16[512,128]{1,0:T(8,128)(2,1)S(1)} %bitcast.68), channel_id=1, source_target_pairs={{0,1},{1,2},{2,3},{3,4},{4,5},{5,6},{6,7},{7,0},{8,9},{9,10},{10,1... | collective-permute-start | bytes 393224 | tf_op jit(solution)/shard_map/ppermute | solution.py:11
  103.4 2.9 %collective-permute-start.2 = (bf16[512,128]{1,0:T(8,128)(2,1)S(1)}, bf16[512,128]{1,0:T(8,128)(2,1)S(1)}, u32[]{:S(2)}, u32[]{:S(2)}) collective-permute-start(bf16[512,128]{1,0:T(8,128)(2,1)S(1)} %bitcast.67), channel_id=1, source_target_pairs={{0,7},{1,0},{2,1},{3,2},{4,3},{5,4},{6,5},{7,6},{8,15},{9,8},{10,9... | collective-permute-start | bytes 393224 | tf_op jit(solution)/shard_map/ppermute | solution.py:11
  107.4 8.2 %copy.13 = bf16[1,1,160,128,128]{3,4,2,1,0:T(8,128)(2,1)} copy(bf16[1,1,160,128,128]{4,3,2,1,0:T(8,128)(2,1)} %bitcast.62) | data formatting | bytes 10485760 | tf_op args[2]
  116.7 3.8 %collective-permute-done.1 = bf16[512,128]{1,0:T(8,128)(2,1)S(1)} collective-permute-done((bf16[512,128]{1,0:T(8,128)(2,1)S(1)}, bf16[512,128]{1,0:T(8,128)(2,1)S(1)}, u32[]{:S(2)}, u32[]{:S(2)}) %collective-permute-start.1) | collective-permute-done | bytes 131104 | tf_op jit(solution)/shard_map/ppermute | solution.py:11
  122.1 3.2 %collective-permute-start.10 = (bf16[512,128]{1,0:T(8,128)(2,1)S(1)}, bf16[512,128]{1,0:T(8,128)(2,1)S(1)}, u32[]{:S(2)}, u32[]{:S(2)}) collective-permute-start(bf16[512,128]{1,0:T(8,128)(2,1)S(1)} %fusion.6), channel_id=1, source_target_pairs={{0,6},{1,7},{2,0},{3,1},{4,2},{5,3},{6,4},{7,5},{8,14},{9,15},{10,... | collective-permute-start | bytes 393224 | tf_op jit(solution)/shard_map/ppermute | solution.py:11
  125.8 2.6 %collective-permute-start.6 = (bf16[512,128]{1,0:T(8,128)(2,1)S(1)}, bf16[512,128]{1,0:T(8,128)(2,1)S(1)}, u32[]{:S(2)}, u32[]{:S(2)}) collective-permute-start(bf16[512,128]{1,0:T(8,128)(2,1)S(1)} %fusion.6), channel_id=1, source_target_pairs={{0,3},{1,4},{2,5},{3,6},{4,7},{5,0},{6,1},{7,2},{8,11},{9,12},{10,... | collective-permute-start | bytes 393224 | tf_op jit(solution)/shard_map/ppermute | solution.py:11
  129.4 10.0 %collective-permute-done.6 = bf16[512,128]{1,0:T(8,128)(2,1)S(1)} collective-permute-done((bf16[512,128]{1,0:T(8,128)(2,1)S(1)}, bf16[512,128]{1,0:T(8,128)(2,1)S(1)}, u32[]{:S(2)}, u32[]{:S(2)}) %collective-permute-start.6) | collective-permute-done | bytes 131104 | tf_op jit(solution)/shard_map/ppermute | solution.py:11
  139.4 6.8 %collective-permute-done.7 = bf16[512,128]{1,0:T(8,128)(2,1)S(1)} collective-permute-done((bf16[512,128]{1,0:T(8,128)(2,1)S(1)}, bf16[512,128]{1,0:T(8,128)(2,1)S(1)}, u32[]{:S(2)}, u32[]{:S(2)}) %collective-permute-start.7) | collective-permute-done | bytes 131104 | tf_op jit(solution)/shard_map/ppermute | solution.py:11
  146.6 41.9 %while.21 = (s32[]{:T(128)}, f32[16,128,128]{2,1,0:T(8,128)S(1)}, s32[]{:T(128)}, s32[160]{0:T(256)S(1)}, bf16[160,128,128]{1,2,0:T(8,128)(2,1)}, /*index=5*/s32...) while((s32[]{:T(128)}, f32[16,128,128]{2,1,0:T(8,128)S(1)}, ...), condition=%wide.region_5.6_spmd, body=%wide.region_3.5_spmd.sunk | while | flops 84476992 | bytes 19474260 | solution.py:62
  149.8 2.6 %scatter_fusion.1 = f32[17,128,128]{2,1,0:T(8,128)S(1)} fusion(f32[17,128,128]{2,1,0:T(8,128)S(1)} %broadcast.88, s32[20]{0:T(128)S(1)} %dynamic_slice.35, f32[20,128,128]{2,1,0:T(8,128)S(1)} %fusion.45), kind=kCustom, calls=%fused_computation.3.clone.1 | custom fusion | flops 327680 | bytes 3932240 | tf_op jit(solution)/shard_map/while/body/scatter-add | solution.py:58
  156.8 2.6 %scatter_fusion.1 = f32[17,128,128]{2,1,0:T(8,128)S(1)} fusion(f32[17,128,128]{2,1,0:T(8,128)S(1)} %broadcast.88, s32[20]{0:T(128)S(1)} %dynamic_slice.35, f32[20,128,128]{2,1,0:T(8,128)S(1)} %fusion.45), kind=kCustom, calls=%fused_computation.3.clone.1 | custom fusion | flops 327680 | bytes 3932240 | tf_op jit(solution)/shard_map/while/body/scatter-add | solution.py:58
  163.7 2.6 %scatter_fusion.1 = f32[17,128,128]{2,1,0:T(8,128)S(1)} fusion(f32[17,128,128]{2,1,0:T(8,128)S(1)} %broadcast.88, s32[20]{0:T(128)S(1)} %dynamic_slice.35, f32[20,128,128]{2,1,0:T(8,128)S(1)} %fusion.45), kind=kCustom, calls=%fused_computation.3.clone.1 | custom fusion | flops 327680 | bytes 3932240 | tf_op jit(solution)/shard_map/while/body/scatter-add | solution.py:58
  170.7 2.6 %scatter_fusion.1 = f32[17,128,128]{2,1,0:T(8,128)S(1)} fusion(f32[17,128,128]{2,1,0:T(8,128)S(1)} %broadcast.88, s32[20]{0:T(128)S(1)} %dynamic_slice.35, f32[20,128,128]{2,1,0:T(8,128)S(1)} %fusion.45), kind=kCustom, calls=%fused_computation.3.clone.1 | custom fusion | flops 327680 | bytes 3932240 | tf_op jit(solution)/shard_map/while/body/scatter-add | solution.py:58
  177.7 2.6 %scatter_fusion.1 = f32[17,128,128]{2,1,0:T(8,128)S(1)} fusion(f32[17,128,128]{2,1,0:T(8,128)S(1)} %broadcast.88, s32[20]{0:T(128)S(1)} %dynamic_slice.35, f32[20,128,128]{2,1,0:T(8,128)S(1)} %fusion.45), kind=kCustom, calls=%fused_computation.3.clone.1 | custom fusion | flops 327680 | bytes 3932240 | tf_op jit(solution)/shard_map/while/body/scatter-add | solution.py:58
  184.7 2.6 %scatter_fusion.1 = f32[17,128,128]{2,1,0:T(8,128)S(1)} fusion(f32[17,128,128]{2,1,0:T(8,128)S(1)} %broadcast.88, s32[20]{0:T(128)S(1)} %dynamic_slice.35, f32[20,128,128]{2,1,0:T(8,128)S(1)} %fusion.45), kind=kCustom, calls=%fused_computation.3.clone.1 | custom fusion | flops 327680 | bytes 3932240 | tf_op jit(solution)/shard_map/while/body/scatter-add | solution.py:58
  189.4 49.8 %psum.15 = f32[256]{0:T(256)S(1)} all-reduce(f32[256]{0:T(256)S(1)} %get-tuple-element.117), channel_id=1, replica_groups=mesh['rep'=4,'blk'=8] {'rep','blk'}, use_global_device_ids=true, to_apply=%region_9.10 | all-reduce | flops 256 | bytes 2048 | tf_op jit(solution)/shard_map/psum | solution.py:88
  239.8 10.2 %all-reduce.2.cloned.1.call-done = f32[128,256]{1,0:T(8,128)} async-done(((f32[128,256]{1,0:T(8,128)}), f32[128,256]{1,0:T(8,128)}) %all-reduce.2.cloned.1.call-update) | async-done | bytes 131088 | tf_op jit(solution)/shard_map/psum | solution.py:88
  (185 shorter events, 65.2 us)
Async XLA Ops:
  8.0 112.7 %copy-start = (bf16[128,256]{1,0:T(8,128)(2,1)S(1)}, bf16[128,256]{1,0:T(8,128)(2,1)}, u32[]{:S(2)}) copy-start(bf16[128,256]{1,0:T(8,128)(2,1)} %param.19) | copy-start | bytes 196612
  8.0 16.9 %copy-start.6 = (s32[1,1,160]{2,1,0:T(1,128)S(1)}, s32[1,1,160]{2,1,0:T(1,128)}, u32[]{:S(2)}) copy-start(s32[1,1,160]{2,1,0:T(1,128)} %param.17) | copy-start | bytes 1924
  8.0 241.9 %all-reduce.2.cloned.1.call-start = ((), (), s32[]{:S(2)}) async-start(), calls=%async_computation.2 | async-start | bytes 262144 | tf_op jit(solution)/shard_map/psum | solution.py:88
  81.2 34.4 %collective-permute-start.5 = (bf16[512,128]{1,0:T(8,128)(2,1)S(1)}, bf16[512,128]{1,0:T(8,128)(2,1)S(1)}, u32[]{:S(2)}, u32[]{:S(2)}) collective-permute-start(bf16[512,128]{1,0:T(8,128)(2,1)S(1)} %bitcast.71), channel_id=1, source_target_pairs={{0,3},{1,4},{2,5},{3,6},{4,7},{5,0},{6,1},{7,2},{8,11},{9,12},{10,... | collective-permute-start | bytes 393224 | tf_op jit(solution)/shard_map/ppermute | solution.py:11
  81.2 35.4 %collective-permute-start = (bf16[512,128]{1,0:T(8,128)(2,1)S(1)}, bf16[512,128]{1,0:T(8,128)(2,1)S(1)}, u32[]{:S(2)}, u32[]{:S(2)}) collective-permute-start(bf16[512,128]{1,0:T(8,128)(2,1)S(1)} %bitcast.70), channel_id=1, source_target_pairs={{0,5},{1,6},{2,7},{3,0},{4,1},{5,2},{6,3},{7,4},{8,13},{9,14},{10,... | collective-permute-start | bytes 393224 | tf_op jit(solution)/shard_map/ppermute | solution.py:11
  90.7 26.0 %collective-permute-start.4 = (bf16[512,128]{1,0:T(8,128)(2,1)S(1)}, bf16[512,128]{1,0:T(8,128)(2,1)S(1)}, u32[]{:S(2)}, u32[]{:S(2)}) collective-permute-start(bf16[512,128]{1,0:T(8,128)(2,1)S(1)} %bitcast.69), channel_id=1, source_target_pairs={{0,2},{1,3},{2,4},{3,5},{4,6},{5,7},{6,0},{7,1},{8,10},{9,11},{10,... | collective-permute-start | bytes 393224 | tf_op jit(solution)/shard_map/ppermute | solution.py:11
  94.5 22.1 %collective-permute-start.3 = (bf16[512,128]{1,0:T(8,128)(2,1)S(1)}, bf16[512,128]{1,0:T(8,128)(2,1)S(1)}, u32[]{:S(2)}, u32[]{:S(2)}) collective-permute-start(bf16[512,128]{1,0:T(8,128)(2,1)S(1)} %bitcast.68), channel_id=1, source_target_pairs={{0,1},{1,2},{2,3},{3,4},{4,5},{5,6},{6,7},{7,0},{8,9},{9,10},{10,1... | collective-permute-start | bytes 393224 | tf_op jit(solution)/shard_map/ppermute | solution.py:11
  103.4 13.2 %collective-permute-start.2 = (bf16[512,128]{1,0:T(8,128)(2,1)S(1)}, bf16[512,128]{1,0:T(8,128)(2,1)S(1)}, u32[]{:S(2)}, u32[]{:S(2)}) collective-permute-start(bf16[512,128]{1,0:T(8,128)(2,1)S(1)} %bitcast.67), channel_id=1, source_target_pairs={{0,7},{1,0},{2,1},{3,2},{4,3},{5,4},{6,5},{7,6},{8,15},{9,8},{10,9... | collective-permute-start | bytes 393224 | tf_op jit(solution)/shard_map/ppermute | solution.py:11
  107.3 13.2 %copy-start.5 = (bf16[512,128]{1,0:T(8,128)(2,1)S(1)}, bf16[512,128]{1,0:T(8,128)(2,1)}, u32[]{:S(2)}) copy-start(bf16[512,128]{1,0:T(8,128)(2,1)} %param.13) | copy-start | bytes 393220
  107.3 13.3 %copy-start.9 = (bf16[512,256]{1,0:T(8,128)(2,1)S(1)}, bf16[512,256]{1,0:T(8,128)(2,1)}, u32[]{:S(2)}) copy-start(bf16[512,256]{1,0:T(8,128)(2,1)} %param.21) | copy-start | bytes 786436
  107.4 13.3 %copy-start.10 = (f32[256]{0:T(256)S(1)}, f32[256]{0:T(256)}, u32[]{:S(2)}) copy-start(f32[256]{0:T(256)} %param.20) | copy-start | bytes 3076
  115.5 5.0 %collective-permute-start.1 = (bf16[512,128]{1,0:T(8,128)(2,1)S(1)}, bf16[512,128]{1,0:T(8,128)(2,1)S(1)}, u32[]{:S(2)}, u32[]{:S(2)}) collective-permute-start(bf16[512,128]{1,0:T(8,128)(2,1)S(1)} %bitcast.66), channel_id=1, source_target_pairs={{0,6},{1,7},{2,0},{3,1},{4,2},{5,3},{6,4},{7,5},{8,14},{9,15},{10,... | collective-permute-start | bytes 393224 | tf_op jit(solution)/shard_map/ppermute | solution.py:11
  122.0 24.4 %copy-start.3 = (bf16[512,128]{1,0:T(8,128)(2,1)}, bf16[512,128]{1,0:T(8,128)(2,1)S(1)}, u32[]{:S(2)}) copy-start(bf16[512,128]{1,0:T(8,128)(2,1)S(1)} %fusion.6) | copy-start | bytes 393220
  122.1 24.4 %collective-permute-start.11 = (bf16[512,128]{1,0:T(8,128)(2,1)S(1)}, bf16[512,128]{1,0:T(8,128)(2,1)S(1)}, u32[]{:S(2)}, u32[]{:S(2)}) collective-permute-start(bf16[512,128]{1,0:T(8,128)(2,1)S(1)} %fusion.6), channel_id=1, source_target_pairs={{0,5},{1,6},{2,7},{3,0},{4,1},{5,2},{6,3},{7,4},{8,13},{9,14},{10,... | collective-permute-start | bytes 393224 | tf_op jit(solution)/shard_map/ppermute | solution.py:11
  122.1 24.3 %collective-permute-start.10 = (bf16[512,128]{1,0:T(8,128)(2,1)S(1)}, bf16[512,128]{1,0:T(8,128)(2,1)S(1)}, u32[]{:S(2)}, u32[]{:S(2)}) collective-permute-start(bf16[512,128]{1,0:T(8,128)(2,1)S(1)} %fusion.6), channel_id=1, source_target_pairs={{0,6},{1,7},{2,0},{3,1},{4,2},{5,3},{6,4},{7,5},{8,14},{9,15},{10,... | collective-permute-start | bytes 393224 | tf_op jit(solution)/shard_map/ppermute | solution.py:11
  125.3 21.0 %collective-permute-start.9 = (bf16[512,128]{1,0:T(8,128)(2,1)S(1)}, bf16[512,128]{1,0:T(8,128)(2,1)S(1)}, u32[]{:S(2)}, u32[]{:S(2)}) collective-permute-start(bf16[512,128]{1,0:T(8,128)(2,1)S(1)} %fusion.6), channel_id=1, source_target_pairs={{0,7},{1,0},{2,1},{3,2},{4,3},{5,4},{6,5},{7,6},{8,15},{9,8},{10,9... | collective-permute-start | bytes 393224 | tf_op jit(solution)/shard_map/ppermute | solution.py:11
  125.5 20.8 %collective-permute-start.8 = (bf16[512,128]{1,0:T(8,128)(2,1)S(1)}, bf16[512,128]{1,0:T(8,128)(2,1)S(1)}, u32[]{:S(2)}, u32[]{:S(2)}) collective-permute-start(bf16[512,128]{1,0:T(8,128)(2,1)S(1)} %fusion.6), channel_id=1, source_target_pairs={{0,1},{1,2},{2,3},{3,4},{4,5},{5,6},{6,7},{7,0},{8,9},{9,10},{10,1... | collective-permute-start | bytes 393224 | tf_op jit(solution)/shard_map/ppermute | solution.py:11
  125.8 13.6 %collective-permute-start.6 = (bf16[512,128]{1,0:T(8,128)(2,1)S(1)}, bf16[512,128]{1,0:T(8,128)(2,1)S(1)}, u32[]{:S(2)}, u32[]{:S(2)}) collective-permute-start(bf16[512,128]{1,0:T(8,128)(2,1)S(1)} %fusion.6), channel_id=1, source_target_pairs={{0,3},{1,4},{2,5},{3,6},{4,7},{5,0},{6,1},{7,2},{8,11},{9,12},{10,... | collective-permute-start | bytes 393224 | tf_op jit(solution)/shard_map/ppermute | solution.py:11
  129.4 122.1 %reduce-scatter.2.cloned.1.call-start = ((), (), s32[]{:S(2)}) async-start(), calls=%async_computation.1 | async-start | bytes 655360 | tf_op jit(solution)/shard_map/reduce_scatter | solution.py:99
  139.4 6.8 %collective-permute-start.7 = (bf16[512,128]{1,0:T(8,128)(2,1)S(1)}, bf16[512,128]{1,0:T(8,128)(2,1)S(1)}, u32[]{:S(2)}, u32[]{:S(2)}) collective-permute-start(bf16[512,128]{1,0:T(8,128)(2,1)S(1)} %fusion.6), channel_id=1, source_target_pairs={{0,2},{1,3},{2,4},{3,5},{4,6},{5,7},{6,0},{7,1},{8,10},{9,11},{10,... | collective-permute-start | bytes 393224 | tf_op jit(solution)/shard_map/ppermute | solution.py:11
  152.4 1.2 copy-start.2
  152.4 1.2 copy-start.8
  159.4 1.2 copy-start.2
  159.4 1.2 copy-start.8
  166.4 1.2 copy-start.2
  166.4 1.2 copy-start.8
  173.3 1.2 copy-start.2
  173.4 1.2 copy-start.8
  180.3 1.2 copy-start.2
  187.3 1.2 copy-start.2
  187.3 1.2 copy-start.8
  188.5 63.0 %copy-start.4 = (bf16[512,128]{1,0:T(8,128)(2,1)S(1)}, bf16[512,128]{1,0:T(8,128)(2,1)}, u32[]{:S(2)}) copy-start(bf16[512,128]{1,0:T(8,128)(2,1)} %copy-done.3) | copy-start | bytes 393220
  (13 other events, 10.3 us)
Sparse Core Ops, SparseCore 0:
  129.5 120.3 all-reduce.1
Sparse Core Ops, SparseCore 1:
  189.5 34.9 reduce-scatter.1
where the time goes:
time: 261 us
  blocking collectives  62 us (24%)
  other arithmetic  60.6 us (23%)
  local copies, waits for them, and re-layouts  38.2 us (15%)
  starting transfers between devices  32.8 us (13%)
  waiting for transfers between devices  30.9 us (12%)
  matrix products  19.2 us (7%)
  between operations  16.4 us (6%)
    psum x1, blocking collectives, on_device(): weight_sum, bias_sum = lax.psum((local_weight, local_bias), ('rep', 'blk'))  49.8 us
    ppermute x12, starting transfers between devices, shifted(): lax.ppermute(value, axis, [(i, (i + by) % length) for i in range(length)])  32.7 us
    scatter-add x12, other arithmetic, add_block(): jax.ops.segment_sum(products, segment_part, segment_total + 1)  31.3 us
    ppermute x12, waiting for transfers between devices, shifted(): lax.ppermute(value, axis, [(i, (i + by) % length) for i in range(length)])  20.7 us
    add x12, other arithmetic, add_block(): running + jax.ops.segment_sum(products, segment_part, segment_total + 1)[...  19.4 us
    dot_general x12, matrix products, add_block(): jnp.einsum(pattern, weights_part, source_tiles[gather_part], preferred_el...  17 us
    gather x12, local copies, waits for them, and re-layouts, add_block(): source_tiles[gather_part]  14.3 us
    all_gather x1, blocking collectives, on_device(): source_rows = lax.all_gather(scaled, 'rep', axis=0, tiled=True)  12.2 us
  transfers between devices with their start and end apart: 14, of which 4 were waited for; matrix products, arithmetic and copies ran while one was open for 17% of the time, Pallas kernels for 0%

commit v1 on v0

v1 whole, which is shorter than its diff:
```python
import functools

import jax
import jax.numpy as jnp
from jax import lax
from jax.experimental import pallas as pl
from jax.experimental.pallas import tpu as pltpu
from jax.sharding import PartitionSpec as P

BOTH = ("rep", "blk")
VMEM = pl.BlockSpec(memory_space=pltpu.VMEM)
SMEM = pl.BlockSpec(memory_space=pltpu.SMEM)
PARAMS = pltpu.CompilerParams(vmem_limit_bytes=48 * 1024 * 1024)
BF = jnp.bfloat16
F32 = jnp.float32


def unroll_of(slot_total):
    return max(u for u in range(1, 17) if slot_total % u == 0)


def node_scale(degrees):
    return 1.0 / jnp.sqrt(degrees.astype(F32) + 1.0)


def move(value, target):
    rep_count, blk_count = lax.axis_size("rep"), lax.axis_size("blk")
    pairs = []
    for r in range(rep_count):
        for k in range(blk_count):
            to_r, to_k = target(r, k)
            pairs.append((r * blk_count + k, to_r * blk_count + to_k))
    return lax.ppermute(value, BOTH, pairs)


def swap_cores(value):
    return move(value, lambda r, k: (r, k ^ 1))


def rep_partner(stage):
    bits = (lax.axis_size("rep") - 1).bit_length()
    return lambda r, k: (r ^ (1 << ((stage + k % 2) % bits)), k)


def rep_place(rep_ids, rep_index, core):
    bits = (lax.axis_size("rep") - 1).bit_length()
    relative = rep_ids ^ rep_index
    place = jnp.zeros_like(relative)
    for stage in range(bits):
        plain = (relative >> stage) & 1
        turned = (relative >> ((stage + 1) % bits)) & 1
        place = place + (jnp.where(core == 0, plain, turned) << stage)
    return place


def pair_place(pair_ids, pair_index):
    pairs = lax.axis_size("blk") // 2
    if pairs == 4:
        return pair_ids ^ pair_index
    ahead = (pair_ids - pair_index) % pairs
    return jnp.where(ahead == 0, 0, jnp.where(ahead == 1, 1, jnp.where(ahead == pairs - 1, 2, 3)))


def pair_partner(place, back):
    blk_count = lax.axis_size("blk")

    def target(r, k):
        if blk_count == 8:
            return (r, k ^ (2 * place))
        step = {1: 2, 2: -2, 3: 4 if k % 2 == 0 else -4}[place]
        return (r, (k + (-step if back else step)) % blk_count)

    return target


def forward_kernel(tiles, unroll, place_ref, col_ref, count_ref, w_ref, x_ref, keep_ref, send_ref, total):
    total[...] = jnp.zeros_like(total)
    tile = w_ref.shape[-1]

    def step(i, carry):
        for u in range(unroll):
            t = i * unroll + u
            x_rows = pl.ds(pl.multiple_of(col_ref[t] * tile, tile), tile)
            part = jnp.dot(w_ref[t], x_ref[x_rows, :], preferred_element_type=F32)
            rows = pl.ds(pl.multiple_of(place_ref[t] * tile, tile), tile)
            total[rows, :] += part
        return carry

    lax.fori_loop(0, (count_ref[0] + unroll - 1) // unroll, step, 0)
    half = tiles // 2 * tile
    keep_ref[...] = total[:half, :].astype(BF)
    send_ref[...] = total[half : 2 * half, :].astype(BF)


def backward_kernel(col_tiles, unroll, place_ref, col_ref, count_ref, w_ref, *refs):
    block_refs, (out_ref, grads, total) = refs[:-3], refs[-3:]
    total[...] = jnp.zeros_like(total)
    tile = w_ref.shape[-1]
    first = 0
    for block_ref in block_refs:
        grads[first : first + block_ref.shape[0], :] = block_ref[...]
        first += block_ref.shape[0]

    def step(i, carry):
        for u in range(unroll):
            t = i * unroll + u
            g_rows = pl.ds(pl.multiple_of(place_ref[t] * tile, tile), tile)
            part = lax.dot_general(
                w_ref[t], grads[g_rows, :], (((0,), (0,)), ((), ())), preferred_element_type=F32
            )
            rows = pl.ds(pl.multiple_of(col_ref[t] * tile, tile), tile)
            total[rows, :] += part
        return carry

    lax.fori_loop(0, (count_ref[0] + unroll - 1) // unroll, step, 0)
    out_ref[...] = total[: col_tiles * tile, :].astype(BF)


def dense_kernel(
    grad_rows,
    core_ref, own_ref, p1_ref, p2_ref, p3_ref, scaled_ref, norm_ref, weight_ref, bias_ref, up_ref,
    hidden_ref, grad_ref, keep_ref, send_ref, full,
):
    norm = norm_ref[...]
    neighbor = (
        own_ref[...].astype(F32) + p1_ref[...].astype(F32) + p2_ref[...].astype(F32)
        + p3_ref[...].astype(F32) + scaled_ref[...].astype(F32)
    )
    aggregated = (norm * neighbor).astype(BF)
    weight = weight_ref[...]
    pre_act = jnp.dot(aggregated, weight, preferred_element_type=F32) + bias_ref[...]
    gate = 1.0 / (1.0 + jnp.exp(-pre_act))
    hidden_ref[...] = (pre_act * gate).astype(BF)
    pre_grad = (up_ref[...].astype(F32) * (gate + pre_act * gate * (1.0 - gate))).astype(BF)
    back = lax.dot_general(pre_grad, weight, (((1,), (1,)), ((), ())), preferred_element_type=F32)
    grad_ref[...] = (norm * back).astype(BF)
    full[...] = lax.dot_general(
        aggregated, pre_grad, (((0,), (0,)), ((), ())), preferred_element_type=F32
    )
    bias_rows = jnp.broadcast_to(
        jnp.sum(pre_grad.astype(F32), axis=0, keepdims=True), (8, pre_grad.shape[1])
    )
    core = core_ref[0]
    keep_ref[:grad_rows, :] = full[pl.ds(pl.multiple_of(core * grad_rows, grad_rows), grad_rows), :]
    send_ref[:grad_rows, :] = full[pl.ds(pl.multiple_of((1 - core) * grad_rows, grad_rows), grad_rows), :]
    keep_ref[grad_rows:, :] = bias_rows
    send_ref[grad_rows:, :] = bias_rows


def on_device(
    features, degrees, tile_weights, tile_rows, tile_cols, tile_counts, weight, layer_bias, upstream
):
    row_count, feat_width = features.shape
    hid_width = weight.shape[1]
    slot_total, tile_size = tile_weights.shape[2], tile_weights.shape[-1]
    row_tiles = row_count // tile_size
    rep_count, blk_count = lax.axis_size("rep"), lax.axis_size("blk")
    rep_index, blk_index = lax.axis_index("rep"), lax.axis_index("blk")
    core, pair_index = blk_index % 2, blk_index // 2
    unroll = unroll_of(slot_total)
    places = 8
    window_tiles = places * row_tiles
    column_tiles = rep_count * row_tiles

    rows_dev, cols_dev, count_dev = tile_rows[0, 0], tile_cols[0, 0], tile_counts[0]
    used = jnp.arange(slot_total, dtype=jnp.int32) < count_dev[0]
    group = rows_dev // row_tiles
    row_place = pair_place(group // 2, pair_index) + jnp.where(group % 2 == core, 0, places // 2)
    row_place = row_place * row_tiles + rows_dev % row_tiles
    col_place = rep_place(cols_dev // row_tiles, rep_index, core) * row_tiles + cols_dev % row_tiles
    row_sum = jnp.where(used, row_place, window_tiles).astype(jnp.int32)
    row_read = jnp.where(used, row_place, 0).astype(jnp.int32)
    col_sum = jnp.where(used, col_place, column_tiles).astype(jnp.int32)
    col_read = jnp.where(used, col_place, 0).astype(jnp.int32)
    tiles_dev = tile_weights[0, 0]

    node_norm = node_scale(degrees)
    norm_wide = jnp.broadcast_to(node_norm[:, None], (row_count, feat_width))
    scaled = (node_norm[:, None] * features.astype(F32)).astype(BF)

    source = scaled
    stages = (rep_count - 1).bit_length()
    for stage in range(stages):
        source = jnp.concatenate([source, move(source, rep_partner(stage))], axis=0)

    half_rows = places // 2 * row_count
    keep, send = pl.pallas_call(
        functools.partial(forward_kernel, window_tiles, unroll),
        out_shape=[jax.ShapeDtypeStruct((half_rows, feat_width), BF)] * 2,
        in_specs=[SMEM, SMEM, SMEM, VMEM, VMEM],
        out_specs=[VMEM, VMEM],
        scratch_shapes=[pltpu.VMEM(((window_tiles + 1) * tile_size, feat_width), F32)],
        compiler_params=PARAMS,
        name="forward_tiles",
    )(row_sum, col_read, count_dev, tiles_dev, source)
    came = swap_cores(send)

    def block(array, place):
        return array[place * row_count : (place + 1) * row_count]

    sums = [
        (block(keep, q).astype(F32) + block(came, q).astype(F32)).astype(BF) for q in range(4)
    ]
    parts = [sums[0]] + [move(sums[q], pair_partner(q, False)) for q in (1, 2, 3)]

    grad_rows = feat_width // 2
    hidden, scaled_grad, grad_keep, grad_send = pl.pallas_call(
        functools.partial(dense_kernel, grad_rows),
        out_shape=[
            jax.ShapeDtypeStruct((row_count, hid_width), BF),
            jax.ShapeDtypeStruct((row_count, feat_width), BF),
            jax.ShapeDtypeStruct((grad_rows + 8, hid_width), F32),
            jax.ShapeDtypeStruct((grad_rows + 8, hid_width), F32),
        ],
        in_specs=[SMEM] + [VMEM] * 9,
        out_specs=[VMEM] * 4,
        scratch_shapes=[pltpu.VMEM((feat_width, hid_width), F32)],
        compiler_params=PARAMS,
        name="dense",
    )(
        core[None].astype(jnp.int32), *parts, scaled, norm_wide, weight, layer_bias[None], upstream
    )

    own_grads = [scaled_grad] + [move(scaled_grad, pair_partner(q, True)) for q in (1, 2, 3)]
    own_grads = jnp.concatenate(own_grads, axis=0)
    other_grads = swap_cores(own_grads)

    column_part = pl.pallas_call(
        functools.partial(backward_kernel, column_tiles, unroll),
        out_shape=jax.ShapeDtypeStruct((column_tiles * tile_size, feat_width), BF),
        in_specs=[SMEM, SMEM, SMEM, VMEM, VMEM, VMEM],
        out_specs=VMEM,
        scratch_shapes=[
            pltpu.VMEM((window_tiles * tile_size, feat_width), BF),
            pltpu.VMEM(((column_tiles + 1) * tile_size, feat_width), F32),
        ],
        compiler_params=PARAMS,
        name="backward_tiles",
    )(row_read, col_sum, count_dev, tiles_dev, own_grads, other_grads)

    for stage in reversed(range(stages)):
        half = column_part.shape[0] // 2
        came = move(column_part[half:], rep_partner(stage))
        column_part = column_part[:half].astype(F32) + came.astype(F32)
        if stage:
            column_part = column_part.astype(BF)
    feature_grad = (norm_wide * (column_part + scaled_grad.astype(F32))).astype(BF)

    grad = grad_keep + swap_cores(grad_send)
    for stage in range(stages):
        grad = grad + move(grad, lambda r, k: (r ^ (1 << stage), k))
    for bit in range(1, (blk_count - 1).bit_length()):
        grad = grad + move(grad, lambda r, k: (r, k ^ (1 << bit)))
    mine = grad[:grad_rows]
    other = swap_cores(mine)
    grad_scale = (row_count * rep_count * blk_count) ** (-0.5)
    weight_grad = jnp.where(
        core == 0, jnp.concatenate([mine, other]), jnp.concatenate([other, mine])
    )
    return (hidden, feature_grad, weight_grad * grad_scale, grad[grad_rows] * grad_scale)


def solution(mesh):
    placed = (
        P(("rep", "blk"), None),
        P(("rep", "blk")),
        P("rep", "blk", None, None, None),
        P("rep", "blk", None),
        P("rep", "blk", None),
        P("rep", "blk"),
        P(),
        P(),
        P(("rep", "blk"), None),
    )
    return jax.shard_map(
        on_device,
        mesh=mesh,
        in_specs=placed,
        out_specs=(P(("rep", "blk"), None), P(("rep", "blk"), None), P(), P()),
        check_vma=False,
    )
```

time: 261 us -> 87.3 us (0.33)
  blocking collectives: 62 us -> 0 us
  other arithmetic: 60.6 us -> 4.84 us
  local copies, waits for them, and re-layouts: 38.2 us -> 0.24 us
  matrix products: 19.2 us -> 0 us
  waiting for transfers between devices: 30.9 us -> 49.6 us
  between operations: 16.4 us -> 1.5 us
  starting transfers between devices: 32.8 us -> 19 us
  Pallas kernels: 0 us -> 11.9 us
    psum x1 -> x0, blocking collectives: 49.8 us -> none  [on_device(): weight_sum, bias_sum = lax.psum((local_weight, local_bias), ('rep', 'blk'))]
    scatter-add x12 -> x0, other arithmetic: 31.3 us -> none  [add_block(): jax.ops.segment_sum(products, segment_part, segment_total + 1)]
    ppermute x12 -> x18, waiting for transfers between devices: 20.7 us -> 49.6 us  [move(): return lax.ppermute(value, BOTH, pairs)]
    add x12 -> x5, other arithmetic: 19.4 us -> 0.06 us  [the longest x2 0.03 us: on_device(): grad = grad + move(grad, lambda r, k: (r, k ^ 1 << bit))]
    dot_general x15 -> x0, matrix products: 19.2 us -> none  [the longest x12 17 us: add_block(): jnp.einsum(pattern, weights_part, source_tiles[gather_part], preferred_el...]
    gather x12 -> x0, local copies, waits for them, and re-layouts: 14.3 us -> none  [add_block(): source_tiles[gather_part]]
    ppermute x12 -> x18, starting transfers between devices: 32.7 us -> 19 us  [move(): return lax.ppermute(value, BOTH, pairs)]
    all_gather x1 -> x0, blocking collectives: 12.2 us -> none  [on_device(): source_rows = lax.all_gather(scaled, 'rep', axis=0, tiled=True)]
  transfers between devices with their start and end apart: 14 -> 18, of which waited for: 4 -> 13; matrix products, arithmetic and copies ran while one was open for 17% -> 2% of each run, Pallas kernels for 0% -> 6%
where the time goes in v1:
time: 87.3 us; the launch traced here: 87.1 us
  waiting for transfers between devices  49.6 us (57%)
  starting transfers between devices  19 us (22%)
  Pallas kernels  11.9 us (14%)
  other arithmetic  4.84 us (6%)
  between operations  1.5 us (2%)
    ppermute x18, waiting for transfers between devices, move(): return lax.ppermute(value, BOTH, pairs)  49.6 us
    ppermute x18, starting transfers between devices, move(): return lax.ppermute(value, BOTH, pairs)  19 us
    pallas_call x1, Pallas kernels, on_device(): pl.pallas_call(functools.partial(backward_kernel, column_tiles, unroll),...  5.46 us
    pallas_call x1, Pallas kernels, on_device(): pl.pallas_call(functools.partial(forward_kernel, window_tiles, unroll), o...  5.31 us
  transfers between devices with their start and end apart: 18, of which 13 were waited for; matrix products, arithmetic and copies ran while one was open for 2% of the time, Pallas kernels for 6%

profile of v1, /device:TPU:0, one launch (start us, length us, event | category | flops | bytes accessed | tf_op | source)
XLA Modules:
  0.0 87.1 jit_solution(5696911911021720481)
XLA Ops:
  0.7 0.7 add_rsqrt_fusion
  1.4 1.0 %multiply_convert_fusion.1.scaled_ref = bf16[512,128]{1,0:T(8,128)(2,1)S(1)} fusion(bf16[512,128]{1,0:T(8,128)(2,1)} %param.9, f32[512]{0:T(512)S(1)} %add_rsqrt_fusion), kind=kLoop, calls=%fused_computation.8 | loop fusion | flops 196608 | bytes 264192 | tf_op jit(solution)/shard_map/convert_element_type | solution.py:179
  2.4 3.0 %collective-permute-start = (bf16[512,128]{1,0:T(8,128)(2,1)S(1)}, bf16[512,128]{1,0:T(8,128)(2,1)S(1)}, u32[]{:S(2)}, u32[]{:S(2)}) collective-permute-start(bf16[512,128]{1,0:T(8,128)(2,1)S(1)} %multiply_convert_fusion.1.scaled_ref), channel_id=1, source_target_pairs={{0,8},{1,17},{2,10},{3,19},{4,12},{5,21},{6,14},{7,23},{8,0},{9,25... | collective-permute-start | bytes 393224 | tf_op jit(solution)/shard_map/ppermute | solution.py:33
  6.1 0.7 fusion.4
  6.8 1.6 %collective-permute-done = bf16[512,128]{1,0:T(8,128)(2,1)S(1)} collective-permute-done((bf16[512,128]{1,0:T(8,128)(2,1)S(1)}, bf16[512,128]{1,0:T(8,128)(2,1)S(1)}, u32[]{:S(2)}, u32[]{:S(2)}) %collective-permute-start) | collective-permute-done | bytes 131104 | tf_op jit(solution)/shard_map/ppermute | solution.py:33
  8.4 2.1 %collective-permute-start.1 = (bf16[1024,128]{1,0:T(8,128)(2,1)S(1)}, bf16[1024,128]{1,0:T(8,128)(2,1)S(1)}, u32[]{:S(2)}, u32[]{:S(2)}) collective-permute-start(bf16[1024,128]{1,0:T(8,128)(2,1)S(1)} %pad_maximum_fusion.1), channel_id=1, source_target_pairs={{0,16},{1,9},{2,18},{3,11},{4,20},{5,13},{6,22},{7,15},{8,24},{9,1... | collective-permute-start | bytes 786440 | tf_op jit(solution)/shard_map/ppermute | solution.py:33
  10.5 4.3 %collective-permute-done.1 = bf16[1024,128]{1,0:T(8,128)(2,1)S(1)} collective-permute-done((bf16[1024,128]{1,0:T(8,128)(2,1)S(1)}, bf16[1024,128]{1,0:T(8,128)(2,1)S(1)}, u32[]{:S(2)}, u32[]{:S(2)}) %collective-permute-start.1) | collective-permute-done | bytes 262176 | tf_op jit(solution)/shard_map/ppermute | solution.py:33
  14.9 5.3 %forward_tiles.1 = (bf16[2048,128]{1,0:T(8,128)(2,1)S(1)}, bf16[2048,128]{1,0:T(8,128)(2,1)S(1)}) custom-call(s32[160]{0:T(256)S(1)} %fusion.7.place_ref, s32[160]{0:T(256)S(1)} %fusion.6.col_ref, s32[1]{0:T(128)} %bitcast.11.count_ref, bf16[160,128,128]{2,1,0:T(8,128)(2,1)} %bitcast.14, bf16[2048,128]{1,0:T(8,128)(2,1)S(1)} %pad_maximum_fusion.x_ref), custom_call_target="tpu_custom_call" | custom-call | tf_op jit(solution)/shard_map/forward_tiles/pallas_call | solution.py:187
  20.3 1.9 %collective-permute-done.2 = bf16[2048,128]{1,0:T(8,128)(2,1)S(1)} collective-permute-done((bf16[2048,128]{1,0:T(8,128)(2,1)S(1)}, bf16[2048,128]{1,0:T(8,128)(2,1)S(1)}, u32[]{:S(2)}, u32[]{:S(2)}) %collective-permute-start.2) | collective-permute-done | bytes 524320 | tf_op jit(solution)/shard_map/ppermute | solution.py:33
  22.4 3.9 %collective-permute-start.5 = (bf16[512,128]{1,0:T(8,128)(2,1)S(1)}, bf16[512,128]{1,0:T(8,128)(2,1)S(1)}, u32[]{:S(2)}, u32[]{:S(2)}) collective-permute-start(bf16[512,128]{1,0:T(8,128)(2,1)S(1)} %get-tuple-element.20), channel_id=1, source_target_pairs={{0,6},{1,7},{2,4},{3,5},{4,2},{5,3},{6,0},{7,1},{8,14},{9,15},{10,... | collective-permute-start | bytes 393224 | tf_op jit(solution)/shard_map/ppermute | solution.py:33
  26.2 0.6 collective-permute-start.3
  26.9 3.8 %collective-permute-done.5.p3_ref = bf16[512,128]{1,0:T(8,128)(2,1)S(1)} collective-permute-done((bf16[512,128]{1,0:T(8,128)(2,1)S(1)}, bf16[512,128]{1,0:T(8,128)(2,1)S(1)}, u32[]{:S(2)}, u32[]{:S(2)}) %collective-permute-start.5) | collective-permute-done | bytes 131104 | tf_op jit(solution)/shard_map/ppermute | solution.py:33
  30.6 7.3 %collective-permute-done.4.p2_ref = bf16[512,128]{1,0:T(8,128)(2,1)S(1)} collective-permute-done((bf16[512,128]{1,0:T(8,128)(2,1)S(1)}, bf16[512,128]{1,0:T(8,128)(2,1)S(1)}, u32[]{:S(2)}, u32[]{:S(2)}) %collective-permute-start.4) | collective-permute-done | bytes 131104 | tf_op jit(solution)/shard_map/ppermute | solution.py:33
  38.1 1.1 %dense.1 = (bf16[512,256]{1,0:T(8,128)(2,1)}, bf16[512,128]{1,0:T(8,128)(2,1)S(1)}, f32[72,256]{1,0:T(8,128)S(1)}, f32[72,256]{1,0:T(8,128)S(1)}) custom-call(s32[1]{0:T(128)} %bitcast.core_ref, bf16[512,128]{1,0:T(8,128)(2,1)S(1)} %get-tuple-element.23.own_ref, bf16[512,128]{1,0:T(8,128)(2,1)S(1)} %collective-permute-done.3.p1_ref, ...), custom_call_target="tpu_custom_call" | custom-call | tf_op jit(solution)/shard_map/dense/pallas_call | solution.py:207
  39.2 2.5 %collective-permute-start.8 = (bf16[512,128]{1,0:T(8,128)(2,1)S(1)}, bf16[512,128]{1,0:T(8,128)(2,1)S(1)}, u32[]{:S(2)}, u32[]{:S(2)}) collective-permute-start(bf16[512,128]{1,0:T(8,128)(2,1)S(1)} %get-tuple-element.13), channel_id=1, source_target_pairs={{0,6},{1,7},{2,4},{3,5},{4,2},{5,3},{6,0},{7,1},{8,14},{9,15},{10,... | collective-permute-start | bytes 393224 | tf_op jit(solution)/shard_map/ppermute | solution.py:33
  41.6 1.0 %collective-permute-start.7 = (bf16[512,128]{1,0:T(8,128)(2,1)S(1)}, bf16[512,128]{1,0:T(8,128)(2,1)S(1)}, u32[]{:S(2)}, u32[]{:S(2)}) collective-permute-start(bf16[512,128]{1,0:T(8,128)(2,1)S(1)} %get-tuple-element.13), channel_id=1, source_target_pairs={{0,4},{1,5},{2,6},{3,7},{4,0},{5,1},{6,2},{7,3},{8,12},{9,13},{10,... | collective-permute-start | bytes 393224 | tf_op jit(solution)/shard_map/ppermute | solution.py:33
  42.7 2.7 %collective-permute-done.6 = bf16[512,128]{1,0:T(8,128)(2,1)S(1)} collective-permute-done((bf16[512,128]{1,0:T(8,128)(2,1)S(1)}, bf16[512,128]{1,0:T(8,128)(2,1)S(1)}, u32[]{:S(2)}, u32[]{:S(2)}) %collective-permute-start.6) | collective-permute-done | bytes 131104 | tf_op jit(solution)/shard_map/ppermute | solution.py:33
  45.4 8.3 %collective-permute-done.7 = bf16[512,128]{1,0:T(8,128)(2,1)S(1)} collective-permute-done((bf16[512,128]{1,0:T(8,128)(2,1)S(1)}, bf16[512,128]{1,0:T(8,128)(2,1)S(1)}, u32[]{:S(2)}, u32[]{:S(2)}) %collective-permute-start.7) | collective-permute-done | bytes 131104 | tf_op jit(solution)/shard_map/ppermute | solution.py:33
  53.8 0.5 collective-permute-start.12
  54.3 1.5 %collective-permute-done.12 = f32[72,256]{1,0:T(8,128)S(1)} collective-permute-done((f32[72,256]{1,0:T(8,128)S(1)}, f32[72,256]{1,0:T(8,128)S(1)}, u32[]{:S(2)}, u32[]{:S(2)}) %collective-permute-start.12) | collective-permute-done | bytes 73760 | tf_op jit(solution)/shard_map/ppermute | solution.py:33
  55.9 1.4 %collective-permute-start.13 = (f32[72,256]{1,0:T(8,128)S(1)}, f32[72,256]{1,0:T(8,128)S(1)}, u32[]{:S(2)}, u32[]{:S(2)}) collective-permute-start(f32[72,256]{1,0:T(8,128)S(1)} %add.89), channel_id=1, source_target_pairs={{0,8},{1,9},{2,10},{3,11},{4,12},{5,13},{6,14},{7,15},{8,0},{9,1},... | collective-permute-start | bytes 221192 | tf_op jit(solution)/shard_map/ppermute | solution.py:33
  57.2 5.5 %backward_tiles.1 = bf16[2048,128]{1,0:T(8,128)(2,1)S(1)} custom-call(s32[160]{0:T(256)S(1)} %get-tuple-element.24.place_ref, s32[160]{0:T(256)S(1)} %get-tuple-element.16.col_ref, s32[1]{0:T(128)} %bitcast.12.count_ref, bf16[160,128,128]{2,1,0:T(8,128)(2,1)} %bitcast.15, bf16[2048,128]{1,0:T(8,128)(2,1)S(1)} %constant_dynamic-update-slice_fusion.refs_0_, ...), custom_call_target="tpu_custom_call" | custom-call | tf_op jit(solution)/shard_map/backward_tiles/pallas_call | solution.py:228
  62.7 2.4 %collective-permute-start.10 = (bf16[1024,128]{1,0:T(8,128)(2,1)S(1)}, bf16[1024,128]{1,0:T(8,128)(2,1)S(1)}, u32[]{:S(2)}, u32[]{:S(2)}) collective-permute-start(bf16[1024,128]{1,0:T(8,128)(2,1)S(1)} %slice.61), channel_id=1, source_target_pairs={{0,16},{1,9},{2,18},{3,11},{4,20},{5,13},{6,22},{7,15},{8,24},{9,1... | collective-permute-start | bytes 786440 | tf_op jit(solution)/shard_map/ppermute | solution.py:33
  65.2 5.3 %collective-permute-done.14 = f32[72,256]{1,0:T(8,128)S(1)} collective-permute-done((f32[72,256]{1,0:T(8,128)S(1)}, f32[72,256]{1,0:T(8,128)S(1)}, u32[]{:S(2)}, u32[]{:S(2)}) %collective-permute-start.14) | collective-permute-done | bytes 73760 | tf_op jit(solution)/shard_map/ppermute | solution.py:33
  70.6 5.1 %collective-permute-done.15 = f32[72,256]{1,0:T(8,128)S(1)} collective-permute-done((f32[72,256]{1,0:T(8,128)S(1)}, f32[72,256]{1,0:T(8,128)S(1)}, u32[]{:S(2)}, u32[]{:S(2)}) %collective-permute-start.15) | collective-permute-done | bytes 73760 | tf_op jit(solution)/shard_map/ppermute | solution.py:33
  75.7 0.9 collective-permute-start.16
  76.6 4.5 %collective-permute-done.16 = f32[72,256]{1,0:T(8,128)S(1)} collective-permute-done((f32[72,256]{1,0:T(8,128)S(1)}, f32[72,256]{1,0:T(8,128)S(1)}, u32[]{:S(2)}, u32[]{:S(2)}) %collective-permute-start.16) | collective-permute-done | bytes 73760 | tf_op jit(solution)/shard_map/ppermute | solution.py:33
  81.3 0.5 collective-permute-start.11
  81.7 0.6 slice_multiply_fusion
  82.4 0.7 fusion
  83.1 3.2 %collective-permute-done.11 = bf16[512,128]{1,0:T(8,128)(2,1)S(1)} collective-permute-done((bf16[512,128]{1,0:T(8,128)(2,1)S(1)}, bf16[512,128]{1,0:T(8,128)(2,1)S(1)}, u32[]{:S(2)}, u32[]{:S(2)}) %collective-permute-start.11) | collective-permute-done | bytes 131104 | tf_op jit(solution)/shard_map/ppermute | solution.py:33
  86.3 0.8 multiply_convert_fusion
  (38 shorter events, 1.1 us)
Async XLA Ops:
  0.6 37.4 %copy-start = (bf16[512,256]{1,0:T(8,128)(2,1)S(1)}, bf16[512,256]{1,0:T(8,128)(2,1)}, u32[]{:S(2)}) copy-start(bf16[512,256]{1,0:T(8,128)(2,1)} %up_ref.1) | copy-start | bytes 786436
  0.6 37.4 %copy-start.2 = (f32[256]{0:T(256)S(1)}, f32[256]{0:T(256)}, u32[]{:S(2)}) copy-start(f32[256]{0:T(256)} %param.16) | copy-start | bytes 3076
  0.7 37.4 %copy-start.1 = (bf16[128,256]{1,0:T(8,128)(2,1)S(1)}, bf16[128,256]{1,0:T(8,128)(2,1)}, u32[]{:S(2)}) copy-start(bf16[128,256]{1,0:T(8,128)(2,1)} %weight_ref.1) | copy-start | bytes 196612
  2.4 6.0 %collective-permute-start = (bf16[512,128]{1,0:T(8,128)(2,1)S(1)}, bf16[512,128]{1,0:T(8,128)(2,1)S(1)}, u32[]{:S(2)}, u32[]{:S(2)}) collective-permute-start(bf16[512,128]{1,0:T(8,128)(2,1)S(1)} %multiply_convert_fusion.1.scaled_ref), channel_id=1, source_target_pairs={{0,8},{1,17},{2,10},{3,19},{4,12},{5,21},{6,14},{7,23},{8,0},{9,25... | collective-permute-start | bytes 393224 | tf_op jit(solution)/shard_map/ppermute | solution.py:33
  8.4 6.5 %collective-permute-start.1 = (bf16[1024,128]{1,0:T(8,128)(2,1)S(1)}, bf16[1024,128]{1,0:T(8,128)(2,1)S(1)}, u32[]{:S(2)}, u32[]{:S(2)}) collective-permute-start(bf16[1024,128]{1,0:T(8,128)(2,1)S(1)} %pad_maximum_fusion.1), channel_id=1, source_target_pairs={{0,16},{1,9},{2,18},{3,11},{4,20},{5,13},{6,22},{7,15},{8,24},{9,1... | collective-permute-start | bytes 786440 | tf_op jit(solution)/shard_map/ppermute | solution.py:33
  20.2 2.0 %collective-permute-start.2 = (bf16[2048,128]{1,0:T(8,128)(2,1)S(1)}, bf16[2048,128]{1,0:T(8,128)(2,1)S(1)}, u32[]{:S(2)}, u32[]{:S(2)}) collective-permute-start(bf16[2048,128]{1,0:T(8,128)(2,1)S(1)} %get-tuple-element.11), channel_id=1, source_target_pairs={{0,1},{1,0},{2,3},{3,2},{4,5},{5,4},{6,7},{7,6},{8,9},{9,8},{10,11... | collective-permute-start | bytes 1572872 | tf_op jit(solution)/shard_map/ppermute | solution.py:33
  22.4 8.3 %collective-permute-start.5 = (bf16[512,128]{1,0:T(8,128)(2,1)S(1)}, bf16[512,128]{1,0:T(8,128)(2,1)S(1)}, u32[]{:S(2)}, u32[]{:S(2)}) collective-permute-start(bf16[512,128]{1,0:T(8,128)(2,1)S(1)} %get-tuple-element.20), channel_id=1, source_target_pairs={{0,6},{1,7},{2,4},{3,5},{4,2},{5,3},{6,0},{7,1},{8,14},{9,15},{10,... | collective-permute-start | bytes 393224 | tf_op jit(solution)/shard_map/ppermute | solution.py:33
  26.2 11.7 %collective-permute-start.4 = (bf16[512,128]{1,0:T(8,128)(2,1)S(1)}, bf16[512,128]{1,0:T(8,128)(2,1)S(1)}, u32[]{:S(2)}, u32[]{:S(2)}) collective-permute-start(bf16[512,128]{1,0:T(8,128)(2,1)S(1)} %get-tuple-element.21), channel_id=1, source_target_pairs={{0,4},{1,5},{2,6},{3,7},{4,0},{5,1},{6,2},{7,3},{8,12},{9,13},{10,... | collective-permute-start | bytes 393224 | tf_op jit(solution)/shard_map/ppermute | solution.py:33
  26.2 11.7 %collective-permute-start.3 = (bf16[512,128]{1,0:T(8,128)(2,1)S(1)}, bf16[512,128]{1,0:T(8,128)(2,1)S(1)}, u32[]{:S(2)}, u32[]{:S(2)}) collective-permute-start(bf16[512,128]{1,0:T(8,128)(2,1)S(1)} %get-tuple-element.22), channel_id=1, source_target_pairs={{0,2},{1,3},{2,0},{3,1},{4,6},{5,7},{6,4},{7,5},{8,10},{9,11},{10,... | collective-permute-start | bytes 393224 | tf_op jit(solution)/shard_map/ppermute | solution.py:33
  39.2 6.2 %collective-permute-start.6 = (bf16[512,128]{1,0:T(8,128)(2,1)S(1)}, bf16[512,128]{1,0:T(8,128)(2,1)S(1)}, u32[]{:S(2)}, u32[]{:S(2)}) collective-permute-start(bf16[512,128]{1,0:T(8,128)(2,1)S(1)} %get-tuple-element.13), channel_id=1, source_target_pairs={{0,2},{1,3},{2,0},{3,1},{4,6},{5,7},{6,4},{7,5},{8,10},{9,11},{10,... | collective-permute-start | bytes 393224 | tf_op jit(solution)/shard_map/ppermute | solution.py:33
  39.2 14.6 %collective-permute-start.8 = (bf16[512,128]{1,0:T(8,128)(2,1)S(1)}, bf16[512,128]{1,0:T(8,128)(2,1)S(1)}, u32[]{:S(2)}, u32[]{:S(2)}) collective-permute-start(bf16[512,128]{1,0:T(8,128)(2,1)S(1)} %get-tuple-element.13), channel_id=1, source_target_pairs={{0,6},{1,7},{2,4},{3,5},{4,2},{5,3},{6,0},{7,1},{8,14},{9,15},{10,... | collective-permute-start | bytes 393224 | tf_op jit(solution)/shard_map/ppermute | solution.py:33
  41.6 12.1 %collective-permute-start.7 = (bf16[512,128]{1,0:T(8,128)(2,1)S(1)}, bf16[512,128]{1,0:T(8,128)(2,1)S(1)}, u32[]{:S(2)}, u32[]{:S(2)}) collective-permute-start(bf16[512,128]{1,0:T(8,128)(2,1)S(1)} %get-tuple-element.13), channel_id=1, source_target_pairs={{0,4},{1,5},{2,6},{3,7},{4,0},{5,1},{6,2},{7,3},{8,12},{9,13},{10,... | collective-permute-start | bytes 393224 | tf_op jit(solution)/shard_map/ppermute | solution.py:33
  53.8 3.5 %collective-permute-start.9 = (bf16[2048,128]{1,0:T(8,128)(2,1)S(1)}, bf16[2048,128]{1,0:T(8,128)(2,1)S(1)}, u32[]{:S(2)}, u32[]{:S(2)}) collective-permute-start(bf16[2048,128]{1,0:T(8,128)(2,1)S(1)} %constant_dynamic-update-slice_fusion.refs_0_), channel_id=1, source_target_pairs={{0,1},{1,0},{2,3},{3,2},{4,5},{5,4},{6,7},{7,6},{8,9},{9,8},{10,11... | collective-permute-start | bytes 1572872 | tf_op jit(solution)/shard_map/ppermute | solution.py:33
  53.8 2.0 %collective-permute-start.12 = (f32[72,256]{1,0:T(8,128)S(1)}, f32[72,256]{1,0:T(8,128)S(1)}, u32[]{:S(2)}, u32[]{:S(2)}) collective-permute-start(f32[72,256]{1,0:T(8,128)S(1)} %get-tuple-element.15), channel_id=1, source_target_pairs={{0,1},{1,0},{2,3},{3,2},{4,5},{5,4},{6,7},{7,6},{8,9},{9,8},{10,11... | collective-permute-start | bytes 221192 | tf_op jit(solution)/shard_map/ppermute | solution.py:33
  55.9 9.2 %collective-permute-start.13 = (f32[72,256]{1,0:T(8,128)S(1)}, f32[72,256]{1,0:T(8,128)S(1)}, u32[]{:S(2)}, u32[]{:S(2)}) collective-permute-start(f32[72,256]{1,0:T(8,128)S(1)} %add.89), channel_id=1, source_target_pairs={{0,8},{1,9},{2,10},{3,11},{4,12},{5,13},{6,14},{7,15},{8,0},{9,1},... | collective-permute-start | bytes 221192 | tf_op jit(solution)/shard_map/ppermute | solution.py:33
  62.7 18.4 %collective-permute-start.10 = (bf16[1024,128]{1,0:T(8,128)(2,1)S(1)}, bf16[1024,128]{1,0:T(8,128)(2,1)S(1)}, u32[]{:S(2)}, u32[]{:S(2)}) collective-permute-start(bf16[1024,128]{1,0:T(8,128)(2,1)S(1)} %slice.61), channel_id=1, source_target_pairs={{0,16},{1,9},{2,18},{3,11},{4,20},{5,13},{6,22},{7,15},{8,24},{9,1... | collective-permute-start | bytes 786440 | tf_op jit(solution)/shard_map/ppermute | solution.py:33
  65.1 5.4 %collective-permute-start.14 = (f32[72,256]{1,0:T(8,128)S(1)}, f32[72,256]{1,0:T(8,128)S(1)}, u32[]{:S(2)}, u32[]{:S(2)}) collective-permute-start(f32[72,256]{1,0:T(8,128)S(1)} %add.90), channel_id=1, source_target_pairs={{0,16},{1,17},{2,18},{3,19},{4,20},{5,21},{6,22},{7,23},{8,24},{9,... | collective-permute-start | bytes 221192 | tf_op jit(solution)/shard_map/ppermute | solution.py:33
  70.5 5.2 %collective-permute-start.15 = (f32[72,256]{1,0:T(8,128)S(1)}, f32[72,256]{1,0:T(8,128)S(1)}, u32[]{:S(2)}, u32[]{:S(2)}) collective-permute-start(f32[72,256]{1,0:T(8,128)S(1)} %add.91), channel_id=1, source_target_pairs={{0,2},{1,3},{2,0},{3,1},{4,6},{5,7},{6,4},{7,5},{8,10},{9,11},{10,... | collective-permute-start | bytes 221192 | tf_op jit(solution)/shard_map/ppermute | solution.py:33
  75.7 5.3 %collective-permute-start.16 = (f32[72,256]{1,0:T(8,128)S(1)}, f32[72,256]{1,0:T(8,128)S(1)}, u32[]{:S(2)}, u32[]{:S(2)}) collective-permute-start(f32[72,256]{1,0:T(8,128)S(1)} %add.92), channel_id=1, source_target_pairs={{0,4},{1,5},{2,6},{3,7},{4,0},{5,1},{6,2},{7,3},{8,12},{9,13},{10,... | collective-permute-start | bytes 221192 | tf_op jit(solution)/shard_map/ppermute | solution.py:33
  81.1 1.3 %collective-permute-start.17 = (f32[64,256]{1,0:T(8,128)S(1)}, f32[64,256]{1,0:T(8,128)S(1)}, u32[]{:S(2)}, u32[]{:S(2)}) collective-permute-start(f32[64,256]{1,0:T(8,128)S(1)} %slice.64), channel_id=1, source_target_pairs={{0,1},{1,0},{2,3},{3,2},{4,5},{5,4},{6,7},{7,6},{8,9},{9,8},{10,11... | collective-permute-start | bytes 196616 | tf_op jit(solution)/shard_map/ppermute | solution.py:33
  81.3 5.0 %collective-permute-start.11 = (bf16[512,128]{1,0:T(8,128)(2,1)S(1)}, bf16[512,128]{1,0:T(8,128)(2,1)S(1)}, u32[]{:S(2)}, u32[]{:S(2)}) collective-permute-start(bf16[512,128]{1,0:T(8,128)(2,1)S(1)} %slice.63), channel_id=1, source_target_pairs={{0,8},{1,17},{2,10},{3,19},{4,12},{5,21},{6,14},{7,23},{8,0},{9,25... | collective-permute-start | bytes 393224 | tf_op jit(solution)/shard_map/ppermute | solution.py:33

commit v2 on v1

v2 whole, which is shorter than its diff:
```python
import functools

import jax
import jax.numpy as jnp
from jax import lax
from jax.experimental import pallas as pl
from jax.experimental.pallas import tpu as pltpu
from jax.sharding import PartitionSpec as P

BOTH = ("rep", "blk")
VMEM = pl.BlockSpec(memory_space=pltpu.VMEM)
SMEM = pl.BlockSpec(memory_space=pltpu.SMEM)
ANY = pl.BlockSpec(memory_space=pl.ANY)
BF = jnp.bfloat16
F32 = jnp.float32
CORES = 2


def params(mib):
    return pltpu.CompilerParams(vmem_limit_bytes=mib * 1024 * 1024)


def cost(flops, size):
    return pl.CostEstimate(flops=flops, bytes_accessed=size, transcendentals=0)


def node_scale(degrees):
    return 1.0 / jnp.sqrt(degrees.astype(F32) + 1.0)


def move(value, target):
    rep_count, blk_count = lax.axis_size("rep"), lax.axis_size("blk")
    pairs = []
    for r in range(rep_count):
        for k in range(blk_count):
            to_r, to_k = target(r, k)
            pairs.append((r * blk_count + k, to_r * blk_count + to_k))
    return lax.ppermute(value, BOTH, pairs)


def swap_cores(value):
    return move(value, lambda r, k: (r, k ^ 1))


def rep_partner(stage):
    bits = (lax.axis_size("rep") - 1).bit_length()
    return lambda r, k: (r ^ (1 << ((stage + k % 2) % bits)), k)


def rep_place(rep_ids, rep_index, core):
    bits = (lax.axis_size("rep") - 1).bit_length()
    relative = rep_ids ^ rep_index
    place = jnp.zeros_like(relative)
    for stage in range(bits):
        plain = (relative >> stage) & 1
        turned = (relative >> ((stage + 1) % bits)) & 1
        place = place + (jnp.where(core == 0, plain, turned) << stage)
    return place


def pair_at(place, pair_index, core):
    pairs = lax.axis_size("blk") // CORES
    if pairs == 4:
        return pair_index ^ (0, 1, 3, 2)[place]
    step = (0, 1, -1, jnp.where(core == 0, -2, 2))[place]
    return (pair_index + step) % pairs


def pair_partner(place, back):
    blk_count = lax.axis_size("blk")

    def target(r, k):
        if place == 3:
            return (r, (k + (3 if k % 2 else -3)) % blk_count)
        if blk_count == 8:
            return (r, k ^ {1: 2, 2: 6}[place])
        step = {1: 2, 2: -2}[place]
        return (r, (k + (-step if back else step)) % blk_count)

    return target


def stage_kernel(w_ref, out_ref, sem):
    copy = pltpu.make_async_copy(w_ref, out_ref, sem)
    copy.start()
    copy.wait()


def gather_blocks(block_refs, held):
    first = 0
    for block_ref in block_refs:
        held[first : first + block_ref.shape[0], :] = block_ref[...]
        first += block_ref.shape[0]


def over_slots(low, high, unroll, slot_total, body):
    def step(i, carry):
        for u in range(unroll):
            t = low + i * unroll + u
            body(jnp.minimum(t, slot_total - 1), t < high)
        return carry

    lax.fori_loop(0, (high - low + unroll - 1) // unroll, step, 0)


def aligned(index, tile):
    return pl.ds(pl.multiple_of(index * tile, tile), tile)


def forward_kernel(places, unroll, bounds_ref, row_ref, col_ref, w_ref, *refs):
    count = 2 if 3 not in places else 1
    x_refs, out_refs, (held, total) = refs[: -2 - count], refs[-2 - count : -2], refs[-2:]
    tile = w_ref.shape[-1]
    block_tiles = x_refs[0].shape[0] // tile
    gather_blocks(x_refs, held)
    total[...] = jnp.zeros_like(total)
    spare = total.shape[0] // tile - 1
    for n, place in enumerate(places):

        def body(t, used):
            row = row_ref[t]
            if count == 1:
                row = row % block_tiles
            row = jnp.where(used, row + n * 2 * block_tiles, spare)
            part = jnp.dot(w_ref[t], held[aligned(col_ref[t], tile), :], preferred_element_type=F32)
            total[aligned(row, tile), :] += part

        over_slots(bounds_ref[place], bounds_ref[4 + place], unroll, w_ref.shape[0], body)
    rows = block_tiles * tile
    for n in range(len(places)):
        for side in range(count):
            first = (n * count + side) * rows
            out_refs[side][n * rows : (n + 1) * rows, :] = total[first : first + rows, :].astype(BF)


def backward_kernel(place, unroll, first_call, last_call, bounds_ref, row_ref, col_ref, w_ref, *refs):
    held = refs[-1]
    tile = w_ref.shape[-1]
    if last_call:
        old_ref, *block_refs = refs[:2]
        out_refs, total = refs[2:-2], refs[-2]
        total[...] = old_ref[...]
    elif first_call:
        block_refs, total = refs[:-2], refs[-2]
        total[...] = jnp.zeros_like(total)
    else:
        old_ref, *block_refs = refs[:-2]
        total = refs[-2]
        total[...] = old_ref[...]
    gather_blocks(block_refs, held)
    spare = total.shape[0] // tile - 1
    held_tiles = held.shape[0] // tile

    def body(t, used):
        row = row_ref[t]
        if len(block_refs) == 1:
            row = row % held_tiles
        part = lax.dot_general(
            w_ref[t], held[aligned(row, tile), :], (((0,), (0,)), ((), ())), preferred_element_type=F32
        )
        total[aligned(jnp.where(used, col_ref[t], spare), tile), :] += part

    over_slots(bounds_ref[place], bounds_ref[4 + place], unroll, w_ref.shape[0], body)
    if last_call:
        rows = out_refs[0].shape[0]
        for n, out_ref in enumerate(out_refs):
            out_ref[...] = total[n * rows : (n + 1) * rows, :].astype(out_ref.dtype)


def dense_kernel(
    own_ref, p1_ref, p2_ref, p3_ref, scaled_ref, norm_ref, weight_ref, bias_ref, up_ref,
    hidden_ref, grad_ref, aggregated_ref, pre_grad_ref,
):
    norm = norm_ref[...]
    neighbor = (
        own_ref[...].astype(F32) + p1_ref[...].astype(F32) + p2_ref[...].astype(F32)
        + p3_ref[...].astype(F32) + scaled_ref[...].astype(F32)
    )
    aggregated = (norm * neighbor).astype(BF)
    weight = weight_ref[...]
    pre_act = jnp.dot(aggregated, weight, preferred_element_type=F32) + bias_ref[...]
    gate = 1.0 / (1.0 + jnp.exp(-pre_act))
    hidden_ref[...] = (pre_act * gate).astype(BF)
    pre_grad = (up_ref[...].astype(F32) * (gate + pre_act * gate * (1.0 - gate))).astype(BF)
    back = lax.dot_general(pre_grad, weight, (((1,), (1,)), ((), ())), preferred_element_type=F32)
    grad_ref[...] = (norm * back).astype(BF)
    aggregated_ref[...] = aggregated
    pre_grad_ref[...] = pre_grad


def weight_kernel(core_ref, aggregated_ref, pre_grad_ref, keep_ref, send_ref, full):
    grad_rows = full.shape[0] // CORES
    pre_grad = pre_grad_ref[...]
    full[...] = lax.dot_general(
        aggregated_ref[...], pre_grad, (((0,), (0,)), ((), ())), preferred_element_type=F32
    )
    bias_rows = jnp.broadcast_to(
        jnp.sum(pre_grad.astype(F32), axis=0, keepdims=True), (8, pre_grad.shape[1])
    )
    core = core_ref[0]
    keep_ref[:grad_rows, :] = full[aligned(core, grad_rows), :]
    send_ref[:grad_rows, :] = full[aligned(1 - core, grad_rows), :]
    keep_ref[grad_rows:, :] = bias_rows
    send_ref[grad_rows:, :] = bias_rows


def on_device(
    features, degrees, tile_weights, tile_rows, tile_cols, tile_counts, weight, layer_bias, upstream
):
    row_count, feat_width = features.shape
    hid_width = weight.shape[1]
    slot_total, tile = tile_weights.shape[2], tile_weights.shape[-1]
    row_tiles = row_count // tile
    rep_count, blk_count = lax.axis_size("rep"), lax.axis_size("blk")
    rep_index, blk_index = lax.axis_index("rep"), lax.axis_index("blk")
    core, pair_index = blk_index % CORES, blk_index // CORES
    stages = (rep_count - 1).bit_length()
    col_tiles = rep_count * row_tiles
    block_shape = jax.ShapeDtypeStruct((row_count, feat_width), BF)

    rows_dev, cols_dev, count_dev = tile_rows[0, 0], tile_cols[0, 0], tile_counts[0, 0]
    used = jnp.arange(slot_total, dtype=jnp.int32) < count_dev
    group = rows_dev // row_tiles
    row_place = jnp.where(group % CORES == core, 0, row_tiles) + rows_dev % row_tiles
    col_place = rep_place(cols_dev // row_tiles, rep_index, core) * row_tiles + cols_dev % row_tiles
    pair_ids = jnp.stack([pair_at(place, pair_index, core) for place in range(4)])
    pair_ids = jnp.concatenate([pair_ids, pair_ids + 1])
    bounds = jnp.sum(used & (group // CORES < pair_ids[:, None]), axis=1).astype(jnp.int32)
    row_place, col_place = row_place.astype(jnp.int32), col_place.astype(jnp.int32)

    node_norm = node_scale(degrees)
    norm_wide = jnp.broadcast_to(node_norm[:, None], (row_count, feat_width))
    scaled = (node_norm[:, None] * features.astype(F32)).astype(BF)

    source = [scaled]
    for stage in range(stages):
        source = source + [move(part, rep_partner(stage)) for part in source]

    tiles_dev = pl.pallas_call(
        stage_kernel,
        out_shape=jax.ShapeDtypeStruct((slot_total, tile, tile), BF),
        in_specs=[ANY],
        out_specs=VMEM,
        scratch_shapes=[pltpu.SemaphoreType.DMA],
        compiler_params=params(16),
        cost_estimate=cost(0, 2 * slot_total * tile * tile * 2),
        name="stage_tiles",
    )(tile_weights[0, 0])

    def forward(places, unroll):
        sides = 1 if 3 in places else 2
        shape = jax.ShapeDtypeStruct((len(places) * row_count, feat_width), BF)
        return pl.pallas_call(
            functools.partial(forward_kernel, places, unroll),
            out_shape=[shape] * sides,
            in_specs=[SMEM, SMEM, SMEM] + [VMEM] * (1 + rep_count),
            out_specs=[VMEM] * sides,
            scratch_shapes=[
                pltpu.VMEM((col_tiles * tile, feat_width), BF),
                pltpu.VMEM(((len(places) * sides * row_tiles + 1) * tile, feat_width), F32),
            ],
            compiler_params=params(16),
            cost_estimate=cost(2 * 48 * len(places) * tile**3, 2**20),
            name="forward_" + "_".join(map(str, places)),
        )(bounds, row_place, col_place, tiles_dev, *source)

    def add(a, b):
        return (a.astype(F32) + b.astype(F32)).astype(BF)

    (part3,) = forward((3,), 12)
    came3 = move(part3, pair_partner(3, False))
    keep2, send2 = forward((2,), 16)
    came2 = move(add(keep2, swap_cores(send2)), pair_partner(2, False))
    keep01, send01 = forward((0, 1), 16)
    sum01 = add(keep01, swap_cores(send01))
    came1 = move(sum01[row_count:], pair_partner(1, False))

    hidden, scaled_grad, aggregated, pre_grad = pl.pallas_call(
        dense_kernel,
        out_shape=[
            jax.ShapeDtypeStruct((row_count, hid_width), BF),
            block_shape,
            block_shape,
            jax.ShapeDtypeStruct((row_count, hid_width), BF),
        ],
        in_specs=[VMEM] * 9,
        out_specs=[VMEM] * 4,
        compiler_params=params(16),
        cost_estimate=cost(2**27, 2**20),
        name="dense",
    )(sum01[:row_count], came1, came2, came3, scaled, norm_wide, weight, layer_bias[None], upstream)

    grads2 = move(scaled_grad, pair_partner(2, True))
    grads3 = move(scaled_grad, pair_partner(3, True))
    grads1 = move(scaled_grad, pair_partner(1, True))

    grad_rows = feat_width // CORES
    grad_shape = jax.ShapeDtypeStruct((grad_rows + 8, hid_width), F32)
    grad_keep, grad_send = pl.pallas_call(
        weight_kernel,
        out_shape=[grad_shape] * 2,
        in_specs=[SMEM, VMEM, VMEM],
        out_specs=[VMEM] * 2,
        scratch_shapes=[pltpu.VMEM((feat_width, hid_width), F32)],
        compiler_params=params(16),
        cost_estimate=cost(2**25, 2**20),
        name="weight_terms",
    )(core[None].astype(jnp.int32), aggregated, pre_grad)

    total_shape = jax.ShapeDtypeStruct(((col_tiles + 1) * tile, feat_width), F32)

    def backward(place, unroll, old, blocks):
        last = place == 3
        out_shape = [total_shape]
        scratch = [pltpu.VMEM((len(blocks) * row_count, feat_width), BF)]
        if last:
            out_shape = [jax.ShapeDtypeStruct((row_count, feat_width), F32)] + [block_shape] * (rep_count - 1)
            scratch = [pltpu.VMEM(total_shape.shape, F32)] + scratch
        return pl.pallas_call(
            functools.partial(backward_kernel, place, unroll, old is None, last),
            out_shape=out_shape,
            in_specs=[SMEM, SMEM, SMEM] + [VMEM] * (1 + (old is not None) + len(blocks)),
            out_specs=[VMEM] * len(out_shape),
            scratch_shapes=scratch,
            input_output_aliases={} if old is None or last else {4: 0},
            compiler_params=params(16),
            cost_estimate=cost(2 * 48 * tile**3, 2**20),
            name=f"backward_{place}",
        )(bounds, row_place, col_place, tiles_dev, *([] if old is None else [old]), *blocks)

    (total,) = backward(0, 16, None, [scaled_grad, swap_cores(scaled_grad)])
    (total,) = backward(1, 16, total, [grads1, swap_cores(grads1)])
    (total,) = backward(2, 16, total, [grads2, swap_cores(grads2)])
    columns = backward(3, 12, total, [grads3])

    for stage in reversed(range(stages)):
        half = len(columns) // 2
        order = range(half - 1, -1, -1)
        came = {n: move(columns[half + n], rep_partner(stage)) for n in order}
        columns = [
            (columns[n].astype(F32) + came[n].astype(F32)).astype(BF if n else F32) for n in range(half)
        ]
    feature_grad = (norm_wide * (columns[0] + scaled_grad.astype(F32))).astype(BF)

    grad = grad_keep + swap_cores(grad_send)
    for stage in range(stages):
        grad = grad + move(grad, rep_partner(stage))
    for bit in range(1, (blk_count - 1).bit_length()):
        grad = grad + move(grad, lambda r, k: (r, k ^ (1 << bit)))
    mine = grad[:grad_rows]
    other = swap_cores(mine)
    grad_scale = (row_count * rep_count * blk_count) ** (-0.5)
    weight_grad = jnp.where(
        core == 0, jnp.concatenate([mine, other]), jnp.concatenate([other, mine])
    )
    return (hidden, feature_grad, weight_grad * grad_scale, grad[grad_rows] * grad_scale)


def solution(mesh):
    placed = (
        P(("rep", "blk"), None),
        P(("rep", "blk")),
        P("rep", "blk", None, None, None),
        P("rep", "blk", None),
        P("rep", "blk", None),
        P("rep", "blk"),
        P(),
        P(),
        P(("rep", "blk"), None),
    )
    return jax.shard_map(
        on_device,
        mesh=mesh,
        in_specs=placed,
        out_specs=(P(("rep", "blk"), None), P(("rep", "blk"), None), P(), P()),
        check_vma=False,
    )
```

time: 87.3 us -> 71.1 us (0.81)
  waiting for transfers between devices: 49.6 us -> 21.8 us
  starting transfers between devices: 19 us -> 25.8 us
  local copies, waits for them, and re-layouts: 0.24 us -> 2.74 us
  Pallas kernels: 11.9 us -> 13.8 us
    ppermute x18 -> x23, waiting for transfers between devices: 49.6 us -> 21.8 us  [move(): return lax.ppermute(value, BOTH, pairs)]
    ppermute x18 -> x23, starting transfers between devices: 19 us -> 25.8 us  [move(): return lax.ppermute(value, BOTH, pairs)]
    unnamed x9 -> x8, local copies, waits for them, and re-layouts: 0.06 us -> 2.51 us
    pallas_call x3 -> x10, Pallas kernels: 11.9 us -> 13.8 us  [the longest x4 6.69 us: backward(): pl.pallas_call(functools.partial(backward_kernel, place, unroll, old is N...]
  transfers between devices with their start and end apart: 18 -> 23, of which waited for: 13 -> 9; matrix products, arithmetic and copies ran while one was open for 2% -> 4% of each run, Pallas kernels for 6% -> 16%
where the time goes in v2:
time: 71.1 us; the launch traced here: 70.7 us
  starting transfers between devices  25.8 us (36%)
  waiting for transfers between devices  21.8 us (31%)
  Pallas kernels  13.8 us (19%)
  other arithmetic  4.95 us (7%)
  local copies, waits for them, and re-layouts  2.74 us (4%)
  between operations  1.56 us (2%)
    ppermute x23, starting transfers between devices, move(): return lax.ppermute(value, BOTH, pairs)  25.8 us
    ppermute x23, waiting for transfers between devices, move(): return lax.ppermute(value, BOTH, pairs)  21.8 us
    pallas_call x4, Pallas kernels, backward(): pl.pallas_call(functools.partial(backward_kernel, place, unroll, old is N...  6.69 us
    pallas_call x3, Pallas kernels, forward(): pl.pallas_call(functools.partial(forward_kernel, places, unroll), out_sha...  5.44 us
    unnamed x8, local copies, waits for them, and re-layouts  2.51 us
  transfers between devices with their start and end apart: 23, of which 9 were waited for; matrix products, arithmetic and copies ran while one was open for 4% of the time, Pallas kernels for 16%

profile of v2, /device:TPU:0, one launch (start us, length us, event | category | flops | bytes accessed | tf_op | source)
XLA Modules:
  0.0 70.7 jit_solution(6640478687213842493)
XLA Ops:
  1.3 1.0 %multiply_convert_fusion.1.refs_0_.scaled_ref = bf16[512,128]{1,0:T(8,128)(2,1)S(1)} fusion(bf16[512,128]{1,0:T(8,128)(2,1)} %param.9, f32[512]{0:T(512)S(1)} %add_rsqrt_fusion), kind=kLoop, calls=%fused_computation.4 | loop fusion | flops 196608 | bytes 264192 | tf_op jit(solution)/shard_map/convert_element_type | solution.py:233
  2.4 3.0 %collective-permute-start = (bf16[512,128]{1,0:T(8,128)(2,1)S(1)}, bf16[512,128]{1,0:T(8,128)(2,1)S(1)}, u32[]{:S(2)}, u32[]{:S(2)}) collective-permute-start(bf16[512,128]{1,0:T(8,128)(2,1)S(1)} %multiply_convert_fusion.1.refs_0_.scaled_ref), channel_id=1, source_target_pairs={{0,8},{1,17},{2,10},{3,19},{4,12},{5,21},{6,14},{7,23},{8,0},{9,25... | collective-permute-start | bytes 393224 | tf_op jit(solution)/shard_map/ppermute | solution.py:38
  5.4 1.5 %collective-permute-start.1 = (bf16[512,128]{1,0:T(8,128)(2,1)S(1)}, bf16[512,128]{1,0:T(8,128)(2,1)S(1)}, u32[]{:S(2)}, u32[]{:S(2)}) collective-permute-start(bf16[512,128]{1,0:T(8,128)(2,1)S(1)} %multiply_convert_fusion.1.refs_0_.scaled_ref), channel_id=1, source_target_pairs={{0,16},{1,9},{2,18},{3,11},{4,20},{5,13},{6,22},{7,15},{8,24},{9,1... | collective-permute-start | bytes 393224 | tf_op jit(solution)/shard_map/ppermute | solution.py:38
  8.3 0.9 %collective-permute-done.refs_1_ = bf16[512,128]{1,0:T(8,128)(2,1)S(1)} collective-permute-done((bf16[512,128]{1,0:T(8,128)(2,1)S(1)}, bf16[512,128]{1,0:T(8,128)(2,1)S(1)}, u32[]{:S(2)}, u32[]{:S(2)}) %collective-permute-start) | collective-permute-done | bytes 131104 | tf_op jit(solution)/shard_map/ppermute | solution.py:38
  9.1 1.6 %collective-permute-start.2 = (bf16[512,128]{1,0:T(8,128)(2,1)S(1)}, bf16[512,128]{1,0:T(8,128)(2,1)S(1)}, u32[]{:S(2)}, u32[]{:S(2)}) collective-permute-start(bf16[512,128]{1,0:T(8,128)(2,1)S(1)} %collective-permute-done.refs_1_), channel_id=1, source_target_pairs={{0,16},{1,9},{2,18},{3,11},{4,20},{5,13},{6,22},{7,15},{8,24},{9,1... | collective-permute-start | bytes 393224 | tf_op jit(solution)/shard_map/ppermute | solution.py:38
  10.9 2.5 %copy-done = bf16[1,1,160,128,128]{4,3,2,1,0:T(8,128)(2,1)S(1)} copy-done((bf16[1,1,160,128,128]{4,3,2,1,0:T(8,128)(2,1)S(1)}, bf16[1,1,160,128,128]{4,3,2,1,0:T(8,128)(2,1)}, u32[]{:S(2)}) %copy-start) | copy-done | bytes 5242904
  14.1 1.6 %forward_2.1 = (bf16[512,128]{1,0:T(8,128)(2,1)S(1)}, bf16[512,128]{1,0:T(8,128)(2,1)S(1)}) custom-call(s32[8]{0:T(128)S(1)} %convert_reduce_fusion.bounds_ref, s32[160]{0:T(256)S(1)} %get-tuple-element.32.row_ref, s32[160]{0:T(256)S(1)} %get-tuple-element.36.col_ref, bf16[160,128,128]{2,1,0:T(8,128)(2,1)S(1)} %stage_tiles.1.w_ref, ...), custom_call_target="tpu_custom_call" | custom-call | flops 201326592 | bytes 1048576 | tf_op jit(solution)/shard_map/forward_2/pallas_call | solution.py:253
  15.8 2.9 %forward_0_1.1 = (bf16[1024,128]{1,0:T(8,128)(2,1)S(1)}, bf16[1024,128]{1,0:T(8,128)(2,1)S(1)}) custom-call(s32[8]{0:T(128)S(1)} %convert_reduce_fusion.bounds_ref, s32[160]{0:T(256)S(1)} %get-tuple-element.32.row_ref, s32[160]{0:T(256)S(1)} %get-tuple-element.36.col_ref, bf16[160,128,128]{2,1,0:T(8,128)(2,1)S(1)} %stage_tiles.1.w_ref, ...), custom_call_target="tpu_custom_call" | custom-call | flops 402653184 | bytes 1048576 | tf_op jit(solution)/shard_map/forward_0_1/pallas_call | solution.py:253
  19.0 0.9 %forward_3.1 = bf16[512,128]{1,0:T(8,128)(2,1)S(1)} custom-call(s32[8]{0:T(128)S(1)} %convert_reduce_fusion.bounds_ref, s32[160]{0:T(256)S(1)} %get-tuple-element.32.row_ref, s32[160]{0:T(256)S(1)} %get-tuple-element.36.col_ref, bf16[160,128,128]{2,1,0:T(8,128)(2,1)S(1)} %stage_tiles.1.w_ref, bf16[512,128]{1,0:T(8,128)(2,1)S(1)} %multiply_convert_fusion.1.refs_0_.scaled_ref, ...), custom_call_target="tpu_custom_call" | custom-call | flops 201326592 | bytes 1048576 | tf_op jit(solution)/shard_map/forward_3/pallas_call | solution.py:253
  19.9 3.3 %collective-permute-start.7 = (bf16[512,128]{1,0:T(8,128)(2,1)S(1)}, bf16[512,128]{1,0:T(8,128)(2,1)S(1)}, u32[]{:S(2)}, u32[]{:S(2)}) collective-permute-start(bf16[512,128]{1,0:T(8,128)(2,1)S(1)} %forward_3.1), channel_id=1, source_target_pairs={{0,5},{1,4},{2,7},{3,6},{4,1},{5,0},{6,3},{7,2},{8,13},{9,12},{10,... | collective-permute-start | bytes 393224 | tf_op jit(solution)/shard_map/ppermute | solution.py:38
  23.2 1.4 %collective-permute-start.6 = (bf16[512,128]{1,0:T(8,128)(2,1)S(1)}, bf16[512,128]{1,0:T(8,128)(2,1)S(1)}, u32[]{:S(2)}, u32[]{:S(2)}) collective-permute-start(bf16[512,128]{1,0:T(8,128)(2,1)S(1)} %add_convert_fusion.2), channel_id=1, source_target_pairs={{0,6},{1,7},{2,4},{3,5},{4,2},{5,3},{6,0},{7,1},{8,14},{9,15},{10,... | collective-permute-start | bytes 393224 | tf_op jit(solution)/shard_map/ppermute | solution.py:38
  24.8 7.5 %collective-permute-done.7.p3_ref = bf16[512,128]{1,0:T(8,128)(2,1)S(1)} collective-permute-done((bf16[512,128]{1,0:T(8,128)(2,1)S(1)}, bf16[512,128]{1,0:T(8,128)(2,1)S(1)}, u32[]{:S(2)}, u32[]{:S(2)}) %collective-permute-start.7) | collective-permute-done | bytes 131104 | tf_op jit(solution)/shard_map/ppermute | solution.py:38
  32.4 2.2 %collective-permute-done.4.p1_ref = bf16[512,128]{1,0:T(8,128)(2,1)S(1)} collective-permute-done((bf16[512,128]{1,0:T(8,128)(2,1)S(1)}, bf16[512,128]{1,0:T(8,128)(2,1)S(1)}, u32[]{:S(2)}, u32[]{:S(2)}) %collective-permute-start.4) | collective-permute-done | bytes 131104 | tf_op jit(solution)/shard_map/ppermute | solution.py:38
  34.7 1.1 %dense.1 = (bf16[512,256]{1,0:T(8,128)(2,1)}, bf16[512,128]{1,0:T(8,128)(2,1)S(1)}, bf16[512,128]{1,0:T(8,128)(2,1)S(1)}, bf16[512,256]{1,0:T(8,128)(2,1)S(1)}) custom-call(bf16[512,128]{1,0:T(8,128)(2,1)S(1)} %get-tuple-element.35.own_ref, bf16[512,128]{1,0:T(8,128)(2,1)S(1)} %collective-permute-done.4.p1_ref, ...), custom_call_target="tpu_custom_call" | custom-call | flops 134217728 | bytes 1048576 | tf_op jit(solution)/shard_map/dense/pallas_call | solution.py:278
  35.8 1.8 %collective-permute-start.9 = (bf16[512,128]{1,0:T(8,128)(2,1)S(1)}, bf16[512,128]{1,0:T(8,128)(2,1)S(1)}, u32[]{:S(2)}, u32[]{:S(2)}) collective-permute-start(bf16[512,128]{1,0:T(8,128)(2,1)S(1)} %get-tuple-element.23.refs_0_), channel_id=1, source_target_pairs={{0,2},{1,3},{2,0},{3,1},{4,6},{5,7},{6,4},{7,5},{8,10},{9,11},{10,... | collective-permute-start | bytes 393224 | tf_op jit(solution)/shard_map/ppermute | solution.py:38
  37.6 3.4 %collective-permute-start.11 = (bf16[512,128]{1,0:T(8,128)(2,1)S(1)}, bf16[512,128]{1,0:T(8,128)(2,1)S(1)}, u32[]{:S(2)}, u32[]{:S(2)}) collective-permute-start(bf16[512,128]{1,0:T(8,128)(2,1)S(1)} %get-tuple-element.23.refs_0_), channel_id=1, source_target_pairs={{0,6},{1,7},{2,4},{3,5},{4,2},{5,3},{6,0},{7,1},{8,14},{9,15},{10,... | collective-permute-start | bytes 393224 | tf_op jit(solution)/shard_map/ppermute | solution.py:38
  42.6 1.7 %collective-permute-start.18 = (f32[72,256]{1,0:T(8,128)S(1)}, f32[72,256]{1,0:T(8,128)S(1)}, u32[]{:S(2)}, u32[]{:S(2)}) collective-permute-start(f32[72,256]{1,0:T(8,128)S(1)} %add.93), channel_id=1, source_target_pairs={{0,8},{1,17},{2,10},{3,19},{4,12},{5,21},{6,14},{7,23},{8,0},{9,25... | collective-permute-start | bytes 221192 | tf_op jit(solution)/shard_map/ppermute | solution.py:38
  44.3 2.8 %collective-permute-done.11.refs_1_ = bf16[512,128]{1,0:T(8,128)(2,1)S(1)} collective-permute-done((bf16[512,128]{1,0:T(8,128)(2,1)S(1)}, bf16[512,128]{1,0:T(8,128)(2,1)S(1)}, u32[]{:S(2)}, u32[]{:S(2)}) %collective-permute-start.11) | collective-permute-done | bytes 131104 | tf_op jit(solution)/shard_map/ppermute | solution.py:38
  47.8 1.0 %collective-permute-start.19 = (f32[72,256]{1,0:T(8,128)S(1)}, f32[72,256]{1,0:T(8,128)S(1)}, u32[]{:S(2)}, u32[]{:S(2)}) collective-permute-start(f32[72,256]{1,0:T(8,128)S(1)} %add.94), channel_id=1, source_target_pairs={{0,16},{1,9},{2,18},{3,11},{4,20},{5,13},{6,22},{7,15},{8,24},{9,1... | collective-permute-start | bytes 221192 | tf_op jit(solution)/shard_map/ppermute | solution.py:38
  48.8 2.4 %backward_0.1.refs_0_ = f32[2176,128]{1,0:T(8,128)S(1)} custom-call(s32[8]{0:T(128)S(1)} %convert_reduce_fusion.bounds_ref, s32[160]{0:T(256)S(1)} %get-tuple-element.32.row_ref, s32[160]{0:T(256)S(1)} %get-tuple-element.36.col_ref, bf16[160,128,128]{2,1,0:T(8,128)(2,1)S(1)} %stage_tiles.1.w_ref, bf16[512,128]{1,0:T(8,128)(2,1)S(1)} %get-tuple-element.23.refs_0_, ...), custom_call_target="tpu_custom_call" | custom-call | flops 201326592 | bytes 1048576 | tf_op jit(solution)/shard_map/backward_0/pallas_call | solution.py:319
  51.2 1.0 %collective-permute-done.19 = f32[72,256]{1,0:T(8,128)S(1)} collective-permute-done((f32[72,256]{1,0:T(8,128)S(1)}, f32[72,256]{1,0:T(8,128)S(1)}, u32[]{:S(2)}, u32[]{:S(2)}) %collective-permute-start.19) | collective-permute-done | bytes 73760 | tf_op jit(solution)/shard_map/ppermute | solution.py:38
  52.2 0.9 %collective-permute-start.20 = (f32[72,256]{1,0:T(8,128)S(1)}, f32[72,256]{1,0:T(8,128)S(1)}, u32[]{:S(2)}, u32[]{:S(2)}) collective-permute-start(f32[72,256]{1,0:T(8,128)S(1)} %add.95), channel_id=1, source_target_pairs={{0,2},{1,3},{2,0},{3,1},{4,6},{5,7},{6,4},{7,5},{8,10},{9,11},{10,... | collective-permute-start | bytes 221192 | tf_op jit(solution)/shard_map/ppermute | solution.py:38
  53.1 1.4 %backward_1.1.refs_0_ = f32[2176,128]{1,0:T(8,128)S(1)} custom-call(s32[8]{0:T(128)S(1)} %convert_reduce_fusion.bounds_ref, s32[160]{0:T(256)S(1)} %get-tuple-element.32.row_ref, s32[160]{0:T(256)S(1)} %get-tuple-element.36.col_ref, bf16[160,128,128]{2,1,0:T(8,128)(2,1)S(1)} %stage_tiles.1.w_ref, ...), custom_call_target="tpu_custom_call", output_to_operand_aliasing={{}: (4, {})} | custom-call | flops 201326592 | bytes 1048576 | tf_op jit(solution)/shard_map/backward_1/pallas_call | solution.py:319
  54.6 1.8 %backward_2.1.refs_0_ = f32[2176,128]{1,0:T(8,128)S(1)} custom-call(s32[8]{0:T(128)S(1)} %convert_reduce_fusion.bounds_ref, s32[160]{0:T(256)S(1)} %get-tuple-element.32.row_ref, s32[160]{0:T(256)S(1)} %get-tuple-element.36.col_ref, bf16[160,128,128]{2,1,0:T(8,128)(2,1)S(1)} %stage_tiles.1.w_ref, ...), custom_call_target="tpu_custom_call", output_to_operand_aliasing={{}: (4, {})} | custom-call | flops 201326592 | bytes 1048576 | tf_op jit(solution)/shard_map/backward_2/pallas_call | solution.py:319
  56.4 1.0 %backward_3.1 = (f32[512,128]{1,0:T(8,128)S(1)}, bf16[512,128]{1,0:T(8,128)(2,1)S(1)}, bf16[512,128]{1,0:T(8,128)(2,1)S(1)}, bf16[512,128]{1,0:T(8,128)(2,1)S(1)}) custom-call(s32[8]{0:T(128)S(1)} %convert_reduce_fusion.bounds_ref, s32[160]{0:T(256)S(1)} %get-tuple-element.32.row_ref, s32[160]{0:T(256)S(1)} %get-tuple-element.36.col_ref, ...), custom_call_target="tpu_custom_call" | custom-call | flops 201326592 | bytes 1048576 | tf_op jit(solution)/shard_map/backward_3/pallas_call | solution.py:319
  57.4 1.0 %collective-permute-start.15 = (bf16[512,128]{1,0:T(8,128)(2,1)S(1)}, bf16[512,128]{1,0:T(8,128)(2,1)S(1)}, u32[]{:S(2)}, u32[]{:S(2)}) collective-permute-start(bf16[512,128]{1,0:T(8,128)(2,1)S(1)} %get-tuple-element.27), channel_id=1, source_target_pairs={{0,16},{1,9},{2,18},{3,11},{4,20},{5,13},{6,22},{7,15},{8,24},{9,1... | collective-permute-start | bytes 393224 | tf_op jit(solution)/shard_map/ppermute | solution.py:38
  58.4 1.2 %collective-permute-start.21 = (f32[72,256]{1,0:T(8,128)S(1)}, f32[72,256]{1,0:T(8,128)S(1)}, u32[]{:S(2)}, u32[]{:S(2)}) collective-permute-start(f32[72,256]{1,0:T(8,128)S(1)} %add.96), channel_id=1, source_target_pairs={{0,4},{1,5},{2,6},{3,7},{4,0},{5,1},{6,2},{7,3},{8,12},{9,13},{10,... | collective-permute-start | bytes 221192 | tf_op jit(solution)/shard_map/ppermute | solution.py:38
  59.7 1.5 %collective-permute-start.14 = (bf16[512,128]{1,0:T(8,128)(2,1)S(1)}, bf16[512,128]{1,0:T(8,128)(2,1)S(1)}, u32[]{:S(2)}, u32[]{:S(2)}) collective-permute-start(bf16[512,128]{1,0:T(8,128)(2,1)S(1)} %get-tuple-element.25), channel_id=1, source_target_pairs={{0,16},{1,9},{2,18},{3,11},{4,20},{5,13},{6,22},{7,15},{8,24},{9,1... | collective-permute-start | bytes 393224 | tf_op jit(solution)/shard_map/ppermute | solution.py:38
  61.1 3.6 %collective-permute-done.21 = f32[72,256]{1,0:T(8,128)S(1)} collective-permute-done((f32[72,256]{1,0:T(8,128)S(1)}, f32[72,256]{1,0:T(8,128)S(1)}, u32[]{:S(2)}, u32[]{:S(2)}) %collective-permute-start.21) | collective-permute-done | bytes 73760 | tf_op jit(solution)/shard_map/ppermute | solution.py:38
  64.9 0.8 %collective-permute-start.16 = (bf16[512,128]{1,0:T(8,128)(2,1)S(1)}, bf16[512,128]{1,0:T(8,128)(2,1)S(1)}, u32[]{:S(2)}, u32[]{:S(2)}) collective-permute-start(bf16[512,128]{1,0:T(8,128)(2,1)S(1)} %add_convert_fusion.1), channel_id=1, source_target_pairs={{0,8},{1,17},{2,10},{3,19},{4,12},{5,21},{6,14},{7,23},{8,0},{9,25... | collective-permute-start | bytes 393224 | tf_op jit(solution)/shard_map/ppermute | solution.py:38
  66.9 2.9 %collective-permute-done.16 = bf16[512,128]{1,0:T(8,128)(2,1)S(1)} collective-permute-done((bf16[512,128]{1,0:T(8,128)(2,1)S(1)}, bf16[512,128]{1,0:T(8,128)(2,1)S(1)}, u32[]{:S(2)}, u32[]{:S(2)}) %collective-permute-start.16) | collective-permute-done | bytes 131104 | tf_op jit(solution)/shard_map/ppermute | solution.py:38
  69.9 0.8 %multiply_convert_fusion = bf16[512,128]{1,0:T(8,128)(2,1)} fusion(bf16[512,128]{1,0:T(8,128)(2,1)S(1)} %get-tuple-element.23.refs_0_, bf16[512,128]{1,0:T(8,128)(2,1)S(1)} %collective-permute-done.16, f32[512,128]{1,0:T(8,128)S(1)} %get-tuple-element.24, bf16[512,128]{1,0:T(8,128)(2,1)S(1)} %collective-permute-done.14, f32[512]{0:T(512)S(1)} %add_rsqrt_fusion), kind=kLoop, calls=%fused_computation.1 | loop fusion | flops 524288 | bytes 788480 | tf_op jit(solution)/shard_map/convert_element_type | solution.py:343
  (54 shorter events, 6.7 us)
Async XLA Ops:
  2.4 6.8 %collective-permute-start = (bf16[512,128]{1,0:T(8,128)(2,1)S(1)}, bf16[512,128]{1,0:T(8,128)(2,1)S(1)}, u32[]{:S(2)}, u32[]{:S(2)}) collective-permute-start(bf16[512,128]{1,0:T(8,128)(2,1)S(1)} %multiply_convert_fusion.1.refs_0_.scaled_ref), channel_id=1, source_target_pairs={{0,8},{1,17},{2,10},{3,19},{4,12},{5,21},{6,14},{7,23},{8,0},{9,25... | collective-permute-start | bytes 393224 | tf_op jit(solution)/shard_map/ppermute | solution.py:38
  5.4 8.6 %collective-permute-start.1 = (bf16[512,128]{1,0:T(8,128)(2,1)S(1)}, bf16[512,128]{1,0:T(8,128)(2,1)S(1)}, u32[]{:S(2)}, u32[]{:S(2)}) collective-permute-start(bf16[512,128]{1,0:T(8,128)(2,1)S(1)} %multiply_convert_fusion.1.refs_0_.scaled_ref), channel_id=1, source_target_pairs={{0,16},{1,9},{2,18},{3,11},{4,20},{5,13},{6,22},{7,15},{8,24},{9,1... | collective-permute-start | bytes 393224 | tf_op jit(solution)/shard_map/ppermute | solution.py:38
  9.1 5.0 %collective-permute-start.2 = (bf16[512,128]{1,0:T(8,128)(2,1)S(1)}, bf16[512,128]{1,0:T(8,128)(2,1)S(1)}, u32[]{:S(2)}, u32[]{:S(2)}) collective-permute-start(bf16[512,128]{1,0:T(8,128)(2,1)S(1)} %collective-permute-done.refs_1_), channel_id=1, source_target_pairs={{0,16},{1,9},{2,18},{3,11},{4,20},{5,13},{6,22},{7,15},{8,24},{9,1... | collective-permute-start | bytes 393224 | tf_op jit(solution)/shard_map/ppermute | solution.py:38
  10.9 2.5 %copy-start = (bf16[1,1,160,128,128]{4,3,2,1,0:T(8,128)(2,1)S(1)}, bf16[1,1,160,128,128]{4,3,2,1,0:T(8,128)(2,1)}, u32[]{:S(2)}) copy-start(bf16[1,1,160,128,128]{4,3,2,1,0:T(8,128)(2,1)} %param.11) | copy-start | bytes 15728644
  15.7 7.5 %collective-permute-start.5 = (bf16[512,128]{1,0:T(8,128)(2,1)S(1)}, bf16[512,128]{1,0:T(8,128)(2,1)S(1)}, u32[]{:S(2)}, u32[]{:S(2)}) collective-permute-start(bf16[512,128]{1,0:T(8,128)(2,1)S(1)} %get-tuple-element.21), channel_id=1, source_target_pairs={{0,1},{1,0},{2,3},{3,2},{4,5},{5,4},{6,7},{7,6},{8,9},{9,8},{10,11... | collective-permute-start | bytes 393224 | tf_op jit(solution)/shard_map/ppermute | solution.py:38
  18.7 5.9 %collective-permute-start.3 = (bf16[1024,128]{1,0:T(8,128)(2,1)S(1)}, bf16[1024,128]{1,0:T(8,128)(2,1)S(1)}, u32[]{:S(2)}, u32[]{:S(2)}) collective-permute-start(bf16[1024,128]{1,0:T(8,128)(2,1)S(1)} %get-tuple-element.19), channel_id=1, source_target_pairs={{0,1},{1,0},{2,3},{3,2},{4,5},{5,4},{6,7},{7,6},{8,9},{9,8},{10,11... | collective-permute-start | bytes 786440 | tf_op jit(solution)/shard_map/ppermute | solution.py:38
  19.9 14.7 %copy-start.1 = (bf16[512,256]{1,0:T(8,128)(2,1)S(1)}, bf16[512,256]{1,0:T(8,128)(2,1)}, u32[]{:S(2)}) copy-start(bf16[512,256]{1,0:T(8,128)(2,1)} %up_ref.1) | copy-start | bytes 786436
  19.9 14.7 %copy-start.2 = (bf16[128,256]{1,0:T(8,128)(2,1)S(1)}, bf16[128,256]{1,0:T(8,128)(2,1)}, u32[]{:S(2)}) copy-start(bf16[128,256]{1,0:T(8,128)(2,1)} %weight_ref.1) | copy-start | bytes 196612
  19.9 14.7 %copy-start.3 = (f32[256]{0:T(256)S(1)}, f32[256]{0:T(256)}, u32[]{:S(2)}) copy-start(f32[256]{0:T(256)} %param.16) | copy-start | bytes 3076
  19.9 12.4 %collective-permute-start.7 = (bf16[512,128]{1,0:T(8,128)(2,1)S(1)}, bf16[512,128]{1,0:T(8,128)(2,1)S(1)}, u32[]{:S(2)}, u32[]{:S(2)}) collective-permute-start(bf16[512,128]{1,0:T(8,128)(2,1)S(1)} %forward_3.1), channel_id=1, source_target_pairs={{0,5},{1,4},{2,7},{3,6},{4,1},{5,0},{6,3},{7,2},{8,13},{9,12},{10,... | collective-permute-start | bytes 393224 | tf_op jit(solution)/shard_map/ppermute | solution.py:38
  23.2 9.1 %collective-permute-start.6 = (bf16[512,128]{1,0:T(8,128)(2,1)S(1)}, bf16[512,128]{1,0:T(8,128)(2,1)S(1)}, u32[]{:S(2)}, u32[]{:S(2)}) collective-permute-start(bf16[512,128]{1,0:T(8,128)(2,1)S(1)} %add_convert_fusion.2), channel_id=1, source_target_pairs={{0,6},{1,7},{2,4},{3,5},{4,2},{5,3},{6,0},{7,1},{8,14},{9,15},{10,... | collective-permute-start | bytes 393224 | tf_op jit(solution)/shard_map/ppermute | solution.py:38
  24.8 9.8 %collective-permute-start.4 = (bf16[512,128]{1,0:T(8,128)(2,1)S(1)}, bf16[512,128]{1,0:T(8,128)(2,1)S(1)}, u32[]{:S(2)}, u32[]{:S(2)}) collective-permute-start(bf16[512,128]{1,0:T(8,128)(2,1)S(1)} %get-tuple-element.34), channel_id=1, source_target_pairs={{0,2},{1,3},{2,0},{3,1},{4,6},{5,7},{6,4},{7,5},{8,10},{9,11},{10,... | collective-permute-start | bytes 393224 | tf_op jit(solution)/shard_map/ppermute | solution.py:38
  35.8 8.5 %collective-permute-start.9 = (bf16[512,128]{1,0:T(8,128)(2,1)S(1)}, bf16[512,128]{1,0:T(8,128)(2,1)S(1)}, u32[]{:S(2)}, u32[]{:S(2)}) collective-permute-start(bf16[512,128]{1,0:T(8,128)(2,1)S(1)} %get-tuple-element.23.refs_0_), channel_id=1, source_target_pairs={{0,2},{1,3},{2,0},{3,1},{4,6},{5,7},{6,4},{7,5},{8,10},{9,11},{10,... | collective-permute-start | bytes 393224 | tf_op jit(solution)/shard_map/ppermute | solution.py:38
  37.6 9.5 %collective-permute-start.11 = (bf16[512,128]{1,0:T(8,128)(2,1)S(1)}, bf16[512,128]{1,0:T(8,128)(2,1)S(1)}, u32[]{:S(2)}, u32[]{:S(2)}) collective-permute-start(bf16[512,128]{1,0:T(8,128)(2,1)S(1)} %get-tuple-element.23.refs_0_), channel_id=1, source_target_pairs={{0,6},{1,7},{2,4},{3,5},{4,2},{5,3},{6,0},{7,1},{8,14},{9,15},{10,... | collective-permute-start | bytes 393224 | tf_op jit(solution)/shard_map/ppermute | solution.py:38
  41.2 1.3 %collective-permute-start.17 = (f32[72,256]{1,0:T(8,128)S(1)}, f32[72,256]{1,0:T(8,128)S(1)}, u32[]{:S(2)}, u32[]{:S(2)}) collective-permute-start(f32[72,256]{1,0:T(8,128)S(1)} %get-tuple-element.31), channel_id=1, source_target_pairs={{0,1},{1,0},{2,3},{3,2},{4,5},{5,4},{6,7},{7,6},{8,9},{9,8},{10,11... | collective-permute-start | bytes 221192 | tf_op jit(solution)/shard_map/ppermute | solution.py:38
  41.3 7.5 %collective-permute-start.8 = (bf16[512,128]{1,0:T(8,128)(2,1)S(1)}, bf16[512,128]{1,0:T(8,128)(2,1)S(1)}, u32[]{:S(2)}, u32[]{:S(2)}) collective-permute-start(bf16[512,128]{1,0:T(8,128)(2,1)S(1)} %get-tuple-element.23.refs_0_), channel_id=1, source_target_pairs={{0,1},{1,0},{2,3},{3,2},{4,5},{5,4},{6,7},{7,6},{8,9},{9,8},{10,11... | collective-permute-start | bytes 393224 | tf_op jit(solution)/shard_map/ppermute | solution.py:38
  42.6 5.2 %collective-permute-start.18 = (f32[72,256]{1,0:T(8,128)S(1)}, f32[72,256]{1,0:T(8,128)S(1)}, u32[]{:S(2)}, u32[]{:S(2)}) collective-permute-start(f32[72,256]{1,0:T(8,128)S(1)} %add.93), channel_id=1, source_target_pairs={{0,8},{1,17},{2,10},{3,19},{4,12},{5,21},{6,14},{7,23},{8,0},{9,25... | collective-permute-start | bytes 221192 | tf_op jit(solution)/shard_map/ppermute | solution.py:38
  44.3 8.8 %collective-permute-start.10 = (bf16[512,128]{1,0:T(8,128)(2,1)S(1)}, bf16[512,128]{1,0:T(8,128)(2,1)S(1)}, u32[]{:S(2)}, u32[]{:S(2)}) collective-permute-start(bf16[512,128]{1,0:T(8,128)(2,1)S(1)} %collective-permute-done.9.refs_1_), channel_id=1, source_target_pairs={{0,1},{1,0},{2,3},{3,2},{4,5},{5,4},{6,7},{7,6},{8,9},{9,8},{10,11... | collective-permute-start | bytes 393224 | tf_op jit(solution)/shard_map/ppermute | solution.py:38
  47.1 7.5 %collective-permute-start.12 = (bf16[512,128]{1,0:T(8,128)(2,1)S(1)}, bf16[512,128]{1,0:T(8,128)(2,1)S(1)}, u32[]{:S(2)}, u32[]{:S(2)}) collective-permute-start(bf16[512,128]{1,0:T(8,128)(2,1)S(1)} %collective-permute-done.11.refs_1_), channel_id=1, source_target_pairs={{0,1},{1,0},{2,3},{3,2},{4,5},{5,4},{6,7},{7,6},{8,9},{9,8},{10,11... | collective-permute-start | bytes 393224 | tf_op jit(solution)/shard_map/ppermute | solution.py:38
  47.1 9.3 %collective-permute-start.13 = (bf16[512,128]{1,0:T(8,128)(2,1)S(1)}, bf16[512,128]{1,0:T(8,128)(2,1)S(1)}, u32[]{:S(2)}, u32[]{:S(2)}) collective-permute-start(bf16[512,128]{1,0:T(8,128)(2,1)S(1)} %get-tuple-element.23.refs_0_), channel_id=1, source_target_pairs={{0,5},{1,4},{2,7},{3,6},{4,1},{5,0},{6,3},{7,2},{8,13},{9,12},{10,... | collective-permute-start | bytes 393224 | tf_op jit(solution)/shard_map/ppermute | solution.py:38
  47.8 4.4 %collective-permute-start.19 = (f32[72,256]{1,0:T(8,128)S(1)}, f32[72,256]{1,0:T(8,128)S(1)}, u32[]{:S(2)}, u32[]{:S(2)}) collective-permute-start(f32[72,256]{1,0:T(8,128)S(1)} %add.94), channel_id=1, source_target_pairs={{0,16},{1,9},{2,18},{3,11},{4,20},{5,13},{6,22},{7,15},{8,24},{9,1... | collective-permute-start | bytes 221192 | tf_op jit(solution)/shard_map/ppermute | solution.py:38
  52.2 6.2 %collective-permute-start.20 = (f32[72,256]{1,0:T(8,128)S(1)}, f32[72,256]{1,0:T(8,128)S(1)}, u32[]{:S(2)}, u32[]{:S(2)}) collective-permute-start(f32[72,256]{1,0:T(8,128)S(1)} %add.95), channel_id=1, source_target_pairs={{0,2},{1,3},{2,0},{3,1},{4,6},{5,7},{6,4},{7,5},{8,10},{9,11},{10,... | collective-permute-start | bytes 221192 | tf_op jit(solution)/shard_map/ppermute | solution.py:38
  57.4 7.4 %collective-permute-start.15 = (bf16[512,128]{1,0:T(8,128)(2,1)S(1)}, bf16[512,128]{1,0:T(8,128)(2,1)S(1)}, u32[]{:S(2)}, u32[]{:S(2)}) collective-permute-start(bf16[512,128]{1,0:T(8,128)(2,1)S(1)} %get-tuple-element.27), channel_id=1, source_target_pairs={{0,16},{1,9},{2,18},{3,11},{4,20},{5,13},{6,22},{7,15},{8,24},{9,1... | collective-permute-start | bytes 393224 | tf_op jit(solution)/shard_map/ppermute | solution.py:38
  58.4 6.3 %collective-permute-start.21 = (f32[72,256]{1,0:T(8,128)S(1)}, f32[72,256]{1,0:T(8,128)S(1)}, u32[]{:S(2)}, u32[]{:S(2)}) collective-permute-start(f32[72,256]{1,0:T(8,128)S(1)} %add.96), channel_id=1, source_target_pairs={{0,4},{1,5},{2,6},{3,7},{4,0},{5,1},{6,2},{7,3},{8,12},{9,13},{10,... | collective-permute-start | bytes 221192 | tf_op jit(solution)/shard_map/ppermute | solution.py:38
  59.7 7.3 %collective-permute-start.14 = (bf16[512,128]{1,0:T(8,128)(2,1)S(1)}, bf16[512,128]{1,0:T(8,128)(2,1)S(1)}, u32[]{:S(2)}, u32[]{:S(2)}) collective-permute-start(bf16[512,128]{1,0:T(8,128)(2,1)S(1)} %get-tuple-element.25), channel_id=1, source_target_pairs={{0,16},{1,9},{2,18},{3,11},{4,20},{5,13},{6,22},{7,15},{8,24},{9,1... | collective-permute-start | bytes 393224 | tf_op jit(solution)/shard_map/ppermute | solution.py:38
  64.7 1.5 %collective-permute-start.22 = (f32[64,256]{1,0:T(8,128)S(1)}, f32[64,256]{1,0:T(8,128)S(1)}, u32[]{:S(2)}, u32[]{:S(2)}) collective-permute-start(f32[64,256]{1,0:T(8,128)S(1)} %slice.18), channel_id=1, source_target_pairs={{0,1},{1,0},{2,3},{3,2},{4,5},{5,4},{6,7},{7,6},{8,9},{9,8},{10,11... | collective-permute-start | bytes 196616 | tf_op jit(solution)/shard_map/ppermute | solution.py:38
  64.9 5.0 %collective-permute-start.16 = (bf16[512,128]{1,0:T(8,128)(2,1)S(1)}, bf16[512,128]{1,0:T(8,128)(2,1)S(1)}, u32[]{:S(2)}, u32[]{:S(2)}) collective-permute-start(bf16[512,128]{1,0:T(8,128)(2,1)S(1)} %add_convert_fusion.1), channel_id=1, source_target_pairs={{0,8},{1,17},{2,10},{3,19},{4,12},{5,21},{6,14},{7,23},{8,0},{9,25... | collective-permute-start | bytes 393224 | tf_op jit(solution)/shard_map/ppermute | solution.py:38

commit v3 on v2

v3 whole, which is shorter than its diff:
```python
import functools

import jax
import jax.numpy as jnp
from jax import lax
from jax.experimental import pallas as pl
from jax.experimental.pallas import tpu as pltpu
from jax.sharding import PartitionSpec as P

BOTH = ("rep", "blk")
VMEM = pl.BlockSpec(memory_space=pltpu.VMEM)
SMEM = pl.BlockSpec(memory_space=pltpu.SMEM)
ANY = pl.BlockSpec(memory_space=pl.ANY)
HBM = pl.BlockSpec(memory_space=pltpu.HBM)
BF = jnp.bfloat16
F32 = jnp.float32
CORES = 2
BIAS_ROWS = 16


def params(mib):
    return pltpu.CompilerParams(vmem_limit_bytes=mib * 1024 * 1024)


def cost(flops, size):
    return pl.CostEstimate(flops=flops, bytes_accessed=size, transcendentals=0)


SMALL = cost(0, 1024)
LARGE = cost(0, 2**26)


def node_scale(degrees):
    return 1.0 / jnp.sqrt(degrees.astype(F32) + 1.0)


def in_hbm(value):
    return pltpu.with_memory_space_constraint(value, pltpu.HBM)


def move(value, target):
    rep_count, blk_count = lax.axis_size("rep"), lax.axis_size("blk")
    pairs = []
    for r in range(rep_count):
        for k in range(blk_count):
            to_r, to_k = target(r, k)
            pairs.append((r * blk_count + k, to_r * blk_count + to_k))
    return lax.ppermute(value, BOTH, pairs)


def block(function, *args):
    shapes = jax.eval_shape(function, *args)
    return lax.cond(
        lax.axis_index("blk") < lax.axis_size("blk"),
        function,
        lambda *unused: jax.tree.map(lambda shape: jnp.zeros(shape.shape, shape.dtype), shapes),
        *args,
    )


def swap_cores(value):
    return move(value, lambda r, k: (r, k ^ 1))


def rep_bits():
    return (lax.axis_size("rep") - 1).bit_length()


def rep_partner(place):
    bits = rep_bits()
    turned = sum(((place >> n) & 1) << ((n + 1) % bits) for n in range(bits))
    return lambda r, k: (r ^ (turned if k % 2 else place), k)


def rep_place(rep_ids, rep_index, core):
    bits = rep_bits()
    relative = rep_ids ^ rep_index
    place = jnp.zeros_like(relative)
    for n in range(bits):
        turned = (relative >> ((n + 1) % bits)) & 1
        place = place + (jnp.where(core == 0, (relative >> n) & 1, turned) << n)
    return place


def far_first(count):
    return sorted(range(1, count), key=lambda place: -bin(place).count("1"))


def pair_at(place, pair_index, core):
    pairs = lax.axis_size("blk") // CORES
    if pairs == 4:
        return pair_index ^ (0, 1, 3, 2)[place]
    step = (0, 1, -1, jnp.where(core == 0, -2, 2))[place]
    return (pair_index + step) % pairs


def pair_partner(place, back, other_core=False):
    blk_count = lax.axis_size("blk")
    if other_core:
        near = pair_partner(place, back)
        return lambda r, k: (r, near(r, k)[1] ^ 1)

    def target(r, k):
        if place == 3:
            return (r, (k + (3 if k % 2 else -3)) % blk_count)
        if blk_count == 8:
            return (r, k ^ {1: 2, 2: 6}[place])
        step = {1: 2, 2: -2}[place]
        return (r, (k + (-step if back else step)) % blk_count)

    return target


def together(values, earlier=(), weigh=None):
    count = len(values)
    return pl.pallas_call(
        lambda *refs: None,
        out_shape=[jax.ShapeDtypeStruct(value.shape, value.dtype) for value in values],
        in_specs=[ANY] * (count + len(earlier)),
        out_specs=[ANY] * count,
        input_output_aliases={n: n for n in range(count)},
        compiler_params=params(16),
        cost_estimate=weigh or SMALL,
        name="together",
    )(*values, *earlier)


def prepare_kernel(degrees_hbm, features_hbm, scaled_ref, norm_ref, degrees_ref, features_ref, sems):
    copies = [
        pltpu.make_async_copy(degrees_hbm, degrees_ref, sems.at[0]),
        pltpu.make_async_copy(features_hbm, features_ref, sems.at[1]),
    ]
    for copy in copies:
        copy.start()
    for copy in copies:
        copy.wait()
    tile = degrees_ref.shape[1]
    for n in range(degrees_ref.shape[0]):
        norm = node_scale(degrees_ref[n : n + 1, :])
        norm = jnp.broadcast_to(norm, (tile, tile)).T
        rows = slice(n * tile, (n + 1) * tile)
        norm_ref[rows, :] = norm
        scaled_ref[rows, :] = (norm * features_ref[rows, :].astype(F32)).astype(BF)


def stage_kernel(w_ref, earlier_ref, out_ref, sem):
    copy = pltpu.make_async_copy(w_ref, out_ref, sem)
    copy.start()
    copy.wait()


def gather_blocks(block_refs, held):
    first = 0
    for block_ref in block_refs:
        held[first : first + block_ref.shape[0], :] = block_ref[...]
        first += block_ref.shape[0]


def over_slots(low, high, unroll, slot_total, body):
    def step(i, carry):
        for u in range(unroll):
            t = low + i * unroll + u
            body(jnp.minimum(t, slot_total - 1), t < high)
        return carry

    lax.fori_loop(0, (high - low + unroll - 1) // unroll, step, 0)


def aligned(index, tile):
    return pl.ds(pl.multiple_of(index * tile, tile), tile)


def forward_kernel(places, unrolls, earlier_ref, bounds_ref, row_ref, col_ref, w_ref, *refs):
    outs = 3 if 3 in places else 2
    x_refs, out_refs, (held, total) = refs[: -2 - outs], refs[-2 - outs : -2], refs[-2:]
    tile = w_ref.shape[-1]
    block_tiles = x_refs[0].shape[0] // tile
    gather_blocks(x_refs, held)
    total[...] = jnp.zeros_like(total)
    spare = total.shape[0] // tile - 1
    for n, place in enumerate(places):

        def body(t, used):
            row = row_ref[t]
            if place == 3:
                row = row % block_tiles
            row = jnp.where(used, row + n * 2 * block_tiles, spare)
            part = jnp.dot(w_ref[t], held[aligned(col_ref[t], tile), :], preferred_element_type=F32)
            total[aligned(row, tile), :] += part

        over_slots(bounds_ref[place], bounds_ref[4 + place], unrolls[n], w_ref.shape[0], body)
    rows = block_tiles * tile
    for n, place in enumerate(places):
        first = n * 2 * rows
        if place == 3:
            out_refs[2][...] = total[first : first + rows, :].astype(BF)
        else:
            for out_ref in out_refs[:2]:
                out_ref[n * rows : (n + 1) * rows, :] = total[first : first + rows, :].astype(BF)
                first += rows


def stream_slots(w_hbm, held, sems, ranges, unroll, body):
    slot_total = w_hbm.shape[0]
    counts = [(high - low + unroll - 1) // unroll for low, high, n in ranges]

    def fetch(low, i, place):
        first = jnp.minimum(low + i * unroll, slot_total - unroll)
        return first, pltpu.make_async_copy(w_hbm.at[pl.ds(first, unroll)], held.at[place], sems.at[place])

    begin = 0
    for (low, high, n), count in zip(ranges, counts):

        def start(i, carry, low=low, begin=begin):
            fetch(low, i, begin + i)[1].start()
            return carry

        lax.fori_loop(0, count, start, 0)
        begin = begin + count
    begin = 0
    for (low, high, n), count in zip(ranges, counts):

        def step(i, carry, low=low, high=high, n=n, begin=begin):
            first, copy = fetch(low, i, begin + i)
            copy.wait()
            for u in range(unroll):
                t = first + u
                body(held[begin + i, u], t, (t >= low + i * unroll) & (t < high), n)
            return carry

        lax.fori_loop(0, count, step, 0)
        begin = begin + count


def backward_kernel(places, unroll, first_call, last_call, bounds_ref, row_ref, col_ref, w_ref, *refs):
    refs, (total, held, tiles_held, sems) = refs[:-4], refs[-4:]
    tile = w_ref.shape[-1]
    if first_call:
        block_refs, out_refs = refs[:2], refs[2:]
        total[...] = jnp.zeros_like(total)
    else:
        old_ref, refs = refs[0], refs[1:]
        inputs = 2 if last_call else 1
        block_refs, out_refs = refs[:inputs], refs[inputs:]
        total[...] = old_ref[...]
    gather_blocks(block_refs, held)
    spare = total.shape[0] // tile - 1
    held_tiles = held.shape[0] // tile

    def body(w, t, used, n):
        row = row_ref[t]
        if places[n] == 3:
            row = row % held_tiles
        elif len(places) > 1:
            block_tiles = held_tiles // (2 * len(places))
            row = jnp.where(row < block_tiles, row, row + (len(places) - 1) * block_tiles) + n * block_tiles
        part = lax.dot_general(
            w, held[aligned(row, tile), :], (((0,), (0,)), ((), ())), preferred_element_type=F32
        )
        total[aligned(jnp.where(used, col_ref[t], spare), tile), :] += part

    ranges = [(bounds_ref[place], bounds_ref[4 + place], n) for n, place in enumerate(places)]
    stream_slots(w_ref, tiles_held, sems, ranges, unroll, body)
    if last_call:
        rows = out_refs[0].shape[0]
        for n, out_ref in enumerate(out_refs):
            out_ref[...] = total[n * rows : (n + 1) * rows, :].astype(out_ref.dtype)
    else:
        out_refs[0][...] = total[...]


def dense_kernel(*refs):
    part_refs, (norm_ref, weight_ref, bias_ref, up_ref) = refs[:-8], refs[-8:-4]
    hidden_ref, grad_ref, aggregated_ref, pre_grad_ref = refs[-4:]
    norm = norm_ref[...]
    neighbor = part_refs[0][...].astype(F32)
    for part_ref in part_refs[1:]:
        neighbor = neighbor + part_ref[...].astype(F32)
    aggregated = (norm * neighbor).astype(BF)
    weight = weight_ref[...]
    pre_act = jnp.dot(aggregated, weight, preferred_element_type=F32) + bias_ref[...]
    gate = 1.0 / (1.0 + jnp.exp(-pre_act))
    hidden_ref[...] = (pre_act * gate).astype(BF)
    pre_grad = (up_ref[...].astype(F32) * (gate + pre_act * gate * (1.0 - gate))).astype(BF)
    back = lax.dot_general(pre_grad, weight, (((1,), (1,)), ((), ())), preferred_element_type=F32)
    grad_ref[...] = (norm * back).astype(BF)
    aggregated_ref[...] = aggregated
    pre_grad_ref[...] = pre_grad


def weight_kernel(core_ref, aggregated_ref, pre_grad_ref, earlier_ref, keep_ref, send_ref, full):
    pre_grad = pre_grad_ref[...]
    half = full.shape[0] // CORES
    full[...] = lax.dot_general(
        aggregated_ref[...], pre_grad, (((0,), (0,)), ((), ())), preferred_element_type=F32
    )
    sums = jnp.sum(pre_grad.astype(F32), axis=0, keepdims=True)
    sums = jnp.broadcast_to(sums, (BIAS_ROWS, pre_grad.shape[1]))
    core = core_ref[0]
    for out_ref, side in ((keep_ref, core), (send_ref, 1 - core)):
        out_ref[:half, :] = full[aligned(side, half), :]
        out_ref[half:, :] = sums


def on_device(
    features, degrees, tile_weights, tile_rows, tile_cols, tile_counts, weight, layer_bias, upstream
):
    row_count, feat_width = features.shape
    hid_width = weight.shape[1]
    slot_total, tile = tile_weights.shape[2], tile_weights.shape[-1]
    row_tiles = row_count // tile
    rep_count, blk_count = lax.axis_size("rep"), lax.axis_size("blk")
    rep_index, blk_index = lax.axis_index("rep"), lax.axis_index("blk")
    core, pair_index = blk_index % CORES, blk_index // CORES
    col_tiles = rep_count * row_tiles
    block_shape = jax.ShapeDtypeStruct((row_count, feat_width), BF)

    rows_dev, cols_dev, count_dev = tile_rows[0, 0], tile_cols[0, 0], tile_counts[0, 0]
    used = jnp.arange(slot_total, dtype=jnp.int32) < count_dev
    group = rows_dev // row_tiles
    row_place = jnp.where(group % CORES == core, 0, row_tiles) + rows_dev % row_tiles
    col_place = rep_place(cols_dev // row_tiles, rep_index, core) * row_tiles + cols_dev % row_tiles
    pair_ids = jnp.stack([pair_at(place, pair_index, core) for place in range(4)])
    pair_ids = jnp.concatenate([pair_ids, pair_ids + 1])
    bounds = jnp.sum(used & (group // CORES < pair_ids[:, None]), axis=1).astype(jnp.int32)
    row_place, col_place = row_place.astype(jnp.int32), col_place.astype(jnp.int32)

    scaled, norm_wide = pl.pallas_call(
        prepare_kernel,
        out_shape=[block_shape, jax.ShapeDtypeStruct((row_count, feat_width), F32)],
        in_specs=[HBM] * 2,
        out_specs=[VMEM] * 2,
        scratch_shapes=[
            pltpu.VMEM((row_tiles, tile), jnp.int32),
            pltpu.VMEM((row_count, feat_width), BF),
            pltpu.SemaphoreType.DMA((2,)),
        ],
        compiler_params=params(16),
        cost_estimate=SMALL,
        name="prepare",
    )(in_hbm(degrees.reshape(row_tiles, tile)), in_hbm(features))

    source = {place: move(scaled, rep_partner(place)) for place in far_first(rep_count)}
    source = [scaled] + [source[place] for place in range(1, rep_count)]

    def stage(earlier):
        return pl.pallas_call(
            stage_kernel,
            out_shape=jax.ShapeDtypeStruct((slot_total, tile, tile), BF),
            in_specs=[HBM, ANY],
            out_specs=VMEM,
            scratch_shapes=[pltpu.SemaphoreType.DMA],
            compiler_params=params(16),
            cost_estimate=cost(0, 2 * slot_total * tile * tile * 2),
            name="stage_tiles",
        )(in_hbm(tile_weights[0, 0]), earlier)

    tiles_dev = stage(scaled)

    def forward(places, unrolls, earlier):
        single = 3 in places
        pairs = len(places) - single
        shape = jax.ShapeDtypeStruct((pairs * row_count, feat_width), BF)
        return pl.pallas_call(
            functools.partial(forward_kernel, places, unrolls),
            out_shape=[shape, shape] + [block_shape] * single,
            in_specs=[ANY, SMEM, SMEM, SMEM] + [VMEM] * (1 + rep_count),
            out_specs=[VMEM] * (2 + single),
            scratch_shapes=[
                pltpu.VMEM((col_tiles * tile, feat_width), BF),
                pltpu.VMEM((((2 * pairs + single) * row_tiles + 1) * tile, feat_width), F32),
            ],
            compiler_params=params(16),
            cost_estimate=SMALL,
            name="forward_" + "_".join(map(str, places)),
        )(earlier, bounds, row_place, col_place, tiles_dev, *source)

    def add(a, b):
        return (a.astype(F32) + b.astype(F32)).astype(BF)

    keep, send, part3 = forward((1, 2, 3), (16, 16, 12), norm_wide)
    sums = add(keep, swap_cores(send))
    came3 = move(part3, pair_partner(3, False))
    came2 = move(sums[row_count:], pair_partner(2, False))
    came1 = move(sums[:row_count], pair_partner(1, False))
    keep0, send0 = forward((0,), (16,), send)
    cross0 = swap_cores(send0)

    hidden, scaled_grad, aggregated, pre_grad = pl.pallas_call(
        dense_kernel,
        out_shape=[
            jax.ShapeDtypeStruct((row_count, hid_width), BF),
            block_shape,
            block_shape,
            jax.ShapeDtypeStruct((row_count, hid_width), BF),
        ],
        in_specs=[VMEM] * 10,
        out_specs=[VMEM] * 4,
        compiler_params=params(16),
        cost_estimate=SMALL,
        name="dense",
    )(keep0, cross0, came1, came2, came3, scaled, norm_wide, weight, layer_bias[None], upstream)

    grads2 = move(scaled_grad, pair_partner(2, True))
    grads3 = move(scaled_grad, pair_partner(3, True))
    grads1 = move(scaled_grad, pair_partner(1, True))

    total_shape = jax.ShapeDtypeStruct(((col_tiles + 1) * tile, feat_width), F32)

    tiles_hbm = in_hbm(tile_weights[0, 0])

    def backward(places, unroll, old, blocks):
        last = len(places) > 1
        out_shape = [total_shape]
        if last:
            out_shape = [jax.ShapeDtypeStruct((row_count, feat_width), F32)] + [block_shape] * (rep_count - 1)
        fetches = slot_total // unroll + len(places)
        return pl.pallas_call(
            functools.partial(backward_kernel, places, unroll, old is None, last),
            out_shape=out_shape,
            in_specs=[SMEM, SMEM, SMEM, HBM] + [VMEM] * ((old is not None) + len(blocks)),
            out_specs=[VMEM] * len(out_shape),
            scratch_shapes=[
                pltpu.VMEM(total_shape.shape, F32),
                pltpu.VMEM((sum(part.shape[0] for part in blocks), feat_width), BF),
                pltpu.VMEM((fetches, unroll, tile, tile), BF),
                pltpu.SemaphoreType.DMA((fetches,)),
            ],
            compiler_params=params(28),
            cost_estimate=SMALL,
            name="backward_" + "_".join(map(str, places)),
        )(bounds, row_place, col_place, tiles_hbm, *([] if old is None else [old]), *blocks)

    grad_rows = feat_width // CORES
    half_shape = jax.ShapeDtypeStruct((grad_rows + BIAS_ROWS, hid_width), F32)

    (total,) = backward((0,), 16, None, [scaled_grad, swap_cores(scaled_grad)])
    halves = pl.pallas_call(
        weight_kernel,
        out_shape=[half_shape] * 2,
        in_specs=[SMEM, VMEM, VMEM, ANY],
        out_specs=[VMEM] * 2,
        scratch_shapes=[pltpu.VMEM((feat_width, hid_width), F32)],
        compiler_params=params(16),
        cost_estimate=SMALL,
        name="weight_terms",
    )(core[None].astype(jnp.int32), aggregated, pre_grad, total)

    def rep_sum(keep, send):
        grad = keep + swap_cores(send)
        for n in range(rep_bits()):
            grad = grad + move(grad.astype(BF), rep_partner(1 << n)).astype(F32)
        return grad

    grad = block(rep_sum, *halves)
    blk_bits = (blk_count - 1).bit_length()
    grads1, grads2, grads3 = together([grads1, grads2, grads3], [grad])
    near_far = jnp.concatenate([grads1, grads2])
    other = swap_cores(near_far)
    (total,) = backward((3,), 10, total, [grads3])
    came = move(grad.astype(BF), lambda r, k: (r, k ^ 2))
    (total,) = together([total], [came])
    columns = backward((1, 2), 16, total, [near_far, other])

    def finish_weight(grad, came):
        grad = grad + came.astype(F32)
        for bit in range(2, blk_bits):
            grad = grad + move(grad.astype(BF), lambda r, k: (r, k ^ (1 << bit))).astype(F32)
        grad = grad * (row_count * rep_count * blk_count) ** (-0.5)
        mine = grad[:grad_rows]
        other = swap_cores(mine)
        weight_grad = jnp.where(
            core == 0, jnp.concatenate([mine, other]), jnp.concatenate([other, mine])
        )
        return weight_grad, grad[grad_rows]

    column_sum = columns[0]
    arrived = {place: move(columns[place], rep_partner(place)) for place in far_first(rep_count)}
    weight_grad, bias_grad = block(finish_weight, grad, came)
    for place in range(1, rep_count):
        column_sum = column_sum + arrived[place].astype(F32)
    feature_grad = (norm_wide * (column_sum + scaled_grad.astype(F32))).astype(BF)
    return (hidden, feature_grad, weight_grad, bias_grad)


def solution(mesh):
    placed = (
        P(("rep", "blk"), None),
        P(("rep", "blk")),
        P("rep", "blk", None, None, None),
        P("rep", "blk", None),
        P("rep", "blk", None),
        P("rep", "blk"),
        P(),
        P(),
        P(("rep", "blk"), None),
    )
    return jax.shard_map(
        on_device,
        mesh=mesh,
        in_specs=placed,
        out_specs=(P(("rep", "blk"), None), P(("rep", "blk"), None), P(), P()),
        check_vma=False,
    )
```

time: 71.1 us -> 67.5 us (0.949)
  Pallas kernels: 13.8 us -> 19.1 us
  starting transfers between devices: 25.8 us -> 22.7 us
  other arithmetic: 4.95 us -> 1.91 us
  local copies, waits for them, and re-layouts: 2.74 us -> 0.18 us
    pallas_call x9 -> x10, Pallas kernels: 12.7 us -> 18 us  [the longest x3 9.36 us: backward(): pl.pallas_call(functools.partial(backward_kernel, places, unroll, old is...]
    ppermute x23 -> x22, starting transfers between devices: 25.8 us -> 22.7 us  [move(): return lax.ppermute(value, BOTH, pairs)]
    unnamed x8 -> x11, local copies, waits for them, and re-layouts: 2.51 us -> 0.04 us
    mul x2 -> x1, other arithmetic: 1.23 us -> 0.02 us  [finish_weight(): grad = grad * (row_count * rep_count * blk_count) ** (-0.5)]
    convert_element_type x3 -> x5, other arithmetic: 1.87 us -> 0.79 us  [the longest x1 0.75 us: on_device(): (norm_wide * (column_sum + scaled_grad.astype(F32))).astype(BF)]
    ppermute x23 -> x22, waiting for transfers between devices: 21.8 us -> 21.9 us  [move(): return lax.ppermute(value, BOTH, pairs)]
  transfers between devices with their start and end apart: 23 -> 22, of which waited for: 9 -> 11; matrix products, arithmetic and copies ran while one was open for 4% -> 2% of each run, Pallas kernels for 16% -> 16%
where the time goes in v3:
time: 67.5 us; the launch traced here: 67.4 us
  starting transfers between devices  22.7 us (34%)
  waiting for transfers between devices  21.9 us (32%)
  Pallas kernels  19.1 us (28%)
  other arithmetic  1.91 us (3%)
  between operations  1.55 us (2%)
    ppermute x22, starting transfers between devices, move(): return lax.ppermute(value, BOTH, pairs)  22.7 us
    ppermute x22, waiting for transfers between devices, move(): return lax.ppermute(value, BOTH, pairs)  21.9 us
    pallas_call x3, Pallas kernels, backward(): pl.pallas_call(functools.partial(backward_kernel, places, unroll, old is...  9.36 us
    pallas_call x2, Pallas kernels, forward(): pl.pallas_call(functools.partial(forward_kernel, places, unrolls), out_sh...  4.85 us
    pallas_call x1, Pallas kernels, stage(): pl.pallas_call(stage_kernel, out_shape=jax.ShapeDtypeStruct((slot_total,...  2.5 us
  transfers between devices with their start and end apart: 22, of which 11 were waited for; matrix products, arithmetic and copies ran while one was open for 2% of the time, Pallas kernels for 16%

profile of v3, /device:TPU:0, one launch (start us, length us, event | category | flops | bytes accessed | tf_op | source)
XLA Modules:
  0.0 67.4 jit_solution(14917129506142670613)
XLA Ops:
  0.6 1.1 %prepare.1 = (bf16[512,128]{1,0:T(8,128)(2,1)S(1)}, f32[512,128]{1,0:T(8,128)S(1)}) custom-call(s32[4,128]{1,0:T(4,128)} %bitcast.18, bf16[512,128]{1,0:T(8,128)(2,1)} %features_hbm.1), custom_call_target="tpu_custom_call" | custom-call | bytes 1024 | tf_op jit(solution)/shard_map/prepare/pallas_call | solution.py:328
  1.7 4.0 %collective-permute-start.7 = (bf16[512,128]{1,0:T(8,128)(2,1)S(1)}, bf16[512,128]{1,0:T(8,128)(2,1)S(1)}, u32[]{:S(2)}, u32[]{:S(2)}) collective-permute-start(bf16[512,128]{1,0:T(8,128)(2,1)S(1)} %get-tuple-element.45.earlier_ref.refs_0_.refs_5_), channel_id=1, source_target_pairs={{0,24},{1,25},{2,26},{3,27},{4,28},{5,29},{6,30},{7,31},{8,16},{9,... | collective-permute-start | bytes 393224 | tf_op jit(solution)/shard_map/ppermute | solution.py:48
  7.9 2.5 %stage_tiles.1.w_ref = bf16[160,128,128]{2,1,0:T(8,128)(2,1)S(1)} custom-call(bf16[160,128,128]{2,1,0:T(8,128)(2,1)} %bitcast.14, bf16[512,128]{1,0:T(8,128)(2,1)S(1)} %get-tuple-element.45.earlier_ref.refs_0_.refs_5_), custom_call_target="tpu_custom_call" | custom-call | bytes 10485760 | tf_op jit(solution)/shard_map/stage_tiles/pallas_call | solution.py:347
  10.6 1.4 %collective-permute-done.6.refs_2_ = bf16[512,128]{1,0:T(8,128)(2,1)S(1)} collective-permute-done((bf16[512,128]{1,0:T(8,128)(2,1)S(1)}, bf16[512,128]{1,0:T(8,128)(2,1)S(1)}, u32[]{:S(2)}, u32[]{:S(2)}) %collective-permute-start.6) | collective-permute-done | bytes 131104 | tf_op jit(solution)/shard_map/ppermute | solution.py:48
  12.2 2.6 %forward_1_2_3.1 = (bf16[1024,128]{1,0:T(8,128)(2,1)S(1)}, bf16[1024,128]{1,0:T(8,128)(2,1)S(1)}, bf16[512,128]{1,0:T(8,128)(2,1)S(1)}) custom-call(f32[512,128]{1,0:T(8,128)S(1)} %get-tuple-element.44.earlier_ref.refs_6_, s32[8]{0:T(128)S(1)} %convert_reduce_fusion.bounds_ref, s32[160]{0:T(256)S(1)} %get-tuple-element.68.row_ref, ...), custom_call_target="tpu_custom_call" | custom-call | bytes 1024 | tf_op jit(solution)/shard_map/forward_1_2_3/pallas_call | solution.py:364
  15.0 2.7 %collective-permute-start.12 = (bf16[512,128]{1,0:T(8,128)(2,1)S(1)}, bf16[512,128]{1,0:T(8,128)(2,1)S(1)}, u32[]{:S(2)}, u32[]{:S(2)}) collective-permute-start(bf16[512,128]{1,0:T(8,128)(2,1)S(1)} %get-tuple-element.50), channel_id=1, source_target_pairs={{0,5},{1,4},{2,7},{3,6},{4,1},{5,0},{6,3},{7,2},{8,13},{9,12},{10,... | collective-permute-start | bytes 393224 | tf_op jit(solution)/shard_map/ppermute | solution.py:48
  17.7 2.2 %forward_0.1 = (bf16[512,128]{1,0:T(8,128)(2,1)S(1)}, bf16[512,128]{1,0:T(8,128)(2,1)S(1)}) custom-call(bf16[1024,128]{1,0:T(8,128)(2,1)S(1)} %get-tuple-element.46.earlier_ref, s32[8]{0:T(128)S(1)} %convert_reduce_fusion.bounds_ref, s32[160]{0:T(256)S(1)} %get-tuple-element.68.row_ref, s32[160]{0:T(256)S(1)} %get-tuple-element.72.col_ref, ...), custom_call_target="tpu_custom_call" | custom-call | bytes 1024 | tf_op jit(solution)/shard_map/forward_0/pallas_call | solution.py:364
  20.1 1.1 %collective-permute-start.11 = (bf16[512,128]{1,0:T(8,128)(2,1)S(1)}, bf16[512,128]{1,0:T(8,128)(2,1)S(1)}, u32[]{:S(2)}, u32[]{:S(2)}) collective-permute-start(bf16[512,128]{1,0:T(8,128)(2,1)S(1)} %get-tuple-element.70), channel_id=1, source_target_pairs={{0,6},{1,7},{2,4},{3,5},{4,2},{5,3},{6,0},{7,1},{8,14},{9,15},{10,... | collective-permute-start | bytes 393224 | tf_op jit(solution)/shard_map/ppermute | solution.py:48
  21.6 2.4 %collective-permute-done.12.refs_4_ = bf16[512,128]{1,0:T(8,128)(2,1)S(1)} collective-permute-done((bf16[512,128]{1,0:T(8,128)(2,1)S(1)}, bf16[512,128]{1,0:T(8,128)(2,1)S(1)}, u32[]{:S(2)}, u32[]{:S(2)}) %collective-permute-start.12) | collective-permute-done | bytes 131104 | tf_op jit(solution)/shard_map/ppermute | solution.py:48
  24.0 4.4 %collective-permute-done.11.refs_3_ = bf16[512,128]{1,0:T(8,128)(2,1)S(1)} collective-permute-done((bf16[512,128]{1,0:T(8,128)(2,1)S(1)}, bf16[512,128]{1,0:T(8,128)(2,1)S(1)}, u32[]{:S(2)}, u32[]{:S(2)}) %collective-permute-start.11) | collective-permute-done | bytes 131104 | tf_op jit(solution)/shard_map/ppermute | solution.py:48
  28.3 1.8 %collective-permute-done.10.refs_2_ = bf16[512,128]{1,0:T(8,128)(2,1)S(1)} collective-permute-done((bf16[512,128]{1,0:T(8,128)(2,1)S(1)}, bf16[512,128]{1,0:T(8,128)(2,1)S(1)}, u32[]{:S(2)}, u32[]{:S(2)}) %collective-permute-start.10) | collective-permute-done | bytes 131104 | tf_op jit(solution)/shard_map/ppermute | solution.py:48
  30.2 1.1 %dense.1 = (bf16[512,256]{1,0:T(8,128)(2,1)}, bf16[512,128]{1,0:T(8,128)(2,1)S(1)}, bf16[512,128]{1,0:T(8,128)(2,1)S(1)}, bf16[512,256]{1,0:T(8,128)(2,1)S(1)}) custom-call(bf16[512,128]{1,0:T(8,128)(2,1)S(1)} %get-tuple-element.47.refs_0_, bf16[512,128]{1,0:T(8,128)(2,1)S(1)} %collective-permute-done.8.refs_1_, ...), custom_call_target="tpu_custom_call" | custom-call | bytes 1024 | tf_op jit(solution)/shard_map/dense/pallas_call | solution.py:389
  31.2 2.8 %collective-permute-start.16 = (bf16[512,128]{1,0:T(8,128)(2,1)S(1)}, bf16[512,128]{1,0:T(8,128)(2,1)S(1)}, u32[]{:S(2)}, u32[]{:S(2)}) collective-permute-start(bf16[512,128]{1,0:T(8,128)(2,1)S(1)} %get-tuple-element.52.refs_0_), channel_id=1, source_target_pairs={{0,5},{1,4},{2,7},{3,6},{4,1},{5,0},{6,3},{7,2},{8,13},{9,12},{10,... | collective-permute-start | bytes 393224 | tf_op jit(solution)/shard_map/ppermute | solution.py:48
  34.0 0.8 %collective-permute-start.15 = (bf16[512,128]{1,0:T(8,128)(2,1)S(1)}, bf16[512,128]{1,0:T(8,128)(2,1)S(1)}, u32[]{:S(2)}, u32[]{:S(2)}) collective-permute-start(bf16[512,128]{1,0:T(8,128)(2,1)S(1)} %get-tuple-element.52.refs_0_), channel_id=1, source_target_pairs={{0,6},{1,7},{2,4},{3,5},{4,2},{5,3},{6,0},{7,1},{8,14},{9,15},{10,... | collective-permute-start | bytes 393224 | tf_op jit(solution)/shard_map/ppermute | solution.py:48
  35.4 3.6 %backward_0.1.earlier_ref.refs_0_ = f32[2176,128]{1,0:T(8,128)S(1)} custom-call(s32[8]{0:T(128)S(1)} %convert_reduce_fusion.bounds_ref, s32[160]{0:T(256)S(1)} %get-tuple-element.68.row_ref, s32[160]{0:T(256)S(1)} %get-tuple-element.72.col_ref, bf16[160,128,128]{2,1,0:T(8,128)(2,1)} %bitcast.15, bf16[512,128]{1,0:T(8,128)(2,1)S(1)} %get-tuple-element.52.refs_0_, ...), custom_call_target="tpu_custom_call" | custom-call | bytes 1024 | tf_op jit(solution)/shard_map/backward_0/pallas_call | solution.py:418
  39.3 9.5 %conditional.2 = (f32[80,256]{1,0:T(8,128)S(1)}) conditional(s32[]{:T(128)} %convert_element_type.59, () %tuple.22, (f32[80,256]{1,0:T(8,128)S(1)}, f32[80,256]{1,0:T(8,128)S(1)}) %tuple.23), branch_computations={%region_1.2_spmd, %region_2.3_spmd} | conditional | flops 184320 | bytes 1351808 | solution.py:53
  39.4 1.3 %collective-permute-done.2 = f32[80,256]{1,0:T(8,128)S(1)} collective-permute-done((f32[80,256]{1,0:T(8,128)S(1)}, f32[80,256]{1,0:T(8,128)S(1)}, u32[]{:S(2)}, u32[]{:S(2)}) %collective-permute-start.2) | collective-permute-done | bytes 81952 | tf_op jit(solution)/shard_map/cond/branch_1_fun/ppermute | solution.py:48
  40.6 1.2 %collective-permute-start.3 = (bf16[80,256]{1,0:T(8,128)(2,1)S(1)}, bf16[80,256]{1,0:T(8,128)(2,1)S(1)}, u32[]{:S(2)}, u32[]{:S(2)}) collective-permute-start(bf16[80,256]{1,0:T(8,128)(2,1)S(1)} %get-tuple-element.66), channel_id=1, source_target_pairs={{0,8},{1,17},{2,10},{3,19},{4,12},{5,21},{6,14},{7,23},{8,0},{9,25... | collective-permute-start | bytes 122888 | tf_op jit(solution)/shard_map/cond/branch_1_fun/ppermute | solution.py:48
  41.9 2.9 %collective-permute-done.3 = bf16[80,256]{1,0:T(8,128)(2,1)S(1)} collective-permute-done((bf16[80,256]{1,0:T(8,128)(2,1)S(1)}, bf16[80,256]{1,0:T(8,128)(2,1)S(1)}, u32[]{:S(2)}, u32[]{:S(2)}) %collective-permute-start.3) | collective-permute-done | bytes 40992 | tf_op jit(solution)/shard_map/cond/branch_1_fun/ppermute | solution.py:48
  44.7 0.8 %collective-permute-start.4 = (bf16[80,256]{1,0:T(8,128)(2,1)S(1)}, bf16[80,256]{1,0:T(8,128)(2,1)S(1)}, u32[]{:S(2)}, u32[]{:S(2)}) collective-permute-start(bf16[80,256]{1,0:T(8,128)(2,1)S(1)} %fusion), channel_id=1, source_target_pairs={{0,16},{1,9},{2,18},{3,11},{4,20},{5,13},{6,22},{7,15},{8,24},{9,1... | collective-permute-start | bytes 122888 | tf_op jit(solution)/shard_map/cond/branch_1_fun/ppermute | solution.py:48
  45.6 3.2 %collective-permute-done.4 = bf16[80,256]{1,0:T(8,128)(2,1)S(1)} collective-permute-done((bf16[80,256]{1,0:T(8,128)(2,1)S(1)}, bf16[80,256]{1,0:T(8,128)(2,1)S(1)}, u32[]{:S(2)}, u32[]{:S(2)}) %collective-permute-start.4) | collective-permute-done | bytes 40992 | tf_op jit(solution)/shard_map/cond/branch_1_fun/ppermute | solution.py:48
  49.0 1.1 %collective-permute-start.17 = (bf16[80,256]{1,0:T(8,128)(2,1)S(1)}, bf16[80,256]{1,0:T(8,128)(2,1)S(1)}, u32[]{:S(2)}, u32[]{:S(2)}) collective-permute-start(bf16[80,256]{1,0:T(8,128)(2,1)S(1)} %convert_element_type.60), channel_id=1, source_target_pairs={{0,2},{1,3},{2,0},{3,1},{4,6},{5,7},{6,4},{7,5},{8,10},{9,11},{10,... | collective-permute-start | bytes 122888 | tf_op jit(solution)/shard_map/ppermute | solution.py:48
  50.1 2.1 %backward_3.1.refs_0_ = f32[2176,128]{1,0:T(8,128)S(1)} custom-call(s32[8]{0:T(128)S(1)} %convert_reduce_fusion.bounds_ref, s32[160]{0:T(256)S(1)} %get-tuple-element.68.row_ref, s32[160]{0:T(256)S(1)} %get-tuple-element.72.col_ref, bf16[160,128,128]{2,1,0:T(8,128)(2,1)} %bitcast.16, f32[2176,128]{1,0:T(8,128)S(1)} %backward_0.1.earlier_ref.refs_0_, ...), custom_call_target="tpu_custom_call" | custom-call | bytes 1024 | tf_op jit(solution)/shard_map/backward_3/pallas_call | solution.py:418
  52.2 0.8 %collective-permute-done.17.refs_1_ = bf16[80,256]{1,0:T(8,128)(2,1)S(1)} collective-permute-done((bf16[80,256]{1,0:T(8,128)(2,1)S(1)}, bf16[80,256]{1,0:T(8,128)(2,1)S(1)}, u32[]{:S(2)}, u32[]{:S(2)}) %collective-permute-start.17) | collective-permute-done | bytes 40992 | tf_op jit(solution)/shard_map/ppermute | solution.py:48
  53.1 3.6 %backward_1_2.1 = (f32[512,128]{1,0:T(8,128)S(1)}, bf16[512,128]{1,0:T(8,128)(2,1)S(1)}, bf16[512,128]{1,0:T(8,128)(2,1)S(1)}, bf16[512,128]{1,0:T(8,128)(2,1)S(1)}) custom-call(s32[8]{0:T(128)S(1)} %convert_reduce_fusion.bounds_ref, s32[160]{0:T(256)S(1)} %get-tuple-element.68.row_ref, s32[160]{0:T(256)S(1)} %get-tuple-element.72.col_ref, ...), custom_call_target="tpu_custom_call" | custom-call | bytes 1024 | tf_op jit(solution)/shard_map/backward_1_2/pallas_call | solution.py:418
  56.7 1.2 %collective-permute-start.19 = (bf16[512,128]{1,0:T(8,128)(2,1)S(1)}, bf16[512,128]{1,0:T(8,128)(2,1)S(1)}, u32[]{:S(2)}, u32[]{:S(2)}) collective-permute-start(bf16[512,128]{1,0:T(8,128)(2,1)S(1)} %get-tuple-element.61), channel_id=1, source_target_pairs={{0,8},{1,17},{2,10},{3,19},{4,12},{5,21},{6,14},{7,23},{8,0},{9,25... | collective-permute-start | bytes 393224 | tf_op jit(solution)/shard_map/ppermute | solution.py:48
  57.9 0.9 %collective-permute-start.20 = (bf16[512,128]{1,0:T(8,128)(2,1)S(1)}, bf16[512,128]{1,0:T(8,128)(2,1)S(1)}, u32[]{:S(2)}, u32[]{:S(2)}) collective-permute-start(bf16[512,128]{1,0:T(8,128)(2,1)S(1)} %get-tuple-element.62), channel_id=1, source_target_pairs={{0,16},{1,9},{2,18},{3,11},{4,20},{5,13},{6,22},{7,15},{8,24},{9,1... | collective-permute-start | bytes 393224 | tf_op jit(solution)/shard_map/ppermute | solution.py:48
  58.8 1.4 %collective-permute-start.21 = (bf16[512,128]{1,0:T(8,128)(2,1)S(1)}, bf16[512,128]{1,0:T(8,128)(2,1)S(1)}, u32[]{:S(2)}, u32[]{:S(2)}) collective-permute-start(bf16[512,128]{1,0:T(8,128)(2,1)S(1)} %get-tuple-element.63), channel_id=1, source_target_pairs={{0,24},{1,25},{2,26},{3,27},{4,28},{5,29},{6,30},{7,31},{8,16},{9,... | collective-permute-start | bytes 393224 | tf_op jit(solution)/shard_map/ppermute | solution.py:48
  60.2 6.3 %conditional.3 = (f32[128,256]{1,0:T(8,128)S(1)}, f32[256]{0:T(256)S(1)}) conditional(s32[]{:T(128)} %convert_element_type.59, () %tuple.24, (s32[]{:T(128)}, bf16[80,256]{1,0:T(8,128)(2,1)S(1)}, f32[80,256]{1,0:T(8,128)S(1)}) %tuple.25), branch_computations={%region_3.4_spmd, %region_4.5_spmd} | conditional | flops 262145 | bytes 1230954 | solution.py:53
  60.3 2.7 %collective-permute-start = (bf16[80,256]{1,0:T(8,128)(2,1)S(1)}, bf16[80,256]{1,0:T(8,128)(2,1)S(1)}, u32[]{:S(2)}, u32[]{:S(2)}) collective-permute-start(bf16[80,256]{1,0:T(8,128)(2,1)S(1)} %fusion.1), channel_id=1, source_target_pairs={{0,4},{1,5},{2,6},{3,7},{4,0},{5,1},{6,2},{7,3},{8,12},{9,13},{10,... | collective-permute-start | bytes 122888 | tf_op jit(solution)/shard_map/cond/branch_1_fun/ppermute | solution.py:48
  62.9 2.3 %collective-permute-done = bf16[80,256]{1,0:T(8,128)(2,1)S(1)} collective-permute-done((bf16[80,256]{1,0:T(8,128)(2,1)S(1)}, bf16[80,256]{1,0:T(8,128)(2,1)S(1)}, u32[]{:S(2)}, u32[]{:S(2)}) %collective-permute-start) | collective-permute-done | bytes 40992 | tf_op jit(solution)/shard_map/cond/branch_1_fun/ppermute | solution.py:48
  65.4 1.2 %collective-permute-done.1 = f32[64,256]{1,0:T(8,128)S(1)} collective-permute-done((f32[64,256]{1,0:T(8,128)S(1)}, f32[64,256]{1,0:T(8,128)S(1)}, u32[]{:S(2)}, u32[]{:S(2)}) %collective-permute-start.1) | collective-permute-done | bytes 65568 | tf_op jit(solution)/shard_map/cond/branch_1_fun/ppermute | solution.py:48
  (55 shorter events, 4.5 us)
Async XLA Ops:
  1.7 8.9 %collective-permute-start.7 = (bf16[512,128]{1,0:T(8,128)(2,1)S(1)}, bf16[512,128]{1,0:T(8,128)(2,1)S(1)}, u32[]{:S(2)}, u32[]{:S(2)}) collective-permute-start(bf16[512,128]{1,0:T(8,128)(2,1)S(1)} %get-tuple-element.45.earlier_ref.refs_0_.refs_5_), channel_id=1, source_target_pairs={{0,24},{1,25},{2,26},{3,27},{4,28},{5,29},{6,30},{7,31},{8,16},{9,... | collective-permute-start | bytes 393224 | tf_op jit(solution)/shard_map/ppermute | solution.py:48
  5.7 6.3 %collective-permute-start.6 = (bf16[512,128]{1,0:T(8,128)(2,1)S(1)}, bf16[512,128]{1,0:T(8,128)(2,1)S(1)}, u32[]{:S(2)}, u32[]{:S(2)}) collective-permute-start(bf16[512,128]{1,0:T(8,128)(2,1)S(1)} %get-tuple-element.45.earlier_ref.refs_0_.refs_5_), channel_id=1, source_target_pairs={{0,16},{1,9},{2,18},{3,11},{4,20},{5,13},{6,22},{7,15},{8,24},{9,1... | collective-permute-start | bytes 393224 | tf_op jit(solution)/shard_map/ppermute | solution.py:48
  6.2 6.0 %collective-permute-start.5 = (bf16[512,128]{1,0:T(8,128)(2,1)S(1)}, bf16[512,128]{1,0:T(8,128)(2,1)S(1)}, u32[]{:S(2)}, u32[]{:S(2)}) collective-permute-start(bf16[512,128]{1,0:T(8,128)(2,1)S(1)} %get-tuple-element.45.earlier_ref.refs_0_.refs_5_), channel_id=1, source_target_pairs={{0,8},{1,17},{2,10},{3,19},{4,12},{5,21},{6,14},{7,23},{8,0},{9,25... | collective-permute-start | bytes 393224 | tf_op jit(solution)/shard_map/ppermute | solution.py:48
  14.9 5.1 %collective-permute-start.9 = (bf16[1024,128]{1,0:T(8,128)(2,1)S(1)}, bf16[1024,128]{1,0:T(8,128)(2,1)S(1)}, u32[]{:S(2)}, u32[]{:S(2)}) collective-permute-start(bf16[1024,128]{1,0:T(8,128)(2,1)S(1)} %get-tuple-element.46.earlier_ref), channel_id=1, source_target_pairs={{0,1},{1,0},{2,3},{3,2},{4,5},{5,4},{6,7},{7,6},{8,9},{9,8},{10,11... | collective-permute-start | bytes 786440 | tf_op jit(solution)/shard_map/ppermute | solution.py:48
  15.0 9.0 %collective-permute-start.12 = (bf16[512,128]{1,0:T(8,128)(2,1)S(1)}, bf16[512,128]{1,0:T(8,128)(2,1)S(1)}, u32[]{:S(2)}, u32[]{:S(2)}) collective-permute-start(bf16[512,128]{1,0:T(8,128)(2,1)S(1)} %get-tuple-element.50), channel_id=1, source_target_pairs={{0,5},{1,4},{2,7},{3,6},{4,1},{5,0},{6,3},{7,2},{8,13},{9,12},{10,... | collective-permute-start | bytes 393224 | tf_op jit(solution)/shard_map/ppermute | solution.py:48
  19.9 10.2 %copy-start = (bf16[512,256]{1,0:T(8,128)(2,1)S(1)}, bf16[512,256]{1,0:T(8,128)(2,1)}, u32[]{:S(2)}) copy-start(bf16[512,256]{1,0:T(8,128)(2,1)} %refs_9_.1) | copy-start | bytes 786436
  19.9 10.2 %copy-start.1 = (bf16[128,256]{1,0:T(8,128)(2,1)S(1)}, bf16[128,256]{1,0:T(8,128)(2,1)}, u32[]{:S(2)}) copy-start(bf16[128,256]{1,0:T(8,128)(2,1)} %refs_7_.1) | copy-start | bytes 196612
  19.9 10.2 %copy-start.2 = (f32[256]{0:T(256)S(1)}, f32[256]{0:T(256)}, u32[]{:S(2)}) copy-start(f32[256]{0:T(256)} %param.20) | copy-start | bytes 3076
  19.9 4.0 %collective-permute-start.8 = (bf16[512,128]{1,0:T(8,128)(2,1)S(1)}, bf16[512,128]{1,0:T(8,128)(2,1)S(1)}, u32[]{:S(2)}, u32[]{:S(2)}) collective-permute-start(bf16[512,128]{1,0:T(8,128)(2,1)S(1)} %get-tuple-element.48), channel_id=1, source_target_pairs={{0,1},{1,0},{2,3},{3,2},{4,5},{5,4},{6,7},{7,6},{8,9},{9,8},{10,11... | collective-permute-start | bytes 393224 | tf_op jit(solution)/shard_map/ppermute | solution.py:48
  20.1 8.2 %collective-permute-start.11 = (bf16[512,128]{1,0:T(8,128)(2,1)S(1)}, bf16[512,128]{1,0:T(8,128)(2,1)S(1)}, u32[]{:S(2)}, u32[]{:S(2)}) collective-permute-start(bf16[512,128]{1,0:T(8,128)(2,1)S(1)} %get-tuple-element.70), channel_id=1, source_target_pairs={{0,6},{1,7},{2,4},{3,5},{4,2},{5,3},{6,0},{7,1},{8,14},{9,15},{10,... | collective-permute-start | bytes 393224 | tf_op jit(solution)/shard_map/ppermute | solution.py:48
  21.3 8.9 %collective-permute-start.10 = (bf16[512,128]{1,0:T(8,128)(2,1)S(1)}, bf16[512,128]{1,0:T(8,128)(2,1)S(1)}, u32[]{:S(2)}, u32[]{:S(2)}) collective-permute-start(bf16[512,128]{1,0:T(8,128)(2,1)S(1)} %get-tuple-element.71), channel_id=1, source_target_pairs={{0,2},{1,3},{2,0},{3,1},{4,6},{5,7},{6,4},{7,5},{8,10},{9,11},{10,... | collective-permute-start | bytes 393224 | tf_op jit(solution)/shard_map/ppermute | solution.py:48
  31.2 4.2 %collective-permute-start.13 = (bf16[512,128]{1,0:T(8,128)(2,1)S(1)}, bf16[512,128]{1,0:T(8,128)(2,1)S(1)}, u32[]{:S(2)}, u32[]{:S(2)}) collective-permute-start(bf16[512,128]{1,0:T(8,128)(2,1)S(1)} %get-tuple-element.52.refs_0_), channel_id=1, source_target_pairs={{0,1},{1,0},{2,3},{3,2},{4,5},{5,4},{6,7},{7,6},{8,9},{9,8},{10,11... | collective-permute-start | bytes 393224 | tf_op jit(solution)/shard_map/ppermute | solution.py:48
  31.2 17.6 %collective-permute-start.16 = (bf16[512,128]{1,0:T(8,128)(2,1)S(1)}, bf16[512,128]{1,0:T(8,128)(2,1)S(1)}, u32[]{:S(2)}, u32[]{:S(2)}) collective-permute-start(bf16[512,128]{1,0:T(8,128)(2,1)S(1)} %get-tuple-element.52.refs_0_), channel_id=1, source_target_pairs={{0,5},{1,4},{2,7},{3,6},{4,1},{5,0},{6,3},{7,2},{8,13},{9,12},{10,... | collective-permute-start | bytes 393224 | tf_op jit(solution)/shard_map/ppermute | solution.py:48
  34.0 14.8 %collective-permute-start.15 = (bf16[512,128]{1,0:T(8,128)(2,1)S(1)}, bf16[512,128]{1,0:T(8,128)(2,1)S(1)}, u32[]{:S(2)}, u32[]{:S(2)}) collective-permute-start(bf16[512,128]{1,0:T(8,128)(2,1)S(1)} %get-tuple-element.52.refs_0_), channel_id=1, source_target_pairs={{0,6},{1,7},{2,4},{3,5},{4,2},{5,3},{6,0},{7,1},{8,14},{9,15},{10,... | collective-permute-start | bytes 393224 | tf_op jit(solution)/shard_map/ppermute | solution.py:48
  34.8 14.1 %collective-permute-start.14 = (bf16[512,128]{1,0:T(8,128)(2,1)S(1)}, bf16[512,128]{1,0:T(8,128)(2,1)S(1)}, u32[]{:S(2)}, u32[]{:S(2)}) collective-permute-start(bf16[512,128]{1,0:T(8,128)(2,1)S(1)} %get-tuple-element.52.refs_0_), channel_id=1, source_target_pairs={{0,2},{1,3},{2,0},{3,1},{4,6},{5,7},{6,4},{7,5},{8,10},{9,11},{10,... | collective-permute-start | bytes 393224 | tf_op jit(solution)/shard_map/ppermute | solution.py:48
  39.3 1.3 %collective-permute-start.2 = (f32[80,256]{1,0:T(8,128)S(1)}, f32[80,256]{1,0:T(8,128)S(1)}, u32[]{:S(2)}, u32[]{:S(2)}) collective-permute-start(f32[80,256]{1,0:T(8,128)S(1)} %get-tuple-element.14), channel_id=1, source_target_pairs={{0,1},{1,0},{2,3},{3,2},{4,5},{5,4},{6,7},{7,6},{8,9},{9,8},{10,11... | collective-permute-start | bytes 245768 | tf_op jit(solution)/shard_map/cond/branch_1_fun/ppermute | solution.py:48
  40.6 4.1 %collective-permute-start.3 = (bf16[80,256]{1,0:T(8,128)(2,1)S(1)}, bf16[80,256]{1,0:T(8,128)(2,1)S(1)}, u32[]{:S(2)}, u32[]{:S(2)}) collective-permute-start(bf16[80,256]{1,0:T(8,128)(2,1)S(1)} %get-tuple-element.66), channel_id=1, source_target_pairs={{0,8},{1,17},{2,10},{3,19},{4,12},{5,21},{6,14},{7,23},{8,0},{9,25... | collective-permute-start | bytes 122888 | tf_op jit(solution)/shard_map/cond/branch_1_fun/ppermute | solution.py:48
  44.7 4.1 %collective-permute-start.4 = (bf16[80,256]{1,0:T(8,128)(2,1)S(1)}, bf16[80,256]{1,0:T(8,128)(2,1)S(1)}, u32[]{:S(2)}, u32[]{:S(2)}) collective-permute-start(bf16[80,256]{1,0:T(8,128)(2,1)S(1)} %fusion), channel_id=1, source_target_pairs={{0,16},{1,9},{2,18},{3,11},{4,20},{5,13},{6,22},{7,15},{8,24},{9,1... | collective-permute-start | bytes 122888 | tf_op jit(solution)/shard_map/cond/branch_1_fun/ppermute | solution.py:48
  48.9 4.2 %collective-permute-start.18 = (bf16[1024,128]{1,0:T(8,128)(2,1)S(1)}, bf16[1024,128]{1,0:T(8,128)(2,1)S(1)}, u32[]{:S(2)}, u32[]{:S(2)}) collective-permute-start(bf16[1024,128]{1,0:T(8,128)(2,1)S(1)} %constant_dynamic-update-slice_fusion.refs_1_), channel_id=1, source_target_pairs={{0,1},{1,0},{2,3},{3,2},{4,5},{5,4},{6,7},{7,6},{8,9},{9,8},{10,11... | collective-permute-start | bytes 786440 | tf_op jit(solution)/shard_map/ppermute | solution.py:48
  49.0 4.1 %collective-permute-start.17 = (bf16[80,256]{1,0:T(8,128)(2,1)S(1)}, bf16[80,256]{1,0:T(8,128)(2,1)S(1)}, u32[]{:S(2)}, u32[]{:S(2)}) collective-permute-start(bf16[80,256]{1,0:T(8,128)(2,1)S(1)} %convert_element_type.60), channel_id=1, source_target_pairs={{0,2},{1,3},{2,0},{3,1},{4,6},{5,7},{6,4},{7,5},{8,10},{9,11},{10,... | collective-permute-start | bytes 122888 | tf_op jit(solution)/shard_map/ppermute | solution.py:48
  56.7 9.9 %collective-permute-start.19 = (bf16[512,128]{1,0:T(8,128)(2,1)S(1)}, bf16[512,128]{1,0:T(8,128)(2,1)S(1)}, u32[]{:S(2)}, u32[]{:S(2)}) collective-permute-start(bf16[512,128]{1,0:T(8,128)(2,1)S(1)} %get-tuple-element.61), channel_id=1, source_target_pairs={{0,8},{1,17},{2,10},{3,19},{4,12},{5,21},{6,14},{7,23},{8,0},{9,25... | collective-permute-start | bytes 393224 | tf_op jit(solution)/shard_map/ppermute | solution.py:48
  57.9 8.7 %collective-permute-start.20 = (bf16[512,128]{1,0:T(8,128)(2,1)S(1)}, bf16[512,128]{1,0:T(8,128)(2,1)S(1)}, u32[]{:S(2)}, u32[]{:S(2)}) collective-permute-start(bf16[512,128]{1,0:T(8,128)(2,1)S(1)} %get-tuple-element.62), channel_id=1, source_target_pairs={{0,16},{1,9},{2,18},{3,11},{4,20},{5,13},{6,22},{7,15},{8,24},{9,1... | collective-permute-start | bytes 393224 | tf_op jit(solution)/shard_map/ppermute | solution.py:48
  58.8 7.8 %collective-permute-start.21 = (bf16[512,128]{1,0:T(8,128)(2,1)S(1)}, bf16[512,128]{1,0:T(8,128)(2,1)S(1)}, u32[]{:S(2)}, u32[]{:S(2)}) collective-permute-start(bf16[512,128]{1,0:T(8,128)(2,1)S(1)} %get-tuple-element.63), channel_id=1, source_target_pairs={{0,24},{1,25},{2,26},{3,27},{4,28},{5,29},{6,30},{7,31},{8,16},{9,... | collective-permute-start | bytes 393224 | tf_op jit(solution)/shard_map/ppermute | solution.py:48
  60.3 5.0 %collective-permute-start = (bf16[80,256]{1,0:T(8,128)(2,1)S(1)}, bf16[80,256]{1,0:T(8,128)(2,1)S(1)}, u32[]{:S(2)}, u32[]{:S(2)}) collective-permute-start(bf16[80,256]{1,0:T(8,128)(2,1)S(1)} %fusion.1), channel_id=1, source_target_pairs={{0,4},{1,5},{2,6},{3,7},{4,0},{5,1},{6,2},{7,3},{8,12},{9,13},{10,... | collective-permute-start | bytes 122888 | tf_op jit(solution)/shard_map/cond/branch_1_fun/ppermute | solution.py:48
  65.3 1.3 %collective-permute-start.1 = (f32[64,256]{1,0:T(8,128)S(1)}, f32[64,256]{1,0:T(8,128)S(1)}, u32[]{:S(2)}, u32[]{:S(2)}) collective-permute-start(f32[64,256]{1,0:T(8,128)S(1)} %slice.14), channel_id=1, source_target_pairs={{0,1},{1,0},{2,3},{3,2},{4,5},{5,4},{6,7},{7,6},{8,9},{9,8},{10,11... | collective-permute-start | bytes 196616 | tf_op jit(solution)/shard_map/cond/branch_1_fun/ppermute | solution.py:48
  66.6 0.8 %copy-start.3 = (f32[128,256]{1,0:T(8,128)}, f32[128,256]{1,0:T(8,128)S(1)}, u32[]{:S(2)}) copy-start(f32[128,256]{1,0:T(8,128)S(1)} %get-tuple-element.42) | copy-start | bytes 393220
  66.6 0.8 %copy-start.4 = (f32[256]{0:T(256)}, f32[256]{0:T(256)S(1)}, u32[]{:S(2)}) copy-start(f32[256]{0:T(256)S(1)} %get-tuple-element.43) | copy-start | bytes 3076

commit v4 on v3

--- a/solution.py
+++ b/solution.py
@@ -200,73 +200,73 @@
                 first += rows
 
 
-def stream_slots(w_hbm, held, sems, ranges, unroll, body):
+def stream_slots(w_hbm, held, sems, ranges, unroll):
     slot_total = w_hbm.shape[0]
-    counts = [(high - low + unroll - 1) // unroll for low, high, n in ranges]
+    begins = [0]
+    for low, high in ranges:
+        begins.append(begins[-1] + (high - low + unroll - 1) // unroll)
 
     def fetch(low, i, place):
         first = jnp.minimum(low + i * unroll, slot_total - unroll)
         return first, pltpu.make_async_copy(w_hbm.at[pl.ds(first, unroll)], held.at[place], sems.at[place])
 
-    begin = 0
-    for (low, high, n), count in zip(ranges, counts):
-
-        def start(i, carry, low=low, begin=begin):
+    for n, (low, high) in enumerate(ranges):
+
+        def start(i, carry, low=low, begin=begins[n]):
             fetch(low, i, begin + i)[1].start()
             return carry
 
-        lax.fori_loop(0, count, start, 0)
-        begin = begin + count
-    begin = 0
-    for (low, high, n), count in zip(ranges, counts):
-
-        def step(i, carry, low=low, high=high, n=n, begin=begin):
-            first, copy = fetch(low, i, begin + i)
-            copy.wait()
-            for u in range(unroll):
-                t = first + u
-                body(held[begin + i, u], t, (t >= low + i * unroll) & (t < high), n)
-            return carry
-
-        lax.fori_loop(0, count, step, 0)
-        begin = begin + count
-
-
-def backward_kernel(places, unroll, first_call, last_call, bounds_ref, row_ref, col_ref, w_ref, *refs):
+        lax.fori_loop(0, begins[n + 1] - begins[n], start, 0)
+
+    def finish(body):
+        for n, (low, high) in enumerate(ranges):
+
+            def step(i, carry, low=low, high=high, n=n, begin=begins[n]):
+                first, copy = fetch(low, i, begin + i)
+                copy.wait()
+                for u in range(unroll):
+                    t = first + u
+                    body(held[begin + i, u], t, (t >= low + i * unroll) & (t < high), n)
+                return carry
+
+            lax.fori_loop(0, begins[n + 1] - begins[n], step, 0)
+
+    return finish
+
+
+def backward_kernel(places, unroll, bounds_ref, row_ref, col_ref, w_ref, *refs):
     refs, (total, held, tiles_held, sems) = refs[:-4], refs[-4:]
+    ranges = [(bounds_ref[place], bounds_ref[4 + place]) for place in places]
+    finish = stream_slots(w_ref, tiles_held, sems, ranges, unroll)
     tile = w_ref.shape[-1]
-    if first_call:
-        block_refs, out_refs = refs[:2], refs[2:]
+    block_refs, out_refs = (refs[:2], refs[2:]) if places == (0,) else (refs[1:4], refs[4:])
+    if places == (0,):
         total[...] = jnp.zeros_like(total)
     else:
-        old_ref, refs = refs[0], refs[1:]
-        inputs = 2 if last_call else 1
-        block_refs, out_refs = refs[:inputs], refs[inputs:]
-        total[...] = old_ref[...]
+        used_rows = refs[0].shape[0]
+        total[:used_rows, :] = refs[0][...].astype(F32)
+        total[used_rows:, :] = jnp.zeros((total.shape[0] - used_rows, total.shape[1]), F32)
     gather_blocks(block_refs, held)
     spare = total.shape[0] // tile - 1
-    held_tiles = held.shape[0] // tile
+    block_tiles = held.shape[0] // tile // (2 if places == (0,) else 5)
 
     def body(w, t, used, n):
         row = row_ref[t]
         if places[n] == 3:
-            row = row % held_tiles
-        elif len(places) > 1:
-            block_tiles = held_tiles // (2 * len(places))
-            row = jnp.where(row < block_tiles, row, row + (len(places) - 1) * block_tiles) + n * block_tiles
+            row = row % block_tiles + 4 * block_tiles
+        elif places[n] > 0:
+            row = jnp.where(row < block_tiles, row, row + block_tiles) + n * block_tiles
         part = lax.dot_general(
             w, held[aligned(row, tile), :], (((0,), (0,)), ((), ())), preferred_element_type=F32
         )
         total[aligned(jnp.where(used, col_ref[t], spare), tile), :] += part
 
-    ranges = [(bounds_ref[place], bounds_ref[4 + place], n) for n, place in enumerate(places)]
-    stream_slots(w_ref, tiles_held, sems, ranges, unroll, body)
-    if last_call:
-        rows = out_refs[0].shape[0]
-        for n, out_ref in enumerate(out_refs):
-            out_ref[...] = total[n * rows : (n + 1) * rows, :].astype(out_ref.dtype)
-    else:
-        out_refs[0][...] = total[...]
+    finish(body)
+    first = 0
+    for out_ref in out_refs:
+        rows = out_ref.shape[0]
+        out_ref[...] = total[first : first + rows, :].astype(out_ref.dtype)
+        first += rows
 
 
 def dense_kernel(*refs):
@@ -288,7 +288,7 @@
     pre_grad_ref[...] = pre_grad
 
 
-def weight_kernel(core_ref, aggregated_ref, pre_grad_ref, earlier_ref, keep_ref, send_ref, full):
+def weight_kernel(core_ref, aggregated_ref, pre_grad_ref, keep_ref, send_ref, full):
     pre_grad = pre_grad_ref[...]
     half = full.shape[0] // CORES
     full[...] = lax.dot_general(
@@ -405,62 +405,60 @@
     grads3 = move(scaled_grad, pair_partner(3, True))
     grads1 = move(scaled_grad, pair_partner(1, True))
 
-    total_shape = jax.ShapeDtypeStruct(((col_tiles + 1) * tile, feat_width), F32)
-
     tiles_hbm = in_hbm(tile_weights[0, 0])
-
-    def backward(places, unroll, old, blocks):
-        last = len(places) > 1
-        out_shape = [total_shape]
-        if last:
-            out_shape = [jax.ShapeDtypeStruct((row_count, feat_width), F32)] + [block_shape] * (rep_count - 1)
+    column_shape = jax.ShapeDtypeStruct((col_tiles * tile, feat_width), BF)
+
+    def backward(places, unroll, out_shape, *blocks):
         fetches = slot_total // unroll + len(places)
+        held_rows = (2 if places == (0,) else 5) * row_count
         return pl.pallas_call(
-            functools.partial(backward_kernel, places, unroll, old is None, last),
+            functools.partial(backward_kernel, places, unroll),
             out_shape=out_shape,
-            in_specs=[SMEM, SMEM, SMEM, HBM] + [VMEM] * ((old is not None) + len(blocks)),
+            in_specs=[SMEM, SMEM, SMEM, HBM] + [VMEM] * len(blocks),
             out_specs=[VMEM] * len(out_shape),
             scratch_shapes=[
-                pltpu.VMEM(total_shape.shape, F32),
-                pltpu.VMEM((sum(part.shape[0] for part in blocks), feat_width), BF),
+                pltpu.VMEM(((col_tiles + 1) * tile, feat_width), F32),
+                pltpu.VMEM((held_rows, feat_width), BF),
                 pltpu.VMEM((fetches, unroll, tile, tile), BF),
                 pltpu.SemaphoreType.DMA((fetches,)),
             ],
             compiler_params=params(28),
             cost_estimate=SMALL,
             name="backward_" + "_".join(map(str, places)),
-        )(bounds, row_place, col_place, tiles_hbm, *([] if old is None else [old]), *blocks)
+        )(bounds, row_place, col_place, tiles_hbm, *blocks)
 
     grad_rows = feat_width // CORES
     half_shape = jax.ShapeDtypeStruct((grad_rows + BIAS_ROWS, hid_width), F32)
 
-    (total,) = backward((0,), 16, None, [scaled_grad, swap_cores(scaled_grad)])
-    halves = pl.pallas_call(
-        weight_kernel,
-        out_shape=[half_shape] * 2,
-        in_specs=[SMEM, VMEM, VMEM, ANY],
-        out_specs=[VMEM] * 2,
-        scratch_shapes=[pltpu.VMEM((feat_width, hid_width), F32)],
-        compiler_params=params(16),
-        cost_estimate=SMALL,
-        name="weight_terms",
-    )(core[None].astype(jnp.int32), aggregated, pre_grad, total)
-
-    def rep_sum(keep, send):
+    def own_pair(scaled_grad, aggregated, pre_grad):
+        other = swap_cores(scaled_grad)
+        keep, send = pl.pallas_call(
+            weight_kernel,
+            out_shape=[half_shape] * 2,
+            in_specs=[SMEM, VMEM, VMEM],
+            out_specs=[VMEM] * 2,
+            scratch_shapes=[pltpu.VMEM((feat_width, hid_width), F32)],
+            compiler_params=params(16),
+            cost_estimate=SMALL,
+            name="weight_terms",
+        )(core[None].astype(jnp.int32), aggregated, pre_grad)
         grad = keep + swap_cores(send)
+        (total,) = backward((0,), 16, [column_shape], scaled_grad, other)
         for n in range(rep_bits()):
-            grad = grad + move(grad.astype(BF), rep_partner(1 << n)).astype(F32)
-        return grad
-
-    grad = block(rep_sum, *halves)
+            came = move(grad.astype(BF), rep_partner(1 << n))
+            if n == 0:
+                (grad,) = together([grad], [total])
+            grad = grad + came.astype(F32)
+        return total, grad
+
+    total, grad = block(own_pair, scaled_grad, aggregated, pre_grad)
     blk_bits = (blk_count - 1).bit_length()
     grads1, grads2, grads3 = together([grads1, grads2, grads3], [grad])
     near_far = jnp.concatenate([grads1, grads2])
-    other = swap_cores(near_far)
-    (total,) = backward((3,), 10, total, [grads3])
     came = move(grad.astype(BF), lambda r, k: (r, k ^ 2))
-    (total,) = together([total], [came])
-    columns = backward((1, 2), 16, total, [near_far, other])
+    column_shapes = [jax.ShapeDtypeStruct((row_count, feat_width), F32)] + [block_shape] * (rep_count - 1)
+    columns = backward((1, 2, 3), 16, column_shapes, total, near_far, swap_cores(near_far), grads3)
+    columns = together(columns, [came])
 
     def finish_weight(grad, came):
         grad = grad + came.astype(F32)

time: 67.5 us -> 63.3 us (0.938)
  waiting for transfers between devices: 21.9 us -> 17.7 us
  Pallas kernels: 19.1 us -> 17.2 us
  starting transfers between devices: 22.7 us -> 24.5 us
    ppermute x22, waiting for transfers between devices: 21.9 us -> 17.7 us  [move(): return lax.ppermute(value, BOTH, pairs)]
    ppermute x22, starting transfers between devices: 22.7 us -> 24.5 us  [move(): return lax.ppermute(value, BOTH, pairs)]
    pallas_call x4 -> x3, Pallas kernels: 9.6 us -> 8.22 us  [the longest x2 7.98 us: backward(): pl.pallas_call(functools.partial(backward_kernel, places, unroll), out_sh...]
  transfers between devices with their start and end apart: 22 -> 22, of which waited for: 11 -> 9; matrix products, arithmetic and copies ran while one was open for 2% -> 2% of each run, Pallas kernels for 16% -> 20%
where the time goes in v4:
time: 63.3 us; the launch traced here: 63 us
  starting transfers between devices  24.5 us (39%)
  waiting for transfers between devices  17.7 us (28%)
  Pallas kernels  17.2 us (27%)
  other arithmetic  1.92 us (3%)
  between operations  1.52 us (2%)
    ppermute x22, starting transfers between devices, move(): return lax.ppermute(value, BOTH, pairs)  24.5 us
    ppermute x22, waiting for transfers between devices, move(): return lax.ppermute(value, BOTH, pairs)  17.7 us
    pallas_call x2, Pallas kernels, backward(): pl.pallas_call(functools.partial(backward_kernel, places, unroll), out_sh...  7.98 us
    pallas_call x2, Pallas kernels, forward(): pl.pallas_call(functools.partial(forward_kernel, places, unrolls), out_sh...  4.27 us
    pallas_call x1, Pallas kernels, stage(): pl.pallas_call(stage_kernel, out_shape=jax.ShapeDtypeStruct((slot_total,...  2.5 us
  transfers between devices with their start and end apart: 22, of which 9 were waited for; matrix products, arithmetic and copies ran while one was open for 2% of the time, Pallas kernels for 20%

profile of v4, /device:TPU:0, one launch (start us, length us, event | category | flops | bytes accessed | tf_op | source)
XLA Modules:
  0.0 63.0 jit_solution(6904593774814057455)
XLA Ops:
  0.6 1.1 %prepare.1 = (bf16[512,128]{1,0:T(8,128)(2,1)S(1)}, f32[512,128]{1,0:T(8,128)S(1)}) custom-call(s32[4,128]{1,0:T(4,128)} %bitcast.17, bf16[512,128]{1,0:T(8,128)(2,1)} %features_hbm.1), custom_call_target="tpu_custom_call" | custom-call | bytes 1024 | tf_op jit(solution)/shard_map/prepare/pallas_call | solution.py:328
  1.7 4.0 %collective-permute-start.8 = (bf16[512,128]{1,0:T(8,128)(2,1)S(1)}, bf16[512,128]{1,0:T(8,128)(2,1)S(1)}, u32[]{:S(2)}, u32[]{:S(2)}) collective-permute-start(bf16[512,128]{1,0:T(8,128)(2,1)S(1)} %get-tuple-element.66.earlier_ref.refs_0_.refs_5_), channel_id=1, source_target_pairs={{0,24},{1,25},{2,26},{3,27},{4,28},{5,29},{6,30},{7,31},{8,16},{9,... | collective-permute-start | bytes 393224 | tf_op jit(solution)/shard_map/ppermute | solution.py:48
  5.7 0.5 collective-permute-start.7
  7.0 0.7 %fusion.2 = (s32[160]{0:T(256)S(1)}, s32[160]{0:T(256)S(1)}, s32[160]{0:T(256)S(1)}) fusion(s32[]{:T(128)} %select_n.72, s32[160]{0:T(256)} %bitcast.18, s32[]{:T(128)S(6)} %axis_index.33, s32[160]{0:T(256)} %bitcast.19, pred[]{:T(512)S(6)} %eq.21), kind=kLoop, calls=%fused_computation.28 | loop fusion | flops 10240 | bytes 3209 | tf_op jit(solution)/shard_map/add | solution.py:321
  7.9 2.5 %stage_tiles.1.w_ref = bf16[160,128,128]{2,1,0:T(8,128)(2,1)S(1)} custom-call(bf16[160,128,128]{2,1,0:T(8,128)(2,1)} %bitcast.14, bf16[512,128]{1,0:T(8,128)(2,1)S(1)} %get-tuple-element.66.earlier_ref.refs_0_.refs_5_), custom_call_target="tpu_custom_call" | custom-call | bytes 10485760 | tf_op jit(solution)/shard_map/stage_tiles/pallas_call | solution.py:347
  10.6 1.4 %collective-permute-done.7.refs_2_ = bf16[512,128]{1,0:T(8,128)(2,1)S(1)} collective-permute-done((bf16[512,128]{1,0:T(8,128)(2,1)S(1)}, bf16[512,128]{1,0:T(8,128)(2,1)S(1)}, u32[]{:S(2)}, u32[]{:S(2)}) %collective-permute-start.7) | collective-permute-done | bytes 131104 | tf_op jit(solution)/shard_map/ppermute | solution.py:48
  12.3 2.3 %forward_1_2_3.1 = (bf16[1024,128]{1,0:T(8,128)(2,1)S(1)}, bf16[1024,128]{1,0:T(8,128)(2,1)S(1)}, bf16[512,128]{1,0:T(8,128)(2,1)S(1)}) custom-call(f32[512,128]{1,0:T(8,128)S(1)} %get-tuple-element.65.earlier_ref.refs_6_, s32[8]{0:T(128)S(1)} %convert_reduce_fusion.bounds_ref, s32[160]{0:T(256)S(1)} %get-tuple-element.93.row_ref, ...), custom_call_target="tpu_custom_call" | custom-call | bytes 1024 | tf_op jit(solution)/shard_map/forward_1_2_3/pallas_call | solution.py:364
  14.7 3.0 %collective-permute-start.13 = (bf16[512,128]{1,0:T(8,128)(2,1)S(1)}, bf16[512,128]{1,0:T(8,128)(2,1)S(1)}, u32[]{:S(2)}, u32[]{:S(2)}) collective-permute-start(bf16[512,128]{1,0:T(8,128)(2,1)S(1)} %get-tuple-element.71), channel_id=1, source_target_pairs={{0,5},{1,4},{2,7},{3,6},{4,1},{5,0},{6,3},{7,2},{8,13},{9,12},{10,... | collective-permute-start | bytes 393224 | tf_op jit(solution)/shard_map/ppermute | solution.py:48
  17.7 1.9 %forward_0.1 = (bf16[512,128]{1,0:T(8,128)(2,1)S(1)}, bf16[512,128]{1,0:T(8,128)(2,1)S(1)}) custom-call(bf16[1024,128]{1,0:T(8,128)(2,1)S(1)} %get-tuple-element.67.earlier_ref, s32[8]{0:T(128)S(1)} %convert_reduce_fusion.bounds_ref, s32[160]{0:T(256)S(1)} %get-tuple-element.93.row_ref, s32[160]{0:T(256)S(1)} %get-tuple-element.97.col_ref, ...), custom_call_target="tpu_custom_call" | custom-call | bytes 1024 | tf_op jit(solution)/shard_map/forward_0/pallas_call | solution.py:364
  19.8 1.1 %collective-permute-start.12 = (bf16[512,128]{1,0:T(8,128)(2,1)S(1)}, bf16[512,128]{1,0:T(8,128)(2,1)S(1)}, u32[]{:S(2)}, u32[]{:S(2)}) collective-permute-start(bf16[512,128]{1,0:T(8,128)(2,1)S(1)} %get-tuple-element.95), channel_id=1, source_target_pairs={{0,6},{1,7},{2,4},{3,5},{4,2},{5,3},{6,0},{7,1},{8,14},{9,15},{10,... | collective-permute-start | bytes 393224 | tf_op jit(solution)/shard_map/ppermute | solution.py:48
  21.2 3.0 %collective-permute-done.13.refs_4_ = bf16[512,128]{1,0:T(8,128)(2,1)S(1)} collective-permute-done((bf16[512,128]{1,0:T(8,128)(2,1)S(1)}, bf16[512,128]{1,0:T(8,128)(2,1)S(1)}, u32[]{:S(2)}, u32[]{:S(2)}) %collective-permute-start.13) | collective-permute-done | bytes 131104 | tf_op jit(solution)/shard_map/ppermute | solution.py:48
  24.2 3.8 %collective-permute-done.12.refs_3_ = bf16[512,128]{1,0:T(8,128)(2,1)S(1)} collective-permute-done((bf16[512,128]{1,0:T(8,128)(2,1)S(1)}, bf16[512,128]{1,0:T(8,128)(2,1)S(1)}, u32[]{:S(2)}, u32[]{:S(2)}) %collective-permute-start.12) | collective-permute-done | bytes 131104 | tf_op jit(solution)/shard_map/ppermute | solution.py:48
  28.0 2.1 %collective-permute-done.11.refs_2_ = bf16[512,128]{1,0:T(8,128)(2,1)S(1)} collective-permute-done((bf16[512,128]{1,0:T(8,128)(2,1)S(1)}, bf16[512,128]{1,0:T(8,128)(2,1)S(1)}, u32[]{:S(2)}, u32[]{:S(2)}) %collective-permute-start.11) | collective-permute-done | bytes 131104 | tf_op jit(solution)/shard_map/ppermute | solution.py:48
  30.1 1.1 %dense.1 = (bf16[512,256]{1,0:T(8,128)(2,1)}, bf16[512,128]{1,0:T(8,128)(2,1)S(1)}, bf16[512,128]{1,0:T(8,128)(2,1)S(1)}, bf16[512,256]{1,0:T(8,128)(2,1)S(1)}) custom-call(bf16[512,128]{1,0:T(8,128)(2,1)S(1)} %get-tuple-element.68.refs_0_, bf16[512,128]{1,0:T(8,128)(2,1)S(1)} %collective-permute-done.9.refs_1_, ...), custom_call_target="tpu_custom_call" | custom-call | bytes 1024 | tf_op jit(solution)/shard_map/dense/pallas_call | solution.py:389
  31.2 1.9 %collective-permute-start.16 = (bf16[512,128]{1,0:T(8,128)(2,1)S(1)}, bf16[512,128]{1,0:T(8,128)(2,1)S(1)}, u32[]{:S(2)}, u32[]{:S(2)}) collective-permute-start(bf16[512,128]{1,0:T(8,128)(2,1)S(1)} %get-tuple-element.73), channel_id=1, source_target_pairs={{0,5},{1,4},{2,7},{3,6},{4,1},{5,0},{6,3},{7,2},{8,13},{9,12},{10,... | collective-permute-start | bytes 393224 | tf_op jit(solution)/shard_map/ppermute | solution.py:48
  33.2 1.4 %collective-permute-start.15 = (bf16[512,128]{1,0:T(8,128)(2,1)S(1)}, bf16[512,128]{1,0:T(8,128)(2,1)S(1)}, u32[]{:S(2)}, u32[]{:S(2)}) collective-permute-start(bf16[512,128]{1,0:T(8,128)(2,1)S(1)} %get-tuple-element.73), channel_id=1, source_target_pairs={{0,6},{1,7},{2,4},{3,5},{4,2},{5,3},{6,0},{7,1},{8,14},{9,15},{10,... | collective-permute-start | bytes 393224 | tf_op jit(solution)/shard_map/ppermute | solution.py:48
  34.8 11.4 %conditional.2 = (bf16[2048,128]{1,0:T(8,128)(2,1)}, f32[80,256]{1,0:T(8,128)S(1)}) conditional(s32[]{:T(128)} %convert_element_type.59, () %tuple.24, (bf16[512,128]{1,0:T(8,128)(2,1)S(1)}, s32[8]{0:T(128)S(1)}, s32[160]{0:T(256)S(1)}, s32[160]{0:T(256)S(1)}, bf16[160,128,128]{2,1,0:T(8,128)(2,1)}, /*index=5*/s32[]{:T(128)}, ...), branch_computations={%region_1.2_spmd, %region_2.3_spmd} | conditional | flops 184320 | bytes 1879216 | solution.py:53
  35.6 0.8 %collective-permute-done.3 = f32[80,256]{1,0:T(8,128)S(1)} collective-permute-done((f32[80,256]{1,0:T(8,128)S(1)}, f32[80,256]{1,0:T(8,128)S(1)}, u32[]{:S(2)}, u32[]{:S(2)}) %collective-permute-start.3) | collective-permute-done | bytes 81952 | tf_op jit(solution)/shard_map/cond/branch_1_fun/ppermute | solution.py:48
  36.4 1.7 %collective-permute-start.4 = (bf16[80,256]{1,0:T(8,128)(2,1)S(1)}, bf16[80,256]{1,0:T(8,128)(2,1)S(1)}, u32[]{:S(2)}, u32[]{:S(2)}) collective-permute-start(bf16[80,256]{1,0:T(8,128)(2,1)S(1)} %get-tuple-element.91), channel_id=1, source_target_pairs={{0,8},{1,17},{2,10},{3,19},{4,12},{5,21},{6,14},{7,23},{8,0},{9,25... | collective-permute-start | bytes 122888 | tf_op jit(solution)/shard_map/cond/branch_1_fun/ppermute | solution.py:48
  38.1 3.9 %backward_0.1.refs_1_ = bf16[2048,128]{1,0:T(8,128)(2,1)} custom-call(s32[8]{0:T(128)S(1)} %get-tuple-element.22.bounds_ref, s32[160]{0:T(256)S(1)} %get-tuple-element.23.row_ref, s32[160]{0:T(256)S(1)} %get-tuple-element.24.col_ref, bf16[160,128,128]{2,1,0:T(8,128)(2,1)} %get-tuple-element.25.w_ref, bf16[512,128]{1,0:T(8,128)(2,1)S(1)} %get-tuple-element.26.refs_0_, ...), custom_call_target="tpu_custom_call" | custom-call | bytes 1024 | tf_op jit(solution)/shard_map/cond/branch_1_fun/backward_0/pallas_call | solution.py:414
  42.1 1.2 %collective-permute-start.5 = (bf16[80,256]{1,0:T(8,128)(2,1)S(1)}, bf16[80,256]{1,0:T(8,128)(2,1)S(1)}, u32[]{:S(2)}, u32[]{:S(2)}) collective-permute-start(bf16[80,256]{1,0:T(8,128)(2,1)S(1)} %fusion), channel_id=1, source_target_pairs={{0,16},{1,9},{2,18},{3,11},{4,20},{5,13},{6,22},{7,15},{8,24},{9,1... | collective-permute-start | bytes 122888 | tf_op jit(solution)/shard_map/cond/branch_1_fun/ppermute | solution.py:48
  43.3 2.9 %collective-permute-done.5 = bf16[80,256]{1,0:T(8,128)(2,1)S(1)} collective-permute-done((bf16[80,256]{1,0:T(8,128)(2,1)S(1)}, bf16[80,256]{1,0:T(8,128)(2,1)S(1)}, u32[]{:S(2)}, u32[]{:S(2)}) %collective-permute-start.5) | collective-permute-done | bytes 40992 | tf_op jit(solution)/shard_map/cond/branch_1_fun/ppermute | solution.py:48
  46.4 1.9 %collective-permute-start.18 = (bf16[80,256]{1,0:T(8,128)(2,1)S(1)}, bf16[80,256]{1,0:T(8,128)(2,1)S(1)}, u32[]{:S(2)}, u32[]{:S(2)}) collective-permute-start(bf16[80,256]{1,0:T(8,128)(2,1)S(1)} %convert_element_type.60), channel_id=1, source_target_pairs={{0,2},{1,3},{2,0},{3,1},{4,6},{5,7},{6,4},{7,5},{8,10},{9,11},{10,... | collective-permute-start | bytes 122888 | tf_op jit(solution)/shard_map/ppermute | solution.py:48
  48.3 4.0 %backward_1_2_3.1 = (f32[512,128]{1,0:T(8,128)S(1)}, bf16[512,128]{1,0:T(8,128)(2,1)S(1)}, bf16[512,128]{1,0:T(8,128)(2,1)S(1)}, bf16[512,128]{1,0:T(8,128)(2,1)S(1)}) custom-call(s32[8]{0:T(128)S(1)} %convert_reduce_fusion.bounds_ref, s32[160]{0:T(256)S(1)} %get-tuple-element.93.row_ref, s32[160]{0:T(256)S(1)} %get-tuple-element.97.col_ref, ...), custom_call_target="tpu_custom_call" | custom-call | bytes 1024 | tf_op jit(solution)/shard_map/backward_1_2_3/pallas_call | solution.py:414
  52.3 1.5 %collective-permute-start.19 = (bf16[512,128]{1,0:T(8,128)(2,1)S(1)}, bf16[512,128]{1,0:T(8,128)(2,1)S(1)}, u32[]{:S(2)}, u32[]{:S(2)}) collective-permute-start(bf16[512,128]{1,0:T(8,128)(2,1)S(1)} %get-tuple-element.86), channel_id=1, source_target_pairs={{0,8},{1,17},{2,10},{3,19},{4,12},{5,21},{6,14},{7,23},{8,0},{9,25... | collective-permute-start | bytes 393224 | tf_op jit(solution)/shard_map/ppermute | solution.py:48
  53.9 0.6 collective-permute-start.20
  54.4 1.5 %collective-permute-start.21 = (bf16[512,128]{1,0:T(8,128)(2,1)S(1)}, bf16[512,128]{1,0:T(8,128)(2,1)S(1)}, u32[]{:S(2)}, u32[]{:S(2)}) collective-permute-start(bf16[512,128]{1,0:T(8,128)(2,1)S(1)} %get-tuple-element.88), channel_id=1, source_target_pairs={{0,24},{1,25},{2,26},{3,27},{4,28},{5,29},{6,30},{7,31},{8,16},{9,... | collective-permute-start | bytes 393224 | tf_op jit(solution)/shard_map/ppermute | solution.py:48
  55.9 6.4 %conditional.3 = (f32[128,256]{1,0:T(8,128)S(1)}, f32[256]{0:T(256)S(1)}) conditional(s32[]{:T(128)} %convert_element_type.59, () %tuple.26, (s32[]{:T(128)}, bf16[80,256]{1,0:T(8,128)(2,1)S(1)}, f32[80,256]{1,0:T(8,128)S(1)}) %tuple.27), branch_computations={%region_3.4_spmd, %region_4.5_spmd} | conditional | flops 262145 | bytes 1230954 | solution.py:53
  55.9 2.7 %collective-permute-start = (bf16[80,256]{1,0:T(8,128)(2,1)S(1)}, bf16[80,256]{1,0:T(8,128)(2,1)S(1)}, u32[]{:S(2)}, u32[]{:S(2)}) collective-permute-start(bf16[80,256]{1,0:T(8,128)(2,1)S(1)} %fusion.1), channel_id=1, source_target_pairs={{0,4},{1,5},{2,6},{3,7},{4,0},{5,1},{6,2},{7,3},{8,12},{9,13},{10,... | collective-permute-start | bytes 122888 | tf_op jit(solution)/shard_map/cond/branch_1_fun/ppermute | solution.py:48
  58.6 2.3 %collective-permute-done = bf16[80,256]{1,0:T(8,128)(2,1)S(1)} collective-permute-done((bf16[80,256]{1,0:T(8,128)(2,1)S(1)}, bf16[80,256]{1,0:T(8,128)(2,1)S(1)}, u32[]{:S(2)}, u32[]{:S(2)}) %collective-permute-start) | collective-permute-done | bytes 40992 | tf_op jit(solution)/shard_map/cond/branch_1_fun/ppermute | solution.py:48
  61.0 1.2 %collective-permute-done.1 = f32[64,256]{1,0:T(8,128)S(1)} collective-permute-done((f32[64,256]{1,0:T(8,128)S(1)}, f32[64,256]{1,0:T(8,128)S(1)}, u32[]{:S(2)}, u32[]{:S(2)}) %collective-permute-start.1) | collective-permute-done | bytes 65568 | tf_op jit(solution)/shard_map/cond/branch_1_fun/ppermute | solution.py:48
  62.3 0.8 %multiply_convert_fusion = bf16[512,128]{1,0:T(8,128)(2,1)} fusion(f32[512,128]{1,0:T(8,128)S(1)} %get-tuple-element.65.earlier_ref.refs_6_, bf16[512,128]{1,0:T(8,128)(2,1)S(1)} %get-tuple-element.73, bf16[512,128]{1,0:T(8,128)(2,1)S(1)} %collective-permute-done.21, bf16[512,128]{1,0:T(8,128)(2,1)S(1)} %collective-permute-done.20, ...), kind=kLoop, calls=%fused_computation.8 | loop fusion | flops 655360 | bytes 1179648 | tf_op jit(solution)/shard_map/convert_element_type | solution.py:480
  (55 shorter events, 2.6 us)
Async XLA Ops:
  1.7 8.9 %collective-permute-start.8 = (bf16[512,128]{1,0:T(8,128)(2,1)S(1)}, bf16[512,128]{1,0:T(8,128)(2,1)S(1)}, u32[]{:S(2)}, u32[]{:S(2)}) collective-permute-start(bf16[512,128]{1,0:T(8,128)(2,1)S(1)} %get-tuple-element.66.earlier_ref.refs_0_.refs_5_), channel_id=1, source_target_pairs={{0,24},{1,25},{2,26},{3,27},{4,28},{5,29},{6,30},{7,31},{8,16},{9,... | collective-permute-start | bytes 393224 | tf_op jit(solution)/shard_map/ppermute | solution.py:48
  5.7 6.3 %collective-permute-start.7 = (bf16[512,128]{1,0:T(8,128)(2,1)S(1)}, bf16[512,128]{1,0:T(8,128)(2,1)S(1)}, u32[]{:S(2)}, u32[]{:S(2)}) collective-permute-start(bf16[512,128]{1,0:T(8,128)(2,1)S(1)} %get-tuple-element.66.earlier_ref.refs_0_.refs_5_), channel_id=1, source_target_pairs={{0,16},{1,9},{2,18},{3,11},{4,20},{5,13},{6,22},{7,15},{8,24},{9,1... | collective-permute-start | bytes 393224 | tf_op jit(solution)/shard_map/ppermute | solution.py:48
  6.2 6.0 %collective-permute-start.6 = (bf16[512,128]{1,0:T(8,128)(2,1)S(1)}, bf16[512,128]{1,0:T(8,128)(2,1)S(1)}, u32[]{:S(2)}, u32[]{:S(2)}) collective-permute-start(bf16[512,128]{1,0:T(8,128)(2,1)S(1)} %get-tuple-element.66.earlier_ref.refs_0_.refs_5_), channel_id=1, source_target_pairs={{0,8},{1,17},{2,10},{3,19},{4,12},{5,21},{6,14},{7,23},{8,0},{9,25... | collective-permute-start | bytes 393224 | tf_op jit(solution)/shard_map/ppermute | solution.py:48
  12.2 17.9 %copy-start = (bf16[512,256]{1,0:T(8,128)(2,1)S(1)}, bf16[512,256]{1,0:T(8,128)(2,1)}, u32[]{:S(2)}) copy-start(bf16[512,256]{1,0:T(8,128)(2,1)} %refs_9_.1) | copy-start | bytes 786436
  12.2 17.9 %copy-start.1 = (bf16[128,256]{1,0:T(8,128)(2,1)S(1)}, bf16[128,256]{1,0:T(8,128)(2,1)}, u32[]{:S(2)}) copy-start(bf16[128,256]{1,0:T(8,128)(2,1)} %refs_7_.1) | copy-start | bytes 196612
  12.2 17.9 %copy-start.2 = (f32[256]{0:T(256)S(1)}, f32[256]{0:T(256)}, u32[]{:S(2)}) copy-start(f32[256]{0:T(256)} %param.20) | copy-start | bytes 3076
  14.6 5.1 %collective-permute-start.10 = (bf16[1024,128]{1,0:T(8,128)(2,1)S(1)}, bf16[1024,128]{1,0:T(8,128)(2,1)S(1)}, u32[]{:S(2)}, u32[]{:S(2)}) collective-permute-start(bf16[1024,128]{1,0:T(8,128)(2,1)S(1)} %get-tuple-element.67.earlier_ref), channel_id=1, source_target_pairs={{0,1},{1,0},{2,3},{3,2},{4,5},{5,4},{6,7},{7,6},{8,9},{9,8},{10,11... | collective-permute-start | bytes 786440 | tf_op jit(solution)/shard_map/ppermute | solution.py:48
  14.7 9.6 %collective-permute-start.13 = (bf16[512,128]{1,0:T(8,128)(2,1)S(1)}, bf16[512,128]{1,0:T(8,128)(2,1)S(1)}, u32[]{:S(2)}, u32[]{:S(2)}) collective-permute-start(bf16[512,128]{1,0:T(8,128)(2,1)S(1)} %get-tuple-element.71), channel_id=1, source_target_pairs={{0,5},{1,4},{2,7},{3,6},{4,1},{5,0},{6,3},{7,2},{8,13},{9,12},{10,... | collective-permute-start | bytes 393224 | tf_op jit(solution)/shard_map/ppermute | solution.py:48
  19.6 4.6 %collective-permute-start.9 = (bf16[512,128]{1,0:T(8,128)(2,1)S(1)}, bf16[512,128]{1,0:T(8,128)(2,1)S(1)}, u32[]{:S(2)}, u32[]{:S(2)}) collective-permute-start(bf16[512,128]{1,0:T(8,128)(2,1)S(1)} %get-tuple-element.69), channel_id=1, source_target_pairs={{0,1},{1,0},{2,3},{3,2},{4,5},{5,4},{6,7},{7,6},{8,9},{9,8},{10,11... | collective-permute-start | bytes 393224 | tf_op jit(solution)/shard_map/ppermute | solution.py:48
  19.8 8.2 %collective-permute-start.12 = (bf16[512,128]{1,0:T(8,128)(2,1)S(1)}, bf16[512,128]{1,0:T(8,128)(2,1)S(1)}, u32[]{:S(2)}, u32[]{:S(2)}) collective-permute-start(bf16[512,128]{1,0:T(8,128)(2,1)S(1)} %get-tuple-element.95), channel_id=1, source_target_pairs={{0,6},{1,7},{2,4},{3,5},{4,2},{5,3},{6,0},{7,1},{8,14},{9,15},{10,... | collective-permute-start | bytes 393224 | tf_op jit(solution)/shard_map/ppermute | solution.py:48
  21.0 9.2 %collective-permute-start.11 = (bf16[512,128]{1,0:T(8,128)(2,1)S(1)}, bf16[512,128]{1,0:T(8,128)(2,1)S(1)}, u32[]{:S(2)}, u32[]{:S(2)}) collective-permute-start(bf16[512,128]{1,0:T(8,128)(2,1)S(1)} %get-tuple-element.96), channel_id=1, source_target_pairs={{0,2},{1,3},{2,0},{3,1},{4,6},{5,7},{6,4},{7,5},{8,10},{9,11},{10,... | collective-permute-start | bytes 393224 | tf_op jit(solution)/shard_map/ppermute | solution.py:48
  31.2 15.0 %collective-permute-start.16 = (bf16[512,128]{1,0:T(8,128)(2,1)S(1)}, bf16[512,128]{1,0:T(8,128)(2,1)S(1)}, u32[]{:S(2)}, u32[]{:S(2)}) collective-permute-start(bf16[512,128]{1,0:T(8,128)(2,1)S(1)} %get-tuple-element.73), channel_id=1, source_target_pairs={{0,5},{1,4},{2,7},{3,6},{4,1},{5,0},{6,3},{7,2},{8,13},{9,12},{10,... | collective-permute-start | bytes 393224 | tf_op jit(solution)/shard_map/ppermute | solution.py:48
  33.2 13.1 %collective-permute-start.15 = (bf16[512,128]{1,0:T(8,128)(2,1)S(1)}, bf16[512,128]{1,0:T(8,128)(2,1)S(1)}, u32[]{:S(2)}, u32[]{:S(2)}) collective-permute-start(bf16[512,128]{1,0:T(8,128)(2,1)S(1)} %get-tuple-element.73), channel_id=1, source_target_pairs={{0,6},{1,7},{2,4},{3,5},{4,2},{5,3},{6,0},{7,1},{8,14},{9,15},{10,... | collective-permute-start | bytes 393224 | tf_op jit(solution)/shard_map/ppermute | solution.py:48
  34.6 11.7 %collective-permute-start.14 = (bf16[512,128]{1,0:T(8,128)(2,1)S(1)}, bf16[512,128]{1,0:T(8,128)(2,1)S(1)}, u32[]{:S(2)}, u32[]{:S(2)}) collective-permute-start(bf16[512,128]{1,0:T(8,128)(2,1)S(1)} %get-tuple-element.73), channel_id=1, source_target_pairs={{0,2},{1,3},{2,0},{3,1},{4,6},{5,7},{6,4},{7,5},{8,10},{9,11},{10,... | collective-permute-start | bytes 393224 | tf_op jit(solution)/shard_map/ppermute | solution.py:48
  35.0 1.3 %collective-permute-start.3 = (f32[80,256]{1,0:T(8,128)S(1)}, f32[80,256]{1,0:T(8,128)S(1)}, u32[]{:S(2)}, u32[]{:S(2)}) collective-permute-start(f32[80,256]{1,0:T(8,128)S(1)} %get-tuple-element.31), channel_id=1, source_target_pairs={{0,1},{1,0},{2,3},{3,2},{4,5},{5,4},{6,7},{7,6},{8,9},{9,8},{10,11... | collective-permute-start | bytes 245768 | tf_op jit(solution)/shard_map/cond/branch_1_fun/ppermute | solution.py:48
  35.3 2.8 %collective-permute-start.2 = (bf16[512,128]{1,0:T(8,128)(2,1)S(1)}, bf16[512,128]{1,0:T(8,128)(2,1)S(1)}, u32[]{:S(2)}, u32[]{:S(2)}) collective-permute-start(bf16[512,128]{1,0:T(8,128)(2,1)S(1)} %get-tuple-element.26.refs_0_), channel_id=1, source_target_pairs={{0,1},{1,0},{2,3},{3,2},{4,5},{5,4},{6,7},{7,6},{8,9},{9,8},{10,11... | collective-permute-start | bytes 393224 | tf_op jit(solution)/shard_map/cond/branch_1_fun/ppermute | solution.py:48
  36.4 5.7 %collective-permute-start.4 = (bf16[80,256]{1,0:T(8,128)(2,1)S(1)}, bf16[80,256]{1,0:T(8,128)(2,1)S(1)}, u32[]{:S(2)}, u32[]{:S(2)}) collective-permute-start(bf16[80,256]{1,0:T(8,128)(2,1)S(1)} %get-tuple-element.91), channel_id=1, source_target_pairs={{0,8},{1,17},{2,10},{3,19},{4,12},{5,21},{6,14},{7,23},{8,0},{9,25... | collective-permute-start | bytes 122888 | tf_op jit(solution)/shard_map/cond/branch_1_fun/ppermute | solution.py:48
  42.1 4.1 %collective-permute-start.5 = (bf16[80,256]{1,0:T(8,128)(2,1)S(1)}, bf16[80,256]{1,0:T(8,128)(2,1)S(1)}, u32[]{:S(2)}, u32[]{:S(2)}) collective-permute-start(bf16[80,256]{1,0:T(8,128)(2,1)S(1)} %fusion), channel_id=1, source_target_pairs={{0,16},{1,9},{2,18},{3,11},{4,20},{5,13},{6,22},{7,15},{8,24},{9,1... | collective-permute-start | bytes 122888 | tf_op jit(solution)/shard_map/cond/branch_1_fun/ppermute | solution.py:48
  46.3 2.0 %collective-permute-start.17 = (bf16[1024,128]{1,0:T(8,128)(2,1)S(1)}, bf16[1024,128]{1,0:T(8,128)(2,1)S(1)}, u32[]{:S(2)}, u32[]{:S(2)}) collective-permute-start(bf16[1024,128]{1,0:T(8,128)(2,1)S(1)} %constant_dynamic-update-slice_fusion.refs_1_), channel_id=1, source_target_pairs={{0,1},{1,0},{2,3},{3,2},{4,5},{5,4},{6,7},{7,6},{8,9},{9,8},{10,11... | collective-permute-start | bytes 786440 | tf_op jit(solution)/shard_map/ppermute | solution.py:48
  46.4 5.9 %collective-permute-start.18 = (bf16[80,256]{1,0:T(8,128)(2,1)S(1)}, bf16[80,256]{1,0:T(8,128)(2,1)S(1)}, u32[]{:S(2)}, u32[]{:S(2)}) collective-permute-start(bf16[80,256]{1,0:T(8,128)(2,1)S(1)} %convert_element_type.60), channel_id=1, source_target_pairs={{0,2},{1,3},{2,0},{3,1},{4,6},{5,7},{6,4},{7,5},{8,10},{9,11},{10,... | collective-permute-start | bytes 122888 | tf_op jit(solution)/shard_map/ppermute | solution.py:48
  52.3 9.9 %collective-permute-start.19 = (bf16[512,128]{1,0:T(8,128)(2,1)S(1)}, bf16[512,128]{1,0:T(8,128)(2,1)S(1)}, u32[]{:S(2)}, u32[]{:S(2)}) collective-permute-start(bf16[512,128]{1,0:T(8,128)(2,1)S(1)} %get-tuple-element.86), channel_id=1, source_target_pairs={{0,8},{1,17},{2,10},{3,19},{4,12},{5,21},{6,14},{7,23},{8,0},{9,25... | collective-permute-start | bytes 393224 | tf_op jit(solution)/shard_map/ppermute | solution.py:48
  53.9 8.4 %collective-permute-start.20 = (bf16[512,128]{1,0:T(8,128)(2,1)S(1)}, bf16[512,128]{1,0:T(8,128)(2,1)S(1)}, u32[]{:S(2)}, u32[]{:S(2)}) collective-permute-start(bf16[512,128]{1,0:T(8,128)(2,1)S(1)} %get-tuple-element.87), channel_id=1, source_target_pairs={{0,16},{1,9},{2,18},{3,11},{4,20},{5,13},{6,22},{7,15},{8,24},{9,1... | collective-permute-start | bytes 393224 | tf_op jit(solution)/shard_map/ppermute | solution.py:48
  54.4 7.9 %collective-permute-start.21 = (bf16[512,128]{1,0:T(8,128)(2,1)S(1)}, bf16[512,128]{1,0:T(8,128)(2,1)S(1)}, u32[]{:S(2)}, u32[]{:S(2)}) collective-permute-start(bf16[512,128]{1,0:T(8,128)(2,1)S(1)} %get-tuple-element.88), channel_id=1, source_target_pairs={{0,24},{1,25},{2,26},{3,27},{4,28},{5,29},{6,30},{7,31},{8,16},{9,... | collective-permute-start | bytes 393224 | tf_op jit(solution)/shard_map/ppermute | solution.py:48
  55.9 5.0 %collective-permute-start = (bf16[80,256]{1,0:T(8,128)(2,1)S(1)}, bf16[80,256]{1,0:T(8,128)(2,1)S(1)}, u32[]{:S(2)}, u32[]{:S(2)}) collective-permute-start(bf16[80,256]{1,0:T(8,128)(2,1)S(1)} %fusion.1), channel_id=1, source_target_pairs={{0,4},{1,5},{2,6},{3,7},{4,0},{5,1},{6,2},{7,3},{8,12},{9,13},{10,... | collective-permute-start | bytes 122888 | tf_op jit(solution)/shard_map/cond/branch_1_fun/ppermute | solution.py:48
  60.9 1.3 %collective-permute-start.1 = (f32[64,256]{1,0:T(8,128)S(1)}, f32[64,256]{1,0:T(8,128)S(1)}, u32[]{:S(2)}, u32[]{:S(2)}) collective-permute-start(f32[64,256]{1,0:T(8,128)S(1)} %slice.14), channel_id=1, source_target_pairs={{0,1},{1,0},{2,3},{3,2},{4,5},{5,4},{6,7},{7,6},{8,9},{9,8},{10,11... | collective-permute-start | bytes 196616 | tf_op jit(solution)/shard_map/cond/branch_1_fun/ppermute | solution.py:48
  62.2 0.8 %copy-start.3 = (f32[128,256]{1,0:T(8,128)}, f32[128,256]{1,0:T(8,128)S(1)}, u32[]{:S(2)}) copy-start(f32[128,256]{1,0:T(8,128)S(1)} %get-tuple-element.63) | copy-start | bytes 393220
  62.2 0.8 %copy-start.4 = (f32[256]{0:T(256)}, f32[256]{0:T(256)S(1)}, u32[]{:S(2)}) copy-start(f32[256]{0:T(256)S(1)} %get-tuple-element.64) | copy-start | bytes 3076

commit v5 on v4

--- a/solution.py
+++ b/solution.py
@@ -143,6 +143,12 @@
         scaled_ref[rows, :] = (norm * features_ref[rows, :].astype(F32)).astype(BF)
 
 
+def write_kernel(value_ref, out_ref, sem):
+    copy = pltpu.make_async_copy(value_ref, out_ref, sem)
+    copy.start()
+    copy.wait()
+
+
 def stage_kernel(w_ref, earlier_ref, out_ref, sem):
     copy = pltpu.make_async_copy(w_ref, out_ref, sem)
     copy.start()
@@ -239,13 +245,17 @@
     ranges = [(bounds_ref[place], bounds_ref[4 + place]) for place in places]
     finish = stream_slots(w_ref, tiles_held, sems, ranges, unroll)
     tile = w_ref.shape[-1]
-    block_refs, out_refs = (refs[:2], refs[2:]) if places == (0,) else (refs[1:4], refs[4:])
+    block_refs, refs = refs[: 2 if places == (0,) else 3], refs[2 if places == (0,) else 3 :]
     if places == (0,):
+        out_refs = refs
         total[...] = jnp.zeros_like(total)
     else:
-        used_rows = refs[0].shape[0]
-        total[:used_rows, :] = refs[0][...].astype(F32)
-        total[used_rows:, :] = jnp.zeros((total.shape[0] - used_rows, total.shape[1]), F32)
+        old_refs, out_refs = refs[: len(refs) // 2], refs[len(refs) // 2 :]
+        first = 0
+        for old_ref in old_refs:
+            total[first : first + old_ref.shape[0], :] = old_ref[...].astype(F32)
+            first += old_ref.shape[0]
+        total[first:, :] = jnp.zeros((total.shape[0] - first, total.shape[1]), F32)
     gather_blocks(block_refs, held)
     spare = total.shape[0] // tile - 1
     block_tiles = held.shape[0] // tile // (2 if places == (0,) else 5)
@@ -279,7 +289,7 @@
     aggregated = (norm * neighbor).astype(BF)
     weight = weight_ref[...]
     pre_act = jnp.dot(aggregated, weight, preferred_element_type=F32) + bias_ref[...]
-    gate = 1.0 / (1.0 + jnp.exp(-pre_act))
+    gate = 0.5 * jnp.tanh(0.5 * pre_act) + 0.5
     hidden_ref[...] = (pre_act * gate).astype(BF)
     pre_grad = (up_ref[...].astype(F32) * (gate + pre_act * gate * (1.0 - gate))).astype(BF)
     back = lax.dot_general(pre_grad, weight, (((1,), (1,)), ((), ())), preferred_element_type=F32)
@@ -378,18 +388,18 @@
     def add(a, b):
         return (a.astype(F32) + b.astype(F32)).astype(BF)
 
-    keep, send, part3 = forward((1, 2, 3), (16, 16, 12), norm_wide)
+    keep, send, part3 = forward((1, 2, 3), (26, 26, 12), norm_wide)
     sums = add(keep, swap_cores(send))
     came3 = move(part3, pair_partner(3, False))
     came2 = move(sums[row_count:], pair_partner(2, False))
     came1 = move(sums[:row_count], pair_partner(1, False))
-    keep0, send0 = forward((0,), (16,), send)
+    keep0, send0 = forward((0,), (20,), send)
     cross0 = swap_cores(send0)
 
     hidden, scaled_grad, aggregated, pre_grad = pl.pallas_call(
         dense_kernel,
         out_shape=[
-            jax.ShapeDtypeStruct((row_count, hid_width), BF),
+            pltpu.VMEM((row_count, hid_width), BF),
             block_shape,
             block_shape,
             jax.ShapeDtypeStruct((row_count, hid_width), BF),
@@ -406,7 +416,6 @@
     grads1 = move(scaled_grad, pair_partner(1, True))
 
     tiles_hbm = in_hbm(tile_weights[0, 0])
-    column_shape = jax.ShapeDtypeStruct((col_tiles * tile, feat_width), BF)
 
     def backward(places, unroll, out_shape, *blocks):
         fetches = slot_total // unroll + len(places)
@@ -443,11 +452,11 @@
             name="weight_terms",
         )(core[None].astype(jnp.int32), aggregated, pre_grad)
         grad = keep + swap_cores(send)
-        (total,) = backward((0,), 16, [column_shape], scaled_grad, other)
+        total = backward((0,), 16, [block_shape] * rep_count, scaled_grad, other)
         for n in range(rep_bits()):
             came = move(grad.astype(BF), rep_partner(1 << n))
             if n == 0:
-                (grad,) = together([grad], [total])
+                (grad,) = together([grad], total)
             grad = grad + came.astype(F32)
         return total, grad
 
@@ -457,10 +466,22 @@
     near_far = jnp.concatenate([grads1, grads2])
     came = move(grad.astype(BF), lambda r, k: (r, k ^ 2))
     column_shapes = [jax.ShapeDtypeStruct((row_count, feat_width), F32)] + [block_shape] * (rep_count - 1)
-    columns = backward((1, 2, 3), 16, column_shapes, total, near_far, swap_cores(near_far), grads3)
+    columns = backward((1, 2, 3), 16, column_shapes, near_far, swap_cores(near_far), grads3, *total)
     columns = together(columns, [came])
 
-    def finish_weight(grad, came):
+    def write(value):
+        return pl.pallas_call(
+            write_kernel,
+            out_shape=jax.ShapeDtypeStruct(value.shape, value.dtype),
+            in_specs=[VMEM],
+            out_specs=HBM,
+            scratch_shapes=[pltpu.SemaphoreType.DMA],
+            compiler_params=params(16),
+            cost_estimate=SMALL,
+            name="write_hidden",
+        )(value)
+
+    def finish(grad, came, hidden):
         grad = grad + came.astype(F32)
         for bit in range(2, blk_bits):
             grad = grad + move(grad.astype(BF), lambda r, k: (r, k ^ (1 << bit))).astype(F32)
@@ -470,11 +491,11 @@
         weight_grad = jnp.where(
             core == 0, jnp.concatenate([mine, other]), jnp.concatenate([other, mine])
         )
-        return weight_grad, grad[grad_rows]
+        return weight_grad, grad[grad_rows], write(hidden)
 
     column_sum = columns[0]
     arrived = {place: move(columns[place], rep_partner(place)) for place in far_first(rep_count)}
-    weight_grad, bias_grad = block(finish_weight, grad, came)
+    weight_grad, bias_grad, hidden = block(finish, grad, came, hidden)
     for place in range(1, rep_count):
         column_sum = column_sum + arrived[place].astype(F32)
     feature_grad = (norm_wide * (column_sum + scaled_grad.astype(F32))).astype(BF)

time: 63.3 us -> 63.1 us (level)
  starting transfers between devices: 24.5 us -> 22.5 us
  waiting for transfers between devices: 17.7 us -> 19 us
  Pallas kernels: 17.2 us -> 18.2 us
    ppermute x22, starting transfers between devices: 24.5 us -> 22.5 us  [move(): return lax.ppermute(value, BOTH, pairs)]
    ppermute x22, waiting for transfers between devices: 17.7 us -> 19 us  [move(): return lax.ppermute(value, BOTH, pairs)]
    pallas_call x2, Pallas kernels: 7.98 us -> 9.02 us  [backward(): pl.pallas_call(functools.partial(backward_kernel, places, unroll), out_sh...]
  transfers between devices with their start and end apart: 22 -> 22, of which waited for: 9 -> 9; matrix products, arithmetic and copies ran while one was open for 2% -> 2% of each run, Pallas kernels for 20% -> 22%
where the time goes in v5:
time: 63.1 us; the launch traced here: 63.5 us
  starting transfers between devices  22.5 us (36%)
  waiting for transfers between devices  19 us (30%)
  Pallas kernels  18.2 us (29%)
  other arithmetic  1.92 us (3%)
  between operations  1.54 us (2%)
    ppermute x22, starting transfers between devices, move(): return lax.ppermute(value, BOTH, pairs)  22.5 us
    ppermute x22, waiting for transfers between devices, move(): return lax.ppermute(value, BOTH, pairs)  19 us
    pallas_call x2, Pallas kernels, backward(): pl.pallas_call(functools.partial(backward_kernel, places, unroll), out_sh...  9.02 us
    pallas_call x2, Pallas kernels, forward(): pl.pallas_call(functools.partial(forward_kernel, places, unrolls), out_sh...  4.86 us
    pallas_call x1, Pallas kernels, stage(): pl.pallas_call(stage_kernel, out_shape=jax.ShapeDtypeStruct((slot_total,...  2.5 us
  transfers between devices with their start and end apart: 22, of which 9 were waited for; matrix products, arithmetic and copies ran while one was open for 2% of the time, Pallas kernels for 22%

profile of v5, /device:TPU:0, one launch (start us, length us, event | category | flops | bytes accessed | tf_op | source)
XLA Modules:
  0.0 63.5 jit_solution(4393944272562456662)
XLA Ops:
  0.6 1.1 %prepare.1 = (bf16[512,128]{1,0:T(8,128)(2,1)S(1)}, f32[512,128]{1,0:T(8,128)S(1)}) custom-call(s32[4,128]{1,0:T(4,128)} %bitcast.17, bf16[512,128]{1,0:T(8,128)(2,1)} %features_hbm.1), custom_call_target="tpu_custom_call" | custom-call | bytes 1024 | tf_op jit(solution)/shard_map/prepare/pallas_call | solution.py:338
  1.7 4.0 %collective-permute-start.8 = (bf16[512,128]{1,0:T(8,128)(2,1)S(1)}, bf16[512,128]{1,0:T(8,128)(2,1)S(1)}, u32[]{:S(2)}, u32[]{:S(2)}) collective-permute-start(bf16[512,128]{1,0:T(8,128)(2,1)S(1)} %get-tuple-element.77.earlier_ref.refs_0_.refs_5_), channel_id=1, source_target_pairs={{0,24},{1,25},{2,26},{3,27},{4,28},{5,29},{6,30},{7,31},{8,16},{9,... | collective-permute-start | bytes 393224 | tf_op jit(solution)/shard_map/ppermute | solution.py:48
  5.7 0.5 collective-permute-start.7
  7.0 0.7 %fusion.2 = (s32[160]{0:T(256)S(1)}, s32[160]{0:T(256)S(1)}, s32[160]{0:T(256)S(1)}) fusion(s32[]{:T(128)} %select_n.68, s32[160]{0:T(256)} %bitcast.18, s32[]{:T(128)S(6)} %axis_index.33, s32[160]{0:T(256)} %bitcast.19, pred[]{:T(512)S(6)} %eq.21), kind=kLoop, calls=%fused_computation.28 | loop fusion | flops 10240 | bytes 3209 | tf_op jit(solution)/shard_map/add | solution.py:331
  7.9 2.5 %stage_tiles.1.w_ref = bf16[160,128,128]{2,1,0:T(8,128)(2,1)S(1)} custom-call(bf16[160,128,128]{2,1,0:T(8,128)(2,1)} %bitcast.14, bf16[512,128]{1,0:T(8,128)(2,1)S(1)} %get-tuple-element.77.earlier_ref.refs_0_.refs_5_), custom_call_target="tpu_custom_call" | custom-call | bytes 10485760 | tf_op jit(solution)/shard_map/stage_tiles/pallas_call | solution.py:357
  10.6 1.4 %collective-permute-done.7.refs_2_ = bf16[512,128]{1,0:T(8,128)(2,1)S(1)} collective-permute-done((bf16[512,128]{1,0:T(8,128)(2,1)S(1)}, bf16[512,128]{1,0:T(8,128)(2,1)S(1)}, u32[]{:S(2)}, u32[]{:S(2)}) %collective-permute-start.7) | collective-permute-done | bytes 131104 | tf_op jit(solution)/shard_map/ppermute | solution.py:48
  12.3 2.7 %forward_1_2_3.1 = (bf16[1024,128]{1,0:T(8,128)(2,1)S(1)}, bf16[1024,128]{1,0:T(8,128)(2,1)S(1)}, bf16[512,128]{1,0:T(8,128)(2,1)S(1)}) custom-call(f32[512,128]{1,0:T(8,128)S(1)} %get-tuple-element.76.earlier_ref.refs_6_, s32[8]{0:T(128)S(1)} %convert_reduce_fusion.bounds_ref, s32[160]{0:T(256)S(1)} %get-tuple-element.108.row_ref, ...), custom_call_target="tpu_custom_call" | custom-call | bytes 1024 | tf_op jit(solution)/shard_map/forward_1_2_3/pallas_call | solution.py:374
  15.1 2.3 %collective-permute-start.13 = (bf16[512,128]{1,0:T(8,128)(2,1)S(1)}, bf16[512,128]{1,0:T(8,128)(2,1)S(1)}, u32[]{:S(2)}, u32[]{:S(2)}) collective-permute-start(bf16[512,128]{1,0:T(8,128)(2,1)S(1)} %get-tuple-element.82), channel_id=1, source_target_pairs={{0,5},{1,4},{2,7},{3,6},{4,1},{5,0},{6,3},{7,2},{8,13},{9,12},{10,... | collective-permute-start | bytes 393224 | tf_op jit(solution)/shard_map/ppermute | solution.py:48
  17.4 2.1 %forward_0.1 = (bf16[512,128]{1,0:T(8,128)(2,1)S(1)}, bf16[512,128]{1,0:T(8,128)(2,1)S(1)}) custom-call(bf16[1024,128]{1,0:T(8,128)(2,1)S(1)} %get-tuple-element.78.earlier_ref, s32[8]{0:T(128)S(1)} %convert_reduce_fusion.bounds_ref, s32[160]{0:T(256)S(1)} %get-tuple-element.108.row_ref, s32[160]{0:T(256)S(1)} %get-tuple-element.112.col_ref, ...), custom_call_target="tpu_custom_call" | custom-call | bytes 1024 | tf_op jit(solution)/shard_map/forward_0/pallas_call | solution.py:374
  19.7 1.1 %collective-permute-start.12 = (bf16[512,128]{1,0:T(8,128)(2,1)S(1)}, bf16[512,128]{1,0:T(8,128)(2,1)S(1)}, u32[]{:S(2)}, u32[]{:S(2)}) collective-permute-start(bf16[512,128]{1,0:T(8,128)(2,1)S(1)} %get-tuple-element.110), channel_id=1, source_target_pairs={{0,6},{1,7},{2,4},{3,5},{4,2},{5,3},{6,0},{7,1},{8,14},{9,15},{10,... | collective-permute-start | bytes 393224 | tf_op jit(solution)/shard_map/ppermute | solution.py:48
  20.8 0.6 %collective-permute-start.11 = (bf16[512,128]{1,0:T(8,128)(2,1)S(1)}, bf16[512,128]{1,0:T(8,128)(2,1)S(1)}, u32[]{:S(2)}, u32[]{:S(2)}) collective-permute-start(bf16[512,128]{1,0:T(8,128)(2,1)S(1)} %get-tuple-element.111), channel_id=1, source_target_pairs={{0,2},{1,3},{2,0},{3,1},{4,6},{5,7},{6,4},{7,5},{8,10},{9,11},{10,... | collective-permute-start | bytes 393224 | tf_op jit(solution)/shard_map/ppermute | solution.py:48
  21.4 2.8 %collective-permute-done.13.refs_4_ = bf16[512,128]{1,0:T(8,128)(2,1)S(1)} collective-permute-done((bf16[512,128]{1,0:T(8,128)(2,1)S(1)}, bf16[512,128]{1,0:T(8,128)(2,1)S(1)}, u32[]{:S(2)}, u32[]{:S(2)}) %collective-permute-start.13) | collective-permute-done | bytes 131104 | tf_op jit(solution)/shard_map/ppermute | solution.py:48
  24.2 3.7 %collective-permute-done.12.refs_3_ = bf16[512,128]{1,0:T(8,128)(2,1)S(1)} collective-permute-done((bf16[512,128]{1,0:T(8,128)(2,1)S(1)}, bf16[512,128]{1,0:T(8,128)(2,1)S(1)}, u32[]{:S(2)}, u32[]{:S(2)}) %collective-permute-start.12) | collective-permute-done | bytes 131104 | tf_op jit(solution)/shard_map/ppermute | solution.py:48
  27.9 2.4 %collective-permute-done.11.refs_2_ = bf16[512,128]{1,0:T(8,128)(2,1)S(1)} collective-permute-done((bf16[512,128]{1,0:T(8,128)(2,1)S(1)}, bf16[512,128]{1,0:T(8,128)(2,1)S(1)}, u32[]{:S(2)}, u32[]{:S(2)}) %collective-permute-start.11) | collective-permute-done | bytes 131104 | tf_op jit(solution)/shard_map/ppermute | solution.py:48
  30.3 0.5 dense.1
  30.8 1.9 %collective-permute-start.17 = (bf16[512,128]{1,0:T(8,128)(2,1)S(1)}, bf16[512,128]{1,0:T(8,128)(2,1)S(1)}, u32[]{:S(2)}, u32[]{:S(2)}) collective-permute-start(bf16[512,128]{1,0:T(8,128)(2,1)S(1)} %get-tuple-element.83), channel_id=1, source_target_pairs={{0,5},{1,4},{2,7},{3,6},{4,1},{5,0},{6,3},{7,2},{8,13},{9,12},{10,... | collective-permute-start | bytes 393224 | tf_op jit(solution)/shard_map/ppermute | solution.py:48
  32.7 1.3 %collective-permute-start.16 = (bf16[512,128]{1,0:T(8,128)(2,1)S(1)}, bf16[512,128]{1,0:T(8,128)(2,1)S(1)}, u32[]{:S(2)}, u32[]{:S(2)}) collective-permute-start(bf16[512,128]{1,0:T(8,128)(2,1)S(1)} %get-tuple-element.83), channel_id=1, source_target_pairs={{0,6},{1,7},{2,4},{3,5},{4,2},{5,3},{6,0},{7,1},{8,14},{9,15},{10,... | collective-permute-start | bytes 393224 | tf_op jit(solution)/shard_map/ppermute | solution.py:48
  34.1 11.5 %conditional.2 = (bf16[512,128]{1,0:T(8,128)(2,1)}, bf16[512,128]{1,0:T(8,128)(2,1)}, bf16[512,128]{1,0:T(8,128)(2,1)}, bf16[512,128]{1,0:T(8,128)(2,1)}, f32[80,256]{1,0:T(8,128)S(1)}) conditional(s32[]{:T(128)} %convert_element_type.55, () %tuple.25, (bf16[512,128]{1,0:T(8,128)(2,1)S(1)}, s32[8]{0:T(128)S(1)}, s32[160]{0:T(256)S(1)}, ...), branch_computations={%region_1.2_spmd, %region_2.3_spmd} | conditional | flops 184320 | bytes 1879240 | solution.py:53
  34.9 0.8 %collective-permute-done.3 = f32[80,256]{1,0:T(8,128)S(1)} collective-permute-done((f32[80,256]{1,0:T(8,128)S(1)}, f32[80,256]{1,0:T(8,128)S(1)}, u32[]{:S(2)}, u32[]{:S(2)}) %collective-permute-start.3) | collective-permute-done | bytes 81952 | tf_op jit(solution)/shard_map/cond/branch_1_fun/ppermute | solution.py:48
  35.7 1.6 %collective-permute-start.4 = (bf16[80,256]{1,0:T(8,128)(2,1)S(1)}, bf16[80,256]{1,0:T(8,128)(2,1)S(1)}, u32[]{:S(2)}, u32[]{:S(2)}) collective-permute-start(bf16[80,256]{1,0:T(8,128)(2,1)S(1)} %get-tuple-element.106), channel_id=1, source_target_pairs={{0,8},{1,17},{2,10},{3,19},{4,12},{5,21},{6,14},{7,23},{8,0},{9,25... | collective-permute-start | bytes 122888 | tf_op jit(solution)/shard_map/cond/branch_1_fun/ppermute | solution.py:48
  37.3 4.2 %backward_0.1 = (bf16[512,128]{1,0:T(8,128)(2,1)}, bf16[512,128]{1,0:T(8,128)(2,1)}, bf16[512,128]{1,0:T(8,128)(2,1)}, bf16[512,128]{1,0:T(8,128)(2,1)}) custom-call(s32[8]{0:T(128)S(1)} %get-tuple-element.24.bounds_ref, s32[160]{0:T(256)S(1)} %get-tuple-element.25.row_ref, s32[160]{0:T(256)S(1)} %get-tuple-element.26.col_ref, ...), custom_call_target="tpu_custom_call" | custom-call | bytes 1024 | tf_op jit(solution)/shard_map/cond/branch_1_fun/backward_0/pallas_call | solution.py:423
  41.6 1.2 %collective-permute-start.5 = (bf16[80,256]{1,0:T(8,128)(2,1)S(1)}, bf16[80,256]{1,0:T(8,128)(2,1)S(1)}, u32[]{:S(2)}, u32[]{:S(2)}) collective-permute-start(bf16[80,256]{1,0:T(8,128)(2,1)S(1)} %fusion), channel_id=1, source_target_pairs={{0,16},{1,9},{2,18},{3,11},{4,20},{5,13},{6,22},{7,15},{8,24},{9,1... | collective-permute-start | bytes 122888 | tf_op jit(solution)/shard_map/cond/branch_1_fun/ppermute | solution.py:48
  42.8 2.9 %collective-permute-done.5 = bf16[80,256]{1,0:T(8,128)(2,1)S(1)} collective-permute-done((bf16[80,256]{1,0:T(8,128)(2,1)S(1)}, bf16[80,256]{1,0:T(8,128)(2,1)S(1)}, u32[]{:S(2)}, u32[]{:S(2)}) %collective-permute-start.5) | collective-permute-done | bytes 40992 | tf_op jit(solution)/shard_map/cond/branch_1_fun/ppermute | solution.py:48
  45.8 1.6 %collective-permute-start.14 = (bf16[80,256]{1,0:T(8,128)(2,1)S(1)}, bf16[80,256]{1,0:T(8,128)(2,1)S(1)}, u32[]{:S(2)}, u32[]{:S(2)}) collective-permute-start(bf16[80,256]{1,0:T(8,128)(2,1)S(1)} %convert_element_type.60), channel_id=1, source_target_pairs={{0,2},{1,3},{2,0},{3,1},{4,6},{5,7},{6,4},{7,5},{8,10},{9,11},{10,... | collective-permute-start | bytes 122888 | tf_op jit(solution)/shard_map/ppermute | solution.py:48
  47.5 4.8 %backward_1_2_3.1 = (f32[512,128]{1,0:T(8,128)S(1)}, bf16[512,128]{1,0:T(8,128)(2,1)S(1)}, bf16[512,128]{1,0:T(8,128)(2,1)S(1)}, bf16[512,128]{1,0:T(8,128)(2,1)S(1)}) custom-call(s32[8]{0:T(128)S(1)} %convert_reduce_fusion.bounds_ref, s32[160]{0:T(256)S(1)} %get-tuple-element.108.row_ref, s32[160]{0:T(256)S(1)} %get-tuple-element.112.col_ref, ...), custom_call_target="tpu_custom_call" | custom-call | bytes 1024 | tf_op jit(solution)/shard_map/backward_1_2_3/pallas_call | solution.py:423
  52.7 1.4 %collective-permute-start.20 = (bf16[512,128]{1,0:T(8,128)(2,1)S(1)}, bf16[512,128]{1,0:T(8,128)(2,1)S(1)}, u32[]{:S(2)}, u32[]{:S(2)}) collective-permute-start(bf16[512,128]{1,0:T(8,128)(2,1)S(1)} %get-tuple-element.102), channel_id=1, source_target_pairs={{0,16},{1,9},{2,18},{3,11},{4,20},{5,13},{6,22},{7,15},{8,24},{9,1... | collective-permute-start | bytes 393224 | tf_op jit(solution)/shard_map/ppermute | solution.py:48
  54.2 1.7 %collective-permute-start.21 = (bf16[512,128]{1,0:T(8,128)(2,1)S(1)}, bf16[512,128]{1,0:T(8,128)(2,1)S(1)}, u32[]{:S(2)}, u32[]{:S(2)}) collective-permute-start(bf16[512,128]{1,0:T(8,128)(2,1)S(1)} %get-tuple-element.103), channel_id=1, source_target_pairs={{0,24},{1,25},{2,26},{3,27},{4,28},{5,29},{6,30},{7,31},{8,16},{9,... | collective-permute-start | bytes 393224 | tf_op jit(solution)/shard_map/ppermute | solution.py:48
  55.8 6.8 %conditional.3 = (f32[128,256]{1,0:T(8,128)S(1)}, f32[256]{0:T(256)S(1)}, bf16[512,256]{1,0:T(8,128)(2,1)S(1)}) conditional(s32[]{:T(128)} %convert_element_type.55, () %tuple.24, (s32[]{:T(128)}, bf16[80,256]{1,0:T(8,128)(2,1)S(1)}, f32[80,256]{1,0:T(8,128)S(1)}, bf16[512,256]{1,0:T(8,128)(2,1)S(1)}) %tuple.27), branch_computations={%region_3.4_spmd, %region_4.5_spmd} | conditional | flops 262145 | bytes 1231986 | solution.py:53
  55.8 1.7 %collective-permute-start = (bf16[80,256]{1,0:T(8,128)(2,1)S(1)}, bf16[80,256]{1,0:T(8,128)(2,1)S(1)}, u32[]{:S(2)}, u32[]{:S(2)}) collective-permute-start(bf16[80,256]{1,0:T(8,128)(2,1)S(1)} %fusion.1), channel_id=1, source_target_pairs={{0,4},{1,5},{2,6},{3,7},{4,0},{5,1},{6,2},{7,3},{8,12},{9,13},{10,... | collective-permute-start | bytes 122888 | tf_op jit(solution)/shard_map/cond/branch_1_fun/ppermute | solution.py:48
  57.6 3.7 %collective-permute-done = bf16[80,256]{1,0:T(8,128)(2,1)S(1)} collective-permute-done((bf16[80,256]{1,0:T(8,128)(2,1)S(1)}, bf16[80,256]{1,0:T(8,128)(2,1)S(1)}, u32[]{:S(2)}, u32[]{:S(2)}) %collective-permute-start) | collective-permute-done | bytes 40992 | tf_op jit(solution)/shard_map/cond/branch_1_fun/ppermute | solution.py:48
  61.4 1.2 %collective-permute-done.1 = f32[64,256]{1,0:T(8,128)S(1)} collective-permute-done((f32[64,256]{1,0:T(8,128)S(1)}, f32[64,256]{1,0:T(8,128)S(1)}, u32[]{:S(2)}, u32[]{:S(2)}) %collective-permute-start.1) | collective-permute-done | bytes 65568 | tf_op jit(solution)/shard_map/cond/branch_1_fun/ppermute | solution.py:48
  62.7 0.8 %multiply_convert_fusion = bf16[512,128]{1,0:T(8,128)(2,1)} fusion(f32[512,128]{1,0:T(8,128)S(1)} %get-tuple-element.76.earlier_ref.refs_6_, bf16[512,128]{1,0:T(8,128)(2,1)S(1)} %get-tuple-element.83, bf16[512,128]{1,0:T(8,128)(2,1)S(1)} %collective-permute-done.21, bf16[512,128]{1,0:T(8,128)(2,1)S(1)} %collective-permute-done.20, ...), kind=kLoop, calls=%fused_computation.8 | loop fusion | flops 655360 | bytes 1179648 | tf_op jit(solution)/shard_map/convert_element_type | solution.py:501
  (58 shorter events, 2.8 us)
Async XLA Ops:
  1.7 8.9 %collective-permute-start.8 = (bf16[512,128]{1,0:T(8,128)(2,1)S(1)}, bf16[512,128]{1,0:T(8,128)(2,1)S(1)}, u32[]{:S(2)}, u32[]{:S(2)}) collective-permute-start(bf16[512,128]{1,0:T(8,128)(2,1)S(1)} %get-tuple-element.77.earlier_ref.refs_0_.refs_5_), channel_id=1, source_target_pairs={{0,24},{1,25},{2,26},{3,27},{4,28},{5,29},{6,30},{7,31},{8,16},{9,... | collective-permute-start | bytes 393224 | tf_op jit(solution)/shard_map/ppermute | solution.py:48
  5.7 6.3 %collective-permute-start.7 = (bf16[512,128]{1,0:T(8,128)(2,1)S(1)}, bf16[512,128]{1,0:T(8,128)(2,1)S(1)}, u32[]{:S(2)}, u32[]{:S(2)}) collective-permute-start(bf16[512,128]{1,0:T(8,128)(2,1)S(1)} %get-tuple-element.77.earlier_ref.refs_0_.refs_5_), channel_id=1, source_target_pairs={{0,16},{1,9},{2,18},{3,11},{4,20},{5,13},{6,22},{7,15},{8,24},{9,1... | collective-permute-start | bytes 393224 | tf_op jit(solution)/shard_map/ppermute | solution.py:48
  6.2 6.0 %collective-permute-start.6 = (bf16[512,128]{1,0:T(8,128)(2,1)S(1)}, bf16[512,128]{1,0:T(8,128)(2,1)S(1)}, u32[]{:S(2)}, u32[]{:S(2)}) collective-permute-start(bf16[512,128]{1,0:T(8,128)(2,1)S(1)} %get-tuple-element.77.earlier_ref.refs_0_.refs_5_), channel_id=1, source_target_pairs={{0,8},{1,17},{2,10},{3,19},{4,12},{5,21},{6,14},{7,23},{8,0},{9,25... | collective-permute-start | bytes 393224 | tf_op jit(solution)/shard_map/ppermute | solution.py:48
  12.2 18.0 %copy-start = (bf16[512,256]{1,0:T(8,128)(2,1)S(1)}, bf16[512,256]{1,0:T(8,128)(2,1)}, u32[]{:S(2)}) copy-start(bf16[512,256]{1,0:T(8,128)(2,1)} %refs_9_.1) | copy-start | bytes 786436
  12.2 18.0 %copy-start.1 = (bf16[128,256]{1,0:T(8,128)(2,1)S(1)}, bf16[128,256]{1,0:T(8,128)(2,1)}, u32[]{:S(2)}) copy-start(bf16[128,256]{1,0:T(8,128)(2,1)} %refs_7_.1) | copy-start | bytes 196612
  12.2 18.0 %copy-start.2 = (f32[256]{0:T(256)S(1)}, f32[256]{0:T(256)}, u32[]{:S(2)}) copy-start(f32[256]{0:T(256)} %param.20) | copy-start | bytes 3076
  15.0 4.6 %collective-permute-start.10 = (bf16[1024,128]{1,0:T(8,128)(2,1)S(1)}, bf16[1024,128]{1,0:T(8,128)(2,1)S(1)}, u32[]{:S(2)}, u32[]{:S(2)}) collective-permute-start(bf16[1024,128]{1,0:T(8,128)(2,1)S(1)} %get-tuple-element.78.earlier_ref), channel_id=1, source_target_pairs={{0,1},{1,0},{2,3},{3,2},{4,5},{5,4},{6,7},{7,6},{8,9},{9,8},{10,11... | collective-permute-start | bytes 786440 | tf_op jit(solution)/shard_map/ppermute | solution.py:48
  15.1 9.1 %collective-permute-start.13 = (bf16[512,128]{1,0:T(8,128)(2,1)S(1)}, bf16[512,128]{1,0:T(8,128)(2,1)S(1)}, u32[]{:S(2)}, u32[]{:S(2)}) collective-permute-start(bf16[512,128]{1,0:T(8,128)(2,1)S(1)} %get-tuple-element.82), channel_id=1, source_target_pairs={{0,5},{1,4},{2,7},{3,6},{4,1},{5,0},{6,3},{7,2},{8,13},{9,12},{10,... | collective-permute-start | bytes 393224 | tf_op jit(solution)/shard_map/ppermute | solution.py:48
  19.5 4.7 %collective-permute-start.9 = (bf16[512,128]{1,0:T(8,128)(2,1)S(1)}, bf16[512,128]{1,0:T(8,128)(2,1)S(1)}, u32[]{:S(2)}, u32[]{:S(2)}) collective-permute-start(bf16[512,128]{1,0:T(8,128)(2,1)S(1)} %get-tuple-element.80), channel_id=1, source_target_pairs={{0,1},{1,0},{2,3},{3,2},{4,5},{5,4},{6,7},{7,6},{8,9},{9,8},{10,11... | collective-permute-start | bytes 393224 | tf_op jit(solution)/shard_map/ppermute | solution.py:48
  19.7 8.2 %collective-permute-start.12 = (bf16[512,128]{1,0:T(8,128)(2,1)S(1)}, bf16[512,128]{1,0:T(8,128)(2,1)S(1)}, u32[]{:S(2)}, u32[]{:S(2)}) collective-permute-start(bf16[512,128]{1,0:T(8,128)(2,1)S(1)} %get-tuple-element.110), channel_id=1, source_target_pairs={{0,6},{1,7},{2,4},{3,5},{4,2},{5,3},{6,0},{7,1},{8,14},{9,15},{10,... | collective-permute-start | bytes 393224 | tf_op jit(solution)/shard_map/ppermute | solution.py:48
  20.8 9.5 %collective-permute-start.11 = (bf16[512,128]{1,0:T(8,128)(2,1)S(1)}, bf16[512,128]{1,0:T(8,128)(2,1)S(1)}, u32[]{:S(2)}, u32[]{:S(2)}) collective-permute-start(bf16[512,128]{1,0:T(8,128)(2,1)S(1)} %get-tuple-element.111), channel_id=1, source_target_pairs={{0,2},{1,3},{2,0},{3,1},{4,6},{5,7},{6,4},{7,5},{8,10},{9,11},{10,... | collective-permute-start | bytes 393224 | tf_op jit(solution)/shard_map/ppermute | solution.py:48
  30.8 14.9 %collective-permute-start.17 = (bf16[512,128]{1,0:T(8,128)(2,1)S(1)}, bf16[512,128]{1,0:T(8,128)(2,1)S(1)}, u32[]{:S(2)}, u32[]{:S(2)}) collective-permute-start(bf16[512,128]{1,0:T(8,128)(2,1)S(1)} %get-tuple-element.83), channel_id=1, source_target_pairs={{0,5},{1,4},{2,7},{3,6},{4,1},{5,0},{6,3},{7,2},{8,13},{9,12},{10,... | collective-permute-start | bytes 393224 | tf_op jit(solution)/shard_map/ppermute | solution.py:48
  32.7 13.0 %collective-permute-start.16 = (bf16[512,128]{1,0:T(8,128)(2,1)S(1)}, bf16[512,128]{1,0:T(8,128)(2,1)S(1)}, u32[]{:S(2)}, u32[]{:S(2)}) collective-permute-start(bf16[512,128]{1,0:T(8,128)(2,1)S(1)} %get-tuple-element.83), channel_id=1, source_target_pairs={{0,6},{1,7},{2,4},{3,5},{4,2},{5,3},{6,0},{7,1},{8,14},{9,15},{10,... | collective-permute-start | bytes 393224 | tf_op jit(solution)/shard_map/ppermute | solution.py:48
  34.0 11.7 %collective-permute-start.15 = (bf16[512,128]{1,0:T(8,128)(2,1)S(1)}, bf16[512,128]{1,0:T(8,128)(2,1)S(1)}, u32[]{:S(2)}, u32[]{:S(2)}) collective-permute-start(bf16[512,128]{1,0:T(8,128)(2,1)S(1)} %get-tuple-element.83), channel_id=1, source_target_pairs={{0,2},{1,3},{2,0},{3,1},{4,6},{5,7},{6,4},{7,5},{8,10},{9,11},{10,... | collective-permute-start | bytes 393224 | tf_op jit(solution)/shard_map/ppermute | solution.py:48
  34.4 1.3 %collective-permute-start.3 = (f32[80,256]{1,0:T(8,128)S(1)}, f32[80,256]{1,0:T(8,128)S(1)}, u32[]{:S(2)}, u32[]{:S(2)}) collective-permute-start(f32[80,256]{1,0:T(8,128)S(1)} %get-tuple-element.37), channel_id=1, source_target_pairs={{0,1},{1,0},{2,3},{3,2},{4,5},{5,4},{6,7},{7,6},{8,9},{9,8},{10,11... | collective-permute-start | bytes 245768 | tf_op jit(solution)/shard_map/cond/branch_1_fun/ppermute | solution.py:48
  34.6 2.7 %collective-permute-start.2 = (bf16[512,128]{1,0:T(8,128)(2,1)S(1)}, bf16[512,128]{1,0:T(8,128)(2,1)S(1)}, u32[]{:S(2)}, u32[]{:S(2)}) collective-permute-start(bf16[512,128]{1,0:T(8,128)(2,1)S(1)} %get-tuple-element.28.refs_0_), channel_id=1, source_target_pairs={{0,1},{1,0},{2,3},{3,2},{4,5},{5,4},{6,7},{7,6},{8,9},{9,8},{10,11... | collective-permute-start | bytes 393224 | tf_op jit(solution)/shard_map/cond/branch_1_fun/ppermute | solution.py:48
  35.7 5.8 %collective-permute-start.4 = (bf16[80,256]{1,0:T(8,128)(2,1)S(1)}, bf16[80,256]{1,0:T(8,128)(2,1)S(1)}, u32[]{:S(2)}, u32[]{:S(2)}) collective-permute-start(bf16[80,256]{1,0:T(8,128)(2,1)S(1)} %get-tuple-element.106), channel_id=1, source_target_pairs={{0,8},{1,17},{2,10},{3,19},{4,12},{5,21},{6,14},{7,23},{8,0},{9,25... | collective-permute-start | bytes 122888 | tf_op jit(solution)/shard_map/cond/branch_1_fun/ppermute | solution.py:48
  41.6 4.1 %collective-permute-start.5 = (bf16[80,256]{1,0:T(8,128)(2,1)S(1)}, bf16[80,256]{1,0:T(8,128)(2,1)S(1)}, u32[]{:S(2)}, u32[]{:S(2)}) collective-permute-start(bf16[80,256]{1,0:T(8,128)(2,1)S(1)} %fusion), channel_id=1, source_target_pairs={{0,16},{1,9},{2,18},{3,11},{4,20},{5,13},{6,22},{7,15},{8,24},{9,1... | collective-permute-start | bytes 122888 | tf_op jit(solution)/shard_map/cond/branch_1_fun/ppermute | solution.py:48
  45.7 1.7 %collective-permute-start.18 = (bf16[1024,128]{1,0:T(8,128)(2,1)S(1)}, bf16[1024,128]{1,0:T(8,128)(2,1)S(1)}, u32[]{:S(2)}, u32[]{:S(2)}) collective-permute-start(bf16[1024,128]{1,0:T(8,128)(2,1)S(1)} %constant_dynamic-update-slice_fusion.refs_0_), channel_id=1, source_target_pairs={{0,1},{1,0},{2,3},{3,2},{4,5},{5,4},{6,7},{7,6},{8,9},{9,8},{10,11... | collective-permute-start | bytes 786440 | tf_op jit(solution)/shard_map/ppermute | solution.py:48
  45.8 6.4 %collective-permute-start.14 = (bf16[80,256]{1,0:T(8,128)(2,1)S(1)}, bf16[80,256]{1,0:T(8,128)(2,1)S(1)}, u32[]{:S(2)}, u32[]{:S(2)}) collective-permute-start(bf16[80,256]{1,0:T(8,128)(2,1)S(1)} %convert_element_type.60), channel_id=1, source_target_pairs={{0,2},{1,3},{2,0},{3,1},{4,6},{5,7},{6,4},{7,5},{8,10},{9,11},{10,... | collective-permute-start | bytes 122888 | tf_op jit(solution)/shard_map/ppermute | solution.py:48
  52.3 10.4 %collective-permute-start.19 = (bf16[512,128]{1,0:T(8,128)(2,1)S(1)}, bf16[512,128]{1,0:T(8,128)(2,1)S(1)}, u32[]{:S(2)}, u32[]{:S(2)}) collective-permute-start(bf16[512,128]{1,0:T(8,128)(2,1)S(1)} %get-tuple-element.101), channel_id=1, source_target_pairs={{0,8},{1,17},{2,10},{3,19},{4,12},{5,21},{6,14},{7,23},{8,0},{9,25... | collective-permute-start | bytes 393224 | tf_op jit(solution)/shard_map/ppermute | solution.py:48
  52.7 9.9 %collective-permute-start.20 = (bf16[512,128]{1,0:T(8,128)(2,1)S(1)}, bf16[512,128]{1,0:T(8,128)(2,1)S(1)}, u32[]{:S(2)}, u32[]{:S(2)}) collective-permute-start(bf16[512,128]{1,0:T(8,128)(2,1)S(1)} %get-tuple-element.102), channel_id=1, source_target_pairs={{0,16},{1,9},{2,18},{3,11},{4,20},{5,13},{6,22},{7,15},{8,24},{9,1... | collective-permute-start | bytes 393224 | tf_op jit(solution)/shard_map/ppermute | solution.py:48
  54.2 8.5 %collective-permute-start.21 = (bf16[512,128]{1,0:T(8,128)(2,1)S(1)}, bf16[512,128]{1,0:T(8,128)(2,1)S(1)}, u32[]{:S(2)}, u32[]{:S(2)}) collective-permute-start(bf16[512,128]{1,0:T(8,128)(2,1)S(1)} %get-tuple-element.103), channel_id=1, source_target_pairs={{0,24},{1,25},{2,26},{3,27},{4,28},{5,29},{6,30},{7,31},{8,16},{9,... | collective-permute-start | bytes 393224 | tf_op jit(solution)/shard_map/ppermute | solution.py:48
  55.8 5.4 %collective-permute-start = (bf16[80,256]{1,0:T(8,128)(2,1)S(1)}, bf16[80,256]{1,0:T(8,128)(2,1)S(1)}, u32[]{:S(2)}, u32[]{:S(2)}) collective-permute-start(bf16[80,256]{1,0:T(8,128)(2,1)S(1)} %fusion.1), channel_id=1, source_target_pairs={{0,4},{1,5},{2,6},{3,7},{4,0},{5,1},{6,2},{7,3},{8,12},{9,13},{10,... | collective-permute-start | bytes 122888 | tf_op jit(solution)/shard_map/cond/branch_1_fun/ppermute | solution.py:48
  61.3 1.3 %collective-permute-start.1 = (f32[64,256]{1,0:T(8,128)S(1)}, f32[64,256]{1,0:T(8,128)S(1)}, u32[]{:S(2)}, u32[]{:S(2)}) collective-permute-start(f32[64,256]{1,0:T(8,128)S(1)} %slice.14), channel_id=1, source_target_pairs={{0,1},{1,0},{2,3},{3,2},{4,5},{5,4},{6,7},{7,6},{8,9},{9,8},{10,11... | collective-permute-start | bytes 196616 | tf_op jit(solution)/shard_map/cond/branch_1_fun/ppermute | solution.py:48
  62.6 0.8 %copy-start.3 = (bf16[512,256]{1,0:T(8,128)(2,1)}, bf16[512,256]{1,0:T(8,128)(2,1)S(1)}, u32[]{:S(2)}) copy-start(bf16[512,256]{1,0:T(8,128)(2,1)S(1)} %get-tuple-element.72) | copy-start | bytes 786436
  62.6 0.8 %copy-start.4 = (f32[128,256]{1,0:T(8,128)}, f32[128,256]{1,0:T(8,128)S(1)}, u32[]{:S(2)}) copy-start(f32[128,256]{1,0:T(8,128)S(1)} %get-tuple-element.74) | copy-start | bytes 393220
  62.6 0.8 %copy-start.5 = (f32[256]{0:T(256)}, f32[256]{0:T(256)S(1)}, u32[]{:S(2)}) copy-start(f32[256]{0:T(256)S(1)} %get-tuple-element.75) | copy-start | bytes 3076

commit v6 on v5

--- a/solution.py
+++ b/solution.py
@@ -16,6 +16,7 @@
 F32 = jnp.float32
 CORES = 2
 BIAS_ROWS = 16
+TOKEN_ROWS = 16
 
 
 def params(mib):
@@ -162,48 +163,8 @@
         first += block_ref.shape[0]
 
 
-def over_slots(low, high, unroll, slot_total, body):
-    def step(i, carry):
-        for u in range(unroll):
-            t = low + i * unroll + u
-            body(jnp.minimum(t, slot_total - 1), t < high)
-        return carry
-
-    lax.fori_loop(0, (high - low + unroll - 1) // unroll, step, 0)
-
-
 def aligned(index, tile):
     return pl.ds(pl.multiple_of(index * tile, tile), tile)
-
-
-def forward_kernel(places, unrolls, earlier_ref, bounds_ref, row_ref, col_ref, w_ref, *refs):
-    outs = 3 if 3 in places else 2
-    x_refs, out_refs, (held, total) = refs[: -2 - outs], refs[-2 - outs : -2], refs[-2:]
-    tile = w_ref.shape[-1]
-    block_tiles = x_refs[0].shape[0] // tile
-    gather_blocks(x_refs, held)
-    total[...] = jnp.zeros_like(total)
-    spare = total.shape[0] // tile - 1
-    for n, place in enumerate(places):
-
-        def body(t, used):
-            row = row_ref[t]
-            if place == 3:
-                row = row % block_tiles
-            row = jnp.where(used, row + n * 2 * block_tiles, spare)
-            part = jnp.dot(w_ref[t], held[aligned(col_ref[t], tile), :], preferred_element_type=F32)
-            total[aligned(row, tile), :] += part
-
-        over_slots(bounds_ref[place], bounds_ref[4 + place], unrolls[n], w_ref.shape[0], body)
-    rows = block_tiles * tile
-    for n, place in enumerate(places):
-        first = n * 2 * rows
-        if place == 3:
-            out_refs[2][...] = total[first : first + rows, :].astype(BF)
-        else:
-            for out_ref in out_refs[:2]:
-                out_ref[n * rows : (n + 1) * rows, :] = total[first : first + rows, :].astype(BF)
-                first += rows
 
 
 def stream_slots(w_hbm, held, sems, ranges, unroll):
@@ -240,6 +201,56 @@
     return finish
 
 
+def held_slots(w_ref, ranges, unroll):
+    slot_total = w_ref.shape[0]
+
+    def finish(body):
+        for n, (low, high) in enumerate(ranges):
+
+            def step(i, carry, low=low, high=high, n=n):
+                for u in range(unroll):
+                    t = low + i * unroll + u
+                    place = jnp.minimum(t, slot_total - 1)
+                    body(w_ref[place], place, t < high, n)
+                return carry
+
+            lax.fori_loop(0, (high - low + unroll - 1) // unroll, step, 0)
+
+    return finish
+
+
+def forward_kernel(places, unroll, stream, earlier_ref, bounds_ref, row_ref, col_ref, w_ref, *refs):
+    ranges = [(bounds_ref[place], bounds_ref[4 + place]) for place in places]
+    if stream:
+        refs, (tiles_held, sems) = refs[:-2], refs[-2:]
+        finish = stream_slots(w_ref, tiles_held, sems, ranges, unroll)
+    else:
+        finish = held_slots(w_ref, ranges, unroll)
+    outs = 1 if 3 in places else 2
+    x_refs, out_refs, (held, total) = refs[: -2 - outs], refs[-2 - outs : -2], refs[-2:]
+    tile = w_ref.shape[-1]
+    block_tiles = x_refs[0].shape[0] // tile
+    gather_blocks(x_refs, held)
+    total[...] = jnp.zeros_like(total)
+    spare = total.shape[0] // tile - 1
+
+    def body(w, t, used, n):
+        row = row_ref[t]
+        if places[n] == 3:
+            row = row % block_tiles
+        row = jnp.where(used, row + n * 2 * block_tiles, spare)
+        part = jnp.dot(w, held[aligned(col_ref[t], tile), :], preferred_element_type=F32)
+        total[aligned(row, tile), :] += part
+
+    finish(body)
+    rows = block_tiles * tile
+    for n, place in enumerate(places):
+        first = n * 2 * rows
+        for out_ref in out_refs:
+            out_ref[n * rows : (n + 1) * rows, :] = total[first : first + rows, :].astype(BF)
+            first += rows
+
+
 def backward_kernel(places, unroll, bounds_ref, row_ref, col_ref, w_ref, *refs):
     refs, (total, held, tiles_held, sems) = refs[:-4], refs[-4:]
     ranges = [(bounds_ref[place], bounds_ref[4 + place]) for place in places]
@@ -247,7 +258,8 @@
     tile = w_ref.shape[-1]
     block_refs, refs = refs[: 2 if places == (0,) else 3], refs[2 if places == (0,) else 3 :]
     if places == (0,):
-        out_refs = refs
+        out_refs, token_ref = refs[:-1], refs[-1]
+        token_ref[...] = jnp.zeros_like(token_ref)
         total[...] = jnp.zeros_like(total)
     else:
         old_refs, out_refs = refs[: len(refs) // 2], refs[len(refs) // 2 :]
@@ -285,7 +297,8 @@
     norm = norm_ref[...]
     neighbor = part_refs[0][...].astype(F32)
     for part_ref in part_refs[1:]:
-        neighbor = neighbor + part_ref[...].astype(F32)
+        part = part_ref[...].astype(F32)
+        neighbor = neighbor + part
     aggregated = (norm * neighbor).astype(BF)
     weight = weight_ref[...]
     pre_act = jnp.dot(aggregated, weight, preferred_element_type=F32) + bias_ref[...]
@@ -367,34 +380,53 @@
 
     tiles_dev = stage(scaled)
 
-    def forward(places, unrolls, earlier):
-        single = 3 in places
-        pairs = len(places) - single
-        shape = jax.ShapeDtypeStruct((pairs * row_count, feat_width), BF)
+    tiles_hbm = in_hbm(tile_weights[0, 0])
+
+    def fetch_scratch(unroll, ranges):
+        fetches = slot_total // unroll + ranges
+        return [pltpu.VMEM((fetches, unroll, tile, tile), BF), pltpu.SemaphoreType.DMA((fetches,))]
+
+    def forward(places, unroll, stream, earlier):
+        outs = 1 if 3 in places else 2
+        shape = jax.ShapeDtypeStruct((len(places) * row_count, feat_width), BF)
         return pl.pallas_call(
-            functools.partial(forward_kernel, places, unrolls),
-            out_shape=[shape, shape] + [block_shape] * single,
-            in_specs=[ANY, SMEM, SMEM, SMEM] + [VMEM] * (1 + rep_count),
-            out_specs=[VMEM] * (2 + single),
+            functools.partial(forward_kernel, places, unroll, stream),
+            out_shape=[shape] * outs,
+            in_specs=[ANY, SMEM, SMEM, SMEM] + [HBM if stream else VMEM] + [VMEM] * rep_count,
+            out_specs=[VMEM] * outs,
             scratch_shapes=[
                 pltpu.VMEM((col_tiles * tile, feat_width), BF),
-                pltpu.VMEM((((2 * pairs + single) * row_tiles + 1) * tile, feat_width), F32),
-            ],
-            compiler_params=params(16),
+                pltpu.VMEM(((outs * len(places) * row_tiles + 1) * tile, feat_width), F32),
+            ]
+            + (fetch_scratch(unroll, len(places)) if stream else []),
+            compiler_params=params(28 if stream else 16),
             cost_estimate=SMALL,
             name="forward_" + "_".join(map(str, places)),
-        )(earlier, bounds, row_place, col_place, tiles_dev, *source)
+        )(earlier, bounds, row_place, col_place, tiles_hbm if stream else tiles_dev, *source)
 
     def add(a, b):
         return (a.astype(F32) + b.astype(F32)).astype(BF)
 
-    keep, send, part3 = forward((1, 2, 3), (26, 26, 12), norm_wide)
-    sums = add(keep, swap_cores(send))
+    (part3,) = forward((3,), 12, False, norm_wide)
     came3 = move(part3, pair_partner(3, False))
-    came2 = move(sums[row_count:], pair_partner(2, False))
-    came1 = move(sums[:row_count], pair_partner(1, False))
-    keep0, send0 = forward((0,), (20,), send)
-    cross0 = swap_cores(send0)
+
+    def pair_sums(keep, send):
+        other = swap_cores(send)
+        near, far = add(keep[:row_count], other[:row_count]), add(keep[row_count:], other[row_count:])
+        return near, far, other[:TOKEN_ROWS]
+
+    near, far, token = block(pair_sums, *forward((1, 2), 16, False, part3))
+    came2 = move(far, pair_partner(2, False))
+    came1 = move(near, pair_partner(1, False))
+
+    def own_sum(earlier):
+        keep, send = forward((0,), 20, True, earlier)
+        return add(keep, swap_cores(send))
+
+    own = block(own_sum, token)
+    (came3,) = together([came3], [own])
+    (came2,) = together([came2], [came3])
+    (came1,) = together([came1], [came2])
 
     hidden, scaled_grad, aggregated, pre_grad = pl.pallas_call(
         dense_kernel,
@@ -404,21 +436,18 @@
             block_shape,
             jax.ShapeDtypeStruct((row_count, hid_width), BF),
         ],
-        in_specs=[VMEM] * 10,
+        in_specs=[VMEM] * 9,
         out_specs=[VMEM] * 4,
         compiler_params=params(16),
         cost_estimate=SMALL,
         name="dense",
-    )(keep0, cross0, came1, came2, came3, scaled, norm_wide, weight, layer_bias[None], upstream)
+    )(own, came1, came2, came3, scaled, norm_wide, weight, layer_bias[None], upstream)
 
     grads2 = move(scaled_grad, pair_partner(2, True))
     grads3 = move(scaled_grad, pair_partner(3, True))
     grads1 = move(scaled_grad, pair_partner(1, True))
 
-    tiles_hbm = in_hbm(tile_weights[0, 0])
-
     def backward(places, unroll, out_shape, *blocks):
-        fetches = slot_total // unroll + len(places)
         held_rows = (2 if places == (0,) else 5) * row_count
         return pl.pallas_call(
             functools.partial(backward_kernel, places, unroll),
@@ -428,9 +457,8 @@
             scratch_shapes=[
                 pltpu.VMEM(((col_tiles + 1) * tile, feat_width), F32),
                 pltpu.VMEM((held_rows, feat_width), BF),
-                pltpu.VMEM((fetches, unroll, tile, tile), BF),
-                pltpu.SemaphoreType.DMA((fetches,)),
-            ],
+            ]
+            + fetch_scratch(unroll, len(places)),
             compiler_params=params(28),
             cost_estimate=SMALL,
             name="backward_" + "_".join(map(str, places)),
@@ -452,11 +480,12 @@
             name="weight_terms",
         )(core[None].astype(jnp.int32), aggregated, pre_grad)
         grad = keep + swap_cores(send)
-        total = backward((0,), 16, [block_shape] * rep_count, scaled_grad, other)
+        token_shape = jax.ShapeDtypeStruct((TOKEN_ROWS, feat_width), BF)
+        *total, token = backward((0,), 16, [block_shape] * rep_count + [token_shape], scaled_grad, other)
         for n in range(rep_bits()):
             came = move(grad.astype(BF), rep_partner(1 << n))
             if n == 0:
-                (grad,) = together([grad], total)
+                (grad,) = together([grad], [token])
             grad = grad + came.astype(F32)
         return total, grad
 

time: 63.1 us -> 60.6 us (0.960); the launches traced: 63.5 us -> 60 us
  waiting for transfers between devices: 19 us -> 15.2 us
    ppermute x22, waiting for transfers between devices: 19 us -> 15.2 us  [move(): return lax.ppermute(value, BOTH, pairs)]
    pallas_call x2, Pallas kernels: 9.02 us -> 7.41 us  [backward(): pl.pallas_call(functools.partial(backward_kernel, places, unroll), out_sh...]
    pallas_call x2 -> x3, Pallas kernels: 4.86 us -> 6.37 us  [forward(): pl.pallas_call(functools.partial(forward_kernel, places, unroll, stream),...]
  transfers between devices with their start and end apart: 22 -> 22, of which waited for: 9 -> 11; matrix products, arithmetic and copies ran while one was open for 2% -> 2% of each run, Pallas kernels for 22% -> 26%
where the time goes in v6:
time: 60.6 us; the launch traced here: 60 us
  starting transfers between devices  22.9 us (38%)
  Pallas kernels  18.1 us (30%)
  waiting for transfers between devices  15.2 us (25%)
  other arithmetic  1.95 us (3%)
  between operations  1.54 us (3%)
    ppermute x22, starting transfers between devices, move(): return lax.ppermute(value, BOTH, pairs)  22.9 us
    ppermute x22, waiting for transfers between devices, move(): return lax.ppermute(value, BOTH, pairs)  15.2 us
    pallas_call x2, Pallas kernels, backward(): pl.pallas_call(functools.partial(backward_kernel, places, unroll), out_sh...  7.41 us
    pallas_call x3, Pallas kernels, forward(): pl.pallas_call(functools.partial(forward_kernel, places, unroll, stream),...  6.37 us
    pallas_call x1, Pallas kernels, stage(): pl.pallas_call(stage_kernel, out_shape=jax.ShapeDtypeStruct((slot_total,...  2.5 us
  transfers between devices with their start and end apart: 22, of which 11 were waited for; matrix products, arithmetic and copies ran while one was open for 2% of the time, Pallas kernels for 26%

profile of v6, /device:TPU:0, one launch (start us, length us, event | category | flops | bytes accessed | tf_op | source)
XLA Modules:
  0.0 60.0 jit_solution(12320326614299287413)
XLA Ops:
  0.6 1.1 %prepare.1 = (bf16[512,128]{1,0:T(8,128)(2,1)S(1)}, f32[512,128]{1,0:T(8,128)S(1)}) custom-call(s32[4,128]{1,0:T(4,128)} %bitcast.18, bf16[512,128]{1,0:T(8,128)(2,1)} %features_hbm.1), custom_call_target="tpu_custom_call" | custom-call | bytes 1024 | tf_op jit(solution)/shard_map/prepare/pallas_call | solution.py:351
  1.7 4.0 %collective-permute-start.10 = (bf16[512,128]{1,0:T(8,128)(2,1)S(1)}, bf16[512,128]{1,0:T(8,128)(2,1)S(1)}, u32[]{:S(2)}, u32[]{:S(2)}) collective-permute-start(bf16[512,128]{1,0:T(8,128)(2,1)S(1)} %get-tuple-element.114.earlier_ref.refs_0_.refs_4_), channel_id=1, source_target_pairs={{0,24},{1,25},{2,26},{3,27},{4,28},{5,29},{6,30},{7,31},{8,16},{9,... | collective-permute-start | bytes 393224 | tf_op jit(solution)/shard_map/ppermute | solution.py:49
  7.9 2.5 %stage_tiles.1.w_ref = bf16[160,128,128]{2,1,0:T(8,128)(2,1)S(1)} custom-call(bf16[160,128,128]{2,1,0:T(8,128)(2,1)} %bitcast.14, bf16[512,128]{1,0:T(8,128)(2,1)S(1)} %get-tuple-element.114.earlier_ref.refs_0_.refs_4_), custom_call_target="tpu_custom_call" | custom-call | bytes 10485760 | tf_op jit(solution)/shard_map/stage_tiles/pallas_call | solution.py:370
  10.6 1.4 %collective-permute-done.9.refs_2_ = bf16[512,128]{1,0:T(8,128)(2,1)S(1)} collective-permute-done((bf16[512,128]{1,0:T(8,128)(2,1)S(1)}, bf16[512,128]{1,0:T(8,128)(2,1)S(1)}, u32[]{:S(2)}, u32[]{:S(2)}) %collective-permute-start.9) | collective-permute-done | bytes 131104 | tf_op jit(solution)/shard_map/ppermute | solution.py:49
  12.2 0.9 %forward_3.1.earlier_ref = bf16[512,128]{1,0:T(8,128)(2,1)S(1)} custom-call(f32[512,128]{1,0:T(8,128)S(1)} %get-tuple-element.113.earlier_ref.refs_5_, s32[8]{0:T(128)S(1)} %convert_reduce_fusion.bounds_ref, s32[160]{0:T(256)S(1)} %get-tuple-element.143.row_ref, s32[160]{0:T(256)S(1)} %get-tuple-element.147.col_ref, ...), custom_call_target="tpu_custom_call" | custom-call | bytes 1024 | tf_op jit(solution)/shard_map/forward_3/pallas_call | solution.py:392
  13.2 1.8 %collective-permute-start.13 = (bf16[512,128]{1,0:T(8,128)(2,1)S(1)}, bf16[512,128]{1,0:T(8,128)(2,1)S(1)}, u32[]{:S(2)}, u32[]{:S(2)}) collective-permute-start(bf16[512,128]{1,0:T(8,128)(2,1)S(1)} %forward_3.1.earlier_ref), channel_id=1, source_target_pairs={{0,5},{1,4},{2,7},{3,6},{4,1},{5,0},{6,3},{7,2},{8,13},{9,12},{10,... | collective-permute-start | bytes 393224 | tf_op jit(solution)/shard_map/ppermute | solution.py:49
  14.9 2.3 %forward_1_2.1 = (bf16[1024,128]{1,0:T(8,128)(2,1)S(1)}, bf16[1024,128]{1,0:T(8,128)(2,1)S(1)}) custom-call(bf16[512,128]{1,0:T(8,128)(2,1)S(1)} %forward_3.1.earlier_ref, s32[8]{0:T(128)S(1)} %convert_reduce_fusion.bounds_ref, s32[160]{0:T(256)S(1)} %get-tuple-element.143.row_ref, s32[160]{0:T(256)S(1)} %get-tuple-element.147.col_ref, ...), custom_call_target="tpu_custom_call" | custom-call | bytes 1024 | tf_op jit(solution)/shard_map/forward_1_2/pallas_call | solution.py:392
  17.3 2.6 %conditional.4 = (bf16[512,128]{1,0:T(8,128)(2,1)S(1)}, bf16[512,128]{1,0:T(8,128)(2,1)S(1)}, bf16[16,128]{1,0:T(8,128)(2,1)S(1)}) conditional(s32[]{:T(128)} %convert_element_type.75, () %tuple.40, (bf16[1024,128]{1,0:T(8,128)(2,1)S(1)}, bf16[1024,128]{1,0:T(8,128)(2,1)S(1)}) %forward_1_2.1), branch_computations={%region_1.2_spmd, %region_2.3_spmd} | conditional | flops 524288 | bytes 1843264 | solution.py:54
  17.3 1.4 %collective-permute-start = (bf16[1024,128]{1,0:T(8,128)(2,1)S(1)}, bf16[1024,128]{1,0:T(8,128)(2,1)S(1)}, u32[]{:S(2)}, u32[]{:S(2)}) collective-permute-start(bf16[1024,128]{1,0:T(8,128)(2,1)S(1)} %get-tuple-element.50), channel_id=1, source_target_pairs={{0,1},{1,0},{2,3},{3,2},{4,5},{5,4},{6,7},{7,6},{8,9},{9,8},{10,11... | collective-permute-start | bytes 786440 | tf_op jit(solution)/shard_map/cond/branch_1_fun/ppermute | solution.py:49
  18.6 1.2 %collective-permute-done = bf16[1024,128]{1,0:T(8,128)(2,1)S(1)} collective-permute-done((bf16[1024,128]{1,0:T(8,128)(2,1)S(1)}, bf16[1024,128]{1,0:T(8,128)(2,1)S(1)}, u32[]{:S(2)}, u32[]{:S(2)}) %collective-permute-start) | collective-permute-done | bytes 262176 | tf_op jit(solution)/shard_map/cond/branch_1_fun/ppermute | solution.py:49
  19.9 1.1 %collective-permute-start.12 = (bf16[512,128]{1,0:T(8,128)(2,1)S(1)}, bf16[512,128]{1,0:T(8,128)(2,1)S(1)}, u32[]{:S(2)}, u32[]{:S(2)}) collective-permute-start(bf16[512,128]{1,0:T(8,128)(2,1)S(1)} %get-tuple-element.117), channel_id=1, source_target_pairs={{0,6},{1,7},{2,4},{3,5},{4,2},{5,3},{6,0},{7,1},{8,14},{9,15},{10,... | collective-permute-start | bytes 393224 | tf_op jit(solution)/shard_map/ppermute | solution.py:49
  21.0 4.6 %conditional.5 = (bf16[512,128]{1,0:T(8,128)(2,1)S(1)}) conditional(s32[]{:T(128)} %convert_element_type.75, () %tuple.39, (bf16[16,128]{1,0:T(8,128)(2,1)S(1)}, s32[8]{0:T(128)S(1)}, s32[160]{0:T(256)S(1)}, s32[160]{0:T(256)S(1)}, bf16[160,128,128]{2,1,0:T(8,128)(2,1)}, /*index=5*/bf16[512,128]{1,0:T(8,128)(2,1)S(1)}, ...), branch_computations={%region_3.4_spmd, %region_4.5_spmd} | conditional | flops 262144 | bytes 918576 | solution.py:54
  21.0 3.2 %forward_0.1 = (bf16[512,128]{1,0:T(8,128)(2,1)S(1)}, bf16[512,128]{1,0:T(8,128)(2,1)S(1)}) custom-call(bf16[16,128]{1,0:T(8,128)(2,1)S(1)} %get-tuple-element.51.earlier_ref, s32[8]{0:T(128)S(1)} %get-tuple-element.52.bounds_ref, s32[160]{0:T(256)S(1)} %get-tuple-element.53.row_ref, s32[160]{0:T(256)S(1)} %get-tuple-element.54.col_ref, ...), custom_call_target="tpu_custom_call" | custom-call | bytes 1024 | tf_op jit(solution)/shard_map/cond/branch_1_fun/forward_0/pallas_call | solution.py:392
  24.3 1.3 %collective-permute-done.1 = bf16[512,128]{1,0:T(8,128)(2,1)S(1)} collective-permute-done((bf16[512,128]{1,0:T(8,128)(2,1)S(1)}, bf16[512,128]{1,0:T(8,128)(2,1)S(1)}, u32[]{:S(2)}, u32[]{:S(2)}) %collective-permute-start.1) | collective-permute-done | bytes 131104 | tf_op jit(solution)/shard_map/cond/branch_1_fun/ppermute | solution.py:49
  25.7 2.4 %collective-permute-done.12.refs_0_ = bf16[512,128]{1,0:T(8,128)(2,1)S(1)} collective-permute-done((bf16[512,128]{1,0:T(8,128)(2,1)S(1)}, bf16[512,128]{1,0:T(8,128)(2,1)S(1)}, u32[]{:S(2)}, u32[]{:S(2)}) %collective-permute-start.12) | collective-permute-done | bytes 131104 | tf_op jit(solution)/shard_map/ppermute | solution.py:49
  28.1 1.2 %collective-permute-done.11.refs_0_ = bf16[512,128]{1,0:T(8,128)(2,1)S(1)} collective-permute-done((bf16[512,128]{1,0:T(8,128)(2,1)S(1)}, bf16[512,128]{1,0:T(8,128)(2,1)S(1)}, u32[]{:S(2)}, u32[]{:S(2)}) %collective-permute-start.11) | collective-permute-done | bytes 131104 | tf_op jit(solution)/shard_map/ppermute | solution.py:49
  29.8 1.2 %collective-permute-start.17 = (bf16[512,128]{1,0:T(8,128)(2,1)S(1)}, bf16[512,128]{1,0:T(8,128)(2,1)S(1)}, u32[]{:S(2)}, u32[]{:S(2)}) collective-permute-start(bf16[512,128]{1,0:T(8,128)(2,1)S(1)} %get-tuple-element.118), channel_id=1, source_target_pairs={{0,5},{1,4},{2,7},{3,6},{4,1},{5,0},{6,3},{7,2},{8,13},{9,12},{10,... | collective-permute-start | bytes 393224 | tf_op jit(solution)/shard_map/ppermute | solution.py:49
  31.0 1.2 %collective-permute-start.16 = (bf16[512,128]{1,0:T(8,128)(2,1)S(1)}, bf16[512,128]{1,0:T(8,128)(2,1)S(1)}, u32[]{:S(2)}, u32[]{:S(2)}) collective-permute-start(bf16[512,128]{1,0:T(8,128)(2,1)S(1)} %get-tuple-element.118), channel_id=1, source_target_pairs={{0,6},{1,7},{2,4},{3,5},{4,2},{5,3},{6,0},{7,1},{8,14},{9,15},{10,... | collective-permute-start | bytes 393224 | tf_op jit(solution)/shard_map/ppermute | solution.py:49
  32.3 11.3 %conditional.6 = (bf16[512,128]{1,0:T(8,128)(2,1)S(1)}, bf16[512,128]{1,0:T(8,128)(2,1)S(1)}, bf16[512,128]{1,0:T(8,128)(2,1)S(1)}, bf16[512,128]{1,0:T(8,128)(2,1)S(1)}, f32[80,256]{1,0:T(8,128)S(1)}) conditional(s32[]{:T(128)} %convert_element_type.75, () %tuple.38, (bf16[512,128]{1,0:T(8,128)(2,1)S(1)}, s32[8]{0:T(128)S(1)}, s32[160]{0:T(256)S(1)}, ...), branch_computations={%region_5.6_spmd, %region_6.7_spmd} | conditional | flops 184320 | bytes 1879240 | solution.py:54
  33.3 0.8 %collective-permute-done.5 = f32[80,256]{1,0:T(8,128)S(1)} collective-permute-done((f32[80,256]{1,0:T(8,128)S(1)}, f32[80,256]{1,0:T(8,128)S(1)}, u32[]{:S(2)}, u32[]{:S(2)}) %collective-permute-start.5) | collective-permute-done | bytes 81952 | tf_op jit(solution)/shard_map/cond/branch_1_fun/ppermute | solution.py:49
  34.2 1.8 %collective-permute-start.6 = (bf16[80,256]{1,0:T(8,128)(2,1)S(1)}, bf16[80,256]{1,0:T(8,128)(2,1)S(1)}, u32[]{:S(2)}, u32[]{:S(2)}) collective-permute-start(bf16[80,256]{1,0:T(8,128)(2,1)S(1)} %get-tuple-element.141), channel_id=1, source_target_pairs={{0,8},{1,17},{2,10},{3,19},{4,12},{5,21},{6,14},{7,23},{8,0},{9,25... | collective-permute-start | bytes 122888 | tf_op jit(solution)/shard_map/cond/branch_1_fun/ppermute | solution.py:49
  36.0 3.5 %backward_0.1 = (bf16[512,128]{1,0:T(8,128)(2,1)S(1)}, bf16[512,128]{1,0:T(8,128)(2,1)S(1)}, bf16[512,128]{1,0:T(8,128)(2,1)S(1)}, bf16[512,128]{1,0:T(8,128)(2,1)S(1)}, bf16[16,128]{1,0:T(8,128)(2,1)S(1)}) custom-call(s32[8]{0:T(128)S(1)} %get-tuple-element.62.bounds_ref, s32[160]{0:T(256)S(1)} %get-tuple-element.63.row_ref, ...), custom_call_target="tpu_custom_call" | custom-call | bytes 1024 | tf_op jit(solution)/shard_map/cond/branch_1_fun/backward_0/pallas_call | solution.py:452
  39.6 1.0 %collective-permute-start.7 = (bf16[80,256]{1,0:T(8,128)(2,1)S(1)}, bf16[80,256]{1,0:T(8,128)(2,1)S(1)}, u32[]{:S(2)}, u32[]{:S(2)}) collective-permute-start(bf16[80,256]{1,0:T(8,128)(2,1)S(1)} %fusion), channel_id=1, source_target_pairs={{0,16},{1,9},{2,18},{3,11},{4,20},{5,13},{6,22},{7,15},{8,24},{9,1... | collective-permute-start | bytes 122888 | tf_op jit(solution)/shard_map/cond/branch_1_fun/ppermute | solution.py:49
  40.5 3.1 %collective-permute-done.7 = bf16[80,256]{1,0:T(8,128)(2,1)S(1)} collective-permute-done((bf16[80,256]{1,0:T(8,128)(2,1)S(1)}, bf16[80,256]{1,0:T(8,128)(2,1)S(1)}, u32[]{:S(2)}, u32[]{:S(2)}) %collective-permute-start.7) | collective-permute-done | bytes 40992 | tf_op jit(solution)/shard_map/cond/branch_1_fun/ppermute | solution.py:49
  43.8 1.4 %collective-permute-start.14 = (bf16[80,256]{1,0:T(8,128)(2,1)S(1)}, bf16[80,256]{1,0:T(8,128)(2,1)S(1)}, u32[]{:S(2)}, u32[]{:S(2)}) collective-permute-start(bf16[80,256]{1,0:T(8,128)(2,1)S(1)} %convert_element_type.77), channel_id=1, source_target_pairs={{0,2},{1,3},{2,0},{3,1},{4,6},{5,7},{6,4},{7,5},{8,10},{9,11},{10,... | collective-permute-start | bytes 122888 | tf_op jit(solution)/shard_map/ppermute | solution.py:49
  45.3 3.9 %backward_1_2_3.1 = (f32[512,128]{1,0:T(8,128)S(1)}, bf16[512,128]{1,0:T(8,128)(2,1)S(1)}, bf16[512,128]{1,0:T(8,128)(2,1)S(1)}, bf16[512,128]{1,0:T(8,128)(2,1)S(1)}) custom-call(s32[8]{0:T(128)S(1)} %convert_reduce_fusion.bounds_ref, s32[160]{0:T(256)S(1)} %get-tuple-element.143.row_ref, s32[160]{0:T(256)S(1)} %get-tuple-element.147.col_ref, ...), custom_call_target="tpu_custom_call" | custom-call | bytes 1024 | tf_op jit(solution)/shard_map/backward_1_2_3/pallas_call | solution.py:452
  49.3 1.5 %collective-permute-start.19 = (bf16[512,128]{1,0:T(8,128)(2,1)S(1)}, bf16[512,128]{1,0:T(8,128)(2,1)S(1)}, u32[]{:S(2)}, u32[]{:S(2)}) collective-permute-start(bf16[512,128]{1,0:T(8,128)(2,1)S(1)} %get-tuple-element.136), channel_id=1, source_target_pairs={{0,8},{1,17},{2,10},{3,19},{4,12},{5,21},{6,14},{7,23},{8,0},{9,25... | collective-permute-start | bytes 393224 | tf_op jit(solution)/shard_map/ppermute | solution.py:49
  51.6 1.3 %collective-permute-start.21 = (bf16[512,128]{1,0:T(8,128)(2,1)S(1)}, bf16[512,128]{1,0:T(8,128)(2,1)S(1)}, u32[]{:S(2)}, u32[]{:S(2)}) collective-permute-start(bf16[512,128]{1,0:T(8,128)(2,1)S(1)} %get-tuple-element.138), channel_id=1, source_target_pairs={{0,24},{1,25},{2,26},{3,27},{4,28},{5,29},{6,30},{7,31},{8,16},{9,... | collective-permute-start | bytes 393224 | tf_op jit(solution)/shard_map/ppermute | solution.py:49
  52.8 6.4 %conditional.7 = (f32[128,256]{1,0:T(8,128)S(1)}, f32[256]{0:T(256)S(1)}, bf16[512,256]{1,0:T(8,128)(2,1)S(1)}) conditional(s32[]{:T(128)} %convert_element_type.75, () %tuple.37, (s32[]{:T(128)}, bf16[80,256]{1,0:T(8,128)(2,1)S(1)}, f32[80,256]{1,0:T(8,128)S(1)}, bf16[512,256]{1,0:T(8,128)(2,1)S(1)}) %tuple.43), branch_computations={%region_7.8_spmd, %region_8.9_spmd} | conditional | flops 262145 | bytes 1231986 | solution.py:54
  52.8 2.8 %collective-permute-start.2 = (bf16[80,256]{1,0:T(8,128)(2,1)S(1)}, bf16[80,256]{1,0:T(8,128)(2,1)S(1)}, u32[]{:S(2)}, u32[]{:S(2)}) collective-permute-start(bf16[80,256]{1,0:T(8,128)(2,1)S(1)} %fusion.1), channel_id=1, source_target_pairs={{0,4},{1,5},{2,6},{3,7},{4,0},{5,1},{6,2},{7,3},{8,12},{9,13},{10,... | collective-permute-start | bytes 122888 | tf_op jit(solution)/shard_map/cond/branch_1_fun/ppermute | solution.py:49
  55.6 2.2 %collective-permute-done.2 = bf16[80,256]{1,0:T(8,128)(2,1)S(1)} collective-permute-done((bf16[80,256]{1,0:T(8,128)(2,1)S(1)}, bf16[80,256]{1,0:T(8,128)(2,1)S(1)}, u32[]{:S(2)}, u32[]{:S(2)}) %collective-permute-start.2) | collective-permute-done | bytes 40992 | tf_op jit(solution)/shard_map/cond/branch_1_fun/ppermute | solution.py:49
  58.0 1.2 %collective-permute-done.3 = f32[64,256]{1,0:T(8,128)S(1)} collective-permute-done((f32[64,256]{1,0:T(8,128)S(1)}, f32[64,256]{1,0:T(8,128)S(1)}, u32[]{:S(2)}, u32[]{:S(2)}) %collective-permute-start.3) | collective-permute-done | bytes 65568 | tf_op jit(solution)/shard_map/cond/branch_1_fun/ppermute | solution.py:49
  (65 shorter events, 5.8 us)
Async XLA Ops:
  1.7 8.9 %collective-permute-start.10 = (bf16[512,128]{1,0:T(8,128)(2,1)S(1)}, bf16[512,128]{1,0:T(8,128)(2,1)S(1)}, u32[]{:S(2)}, u32[]{:S(2)}) collective-permute-start(bf16[512,128]{1,0:T(8,128)(2,1)S(1)} %get-tuple-element.114.earlier_ref.refs_0_.refs_4_), channel_id=1, source_target_pairs={{0,24},{1,25},{2,26},{3,27},{4,28},{5,29},{6,30},{7,31},{8,16},{9,... | collective-permute-start | bytes 393224 | tf_op jit(solution)/shard_map/ppermute | solution.py:49
  5.7 6.3 %collective-permute-start.9 = (bf16[512,128]{1,0:T(8,128)(2,1)S(1)}, bf16[512,128]{1,0:T(8,128)(2,1)S(1)}, u32[]{:S(2)}, u32[]{:S(2)}) collective-permute-start(bf16[512,128]{1,0:T(8,128)(2,1)S(1)} %get-tuple-element.114.earlier_ref.refs_0_.refs_4_), channel_id=1, source_target_pairs={{0,16},{1,9},{2,18},{3,11},{4,20},{5,13},{6,22},{7,15},{8,24},{9,1... | collective-permute-start | bytes 393224 | tf_op jit(solution)/shard_map/ppermute | solution.py:49
  6.2 6.0 %collective-permute-start.8 = (bf16[512,128]{1,0:T(8,128)(2,1)S(1)}, bf16[512,128]{1,0:T(8,128)(2,1)S(1)}, u32[]{:S(2)}, u32[]{:S(2)}) collective-permute-start(bf16[512,128]{1,0:T(8,128)(2,1)S(1)} %get-tuple-element.114.earlier_ref.refs_0_.refs_4_), channel_id=1, source_target_pairs={{0,8},{1,17},{2,10},{3,19},{4,12},{5,21},{6,14},{7,23},{8,0},{9,25... | collective-permute-start | bytes 393224 | tf_op jit(solution)/shard_map/ppermute | solution.py:49
  13.2 12.5 %collective-permute-start.13 = (bf16[512,128]{1,0:T(8,128)(2,1)S(1)}, bf16[512,128]{1,0:T(8,128)(2,1)S(1)}, u32[]{:S(2)}, u32[]{:S(2)}) collective-permute-start(bf16[512,128]{1,0:T(8,128)(2,1)S(1)} %forward_3.1.earlier_ref), channel_id=1, source_target_pairs={{0,5},{1,4},{2,7},{3,6},{4,1},{5,0},{6,3},{7,2},{8,13},{9,12},{10,... | collective-permute-start | bytes 393224 | tf_op jit(solution)/shard_map/ppermute | solution.py:49
  17.2 12.1 %copy-start = (bf16[512,256]{1,0:T(8,128)(2,1)S(1)}, bf16[512,256]{1,0:T(8,128)(2,1)}, u32[]{:S(2)}) copy-start(bf16[512,256]{1,0:T(8,128)(2,1)} %refs_8_.1) | copy-start | bytes 786436
  17.2 12.1 %copy-start.1 = (bf16[128,256]{1,0:T(8,128)(2,1)S(1)}, bf16[128,256]{1,0:T(8,128)(2,1)}, u32[]{:S(2)}) copy-start(bf16[128,256]{1,0:T(8,128)(2,1)} %refs_6_.1) | copy-start | bytes 196612
  17.3 12.1 %copy-start.2 = (f32[256]{0:T(256)S(1)}, f32[256]{0:T(256)}, u32[]{:S(2)}) copy-start(f32[256]{0:T(256)} %param.24) | copy-start | bytes 3076
  17.3 2.5 %collective-permute-start = (bf16[1024,128]{1,0:T(8,128)(2,1)S(1)}, bf16[1024,128]{1,0:T(8,128)(2,1)S(1)}, u32[]{:S(2)}, u32[]{:S(2)}) collective-permute-start(bf16[1024,128]{1,0:T(8,128)(2,1)S(1)} %get-tuple-element.50), channel_id=1, source_target_pairs={{0,1},{1,0},{2,3},{3,2},{4,5},{5,4},{6,7},{7,6},{8,9},{9,8},{10,11... | collective-permute-start | bytes 786440 | tf_op jit(solution)/shard_map/cond/branch_1_fun/ppermute | solution.py:49
  19.9 8.2 %collective-permute-start.12 = (bf16[512,128]{1,0:T(8,128)(2,1)S(1)}, bf16[512,128]{1,0:T(8,128)(2,1)S(1)}, u32[]{:S(2)}, u32[]{:S(2)}) collective-permute-start(bf16[512,128]{1,0:T(8,128)(2,1)S(1)} %get-tuple-element.117), channel_id=1, source_target_pairs={{0,6},{1,7},{2,4},{3,5},{4,2},{5,3},{6,0},{7,1},{8,14},{9,15},{10,... | collective-permute-start | bytes 393224 | tf_op jit(solution)/shard_map/ppermute | solution.py:49
  21.0 8.3 %collective-permute-start.11 = (bf16[512,128]{1,0:T(8,128)(2,1)S(1)}, bf16[512,128]{1,0:T(8,128)(2,1)S(1)}, u32[]{:S(2)}, u32[]{:S(2)}) collective-permute-start(bf16[512,128]{1,0:T(8,128)(2,1)S(1)} %get-tuple-element.116), channel_id=1, source_target_pairs={{0,2},{1,3},{2,0},{3,1},{4,6},{5,7},{6,4},{7,5},{8,10},{9,11},{10,... | collective-permute-start | bytes 393224 | tf_op jit(solution)/shard_map/ppermute | solution.py:49
  24.2 1.4 %collective-permute-start.1 = (bf16[512,128]{1,0:T(8,128)(2,1)S(1)}, bf16[512,128]{1,0:T(8,128)(2,1)S(1)}, u32[]{:S(2)}, u32[]{:S(2)}) collective-permute-start(bf16[512,128]{1,0:T(8,128)(2,1)S(1)} %get-tuple-element.61), channel_id=1, source_target_pairs={{0,1},{1,0},{2,3},{3,2},{4,5},{5,4},{6,7},{7,6},{8,9},{9,8},{10,11... | collective-permute-start | bytes 393224 | tf_op jit(solution)/shard_map/cond/branch_1_fun/ppermute | solution.py:49
  29.8 13.8 %collective-permute-start.17 = (bf16[512,128]{1,0:T(8,128)(2,1)S(1)}, bf16[512,128]{1,0:T(8,128)(2,1)S(1)}, u32[]{:S(2)}, u32[]{:S(2)}) collective-permute-start(bf16[512,128]{1,0:T(8,128)(2,1)S(1)} %get-tuple-element.118), channel_id=1, source_target_pairs={{0,5},{1,4},{2,7},{3,6},{4,1},{5,0},{6,3},{7,2},{8,13},{9,12},{10,... | collective-permute-start | bytes 393224 | tf_op jit(solution)/shard_map/ppermute | solution.py:49
  31.0 12.7 %collective-permute-start.16 = (bf16[512,128]{1,0:T(8,128)(2,1)S(1)}, bf16[512,128]{1,0:T(8,128)(2,1)S(1)}, u32[]{:S(2)}, u32[]{:S(2)}) collective-permute-start(bf16[512,128]{1,0:T(8,128)(2,1)S(1)} %get-tuple-element.118), channel_id=1, source_target_pairs={{0,6},{1,7},{2,4},{3,5},{4,2},{5,3},{6,0},{7,1},{8,14},{9,15},{10,... | collective-permute-start | bytes 393224 | tf_op jit(solution)/shard_map/ppermute | solution.py:49
  32.2 11.5 %collective-permute-start.15 = (bf16[512,128]{1,0:T(8,128)(2,1)S(1)}, bf16[512,128]{1,0:T(8,128)(2,1)S(1)}, u32[]{:S(2)}, u32[]{:S(2)}) collective-permute-start(bf16[512,128]{1,0:T(8,128)(2,1)S(1)} %get-tuple-element.118), channel_id=1, source_target_pairs={{0,2},{1,3},{2,0},{3,1},{4,6},{5,7},{6,4},{7,5},{8,10},{9,11},{10,... | collective-permute-start | bytes 393224 | tf_op jit(solution)/shard_map/ppermute | solution.py:49
  32.5 1.6 %collective-permute-start.5 = (f32[80,256]{1,0:T(8,128)S(1)}, f32[80,256]{1,0:T(8,128)S(1)}, u32[]{:S(2)}, u32[]{:S(2)}) collective-permute-start(f32[80,256]{1,0:T(8,128)S(1)} %get-tuple-element.75), channel_id=1, source_target_pairs={{0,1},{1,0},{2,3},{3,2},{4,5},{5,4},{6,7},{7,6},{8,9},{9,8},{10,11... | collective-permute-start | bytes 245768 | tf_op jit(solution)/shard_map/cond/branch_1_fun/ppermute | solution.py:49
  33.2 2.8 %collective-permute-start.4 = (bf16[512,128]{1,0:T(8,128)(2,1)S(1)}, bf16[512,128]{1,0:T(8,128)(2,1)S(1)}, u32[]{:S(2)}, u32[]{:S(2)}) collective-permute-start(bf16[512,128]{1,0:T(8,128)(2,1)S(1)} %get-tuple-element.66.refs_0_), channel_id=1, source_target_pairs={{0,1},{1,0},{2,3},{3,2},{4,5},{5,4},{6,7},{7,6},{8,9},{9,8},{10,11... | collective-permute-start | bytes 393224 | tf_op jit(solution)/shard_map/cond/branch_1_fun/ppermute | solution.py:49
  34.2 5.4 %collective-permute-start.6 = (bf16[80,256]{1,0:T(8,128)(2,1)S(1)}, bf16[80,256]{1,0:T(8,128)(2,1)S(1)}, u32[]{:S(2)}, u32[]{:S(2)}) collective-permute-start(bf16[80,256]{1,0:T(8,128)(2,1)S(1)} %get-tuple-element.141), channel_id=1, source_target_pairs={{0,8},{1,17},{2,10},{3,19},{4,12},{5,21},{6,14},{7,23},{8,0},{9,25... | collective-permute-start | bytes 122888 | tf_op jit(solution)/shard_map/cond/branch_1_fun/ppermute | solution.py:49
  39.6 4.1 %collective-permute-start.7 = (bf16[80,256]{1,0:T(8,128)(2,1)S(1)}, bf16[80,256]{1,0:T(8,128)(2,1)S(1)}, u32[]{:S(2)}, u32[]{:S(2)}) collective-permute-start(bf16[80,256]{1,0:T(8,128)(2,1)S(1)} %fusion), channel_id=1, source_target_pairs={{0,16},{1,9},{2,18},{3,11},{4,20},{5,13},{6,22},{7,15},{8,24},{9,1... | collective-permute-start | bytes 122888 | tf_op jit(solution)/shard_map/cond/branch_1_fun/ppermute | solution.py:49
  43.7 1.6 %collective-permute-start.18 = (bf16[1024,128]{1,0:T(8,128)(2,1)S(1)}, bf16[1024,128]{1,0:T(8,128)(2,1)S(1)}, u32[]{:S(2)}, u32[]{:S(2)}) collective-permute-start(bf16[1024,128]{1,0:T(8,128)(2,1)S(1)} %constant_dynamic-update-slice_fusion.refs_0_), channel_id=1, source_target_pairs={{0,1},{1,0},{2,3},{3,2},{4,5},{5,4},{6,7},{7,6},{8,9},{9,8},{10,11... | collective-permute-start | bytes 786440 | tf_op jit(solution)/shard_map/ppermute | solution.py:49
  43.8 5.4 %collective-permute-start.14 = (bf16[80,256]{1,0:T(8,128)(2,1)S(1)}, bf16[80,256]{1,0:T(8,128)(2,1)S(1)}, u32[]{:S(2)}, u32[]{:S(2)}) collective-permute-start(bf16[80,256]{1,0:T(8,128)(2,1)S(1)} %convert_element_type.77), channel_id=1, source_target_pairs={{0,2},{1,3},{2,0},{3,1},{4,6},{5,7},{6,4},{7,5},{8,10},{9,11},{10,... | collective-permute-start | bytes 122888 | tf_op jit(solution)/shard_map/ppermute | solution.py:49
  49.3 9.9 %collective-permute-start.19 = (bf16[512,128]{1,0:T(8,128)(2,1)S(1)}, bf16[512,128]{1,0:T(8,128)(2,1)S(1)}, u32[]{:S(2)}, u32[]{:S(2)}) collective-permute-start(bf16[512,128]{1,0:T(8,128)(2,1)S(1)} %get-tuple-element.136), channel_id=1, source_target_pairs={{0,8},{1,17},{2,10},{3,19},{4,12},{5,21},{6,14},{7,23},{8,0},{9,25... | collective-permute-start | bytes 393224 | tf_op jit(solution)/shard_map/ppermute | solution.py:49
  50.8 8.4 %collective-permute-start.20 = (bf16[512,128]{1,0:T(8,128)(2,1)S(1)}, bf16[512,128]{1,0:T(8,128)(2,1)S(1)}, u32[]{:S(2)}, u32[]{:S(2)}) collective-permute-start(bf16[512,128]{1,0:T(8,128)(2,1)S(1)} %get-tuple-element.137), channel_id=1, source_target_pairs={{0,16},{1,9},{2,18},{3,11},{4,20},{5,13},{6,22},{7,15},{8,24},{9,1... | collective-permute-start | bytes 393224 | tf_op jit(solution)/shard_map/ppermute | solution.py:49
  51.6 7.7 %collective-permute-start.21 = (bf16[512,128]{1,0:T(8,128)(2,1)S(1)}, bf16[512,128]{1,0:T(8,128)(2,1)S(1)}, u32[]{:S(2)}, u32[]{:S(2)}) collective-permute-start(bf16[512,128]{1,0:T(8,128)(2,1)S(1)} %get-tuple-element.138), channel_id=1, source_target_pairs={{0,24},{1,25},{2,26},{3,27},{4,28},{5,29},{6,30},{7,31},{8,16},{9,... | collective-permute-start | bytes 393224 | tf_op jit(solution)/shard_map/ppermute | solution.py:49
  52.8 5.0 %collective-permute-start.2 = (bf16[80,256]{1,0:T(8,128)(2,1)S(1)}, bf16[80,256]{1,0:T(8,128)(2,1)S(1)}, u32[]{:S(2)}, u32[]{:S(2)}) collective-permute-start(bf16[80,256]{1,0:T(8,128)(2,1)S(1)} %fusion.1), channel_id=1, source_target_pairs={{0,4},{1,5},{2,6},{3,7},{4,0},{5,1},{6,2},{7,3},{8,12},{9,13},{10,... | collective-permute-start | bytes 122888 | tf_op jit(solution)/shard_map/cond/branch_1_fun/ppermute | solution.py:49
  57.8 1.3 %collective-permute-start.3 = (f32[64,256]{1,0:T(8,128)S(1)}, f32[64,256]{1,0:T(8,128)S(1)}, u32[]{:S(2)}, u32[]{:S(2)}) collective-permute-start(f32[64,256]{1,0:T(8,128)S(1)} %slice.24), channel_id=1, source_target_pairs={{0,1},{1,0},{2,3},{3,2},{4,5},{5,4},{6,7},{7,6},{8,9},{9,8},{10,11... | collective-permute-start | bytes 196616 | tf_op jit(solution)/shard_map/cond/branch_1_fun/ppermute | solution.py:49
  59.2 0.8 %copy-start.3 = (bf16[512,256]{1,0:T(8,128)(2,1)}, bf16[512,256]{1,0:T(8,128)(2,1)S(1)}, u32[]{:S(2)}) copy-start(bf16[512,256]{1,0:T(8,128)(2,1)S(1)} %get-tuple-element.109) | copy-start | bytes 786436
  59.2 0.8 %copy-start.4 = (f32[128,256]{1,0:T(8,128)}, f32[128,256]{1,0:T(8,128)S(1)}, u32[]{:S(2)}) copy-start(f32[128,256]{1,0:T(8,128)S(1)} %get-tuple-element.111) | copy-start | bytes 393220
  59.2 0.8 %copy-start.5 = (f32[256]{0:T(256)}, f32[256]{0:T(256)S(1)}, u32[]{:S(2)}) copy-start(f32[256]{0:T(256)S(1)} %get-tuple-element.112) | copy-start | bytes 3076

commit v7 on v6

--- a/solution.py
+++ b/solution.py
@@ -148,6 +148,16 @@
     copy = pltpu.make_async_copy(value_ref, out_ref, sem)
     copy.start()
     copy.wait()
+
+
+def scalars_kernel(*refs):
+    refs, sems = refs[:-1], refs[-1]
+    count = len(refs) // 2
+    copies = [pltpu.make_async_copy(refs[n], refs[count + n], sems.at[n]) for n in range(count)]
+    for copy in copies:
+        copy.start()
+    for copy in copies:
+        copy.wait()
 
 
 def stage_kernel(w_ref, earlier_ref, out_ref, sem):
@@ -347,6 +357,16 @@
     pair_ids = jnp.concatenate([pair_ids, pair_ids + 1])
     bounds = jnp.sum(used & (group // CORES < pair_ids[:, None]), axis=1).astype(jnp.int32)
     row_place, col_place = row_place.astype(jnp.int32), col_place.astype(jnp.int32)
+    bounds, row_place, col_place = pl.pallas_call(
+        scalars_kernel,
+        out_shape=[pltpu.SMEM(value.shape, jnp.int32) for value in (bounds, row_place, col_place)],
+        in_specs=[ANY] * 3,
+        out_specs=[SMEM] * 3,
+        scratch_shapes=[pltpu.SemaphoreType.DMA((3,))],
+        compiler_params=params(16),
+        cost_estimate=SMALL,
+        name="scalars",
+    )(bounds, row_place, col_place)
 
     scaled, norm_wide = pl.pallas_call(
         prepare_kernel,

time: 60.6 us -> 59.3 us (0.979)
  Pallas kernels: 18.1 us -> 14.1 us
  starting transfers between devices: 22.9 us -> 26.3 us
  waiting for transfers between devices: 15.2 us -> 14.4 us
    ppermute x22, starting transfers between devices: 22.9 us -> 26.3 us  [move(): return lax.ppermute(value, BOTH, pairs)]
    pallas_call x3, Pallas kernels: 6.37 us -> 3.97 us  [forward(): pl.pallas_call(functools.partial(forward_kernel, places, unroll, stream),...]
    pallas_call x2, Pallas kernels: 7.41 us -> 5.19 us  [backward(): pl.pallas_call(functools.partial(backward_kernel, places, unroll), out_sh...]
    ppermute x22, waiting for transfers between devices: 15.2 us -> 14.4 us  [move(): return lax.ppermute(value, BOTH, pairs)]
  transfers between devices with their start and end apart: 22 -> 22, of which waited for: 11 -> 11; matrix products, arithmetic and copies ran while one was open for 2% -> 2% of each run, Pallas kernels for 26% -> 21%
where the time goes in v7:
time: 59.3 us; the launch traced here: 58.6 us
  starting transfers between devices  26.3 us (44%)
  waiting for transfers between devices  14.4 us (24%)
  Pallas kernels  14.1 us (24%)
  other arithmetic  1.95 us (3%)
  between operations  1.54 us (3%)
    ppermute x22, starting transfers between devices, move(): return lax.ppermute(value, BOTH, pairs)  26.3 us
    ppermute x22, waiting for transfers between devices, move(): return lax.ppermute(value, BOTH, pairs)  14.4 us
    pallas_call x2, Pallas kernels, backward(): pl.pallas_call(functools.partial(backward_kernel, places, unroll), out_sh...  5.19 us
    pallas_call x3, Pallas kernels, forward(): pl.pallas_call(functools.partial(forward_kernel, places, unroll, stream),...  3.97 us
    pallas_call x1, Pallas kernels, stage(): pl.pallas_call(stage_kernel, out_shape=jax.ShapeDtypeStruct((slot_total,...  2.5 us
  transfers between devices with their start and end apart: 22, of which 11 were waited for; matrix products, arithmetic and copies ran while one was open for 2% of the time, Pallas kernels for 21%

profile of v7, /device:TPU:0, one launch (start us, length us, event | category | flops | bytes accessed | tf_op | source)
XLA Modules:
  0.0 58.6 jit_solution(1148028500860346928)
XLA Ops:
  0.6 1.1 %prepare.1 = (bf16[512,128]{1,0:T(8,128)(2,1)S(1)}, f32[512,128]{1,0:T(8,128)S(1)}) custom-call(s32[4,128]{1,0:T(4,128)} %bitcast.18, bf16[512,128]{1,0:T(8,128)(2,1)} %features_hbm.1), custom_call_target="tpu_custom_call" | custom-call | bytes 1024 | tf_op jit(solution)/shard_map/prepare/pallas_call | solution.py:371
  1.7 4.0 %collective-permute-start.10 = (bf16[512,128]{1,0:T(8,128)(2,1)S(1)}, bf16[512,128]{1,0:T(8,128)(2,1)S(1)}, u32[]{:S(2)}, u32[]{:S(2)}) collective-permute-start(bf16[512,128]{1,0:T(8,128)(2,1)S(1)} %get-tuple-element.120.earlier_ref.refs_0_.refs_4_), channel_id=1, source_target_pairs={{0,24},{1,25},{2,26},{3,27},{4,28},{5,29},{6,30},{7,31},{8,16},{9,... | collective-permute-start | bytes 393224 | tf_op jit(solution)/shard_map/ppermute | solution.py:49
  7.9 2.5 %stage_tiles.1.w_ref = bf16[160,128,128]{2,1,0:T(8,128)(2,1)S(1)} custom-call(bf16[160,128,128]{2,1,0:T(8,128)(2,1)} %bitcast.14, bf16[512,128]{1,0:T(8,128)(2,1)S(1)} %get-tuple-element.120.earlier_ref.refs_0_.refs_4_), custom_call_target="tpu_custom_call" | custom-call | bytes 10485760 | tf_op jit(solution)/shard_map/stage_tiles/pallas_call | solution.py:390
  11.2 0.8 %collective-permute-done.9.refs_2_ = bf16[512,128]{1,0:T(8,128)(2,1)S(1)} collective-permute-done((bf16[512,128]{1,0:T(8,128)(2,1)S(1)}, bf16[512,128]{1,0:T(8,128)(2,1)S(1)}, u32[]{:S(2)}, u32[]{:S(2)}) %collective-permute-start.9) | collective-permute-done | bytes 131104 | tf_op jit(solution)/shard_map/ppermute | solution.py:49
  12.6 1.8 %collective-permute-start.13 = (bf16[512,128]{1,0:T(8,128)(2,1)S(1)}, bf16[512,128]{1,0:T(8,128)(2,1)S(1)}, u32[]{:S(2)}, u32[]{:S(2)}) collective-permute-start(bf16[512,128]{1,0:T(8,128)(2,1)S(1)} %forward_3.1.earlier_ref), channel_id=1, source_target_pairs={{0,5},{1,4},{2,7},{3,6},{4,1},{5,0},{6,3},{7,2},{8,13},{9,12},{10,... | collective-permute-start | bytes 393224 | tf_op jit(solution)/shard_map/ppermute | solution.py:49
  14.4 1.4 %forward_1_2.1 = (bf16[1024,128]{1,0:T(8,128)(2,1)S(1)}, bf16[1024,128]{1,0:T(8,128)(2,1)S(1)}) custom-call(bf16[512,128]{1,0:T(8,128)(2,1)S(1)} %forward_3.1.earlier_ref, s32[8]{0:T(128)S(4)} %get-tuple-element.117.bounds_ref, s32[160]{0:T(256)S(4)} %get-tuple-element.118.row_ref, s32[160]{0:T(256)S(4)} %get-tuple-element.119.col_ref, ...), custom_call_target="tpu_custom_call" | custom-call | bytes 1024 | tf_op jit(solution)/shard_map/forward_1_2/pallas_call | solution.py:412
  15.8 2.6 %conditional.4 = (bf16[512,128]{1,0:T(8,128)(2,1)S(1)}, bf16[512,128]{1,0:T(8,128)(2,1)S(1)}, bf16[16,128]{1,0:T(8,128)(2,1)S(1)}) conditional(s32[]{:T(128)} %convert_element_type.75, () %tuple.40, (bf16[1024,128]{1,0:T(8,128)(2,1)S(1)}, bf16[1024,128]{1,0:T(8,128)(2,1)S(1)}) %forward_1_2.1), branch_computations={%region_1.2_spmd, %region_2.3_spmd} | conditional | flops 524288 | bytes 1843264 | solution.py:54
  15.8 1.4 %collective-permute-start = (bf16[1024,128]{1,0:T(8,128)(2,1)S(1)}, bf16[1024,128]{1,0:T(8,128)(2,1)S(1)}, u32[]{:S(2)}, u32[]{:S(2)}) collective-permute-start(bf16[1024,128]{1,0:T(8,128)(2,1)S(1)} %get-tuple-element.50), channel_id=1, source_target_pairs={{0,1},{1,0},{2,3},{3,2},{4,5},{5,4},{6,7},{7,6},{8,9},{9,8},{10,11... | collective-permute-start | bytes 786440 | tf_op jit(solution)/shard_map/cond/branch_1_fun/ppermute | solution.py:49
  17.2 1.2 %collective-permute-done = bf16[1024,128]{1,0:T(8,128)(2,1)S(1)} collective-permute-done((bf16[1024,128]{1,0:T(8,128)(2,1)S(1)}, bf16[1024,128]{1,0:T(8,128)(2,1)S(1)}, u32[]{:S(2)}, u32[]{:S(2)}) %collective-permute-start) | collective-permute-done | bytes 262176 | tf_op jit(solution)/shard_map/cond/branch_1_fun/ppermute | solution.py:49
  18.4 1.4 %collective-permute-start.12 = (bf16[512,128]{1,0:T(8,128)(2,1)S(1)}, bf16[512,128]{1,0:T(8,128)(2,1)S(1)}, u32[]{:S(2)}, u32[]{:S(2)}) collective-permute-start(bf16[512,128]{1,0:T(8,128)(2,1)S(1)} %get-tuple-element.123), channel_id=1, source_target_pairs={{0,6},{1,7},{2,4},{3,5},{4,2},{5,3},{6,0},{7,1},{8,14},{9,15},{10,... | collective-permute-start | bytes 393224 | tf_op jit(solution)/shard_map/ppermute | solution.py:49
  19.9 3.7 %conditional.5 = (bf16[512,128]{1,0:T(8,128)(2,1)S(1)}) conditional(s32[]{:T(128)} %convert_element_type.75, () %tuple.39, (bf16[16,128]{1,0:T(8,128)(2,1)S(1)}, s32[8]{0:T(128)S(4)}, s32[160]{0:T(256)S(4)}, s32[160]{0:T(256)S(4)}, bf16[160,128,128]{2,1,0:T(8,128)(2,1)}, /*index=5*/bf16[512,128]{1,0:T(8,128)(2,1)S(1)}, ...), branch_computations={%region_3.4_spmd, %region_4.5_spmd} | conditional | flops 262144 | bytes 918576 | solution.py:54
  19.9 2.2 %forward_0.1 = (bf16[512,128]{1,0:T(8,128)(2,1)S(1)}, bf16[512,128]{1,0:T(8,128)(2,1)S(1)}) custom-call(bf16[16,128]{1,0:T(8,128)(2,1)S(1)} %get-tuple-element.51.earlier_ref, s32[8]{0:T(128)S(4)} %get-tuple-element.52.bounds_ref, s32[160]{0:T(256)S(4)} %get-tuple-element.53.row_ref, s32[160]{0:T(256)S(4)} %get-tuple-element.54.col_ref, ...), custom_call_target="tpu_custom_call" | custom-call | bytes 1024 | tf_op jit(solution)/shard_map/cond/branch_1_fun/forward_0/pallas_call | solution.py:412
  22.2 1.3 %collective-permute-done.1 = bf16[512,128]{1,0:T(8,128)(2,1)S(1)} collective-permute-done((bf16[512,128]{1,0:T(8,128)(2,1)S(1)}, bf16[512,128]{1,0:T(8,128)(2,1)S(1)}, u32[]{:S(2)}, u32[]{:S(2)}) %collective-permute-start.1) | collective-permute-done | bytes 131104 | tf_op jit(solution)/shard_map/cond/branch_1_fun/ppermute | solution.py:49
  23.6 3.1 %collective-permute-done.12.refs_0_ = bf16[512,128]{1,0:T(8,128)(2,1)S(1)} collective-permute-done((bf16[512,128]{1,0:T(8,128)(2,1)S(1)}, bf16[512,128]{1,0:T(8,128)(2,1)S(1)}, u32[]{:S(2)}, u32[]{:S(2)}) %collective-permute-start.12) | collective-permute-done | bytes 131104 | tf_op jit(solution)/shard_map/ppermute | solution.py:49
  26.7 1.2 %collective-permute-done.11.refs_0_ = bf16[512,128]{1,0:T(8,128)(2,1)S(1)} collective-permute-done((bf16[512,128]{1,0:T(8,128)(2,1)S(1)}, bf16[512,128]{1,0:T(8,128)(2,1)S(1)}, u32[]{:S(2)}, u32[]{:S(2)}) %collective-permute-start.11) | collective-permute-done | bytes 131104 | tf_op jit(solution)/shard_map/ppermute | solution.py:49
  28.4 2.0 %collective-permute-start.17 = (bf16[512,128]{1,0:T(8,128)(2,1)S(1)}, bf16[512,128]{1,0:T(8,128)(2,1)S(1)}, u32[]{:S(2)}, u32[]{:S(2)}) collective-permute-start(bf16[512,128]{1,0:T(8,128)(2,1)S(1)} %get-tuple-element.124), channel_id=1, source_target_pairs={{0,5},{1,4},{2,7},{3,6},{4,1},{5,0},{6,3},{7,2},{8,13},{9,12},{10,... | collective-permute-start | bytes 393224 | tf_op jit(solution)/shard_map/ppermute | solution.py:49
  30.4 1.2 %collective-permute-start.16 = (bf16[512,128]{1,0:T(8,128)(2,1)S(1)}, bf16[512,128]{1,0:T(8,128)(2,1)S(1)}, u32[]{:S(2)}, u32[]{:S(2)}) collective-permute-start(bf16[512,128]{1,0:T(8,128)(2,1)S(1)} %get-tuple-element.124), channel_id=1, source_target_pairs={{0,6},{1,7},{2,4},{3,5},{4,2},{5,3},{6,0},{7,1},{8,14},{9,15},{10,... | collective-permute-start | bytes 393224 | tf_op jit(solution)/shard_map/ppermute | solution.py:49
  31.7 9.8 %conditional.6 = (bf16[512,128]{1,0:T(8,128)(2,1)S(1)}, bf16[512,128]{1,0:T(8,128)(2,1)S(1)}, bf16[512,128]{1,0:T(8,128)(2,1)S(1)}, bf16[512,128]{1,0:T(8,128)(2,1)S(1)}, f32[80,256]{1,0:T(8,128)S(1)}) conditional(s32[]{:T(128)} %convert_element_type.75, () %tuple.38, (bf16[512,128]{1,0:T(8,128)(2,1)S(1)}, s32[8]{0:T(128)S(4)}, s32[160]{0:T(256)S(4)}, ...), branch_computations={%region_5.6_spmd, %region_6.7_spmd} | conditional | flops 184320 | bytes 1879240 | solution.py:54
  32.6 0.8 %collective-permute-done.5 = f32[80,256]{1,0:T(8,128)S(1)} collective-permute-done((f32[80,256]{1,0:T(8,128)S(1)}, f32[80,256]{1,0:T(8,128)S(1)}, u32[]{:S(2)}, u32[]{:S(2)}) %collective-permute-start.5) | collective-permute-done | bytes 81952 | tf_op jit(solution)/shard_map/cond/branch_1_fun/ppermute | solution.py:49
  33.3 1.8 %collective-permute-start.6 = (bf16[80,256]{1,0:T(8,128)(2,1)S(1)}, bf16[80,256]{1,0:T(8,128)(2,1)S(1)}, u32[]{:S(2)}, u32[]{:S(2)}) collective-permute-start(bf16[80,256]{1,0:T(8,128)(2,1)S(1)} %get-tuple-element.147), channel_id=1, source_target_pairs={{0,8},{1,17},{2,10},{3,19},{4,12},{5,21},{6,14},{7,23},{8,0},{9,25... | collective-permute-start | bytes 122888 | tf_op jit(solution)/shard_map/cond/branch_1_fun/ppermute | solution.py:49
  35.2 2.2 %backward_0.1 = (bf16[512,128]{1,0:T(8,128)(2,1)S(1)}, bf16[512,128]{1,0:T(8,128)(2,1)S(1)}, bf16[512,128]{1,0:T(8,128)(2,1)S(1)}, bf16[512,128]{1,0:T(8,128)(2,1)S(1)}, bf16[16,128]{1,0:T(8,128)(2,1)S(1)}) custom-call(s32[8]{0:T(128)S(4)} %get-tuple-element.62.bounds_ref, s32[160]{0:T(256)S(4)} %get-tuple-element.63.row_ref, ...), custom_call_target="tpu_custom_call" | custom-call | bytes 1024 | tf_op jit(solution)/shard_map/cond/branch_1_fun/backward_0/pallas_call | solution.py:472
  37.5 1.9 %collective-permute-start.7 = (bf16[80,256]{1,0:T(8,128)(2,1)S(1)}, bf16[80,256]{1,0:T(8,128)(2,1)S(1)}, u32[]{:S(2)}, u32[]{:S(2)}) collective-permute-start(bf16[80,256]{1,0:T(8,128)(2,1)S(1)} %fusion), channel_id=1, source_target_pairs={{0,16},{1,9},{2,18},{3,11},{4,20},{5,13},{6,22},{7,15},{8,24},{9,1... | collective-permute-start | bytes 122888 | tf_op jit(solution)/shard_map/cond/branch_1_fun/ppermute | solution.py:49
  39.4 2.2 %collective-permute-done.7 = bf16[80,256]{1,0:T(8,128)(2,1)S(1)} collective-permute-done((bf16[80,256]{1,0:T(8,128)(2,1)S(1)}, bf16[80,256]{1,0:T(8,128)(2,1)S(1)}, u32[]{:S(2)}, u32[]{:S(2)}) %collective-permute-start.7) | collective-permute-done | bytes 40992 | tf_op jit(solution)/shard_map/cond/branch_1_fun/ppermute | solution.py:49
  42.2 2.0 %collective-permute-start.14 = (bf16[80,256]{1,0:T(8,128)(2,1)S(1)}, bf16[80,256]{1,0:T(8,128)(2,1)S(1)}, u32[]{:S(2)}, u32[]{:S(2)}) collective-permute-start(bf16[80,256]{1,0:T(8,128)(2,1)S(1)} %convert_element_type.77), channel_id=1, source_target_pairs={{0,2},{1,3},{2,0},{3,1},{4,6},{5,7},{6,4},{7,5},{8,10},{9,11},{10,... | collective-permute-start | bytes 122888 | tf_op jit(solution)/shard_map/ppermute | solution.py:49
  44.2 3.0 %backward_1_2_3.1 = (f32[512,128]{1,0:T(8,128)S(1)}, bf16[512,128]{1,0:T(8,128)(2,1)S(1)}, bf16[512,128]{1,0:T(8,128)(2,1)S(1)}, bf16[512,128]{1,0:T(8,128)(2,1)S(1)}) custom-call(s32[8]{0:T(128)S(4)} %get-tuple-element.117.bounds_ref, s32[160]{0:T(256)S(4)} %get-tuple-element.118.row_ref, s32[160]{0:T(256)S(4)} %get-tuple-element.119.col_ref, ...), custom_call_target="tpu_custom_call" | custom-call | bytes 1024 | tf_op jit(solution)/shard_map/backward_1_2_3/pallas_call | solution.py:472
  47.2 2.6 %collective-permute-start.19 = (bf16[512,128]{1,0:T(8,128)(2,1)S(1)}, bf16[512,128]{1,0:T(8,128)(2,1)S(1)}, u32[]{:S(2)}, u32[]{:S(2)}) collective-permute-start(bf16[512,128]{1,0:T(8,128)(2,1)S(1)} %get-tuple-element.142), channel_id=1, source_target_pairs={{0,8},{1,17},{2,10},{3,19},{4,12},{5,21},{6,14},{7,23},{8,0},{9,25... | collective-permute-start | bytes 393224 | tf_op jit(solution)/shard_map/ppermute | solution.py:49
  49.8 0.8 %collective-permute-start.20 = (bf16[512,128]{1,0:T(8,128)(2,1)S(1)}, bf16[512,128]{1,0:T(8,128)(2,1)S(1)}, u32[]{:S(2)}, u32[]{:S(2)}) collective-permute-start(bf16[512,128]{1,0:T(8,128)(2,1)S(1)} %get-tuple-element.143), channel_id=1, source_target_pairs={{0,16},{1,9},{2,18},{3,11},{4,20},{5,13},{6,22},{7,15},{8,24},{9,1... | collective-permute-start | bytes 393224 | tf_op jit(solution)/shard_map/ppermute | solution.py:49
  51.4 6.4 %conditional.7 = (f32[128,256]{1,0:T(8,128)S(1)}, f32[256]{0:T(256)S(1)}, bf16[512,256]{1,0:T(8,128)(2,1)S(1)}) conditional(s32[]{:T(128)} %convert_element_type.75, () %tuple.37, (s32[]{:T(128)}, bf16[80,256]{1,0:T(8,128)(2,1)S(1)}, f32[80,256]{1,0:T(8,128)S(1)}, bf16[512,256]{1,0:T(8,128)(2,1)S(1)}) %tuple.43), branch_computations={%region_7.8_spmd, %region_8.9_spmd} | conditional | flops 262145 | bytes 1231986 | solution.py:54
  51.4 3.1 %collective-permute-start.2 = (bf16[80,256]{1,0:T(8,128)(2,1)S(1)}, bf16[80,256]{1,0:T(8,128)(2,1)S(1)}, u32[]{:S(2)}, u32[]{:S(2)}) collective-permute-start(bf16[80,256]{1,0:T(8,128)(2,1)S(1)} %fusion.1), channel_id=1, source_target_pairs={{0,4},{1,5},{2,6},{3,7},{4,0},{5,1},{6,2},{7,3},{8,12},{9,13},{10,... | collective-permute-start | bytes 122888 | tf_op jit(solution)/shard_map/cond/branch_1_fun/ppermute | solution.py:49
  54.4 2.0 %collective-permute-done.2 = bf16[80,256]{1,0:T(8,128)(2,1)S(1)} collective-permute-done((bf16[80,256]{1,0:T(8,128)(2,1)S(1)}, bf16[80,256]{1,0:T(8,128)(2,1)S(1)}, u32[]{:S(2)}, u32[]{:S(2)}) %collective-permute-start.2) | collective-permute-done | bytes 40992 | tf_op jit(solution)/shard_map/cond/branch_1_fun/ppermute | solution.py:49
  56.6 1.2 %collective-permute-done.3 = f32[64,256]{1,0:T(8,128)S(1)} collective-permute-done((f32[64,256]{1,0:T(8,128)S(1)}, f32[64,256]{1,0:T(8,128)S(1)}, u32[]{:S(2)}, u32[]{:S(2)}) %collective-permute-start.3) | collective-permute-done | bytes 65568 | tf_op jit(solution)/shard_map/cond/branch_1_fun/ppermute | solution.py:49
  57.9 0.8 %multiply_convert_fusion = bf16[512,128]{1,0:T(8,128)(2,1)} fusion(f32[512,128]{1,0:T(8,128)S(1)} %get-tuple-element.116.earlier_ref.refs_5_, bf16[512,128]{1,0:T(8,128)(2,1)S(1)} %get-tuple-element.124, bf16[512,128]{1,0:T(8,128)(2,1)S(1)} %collective-permute-done.21, bf16[512,128]{1,0:T(8,128)(2,1)S(1)} %collective-permute-done.20, ...), kind=kLoop, calls=%fused_computation.10 | loop fusion | flops 655360 | bytes 1179648 | tf_op jit(solution)/shard_map/convert_element_type | solution.py:550
  (66 shorter events, 6.3 us)
Async XLA Ops:
  1.7 9.5 %collective-permute-start.10 = (bf16[512,128]{1,0:T(8,128)(2,1)S(1)}, bf16[512,128]{1,0:T(8,128)(2,1)S(1)}, u32[]{:S(2)}, u32[]{:S(2)}) collective-permute-start(bf16[512,128]{1,0:T(8,128)(2,1)S(1)} %get-tuple-element.120.earlier_ref.refs_0_.refs_4_), channel_id=1, source_target_pairs={{0,24},{1,25},{2,26},{3,27},{4,28},{5,29},{6,30},{7,31},{8,16},{9,... | collective-permute-start | bytes 393224 | tf_op jit(solution)/shard_map/ppermute | solution.py:49
  5.7 6.3 %collective-permute-start.9 = (bf16[512,128]{1,0:T(8,128)(2,1)S(1)}, bf16[512,128]{1,0:T(8,128)(2,1)S(1)}, u32[]{:S(2)}, u32[]{:S(2)}) collective-permute-start(bf16[512,128]{1,0:T(8,128)(2,1)S(1)} %get-tuple-element.120.earlier_ref.refs_0_.refs_4_), channel_id=1, source_target_pairs={{0,16},{1,9},{2,18},{3,11},{4,20},{5,13},{6,22},{7,15},{8,24},{9,1... | collective-permute-start | bytes 393224 | tf_op jit(solution)/shard_map/ppermute | solution.py:49
  6.2 6.0 %collective-permute-start.8 = (bf16[512,128]{1,0:T(8,128)(2,1)S(1)}, bf16[512,128]{1,0:T(8,128)(2,1)S(1)}, u32[]{:S(2)}, u32[]{:S(2)}) collective-permute-start(bf16[512,128]{1,0:T(8,128)(2,1)S(1)} %get-tuple-element.120.earlier_ref.refs_0_.refs_4_), channel_id=1, source_target_pairs={{0,8},{1,17},{2,10},{3,19},{4,12},{5,21},{6,14},{7,23},{8,0},{9,25... | collective-permute-start | bytes 393224 | tf_op jit(solution)/shard_map/ppermute | solution.py:49
  12.6 11.0 %collective-permute-start.13 = (bf16[512,128]{1,0:T(8,128)(2,1)S(1)}, bf16[512,128]{1,0:T(8,128)(2,1)S(1)}, u32[]{:S(2)}, u32[]{:S(2)}) collective-permute-start(bf16[512,128]{1,0:T(8,128)(2,1)S(1)} %forward_3.1.earlier_ref), channel_id=1, source_target_pairs={{0,5},{1,4},{2,7},{3,6},{4,1},{5,0},{6,3},{7,2},{8,13},{9,12},{10,... | collective-permute-start | bytes 393224 | tf_op jit(solution)/shard_map/ppermute | solution.py:49
  15.8 12.1 %copy-start = (bf16[512,256]{1,0:T(8,128)(2,1)S(1)}, bf16[512,256]{1,0:T(8,128)(2,1)}, u32[]{:S(2)}) copy-start(bf16[512,256]{1,0:T(8,128)(2,1)} %refs_8_.1) | copy-start | bytes 786436
  15.8 12.1 %copy-start.1 = (bf16[128,256]{1,0:T(8,128)(2,1)S(1)}, bf16[128,256]{1,0:T(8,128)(2,1)}, u32[]{:S(2)}) copy-start(bf16[128,256]{1,0:T(8,128)(2,1)} %refs_6_.1) | copy-start | bytes 196612
  15.8 12.1 %copy-start.2 = (f32[256]{0:T(256)S(1)}, f32[256]{0:T(256)}, u32[]{:S(2)}) copy-start(f32[256]{0:T(256)} %param.24) | copy-start | bytes 3076
  15.8 2.5 %collective-permute-start = (bf16[1024,128]{1,0:T(8,128)(2,1)S(1)}, bf16[1024,128]{1,0:T(8,128)(2,1)S(1)}, u32[]{:S(2)}, u32[]{:S(2)}) collective-permute-start(bf16[1024,128]{1,0:T(8,128)(2,1)S(1)} %get-tuple-element.50), channel_id=1, source_target_pairs={{0,1},{1,0},{2,3},{3,2},{4,5},{5,4},{6,7},{7,6},{8,9},{9,8},{10,11... | collective-permute-start | bytes 786440 | tf_op jit(solution)/shard_map/cond/branch_1_fun/ppermute | solution.py:49
  18.4 8.2 %collective-permute-start.12 = (bf16[512,128]{1,0:T(8,128)(2,1)S(1)}, bf16[512,128]{1,0:T(8,128)(2,1)S(1)}, u32[]{:S(2)}, u32[]{:S(2)}) collective-permute-start(bf16[512,128]{1,0:T(8,128)(2,1)S(1)} %get-tuple-element.123), channel_id=1, source_target_pairs={{0,6},{1,7},{2,4},{3,5},{4,2},{5,3},{6,0},{7,1},{8,14},{9,15},{10,... | collective-permute-start | bytes 393224 | tf_op jit(solution)/shard_map/ppermute | solution.py:49
  19.8 8.1 %collective-permute-start.11 = (bf16[512,128]{1,0:T(8,128)(2,1)S(1)}, bf16[512,128]{1,0:T(8,128)(2,1)S(1)}, u32[]{:S(2)}, u32[]{:S(2)}) collective-permute-start(bf16[512,128]{1,0:T(8,128)(2,1)S(1)} %get-tuple-element.122), channel_id=1, source_target_pairs={{0,2},{1,3},{2,0},{3,1},{4,6},{5,7},{6,4},{7,5},{8,10},{9,11},{10,... | collective-permute-start | bytes 393224 | tf_op jit(solution)/shard_map/ppermute | solution.py:49
  22.1 1.4 %collective-permute-start.1 = (bf16[512,128]{1,0:T(8,128)(2,1)S(1)}, bf16[512,128]{1,0:T(8,128)(2,1)S(1)}, u32[]{:S(2)}, u32[]{:S(2)}) collective-permute-start(bf16[512,128]{1,0:T(8,128)(2,1)S(1)} %get-tuple-element.61), channel_id=1, source_target_pairs={{0,1},{1,0},{2,3},{3,2},{4,5},{5,4},{6,7},{7,6},{8,9},{9,8},{10,11... | collective-permute-start | bytes 393224 | tf_op jit(solution)/shard_map/cond/branch_1_fun/ppermute | solution.py:49
  28.4 13.2 %collective-permute-start.17 = (bf16[512,128]{1,0:T(8,128)(2,1)S(1)}, bf16[512,128]{1,0:T(8,128)(2,1)S(1)}, u32[]{:S(2)}, u32[]{:S(2)}) collective-permute-start(bf16[512,128]{1,0:T(8,128)(2,1)S(1)} %get-tuple-element.124), channel_id=1, source_target_pairs={{0,5},{1,4},{2,7},{3,6},{4,1},{5,0},{6,3},{7,2},{8,13},{9,12},{10,... | collective-permute-start | bytes 393224 | tf_op jit(solution)/shard_map/ppermute | solution.py:49
  30.4 11.2 %collective-permute-start.16 = (bf16[512,128]{1,0:T(8,128)(2,1)S(1)}, bf16[512,128]{1,0:T(8,128)(2,1)S(1)}, u32[]{:S(2)}, u32[]{:S(2)}) collective-permute-start(bf16[512,128]{1,0:T(8,128)(2,1)S(1)} %get-tuple-element.124), channel_id=1, source_target_pairs={{0,6},{1,7},{2,4},{3,5},{4,2},{5,3},{6,0},{7,1},{8,14},{9,15},{10,... | collective-permute-start | bytes 393224 | tf_op jit(solution)/shard_map/ppermute | solution.py:49
  31.6 10.5 %collective-permute-start.15 = (bf16[512,128]{1,0:T(8,128)(2,1)S(1)}, bf16[512,128]{1,0:T(8,128)(2,1)S(1)}, u32[]{:S(2)}, u32[]{:S(2)}) collective-permute-start(bf16[512,128]{1,0:T(8,128)(2,1)S(1)} %get-tuple-element.124), channel_id=1, source_target_pairs={{0,2},{1,3},{2,0},{3,1},{4,6},{5,7},{6,4},{7,5},{8,10},{9,11},{10,... | collective-permute-start | bytes 393224 | tf_op jit(solution)/shard_map/ppermute | solution.py:49
  32.0 1.3 %collective-permute-start.5 = (f32[80,256]{1,0:T(8,128)S(1)}, f32[80,256]{1,0:T(8,128)S(1)}, u32[]{:S(2)}, u32[]{:S(2)}) collective-permute-start(f32[80,256]{1,0:T(8,128)S(1)} %get-tuple-element.75), channel_id=1, source_target_pairs={{0,1},{1,0},{2,3},{3,2},{4,5},{5,4},{6,7},{7,6},{8,9},{9,8},{10,11... | collective-permute-start | bytes 245768 | tf_op jit(solution)/shard_map/cond/branch_1_fun/ppermute | solution.py:49
  32.3 2.9 %collective-permute-start.4 = (bf16[512,128]{1,0:T(8,128)(2,1)S(1)}, bf16[512,128]{1,0:T(8,128)(2,1)S(1)}, u32[]{:S(2)}, u32[]{:S(2)}) collective-permute-start(bf16[512,128]{1,0:T(8,128)(2,1)S(1)} %get-tuple-element.66.refs_0_), channel_id=1, source_target_pairs={{0,1},{1,0},{2,3},{3,2},{4,5},{5,4},{6,7},{7,6},{8,9},{9,8},{10,11... | collective-permute-start | bytes 393224 | tf_op jit(solution)/shard_map/cond/branch_1_fun/ppermute | solution.py:49
  33.3 4.1 %collective-permute-start.6 = (bf16[80,256]{1,0:T(8,128)(2,1)S(1)}, bf16[80,256]{1,0:T(8,128)(2,1)S(1)}, u32[]{:S(2)}, u32[]{:S(2)}) collective-permute-start(bf16[80,256]{1,0:T(8,128)(2,1)S(1)} %get-tuple-element.147), channel_id=1, source_target_pairs={{0,8},{1,17},{2,10},{3,19},{4,12},{5,21},{6,14},{7,23},{8,0},{9,25... | collective-permute-start | bytes 122888 | tf_op jit(solution)/shard_map/cond/branch_1_fun/ppermute | solution.py:49
  37.5 4.1 %collective-permute-start.7 = (bf16[80,256]{1,0:T(8,128)(2,1)S(1)}, bf16[80,256]{1,0:T(8,128)(2,1)S(1)}, u32[]{:S(2)}, u32[]{:S(2)}) collective-permute-start(bf16[80,256]{1,0:T(8,128)(2,1)S(1)} %fusion), channel_id=1, source_target_pairs={{0,16},{1,9},{2,18},{3,11},{4,20},{5,13},{6,22},{7,15},{8,24},{9,1... | collective-permute-start | bytes 122888 | tf_op jit(solution)/shard_map/cond/branch_1_fun/ppermute | solution.py:49
  42.1 2.1 %collective-permute-start.18 = (bf16[1024,128]{1,0:T(8,128)(2,1)S(1)}, bf16[1024,128]{1,0:T(8,128)(2,1)S(1)}, u32[]{:S(2)}, u32[]{:S(2)}) collective-permute-start(bf16[1024,128]{1,0:T(8,128)(2,1)S(1)} %constant_dynamic-update-slice_fusion.refs_0_), channel_id=1, source_target_pairs={{0,1},{1,0},{2,3},{3,2},{4,5},{5,4},{6,7},{7,6},{8,9},{9,8},{10,11... | collective-permute-start | bytes 786440 | tf_op jit(solution)/shard_map/ppermute | solution.py:49
  42.2 5.0 %collective-permute-start.14 = (bf16[80,256]{1,0:T(8,128)(2,1)S(1)}, bf16[80,256]{1,0:T(8,128)(2,1)S(1)}, u32[]{:S(2)}, u32[]{:S(2)}) collective-permute-start(bf16[80,256]{1,0:T(8,128)(2,1)S(1)} %convert_element_type.77), channel_id=1, source_target_pairs={{0,2},{1,3},{2,0},{3,1},{4,6},{5,7},{6,4},{7,5},{8,10},{9,11},{10,... | collective-permute-start | bytes 122888 | tf_op jit(solution)/shard_map/ppermute | solution.py:49
  47.2 10.6 %collective-permute-start.19 = (bf16[512,128]{1,0:T(8,128)(2,1)S(1)}, bf16[512,128]{1,0:T(8,128)(2,1)S(1)}, u32[]{:S(2)}, u32[]{:S(2)}) collective-permute-start(bf16[512,128]{1,0:T(8,128)(2,1)S(1)} %get-tuple-element.142), channel_id=1, source_target_pairs={{0,8},{1,17},{2,10},{3,19},{4,12},{5,21},{6,14},{7,23},{8,0},{9,25... | collective-permute-start | bytes 393224 | tf_op jit(solution)/shard_map/ppermute | solution.py:49
  49.8 8.0 %collective-permute-start.20 = (bf16[512,128]{1,0:T(8,128)(2,1)S(1)}, bf16[512,128]{1,0:T(8,128)(2,1)S(1)}, u32[]{:S(2)}, u32[]{:S(2)}) collective-permute-start(bf16[512,128]{1,0:T(8,128)(2,1)S(1)} %get-tuple-element.143), channel_id=1, source_target_pairs={{0,16},{1,9},{2,18},{3,11},{4,20},{5,13},{6,22},{7,15},{8,24},{9,1... | collective-permute-start | bytes 393224 | tf_op jit(solution)/shard_map/ppermute | solution.py:49
  50.6 7.2 %collective-permute-start.21 = (bf16[512,128]{1,0:T(8,128)(2,1)S(1)}, bf16[512,128]{1,0:T(8,128)(2,1)S(1)}, u32[]{:S(2)}, u32[]{:S(2)}) collective-permute-start(bf16[512,128]{1,0:T(8,128)(2,1)S(1)} %get-tuple-element.144), channel_id=1, source_target_pairs={{0,24},{1,25},{2,26},{3,27},{4,28},{5,29},{6,30},{7,31},{8,16},{9,... | collective-permute-start | bytes 393224 | tf_op jit(solution)/shard_map/ppermute | solution.py:49
  51.4 5.0 %collective-permute-start.2 = (bf16[80,256]{1,0:T(8,128)(2,1)S(1)}, bf16[80,256]{1,0:T(8,128)(2,1)S(1)}, u32[]{:S(2)}, u32[]{:S(2)}) collective-permute-start(bf16[80,256]{1,0:T(8,128)(2,1)S(1)} %fusion.1), channel_id=1, source_target_pairs={{0,4},{1,5},{2,6},{3,7},{4,0},{5,1},{6,2},{7,3},{8,12},{9,13},{10,... | collective-permute-start | bytes 122888 | tf_op jit(solution)/shard_map/cond/branch_1_fun/ppermute | solution.py:49
  56.5 1.3 %collective-permute-start.3 = (f32[64,256]{1,0:T(8,128)S(1)}, f32[64,256]{1,0:T(8,128)S(1)}, u32[]{:S(2)}, u32[]{:S(2)}) collective-permute-start(f32[64,256]{1,0:T(8,128)S(1)} %slice.24), channel_id=1, source_target_pairs={{0,1},{1,0},{2,3},{3,2},{4,5},{5,4},{6,7},{7,6},{8,9},{9,8},{10,11... | collective-permute-start | bytes 196616 | tf_op jit(solution)/shard_map/cond/branch_1_fun/ppermute | solution.py:49
  57.8 0.8 %copy-start.3 = (bf16[512,256]{1,0:T(8,128)(2,1)}, bf16[512,256]{1,0:T(8,128)(2,1)S(1)}, u32[]{:S(2)}) copy-start(bf16[512,256]{1,0:T(8,128)(2,1)S(1)} %get-tuple-element.112) | copy-start | bytes 786436
  57.8 0.8 %copy-start.4 = (f32[128,256]{1,0:T(8,128)}, f32[128,256]{1,0:T(8,128)S(1)}, u32[]{:S(2)}) copy-start(f32[128,256]{1,0:T(8,128)S(1)} %get-tuple-element.114) | copy-start | bytes 393220
  57.8 0.8 %copy-start.5 = (f32[256]{0:T(256)}, f32[256]{0:T(256)S(1)}, u32[]{:S(2)}) copy-start(f32[256]{0:T(256)S(1)} %get-tuple-element.115) | copy-start | bytes 3076

commit v8 on v7

--- a/solution.py
+++ b/solution.py
@@ -133,15 +133,13 @@
     ]
     for copy in copies:
         copy.start()
-    for copy in copies:
-        copy.wait()
     tile = degrees_ref.shape[1]
+    copies[0].wait()
     for n in range(degrees_ref.shape[0]):
-        norm = node_scale(degrees_ref[n : n + 1, :])
-        norm = jnp.broadcast_to(norm, (tile, tile)).T
-        rows = slice(n * tile, (n + 1) * tile)
-        norm_ref[rows, :] = norm
-        scaled_ref[rows, :] = (norm * features_ref[rows, :].astype(F32)).astype(BF)
+        norm = jnp.broadcast_to(node_scale(degrees_ref[n : n + 1, :]), (tile, tile)).T
+        norm_ref[n * tile : (n + 1) * tile, :] = norm
+    copies[1].wait()
+    scaled_ref[...] = (norm_ref[...] * features_ref[...].astype(F32)).astype(BF)
 
 
 def write_kernel(value_ref, out_ref, sem):

time: 59.3 us -> 58.7 us (0.990)
  starting transfers between devices: 26.3 us -> 25.4 us
  Pallas kernels: 14.1 us -> 15 us
    ppermute x22, starting transfers between devices: 26.3 us -> 25.4 us  [move(): return lax.ppermute(value, BOTH, pairs)]
    pallas_call x2, Pallas kernels: 5.19 us -> 5.88 us  [backward(): pl.pallas_call(functools.partial(backward_kernel, places, unroll), out_sh...]
  transfers between devices with their start and end apart: 22 -> 22, of which waited for: 11 -> 11; matrix products, arithmetic and copies ran while one was open for 2% -> 2% of each run, Pallas kernels for 21% -> 23%
where the time goes in v8:
time: 58.7 us; the launch traced here: 58.5 us
  starting transfers between devices  25.4 us (43%)
  Pallas kernels  15 us (26%)
  waiting for transfers between devices  14.3 us (24%)
  other arithmetic  1.95 us (3%)
  between operations  1.54 us (3%)
    ppermute x22, starting transfers between devices, move(): return lax.ppermute(value, BOTH, pairs)  25.4 us
    ppermute x22, waiting for transfers between devices, move(): return lax.ppermute(value, BOTH, pairs)  14.3 us
    pallas_call x2, Pallas kernels, backward(): pl.pallas_call(functools.partial(backward_kernel, places, unroll), out_sh...  5.88 us
    pallas_call x3, Pallas kernels, forward(): pl.pallas_call(functools.partial(forward_kernel, places, unroll, stream),...  4.28 us
    pallas_call x1, Pallas kernels, stage(): pl.pallas_call(stage_kernel, out_shape=jax.ShapeDtypeStruct((slot_total,...  2.5 us
  transfers between devices with their start and end apart: 22, of which 11 were waited for; matrix products, arithmetic and copies ran while one was open for 2% of the time, Pallas kernels for 23%

profile of v8, /device:TPU:0, one launch (start us, length us, event | category | flops | bytes accessed | tf_op | source)
XLA Modules:
  0.0 58.5 jit_solution(1304190694388486278)
XLA Ops:
  0.6 1.0 %prepare.1 = (bf16[512,128]{1,0:T(8,128)(2,1)S(1)}, f32[512,128]{1,0:T(8,128)S(1)}) custom-call(s32[4,128]{1,0:T(4,128)} %bitcast.18, bf16[512,128]{1,0:T(8,128)(2,1)} %features_hbm.1), custom_call_target="tpu_custom_call" | custom-call | bytes 1024 | tf_op jit(solution)/shard_map/prepare/pallas_call | solution.py:369
  1.6 4.0 %collective-permute-start.10 = (bf16[512,128]{1,0:T(8,128)(2,1)S(1)}, bf16[512,128]{1,0:T(8,128)(2,1)S(1)}, u32[]{:S(2)}, u32[]{:S(2)}) collective-permute-start(bf16[512,128]{1,0:T(8,128)(2,1)S(1)} %get-tuple-element.120.earlier_ref.refs_0_.refs_4_), channel_id=1, source_target_pairs={{0,24},{1,25},{2,26},{3,27},{4,28},{5,29},{6,30},{7,31},{8,16},{9,... | collective-permute-start | bytes 393224 | tf_op jit(solution)/shard_map/ppermute | solution.py:49
  7.8 2.5 %stage_tiles.1.w_ref = bf16[160,128,128]{2,1,0:T(8,128)(2,1)S(1)} custom-call(bf16[160,128,128]{2,1,0:T(8,128)(2,1)} %bitcast.14, bf16[512,128]{1,0:T(8,128)(2,1)S(1)} %get-tuple-element.120.earlier_ref.refs_0_.refs_4_), custom_call_target="tpu_custom_call" | custom-call | bytes 10485760 | tf_op jit(solution)/shard_map/stage_tiles/pallas_call | solution.py:388
  11.1 0.8 %collective-permute-done.9.refs_2_ = bf16[512,128]{1,0:T(8,128)(2,1)S(1)} collective-permute-done((bf16[512,128]{1,0:T(8,128)(2,1)S(1)}, bf16[512,128]{1,0:T(8,128)(2,1)S(1)}, u32[]{:S(2)}, u32[]{:S(2)}) %collective-permute-start.9) | collective-permute-done | bytes 131104 | tf_op jit(solution)/shard_map/ppermute | solution.py:49
  12.5 1.8 %collective-permute-start.13 = (bf16[512,128]{1,0:T(8,128)(2,1)S(1)}, bf16[512,128]{1,0:T(8,128)(2,1)S(1)}, u32[]{:S(2)}, u32[]{:S(2)}) collective-permute-start(bf16[512,128]{1,0:T(8,128)(2,1)S(1)} %forward_3.1.earlier_ref), channel_id=1, source_target_pairs={{0,5},{1,4},{2,7},{3,6},{4,1},{5,0},{6,3},{7,2},{8,13},{9,12},{10,... | collective-permute-start | bytes 393224 | tf_op jit(solution)/shard_map/ppermute | solution.py:49
  14.2 1.7 %forward_1_2.1 = (bf16[1024,128]{1,0:T(8,128)(2,1)S(1)}, bf16[1024,128]{1,0:T(8,128)(2,1)S(1)}) custom-call(bf16[512,128]{1,0:T(8,128)(2,1)S(1)} %forward_3.1.earlier_ref, s32[8]{0:T(128)S(4)} %get-tuple-element.117.bounds_ref, s32[160]{0:T(256)S(4)} %get-tuple-element.118.row_ref, s32[160]{0:T(256)S(4)} %get-tuple-element.119.col_ref, ...), custom_call_target="tpu_custom_call" | custom-call | bytes 1024 | tf_op jit(solution)/shard_map/forward_1_2/pallas_call | solution.py:410
  16.0 2.3 %conditional.4 = (bf16[512,128]{1,0:T(8,128)(2,1)S(1)}, bf16[512,128]{1,0:T(8,128)(2,1)S(1)}, bf16[16,128]{1,0:T(8,128)(2,1)S(1)}) conditional(s32[]{:T(128)} %convert_element_type.75, () %tuple.40, (bf16[1024,128]{1,0:T(8,128)(2,1)S(1)}, bf16[1024,128]{1,0:T(8,128)(2,1)S(1)}) %forward_1_2.1), branch_computations={%region_1.2_spmd, %region_2.3_spmd} | conditional | flops 524288 | bytes 1843264 | solution.py:54
  16.0 1.1 %collective-permute-start = (bf16[1024,128]{1,0:T(8,128)(2,1)S(1)}, bf16[1024,128]{1,0:T(8,128)(2,1)S(1)}, u32[]{:S(2)}, u32[]{:S(2)}) collective-permute-start(bf16[1024,128]{1,0:T(8,128)(2,1)S(1)} %get-tuple-element.50), channel_id=1, source_target_pairs={{0,1},{1,0},{2,3},{3,2},{4,5},{5,4},{6,7},{7,6},{8,9},{9,8},{10,11... | collective-permute-start | bytes 786440 | tf_op jit(solution)/shard_map/cond/branch_1_fun/ppermute | solution.py:49
  17.1 1.2 %collective-permute-done = bf16[1024,128]{1,0:T(8,128)(2,1)S(1)} collective-permute-done((bf16[1024,128]{1,0:T(8,128)(2,1)S(1)}, bf16[1024,128]{1,0:T(8,128)(2,1)S(1)}, u32[]{:S(2)}, u32[]{:S(2)}) %collective-permute-start) | collective-permute-done | bytes 262176 | tf_op jit(solution)/shard_map/cond/branch_1_fun/ppermute | solution.py:49
  18.3 1.7 %collective-permute-start.12 = (bf16[512,128]{1,0:T(8,128)(2,1)S(1)}, bf16[512,128]{1,0:T(8,128)(2,1)S(1)}, u32[]{:S(2)}, u32[]{:S(2)}) collective-permute-start(bf16[512,128]{1,0:T(8,128)(2,1)S(1)} %get-tuple-element.123), channel_id=1, source_target_pairs={{0,6},{1,7},{2,4},{3,5},{4,2},{5,3},{6,0},{7,1},{8,14},{9,15},{10,... | collective-permute-start | bytes 393224 | tf_op jit(solution)/shard_map/ppermute | solution.py:49
  20.0 3.7 %conditional.5 = (bf16[512,128]{1,0:T(8,128)(2,1)S(1)}) conditional(s32[]{:T(128)} %convert_element_type.75, () %tuple.39, (bf16[16,128]{1,0:T(8,128)(2,1)S(1)}, s32[8]{0:T(128)S(4)}, s32[160]{0:T(256)S(4)}, s32[160]{0:T(256)S(4)}, bf16[160,128,128]{2,1,0:T(8,128)(2,1)}, /*index=5*/bf16[512,128]{1,0:T(8,128)(2,1)S(1)}, ...), branch_computations={%region_3.4_spmd, %region_4.5_spmd} | conditional | flops 262144 | bytes 918576 | solution.py:54
  20.0 2.2 %forward_0.1 = (bf16[512,128]{1,0:T(8,128)(2,1)S(1)}, bf16[512,128]{1,0:T(8,128)(2,1)S(1)}) custom-call(bf16[16,128]{1,0:T(8,128)(2,1)S(1)} %get-tuple-element.51.earlier_ref, s32[8]{0:T(128)S(4)} %get-tuple-element.52.bounds_ref, s32[160]{0:T(256)S(4)} %get-tuple-element.53.row_ref, s32[160]{0:T(256)S(4)} %get-tuple-element.54.col_ref, ...), custom_call_target="tpu_custom_call" | custom-call | bytes 1024 | tf_op jit(solution)/shard_map/cond/branch_1_fun/forward_0/pallas_call | solution.py:410
  22.4 1.3 %collective-permute-done.1 = bf16[512,128]{1,0:T(8,128)(2,1)S(1)} collective-permute-done((bf16[512,128]{1,0:T(8,128)(2,1)S(1)}, bf16[512,128]{1,0:T(8,128)(2,1)S(1)}, u32[]{:S(2)}, u32[]{:S(2)}) %collective-permute-start.1) | collective-permute-done | bytes 131104 | tf_op jit(solution)/shard_map/cond/branch_1_fun/ppermute | solution.py:49
  23.8 2.8 %collective-permute-done.12.refs_0_ = bf16[512,128]{1,0:T(8,128)(2,1)S(1)} collective-permute-done((bf16[512,128]{1,0:T(8,128)(2,1)S(1)}, bf16[512,128]{1,0:T(8,128)(2,1)S(1)}, u32[]{:S(2)}, u32[]{:S(2)}) %collective-permute-start.12) | collective-permute-done | bytes 131104 | tf_op jit(solution)/shard_map/ppermute | solution.py:49
  26.6 1.5 %collective-permute-done.11.refs_0_ = bf16[512,128]{1,0:T(8,128)(2,1)S(1)} collective-permute-done((bf16[512,128]{1,0:T(8,128)(2,1)S(1)}, bf16[512,128]{1,0:T(8,128)(2,1)S(1)}, u32[]{:S(2)}, u32[]{:S(2)}) %collective-permute-start.11) | collective-permute-done | bytes 131104 | tf_op jit(solution)/shard_map/ppermute | solution.py:49
  28.6 1.7 %collective-permute-start.17 = (bf16[512,128]{1,0:T(8,128)(2,1)S(1)}, bf16[512,128]{1,0:T(8,128)(2,1)S(1)}, u32[]{:S(2)}, u32[]{:S(2)}) collective-permute-start(bf16[512,128]{1,0:T(8,128)(2,1)S(1)} %get-tuple-element.124), channel_id=1, source_target_pairs={{0,5},{1,4},{2,7},{3,6},{4,1},{5,0},{6,3},{7,2},{8,13},{9,12},{10,... | collective-permute-start | bytes 393224 | tf_op jit(solution)/shard_map/ppermute | solution.py:49
  30.3 1.2 %collective-permute-start.16 = (bf16[512,128]{1,0:T(8,128)(2,1)S(1)}, bf16[512,128]{1,0:T(8,128)(2,1)S(1)}, u32[]{:S(2)}, u32[]{:S(2)}) collective-permute-start(bf16[512,128]{1,0:T(8,128)(2,1)S(1)} %get-tuple-element.124), channel_id=1, source_target_pairs={{0,6},{1,7},{2,4},{3,5},{4,2},{5,3},{6,0},{7,1},{8,14},{9,15},{10,... | collective-permute-start | bytes 393224 | tf_op jit(solution)/shard_map/ppermute | solution.py:49
  31.6 10.2 %conditional.6 = (bf16[512,128]{1,0:T(8,128)(2,1)S(1)}, bf16[512,128]{1,0:T(8,128)(2,1)S(1)}, bf16[512,128]{1,0:T(8,128)(2,1)S(1)}, bf16[512,128]{1,0:T(8,128)(2,1)S(1)}, f32[80,256]{1,0:T(8,128)S(1)}) conditional(s32[]{:T(128)} %convert_element_type.75, () %tuple.38, (bf16[512,128]{1,0:T(8,128)(2,1)S(1)}, s32[8]{0:T(128)S(4)}, s32[160]{0:T(256)S(4)}, ...), branch_computations={%region_5.6_spmd, %region_6.7_spmd} | conditional | flops 184320 | bytes 1879240 | solution.py:54
  32.4 0.8 %collective-permute-done.5 = f32[80,256]{1,0:T(8,128)S(1)} collective-permute-done((f32[80,256]{1,0:T(8,128)S(1)}, f32[80,256]{1,0:T(8,128)S(1)}, u32[]{:S(2)}, u32[]{:S(2)}) %collective-permute-start.5) | collective-permute-done | bytes 81952 | tf_op jit(solution)/shard_map/cond/branch_1_fun/ppermute | solution.py:49
  33.2 1.8 %collective-permute-start.6 = (bf16[80,256]{1,0:T(8,128)(2,1)S(1)}, bf16[80,256]{1,0:T(8,128)(2,1)S(1)}, u32[]{:S(2)}, u32[]{:S(2)}) collective-permute-start(bf16[80,256]{1,0:T(8,128)(2,1)S(1)} %get-tuple-element.147), channel_id=1, source_target_pairs={{0,8},{1,17},{2,10},{3,19},{4,12},{5,21},{6,14},{7,23},{8,0},{9,25... | collective-permute-start | bytes 122888 | tf_op jit(solution)/shard_map/cond/branch_1_fun/ppermute | solution.py:49
  35.1 2.6 %backward_0.1 = (bf16[512,128]{1,0:T(8,128)(2,1)S(1)}, bf16[512,128]{1,0:T(8,128)(2,1)S(1)}, bf16[512,128]{1,0:T(8,128)(2,1)S(1)}, bf16[512,128]{1,0:T(8,128)(2,1)S(1)}, bf16[16,128]{1,0:T(8,128)(2,1)S(1)}) custom-call(s32[8]{0:T(128)S(4)} %get-tuple-element.62.bounds_ref, s32[160]{0:T(256)S(4)} %get-tuple-element.63.row_ref, ...), custom_call_target="tpu_custom_call" | custom-call | bytes 1024 | tf_op jit(solution)/shard_map/cond/branch_1_fun/backward_0/pallas_call | solution.py:470
  37.7 1.5 %collective-permute-start.7 = (bf16[80,256]{1,0:T(8,128)(2,1)S(1)}, bf16[80,256]{1,0:T(8,128)(2,1)S(1)}, u32[]{:S(2)}, u32[]{:S(2)}) collective-permute-start(bf16[80,256]{1,0:T(8,128)(2,1)S(1)} %fusion), channel_id=1, source_target_pairs={{0,16},{1,9},{2,18},{3,11},{4,20},{5,13},{6,22},{7,15},{8,24},{9,1... | collective-permute-start | bytes 122888 | tf_op jit(solution)/shard_map/cond/branch_1_fun/ppermute | solution.py:49
  39.2 2.5 %collective-permute-done.7 = bf16[80,256]{1,0:T(8,128)(2,1)S(1)} collective-permute-done((bf16[80,256]{1,0:T(8,128)(2,1)S(1)}, bf16[80,256]{1,0:T(8,128)(2,1)S(1)}, u32[]{:S(2)}, u32[]{:S(2)}) %collective-permute-start.7) | collective-permute-done | bytes 40992 | tf_op jit(solution)/shard_map/cond/branch_1_fun/ppermute | solution.py:49
  42.0 2.0 %collective-permute-start.14 = (bf16[80,256]{1,0:T(8,128)(2,1)S(1)}, bf16[80,256]{1,0:T(8,128)(2,1)S(1)}, u32[]{:S(2)}, u32[]{:S(2)}) collective-permute-start(bf16[80,256]{1,0:T(8,128)(2,1)S(1)} %convert_element_type.77), channel_id=1, source_target_pairs={{0,2},{1,3},{2,0},{3,1},{4,6},{5,7},{6,4},{7,5},{8,10},{9,11},{10,... | collective-permute-start | bytes 122888 | tf_op jit(solution)/shard_map/ppermute | solution.py:49
  44.0 3.3 %backward_1_2_3.1 = (f32[512,128]{1,0:T(8,128)S(1)}, bf16[512,128]{1,0:T(8,128)(2,1)S(1)}, bf16[512,128]{1,0:T(8,128)(2,1)S(1)}, bf16[512,128]{1,0:T(8,128)(2,1)S(1)}) custom-call(s32[8]{0:T(128)S(4)} %get-tuple-element.117.bounds_ref, s32[160]{0:T(256)S(4)} %get-tuple-element.118.row_ref, s32[160]{0:T(256)S(4)} %get-tuple-element.119.col_ref, ...), custom_call_target="tpu_custom_call" | custom-call | bytes 1024 | tf_op jit(solution)/shard_map/backward_1_2_3/pallas_call | solution.py:470
  47.3 2.1 %collective-permute-start.19 = (bf16[512,128]{1,0:T(8,128)(2,1)S(1)}, bf16[512,128]{1,0:T(8,128)(2,1)S(1)}, u32[]{:S(2)}, u32[]{:S(2)}) collective-permute-start(bf16[512,128]{1,0:T(8,128)(2,1)S(1)} %get-tuple-element.142), channel_id=1, source_target_pairs={{0,8},{1,17},{2,10},{3,19},{4,12},{5,21},{6,14},{7,23},{8,0},{9,25... | collective-permute-start | bytes 393224 | tf_op jit(solution)/shard_map/ppermute | solution.py:49
  49.4 1.3 %collective-permute-start.20 = (bf16[512,128]{1,0:T(8,128)(2,1)S(1)}, bf16[512,128]{1,0:T(8,128)(2,1)S(1)}, u32[]{:S(2)}, u32[]{:S(2)}) collective-permute-start(bf16[512,128]{1,0:T(8,128)(2,1)S(1)} %get-tuple-element.143), channel_id=1, source_target_pairs={{0,16},{1,9},{2,18},{3,11},{4,20},{5,13},{6,22},{7,15},{8,24},{9,1... | collective-permute-start | bytes 393224 | tf_op jit(solution)/shard_map/ppermute | solution.py:49
  50.9 6.7 %conditional.7 = (f32[128,256]{1,0:T(8,128)S(1)}, f32[256]{0:T(256)S(1)}, bf16[512,256]{1,0:T(8,128)(2,1)S(1)}) conditional(s32[]{:T(128)} %convert_element_type.75, () %tuple.37, (s32[]{:T(128)}, bf16[80,256]{1,0:T(8,128)(2,1)S(1)}, f32[80,256]{1,0:T(8,128)S(1)}, bf16[512,256]{1,0:T(8,128)(2,1)S(1)}) %tuple.43), branch_computations={%region_7.8_spmd, %region_8.9_spmd} | conditional | flops 262145 | bytes 1231986 | solution.py:54
  50.9 3.4 %collective-permute-start.2 = (bf16[80,256]{1,0:T(8,128)(2,1)S(1)}, bf16[80,256]{1,0:T(8,128)(2,1)S(1)}, u32[]{:S(2)}, u32[]{:S(2)}) collective-permute-start(bf16[80,256]{1,0:T(8,128)(2,1)S(1)} %fusion.1), channel_id=1, source_target_pairs={{0,4},{1,5},{2,6},{3,7},{4,0},{5,1},{6,2},{7,3},{8,12},{9,13},{10,... | collective-permute-start | bytes 122888 | tf_op jit(solution)/shard_map/cond/branch_1_fun/ppermute | solution.py:49
  54.3 2.0 %collective-permute-done.2 = bf16[80,256]{1,0:T(8,128)(2,1)S(1)} collective-permute-done((bf16[80,256]{1,0:T(8,128)(2,1)S(1)}, bf16[80,256]{1,0:T(8,128)(2,1)S(1)}, u32[]{:S(2)}, u32[]{:S(2)}) %collective-permute-start.2) | collective-permute-done | bytes 40992 | tf_op jit(solution)/shard_map/cond/branch_1_fun/ppermute | solution.py:49
  56.4 1.2 %collective-permute-done.3 = f32[64,256]{1,0:T(8,128)S(1)} collective-permute-done((f32[64,256]{1,0:T(8,128)S(1)}, f32[64,256]{1,0:T(8,128)S(1)}, u32[]{:S(2)}, u32[]{:S(2)}) %collective-permute-start.3) | collective-permute-done | bytes 65568 | tf_op jit(solution)/shard_map/cond/branch_1_fun/ppermute | solution.py:49
  57.7 0.8 %multiply_convert_fusion = bf16[512,128]{1,0:T(8,128)(2,1)} fusion(f32[512,128]{1,0:T(8,128)S(1)} %get-tuple-element.116.earlier_ref.refs_5_, bf16[512,128]{1,0:T(8,128)(2,1)S(1)} %get-tuple-element.124, bf16[512,128]{1,0:T(8,128)(2,1)S(1)} %collective-permute-done.21, bf16[512,128]{1,0:T(8,128)(2,1)S(1)} %collective-permute-done.20, ...), kind=kLoop, calls=%fused_computation.10 | loop fusion | flops 655360 | bytes 1179648 | tf_op jit(solution)/shard_map/convert_element_type | solution.py:548
  (66 shorter events, 5.4 us)
Async XLA Ops:
  1.6 9.5 %collective-permute-start.10 = (bf16[512,128]{1,0:T(8,128)(2,1)S(1)}, bf16[512,128]{1,0:T(8,128)(2,1)S(1)}, u32[]{:S(2)}, u32[]{:S(2)}) collective-permute-start(bf16[512,128]{1,0:T(8,128)(2,1)S(1)} %get-tuple-element.120.earlier_ref.refs_0_.refs_4_), channel_id=1, source_target_pairs={{0,24},{1,25},{2,26},{3,27},{4,28},{5,29},{6,30},{7,31},{8,16},{9,... | collective-permute-start | bytes 393224 | tf_op jit(solution)/shard_map/ppermute | solution.py:49
  5.6 6.3 %collective-permute-start.9 = (bf16[512,128]{1,0:T(8,128)(2,1)S(1)}, bf16[512,128]{1,0:T(8,128)(2,1)S(1)}, u32[]{:S(2)}, u32[]{:S(2)}) collective-permute-start(bf16[512,128]{1,0:T(8,128)(2,1)S(1)} %get-tuple-element.120.earlier_ref.refs_0_.refs_4_), channel_id=1, source_target_pairs={{0,16},{1,9},{2,18},{3,11},{4,20},{5,13},{6,22},{7,15},{8,24},{9,1... | collective-permute-start | bytes 393224 | tf_op jit(solution)/shard_map/ppermute | solution.py:49
  6.1 6.0 %collective-permute-start.8 = (bf16[512,128]{1,0:T(8,128)(2,1)S(1)}, bf16[512,128]{1,0:T(8,128)(2,1)S(1)}, u32[]{:S(2)}, u32[]{:S(2)}) collective-permute-start(bf16[512,128]{1,0:T(8,128)(2,1)S(1)} %get-tuple-element.120.earlier_ref.refs_0_.refs_4_), channel_id=1, source_target_pairs={{0,8},{1,17},{2,10},{3,19},{4,12},{5,21},{6,14},{7,23},{8,0},{9,25... | collective-permute-start | bytes 393224 | tf_op jit(solution)/shard_map/ppermute | solution.py:49
  12.5 11.3 %collective-permute-start.13 = (bf16[512,128]{1,0:T(8,128)(2,1)S(1)}, bf16[512,128]{1,0:T(8,128)(2,1)S(1)}, u32[]{:S(2)}, u32[]{:S(2)}) collective-permute-start(bf16[512,128]{1,0:T(8,128)(2,1)S(1)} %forward_3.1.earlier_ref), channel_id=1, source_target_pairs={{0,5},{1,4},{2,7},{3,6},{4,1},{5,0},{6,3},{7,2},{8,13},{9,12},{10,... | collective-permute-start | bytes 393224 | tf_op jit(solution)/shard_map/ppermute | solution.py:49
  16.0 12.1 %copy-start = (bf16[512,256]{1,0:T(8,128)(2,1)S(1)}, bf16[512,256]{1,0:T(8,128)(2,1)}, u32[]{:S(2)}) copy-start(bf16[512,256]{1,0:T(8,128)(2,1)} %refs_8_.1) | copy-start | bytes 786436
  16.0 12.1 %copy-start.1 = (bf16[128,256]{1,0:T(8,128)(2,1)S(1)}, bf16[128,256]{1,0:T(8,128)(2,1)}, u32[]{:S(2)}) copy-start(bf16[128,256]{1,0:T(8,128)(2,1)} %refs_6_.1) | copy-start | bytes 196612
  16.0 12.1 %copy-start.2 = (f32[256]{0:T(256)S(1)}, f32[256]{0:T(256)}, u32[]{:S(2)}) copy-start(f32[256]{0:T(256)} %param.24) | copy-start | bytes 3076
  16.0 2.2 %collective-permute-start = (bf16[1024,128]{1,0:T(8,128)(2,1)S(1)}, bf16[1024,128]{1,0:T(8,128)(2,1)S(1)}, u32[]{:S(2)}, u32[]{:S(2)}) collective-permute-start(bf16[1024,128]{1,0:T(8,128)(2,1)S(1)} %get-tuple-element.50), channel_id=1, source_target_pairs={{0,1},{1,0},{2,3},{3,2},{4,5},{5,4},{6,7},{7,6},{8,9},{9,8},{10,11... | collective-permute-start | bytes 786440 | tf_op jit(solution)/shard_map/cond/branch_1_fun/ppermute | solution.py:49
  18.3 8.2 %collective-permute-start.12 = (bf16[512,128]{1,0:T(8,128)(2,1)S(1)}, bf16[512,128]{1,0:T(8,128)(2,1)S(1)}, u32[]{:S(2)}, u32[]{:S(2)}) collective-permute-start(bf16[512,128]{1,0:T(8,128)(2,1)S(1)} %get-tuple-element.123), channel_id=1, source_target_pairs={{0,6},{1,7},{2,4},{3,5},{4,2},{5,3},{6,0},{7,1},{8,14},{9,15},{10,... | collective-permute-start | bytes 393224 | tf_op jit(solution)/shard_map/ppermute | solution.py:49
  20.0 8.1 %collective-permute-start.11 = (bf16[512,128]{1,0:T(8,128)(2,1)S(1)}, bf16[512,128]{1,0:T(8,128)(2,1)S(1)}, u32[]{:S(2)}, u32[]{:S(2)}) collective-permute-start(bf16[512,128]{1,0:T(8,128)(2,1)S(1)} %get-tuple-element.122), channel_id=1, source_target_pairs={{0,2},{1,3},{2,0},{3,1},{4,6},{5,7},{6,4},{7,5},{8,10},{9,11},{10,... | collective-permute-start | bytes 393224 | tf_op jit(solution)/shard_map/ppermute | solution.py:49
  22.3 1.4 %collective-permute-start.1 = (bf16[512,128]{1,0:T(8,128)(2,1)S(1)}, bf16[512,128]{1,0:T(8,128)(2,1)S(1)}, u32[]{:S(2)}, u32[]{:S(2)}) collective-permute-start(bf16[512,128]{1,0:T(8,128)(2,1)S(1)} %get-tuple-element.61), channel_id=1, source_target_pairs={{0,1},{1,0},{2,3},{3,2},{4,5},{5,4},{6,7},{7,6},{8,9},{9,8},{10,11... | collective-permute-start | bytes 393224 | tf_op jit(solution)/shard_map/cond/branch_1_fun/ppermute | solution.py:49
  28.6 13.2 %collective-permute-start.17 = (bf16[512,128]{1,0:T(8,128)(2,1)S(1)}, bf16[512,128]{1,0:T(8,128)(2,1)S(1)}, u32[]{:S(2)}, u32[]{:S(2)}) collective-permute-start(bf16[512,128]{1,0:T(8,128)(2,1)S(1)} %get-tuple-element.124), channel_id=1, source_target_pairs={{0,5},{1,4},{2,7},{3,6},{4,1},{5,0},{6,3},{7,2},{8,13},{9,12},{10,... | collective-permute-start | bytes 393224 | tf_op jit(solution)/shard_map/ppermute | solution.py:49
  30.3 11.5 %collective-permute-start.16 = (bf16[512,128]{1,0:T(8,128)(2,1)S(1)}, bf16[512,128]{1,0:T(8,128)(2,1)S(1)}, u32[]{:S(2)}, u32[]{:S(2)}) collective-permute-start(bf16[512,128]{1,0:T(8,128)(2,1)S(1)} %get-tuple-element.124), channel_id=1, source_target_pairs={{0,6},{1,7},{2,4},{3,5},{4,2},{5,3},{6,0},{7,1},{8,14},{9,15},{10,... | collective-permute-start | bytes 393224 | tf_op jit(solution)/shard_map/ppermute | solution.py:49
  31.5 10.4 %collective-permute-start.15 = (bf16[512,128]{1,0:T(8,128)(2,1)S(1)}, bf16[512,128]{1,0:T(8,128)(2,1)S(1)}, u32[]{:S(2)}, u32[]{:S(2)}) collective-permute-start(bf16[512,128]{1,0:T(8,128)(2,1)S(1)} %get-tuple-element.124), channel_id=1, source_target_pairs={{0,2},{1,3},{2,0},{3,1},{4,6},{5,7},{6,4},{7,5},{8,10},{9,11},{10,... | collective-permute-start | bytes 393224 | tf_op jit(solution)/shard_map/ppermute | solution.py:49
  31.9 1.3 %collective-permute-start.5 = (f32[80,256]{1,0:T(8,128)S(1)}, f32[80,256]{1,0:T(8,128)S(1)}, u32[]{:S(2)}, u32[]{:S(2)}) collective-permute-start(f32[80,256]{1,0:T(8,128)S(1)} %get-tuple-element.75), channel_id=1, source_target_pairs={{0,1},{1,0},{2,3},{3,2},{4,5},{5,4},{6,7},{7,6},{8,9},{9,8},{10,11... | collective-permute-start | bytes 245768 | tf_op jit(solution)/shard_map/cond/branch_1_fun/ppermute | solution.py:49
  32.1 2.9 %collective-permute-start.4 = (bf16[512,128]{1,0:T(8,128)(2,1)S(1)}, bf16[512,128]{1,0:T(8,128)(2,1)S(1)}, u32[]{:S(2)}, u32[]{:S(2)}) collective-permute-start(bf16[512,128]{1,0:T(8,128)(2,1)S(1)} %get-tuple-element.66.refs_0_), channel_id=1, source_target_pairs={{0,1},{1,0},{2,3},{3,2},{4,5},{5,4},{6,7},{7,6},{8,9},{9,8},{10,11... | collective-permute-start | bytes 393224 | tf_op jit(solution)/shard_map/cond/branch_1_fun/ppermute | solution.py:49
  33.2 4.4 %collective-permute-start.6 = (bf16[80,256]{1,0:T(8,128)(2,1)S(1)}, bf16[80,256]{1,0:T(8,128)(2,1)S(1)}, u32[]{:S(2)}, u32[]{:S(2)}) collective-permute-start(bf16[80,256]{1,0:T(8,128)(2,1)S(1)} %get-tuple-element.147), channel_id=1, source_target_pairs={{0,8},{1,17},{2,10},{3,19},{4,12},{5,21},{6,14},{7,23},{8,0},{9,25... | collective-permute-start | bytes 122888 | tf_op jit(solution)/shard_map/cond/branch_1_fun/ppermute | solution.py:49
  37.7 4.1 %collective-permute-start.7 = (bf16[80,256]{1,0:T(8,128)(2,1)S(1)}, bf16[80,256]{1,0:T(8,128)(2,1)S(1)}, u32[]{:S(2)}, u32[]{:S(2)}) collective-permute-start(bf16[80,256]{1,0:T(8,128)(2,1)S(1)} %fusion), channel_id=1, source_target_pairs={{0,16},{1,9},{2,18},{3,11},{4,20},{5,13},{6,22},{7,15},{8,24},{9,1... | collective-permute-start | bytes 122888 | tf_op jit(solution)/shard_map/cond/branch_1_fun/ppermute | solution.py:49
  41.9 2.1 %collective-permute-start.18 = (bf16[1024,128]{1,0:T(8,128)(2,1)S(1)}, bf16[1024,128]{1,0:T(8,128)(2,1)S(1)}, u32[]{:S(2)}, u32[]{:S(2)}) collective-permute-start(bf16[1024,128]{1,0:T(8,128)(2,1)S(1)} %constant_dynamic-update-slice_fusion.refs_0_), channel_id=1, source_target_pairs={{0,1},{1,0},{2,3},{3,2},{4,5},{5,4},{6,7},{7,6},{8,9},{9,8},{10,11... | collective-permute-start | bytes 786440 | tf_op jit(solution)/shard_map/ppermute | solution.py:49
  42.0 5.3 %collective-permute-start.14 = (bf16[80,256]{1,0:T(8,128)(2,1)S(1)}, bf16[80,256]{1,0:T(8,128)(2,1)S(1)}, u32[]{:S(2)}, u32[]{:S(2)}) collective-permute-start(bf16[80,256]{1,0:T(8,128)(2,1)S(1)} %convert_element_type.77), channel_id=1, source_target_pairs={{0,2},{1,3},{2,0},{3,1},{4,6},{5,7},{6,4},{7,5},{8,10},{9,11},{10,... | collective-permute-start | bytes 122888 | tf_op jit(solution)/shard_map/ppermute | solution.py:49
  47.3 10.4 %collective-permute-start.19 = (bf16[512,128]{1,0:T(8,128)(2,1)S(1)}, bf16[512,128]{1,0:T(8,128)(2,1)S(1)}, u32[]{:S(2)}, u32[]{:S(2)}) collective-permute-start(bf16[512,128]{1,0:T(8,128)(2,1)S(1)} %get-tuple-element.142), channel_id=1, source_target_pairs={{0,8},{1,17},{2,10},{3,19},{4,12},{5,21},{6,14},{7,23},{8,0},{9,25... | collective-permute-start | bytes 393224 | tf_op jit(solution)/shard_map/ppermute | solution.py:49
  49.4 8.3 %collective-permute-start.20 = (bf16[512,128]{1,0:T(8,128)(2,1)S(1)}, bf16[512,128]{1,0:T(8,128)(2,1)S(1)}, u32[]{:S(2)}, u32[]{:S(2)}) collective-permute-start(bf16[512,128]{1,0:T(8,128)(2,1)S(1)} %get-tuple-element.143), channel_id=1, source_target_pairs={{0,16},{1,9},{2,18},{3,11},{4,20},{5,13},{6,22},{7,15},{8,24},{9,1... | collective-permute-start | bytes 393224 | tf_op jit(solution)/shard_map/ppermute | solution.py:49
  50.6 7.1 %collective-permute-start.21 = (bf16[512,128]{1,0:T(8,128)(2,1)S(1)}, bf16[512,128]{1,0:T(8,128)(2,1)S(1)}, u32[]{:S(2)}, u32[]{:S(2)}) collective-permute-start(bf16[512,128]{1,0:T(8,128)(2,1)S(1)} %get-tuple-element.144), channel_id=1, source_target_pairs={{0,24},{1,25},{2,26},{3,27},{4,28},{5,29},{6,30},{7,31},{8,16},{9,... | collective-permute-start | bytes 393224 | tf_op jit(solution)/shard_map/ppermute | solution.py:49
  50.9 5.4 %collective-permute-start.2 = (bf16[80,256]{1,0:T(8,128)(2,1)S(1)}, bf16[80,256]{1,0:T(8,128)(2,1)S(1)}, u32[]{:S(2)}, u32[]{:S(2)}) collective-permute-start(bf16[80,256]{1,0:T(8,128)(2,1)S(1)} %fusion.1), channel_id=1, source_target_pairs={{0,4},{1,5},{2,6},{3,7},{4,0},{5,1},{6,2},{7,3},{8,12},{9,13},{10,... | collective-permute-start | bytes 122888 | tf_op jit(solution)/shard_map/cond/branch_1_fun/ppermute | solution.py:49
  56.3 1.3 %collective-permute-start.3 = (f32[64,256]{1,0:T(8,128)S(1)}, f32[64,256]{1,0:T(8,128)S(1)}, u32[]{:S(2)}, u32[]{:S(2)}) collective-permute-start(f32[64,256]{1,0:T(8,128)S(1)} %slice.24), channel_id=1, source_target_pairs={{0,1},{1,0},{2,3},{3,2},{4,5},{5,4},{6,7},{7,6},{8,9},{9,8},{10,11... | collective-permute-start | bytes 196616 | tf_op jit(solution)/shard_map/cond/branch_1_fun/ppermute | solution.py:49
  57.6 0.8 %copy-start.3 = (bf16[512,256]{1,0:T(8,128)(2,1)}, bf16[512,256]{1,0:T(8,128)(2,1)S(1)}, u32[]{:S(2)}) copy-start(bf16[512,256]{1,0:T(8,128)(2,1)S(1)} %get-tuple-element.112) | copy-start | bytes 786436
  57.7 0.8 %copy-start.4 = (f32[128,256]{1,0:T(8,128)}, f32[128,256]{1,0:T(8,128)S(1)}, u32[]{:S(2)}) copy-start(f32[128,256]{1,0:T(8,128)S(1)} %get-tuple-element.114) | copy-start | bytes 393220
  57.7 0.8 %copy-start.5 = (f32[256]{0:T(256)}, f32[256]{0:T(256)S(1)}, u32[]{:S(2)}) copy-start(f32[256]{0:T(256)S(1)} %get-tuple-element.115) | copy-start | bytes 3076

commit v9 on v8

--- a/solution.py
+++ b/solution.py
@@ -433,7 +433,7 @@
         near, far = add(keep[:row_count], other[:row_count]), add(keep[row_count:], other[row_count:])
         return near, far, other[:TOKEN_ROWS]
 
-    near, far, token = block(pair_sums, *forward((1, 2), 16, False, part3))
+    near, far, token = block(pair_sums, *forward((1, 2), 26, False, part3))
     came2 = move(far, pair_partner(2, False))
     came1 = move(near, pair_partner(1, False))
 
@@ -499,7 +499,7 @@
         )(core[None].astype(jnp.int32), aggregated, pre_grad)
         grad = keep + swap_cores(send)
         token_shape = jax.ShapeDtypeStruct((TOKEN_ROWS, feat_width), BF)
-        *total, token = backward((0,), 16, [block_shape] * rep_count + [token_shape], scaled_grad, other)
+        *total, token = backward((0,), 24, [block_shape] * rep_count + [token_shape], scaled_grad, other)
         for n in range(rep_bits()):
             came = move(grad.astype(BF), rep_partner(1 << n))
             if n == 0:

time: 58.7 us -> 59.2 us (level)
  Pallas kernels: 15 us -> 15.7 us
  transfers between devices with their start and end apart: 22 -> 22, of which waited for: 11 -> 11; matrix products, arithmetic and copies ran while one was open for 2% -> 2% of each run, Pallas kernels for 23% -> 24%
where the time goes in v9:
time: 59.2 us; the launch traced here: 59 us
  starting transfers between devices  25.3 us (43%)
  Pallas kernels  15.7 us (27%)
  waiting for transfers between devices  14.2 us (24%)
  other arithmetic  1.95 us (3%)
  between operations  1.54 us (3%)
    ppermute x22, starting transfers between devices, move(): return lax.ppermute(value, BOTH, pairs)  25.3 us
    ppermute x22, waiting for transfers between devices, move(): return lax.ppermute(value, BOTH, pairs)  14.2 us
    pallas_call x2, Pallas kernels, backward(): pl.pallas_call(functools.partial(backward_kernel, places, unroll), out_sh...  6.15 us
    pallas_call x3, Pallas kernels, forward(): pl.pallas_call(functools.partial(forward_kernel, places, unroll, stream),...  4.73 us
    pallas_call x1, Pallas kernels, stage(): pl.pallas_call(stage_kernel, out_shape=jax.ShapeDtypeStruct((slot_total,...  2.5 us
  transfers between devices with their start and end apart: 22, of which 11 were waited for; matrix products, arithmetic and copies ran while one was open for 2% of the time, Pallas kernels for 24%

profile of v9, /device:TPU:0, one launch (start us, length us, event | category | flops | bytes accessed | tf_op | source)
XLA Modules:
  0.0 59.0 jit_solution(865170817691771464)
XLA Ops:
  0.6 1.0 %prepare.1 = (bf16[512,128]{1,0:T(8,128)(2,1)S(1)}, f32[512,128]{1,0:T(8,128)S(1)}) custom-call(s32[4,128]{1,0:T(4,128)} %bitcast.18, bf16[512,128]{1,0:T(8,128)(2,1)} %features_hbm.1), custom_call_target="tpu_custom_call" | custom-call | bytes 1024 | tf_op jit(solution)/shard_map/prepare/pallas_call | solution.py:369
  1.6 4.0 %collective-permute-start.10 = (bf16[512,128]{1,0:T(8,128)(2,1)S(1)}, bf16[512,128]{1,0:T(8,128)(2,1)S(1)}, u32[]{:S(2)}, u32[]{:S(2)}) collective-permute-start(bf16[512,128]{1,0:T(8,128)(2,1)S(1)} %get-tuple-element.120.earlier_ref.refs_0_.refs_4_), channel_id=1, source_target_pairs={{0,24},{1,25},{2,26},{3,27},{4,28},{5,29},{6,30},{7,31},{8,16},{9,... | collective-permute-start | bytes 393224 | tf_op jit(solution)/shard_map/ppermute | solution.py:49
  6.9 0.7 %fusion.2 = (s32[160]{0:T(256)S(1)}, s32[160]{0:T(256)S(1)}, s32[160]{0:T(256)S(1)}) fusion(s32[]{:T(128)} %select_n.68, s32[160]{0:T(256)} %bitcast.19, s32[]{:T(128)S(6)} %axis_index.17, s32[160]{0:T(256)} %bitcast.20, pred[]{:T(512)S(6)} %eq.21), kind=kLoop, calls=%fused_computation.30 | loop fusion | flops 10240 | bytes 3209 | tf_op jit(solution)/shard_map/add | solution.py:352
  7.8 2.5 %stage_tiles.1.w_ref = bf16[160,128,128]{2,1,0:T(8,128)(2,1)S(1)} custom-call(bf16[160,128,128]{2,1,0:T(8,128)(2,1)} %bitcast.14, bf16[512,128]{1,0:T(8,128)(2,1)S(1)} %get-tuple-element.120.earlier_ref.refs_0_.refs_4_), custom_call_target="tpu_custom_call" | custom-call | bytes 10485760 | tf_op jit(solution)/shard_map/stage_tiles/pallas_call | solution.py:388
  11.1 0.8 %collective-permute-done.9.refs_2_ = bf16[512,128]{1,0:T(8,128)(2,1)S(1)} collective-permute-done((bf16[512,128]{1,0:T(8,128)(2,1)S(1)}, bf16[512,128]{1,0:T(8,128)(2,1)S(1)}, u32[]{:S(2)}, u32[]{:S(2)}) %collective-permute-start.9) | collective-permute-done | bytes 131104 | tf_op jit(solution)/shard_map/ppermute | solution.py:49
  12.5 1.8 %collective-permute-start.13 = (bf16[512,128]{1,0:T(8,128)(2,1)S(1)}, bf16[512,128]{1,0:T(8,128)(2,1)S(1)}, u32[]{:S(2)}, u32[]{:S(2)}) collective-permute-start(bf16[512,128]{1,0:T(8,128)(2,1)S(1)} %forward_3.1.earlier_ref), channel_id=1, source_target_pairs={{0,5},{1,4},{2,7},{3,6},{4,1},{5,0},{6,3},{7,2},{8,13},{9,12},{10,... | collective-permute-start | bytes 393224 | tf_op jit(solution)/shard_map/ppermute | solution.py:49
  14.2 1.8 %forward_1_2.1 = (bf16[1024,128]{1,0:T(8,128)(2,1)S(1)}, bf16[1024,128]{1,0:T(8,128)(2,1)S(1)}) custom-call(bf16[512,128]{1,0:T(8,128)(2,1)S(1)} %forward_3.1.earlier_ref, s32[8]{0:T(128)S(4)} %get-tuple-element.117.bounds_ref, s32[160]{0:T(256)S(4)} %get-tuple-element.118.row_ref, s32[160]{0:T(256)S(4)} %get-tuple-element.119.col_ref, ...), custom_call_target="tpu_custom_call" | custom-call | bytes 1024 | tf_op jit(solution)/shard_map/forward_1_2/pallas_call | solution.py:410
  16.1 1.9 %conditional.4 = (bf16[512,128]{1,0:T(8,128)(2,1)S(1)}, bf16[512,128]{1,0:T(8,128)(2,1)S(1)}, bf16[16,128]{1,0:T(8,128)(2,1)S(1)}) conditional(s32[]{:T(128)} %convert_element_type.75, () %tuple.40, (bf16[1024,128]{1,0:T(8,128)(2,1)S(1)}, bf16[1024,128]{1,0:T(8,128)(2,1)S(1)}) %forward_1_2.1), branch_computations={%region_1.2_spmd, %region_2.3_spmd} | conditional | flops 524288 | bytes 1843264 | solution.py:54
  16.7 1.2 %collective-permute-done = bf16[1024,128]{1,0:T(8,128)(2,1)S(1)} collective-permute-done((bf16[1024,128]{1,0:T(8,128)(2,1)S(1)}, bf16[1024,128]{1,0:T(8,128)(2,1)S(1)}, u32[]{:S(2)}, u32[]{:S(2)}) %collective-permute-start) | collective-permute-done | bytes 262176 | tf_op jit(solution)/shard_map/cond/branch_1_fun/ppermute | solution.py:49
  18.0 1.4 %collective-permute-start.12 = (bf16[512,128]{1,0:T(8,128)(2,1)S(1)}, bf16[512,128]{1,0:T(8,128)(2,1)S(1)}, u32[]{:S(2)}, u32[]{:S(2)}) collective-permute-start(bf16[512,128]{1,0:T(8,128)(2,1)S(1)} %get-tuple-element.123), channel_id=1, source_target_pairs={{0,6},{1,7},{2,4},{3,5},{4,2},{5,3},{6,0},{7,1},{8,14},{9,15},{10,... | collective-permute-start | bytes 393224 | tf_op jit(solution)/shard_map/ppermute | solution.py:49
  20.1 4.0 %conditional.5 = (bf16[512,128]{1,0:T(8,128)(2,1)S(1)}) conditional(s32[]{:T(128)} %convert_element_type.75, () %tuple.39, (bf16[16,128]{1,0:T(8,128)(2,1)S(1)}, s32[8]{0:T(128)S(4)}, s32[160]{0:T(256)S(4)}, s32[160]{0:T(256)S(4)}, bf16[160,128,128]{2,1,0:T(8,128)(2,1)}, /*index=5*/bf16[512,128]{1,0:T(8,128)(2,1)S(1)}, ...), branch_computations={%region_3.4_spmd, %region_4.5_spmd} | conditional | flops 262144 | bytes 918576 | solution.py:54
  20.1 2.6 %forward_0.1 = (bf16[512,128]{1,0:T(8,128)(2,1)S(1)}, bf16[512,128]{1,0:T(8,128)(2,1)S(1)}) custom-call(bf16[16,128]{1,0:T(8,128)(2,1)S(1)} %get-tuple-element.51.earlier_ref, s32[8]{0:T(128)S(4)} %get-tuple-element.52.bounds_ref, s32[160]{0:T(256)S(4)} %get-tuple-element.53.row_ref, s32[160]{0:T(256)S(4)} %get-tuple-element.54.col_ref, ...), custom_call_target="tpu_custom_call" | custom-call | bytes 1024 | tf_op jit(solution)/shard_map/cond/branch_1_fun/forward_0/pallas_call | solution.py:410
  22.8 1.3 %collective-permute-done.1 = bf16[512,128]{1,0:T(8,128)(2,1)S(1)} collective-permute-done((bf16[512,128]{1,0:T(8,128)(2,1)S(1)}, bf16[512,128]{1,0:T(8,128)(2,1)S(1)}, u32[]{:S(2)}, u32[]{:S(2)}) %collective-permute-start.1) | collective-permute-done | bytes 131104 | tf_op jit(solution)/shard_map/cond/branch_1_fun/ppermute | solution.py:49
  24.2 2.0 %collective-permute-done.12.refs_0_ = bf16[512,128]{1,0:T(8,128)(2,1)S(1)} collective-permute-done((bf16[512,128]{1,0:T(8,128)(2,1)S(1)}, bf16[512,128]{1,0:T(8,128)(2,1)S(1)}, u32[]{:S(2)}, u32[]{:S(2)}) %collective-permute-start.12) | collective-permute-done | bytes 131104 | tf_op jit(solution)/shard_map/ppermute | solution.py:49
  26.2 1.5 %collective-permute-done.11.refs_0_ = bf16[512,128]{1,0:T(8,128)(2,1)S(1)} collective-permute-done((bf16[512,128]{1,0:T(8,128)(2,1)S(1)}, bf16[512,128]{1,0:T(8,128)(2,1)S(1)}, u32[]{:S(2)}, u32[]{:S(2)}) %collective-permute-start.11) | collective-permute-done | bytes 131104 | tf_op jit(solution)/shard_map/ppermute | solution.py:49
  28.2 2.0 %collective-permute-start.17 = (bf16[512,128]{1,0:T(8,128)(2,1)S(1)}, bf16[512,128]{1,0:T(8,128)(2,1)S(1)}, u32[]{:S(2)}, u32[]{:S(2)}) collective-permute-start(bf16[512,128]{1,0:T(8,128)(2,1)S(1)} %get-tuple-element.124), channel_id=1, source_target_pairs={{0,5},{1,4},{2,7},{3,6},{4,1},{5,0},{6,3},{7,2},{8,13},{9,12},{10,... | collective-permute-start | bytes 393224 | tf_op jit(solution)/shard_map/ppermute | solution.py:49
  30.3 1.2 %collective-permute-start.16 = (bf16[512,128]{1,0:T(8,128)(2,1)S(1)}, bf16[512,128]{1,0:T(8,128)(2,1)S(1)}, u32[]{:S(2)}, u32[]{:S(2)}) collective-permute-start(bf16[512,128]{1,0:T(8,128)(2,1)S(1)} %get-tuple-element.124), channel_id=1, source_target_pairs={{0,6},{1,7},{2,4},{3,5},{4,2},{5,3},{6,0},{7,1},{8,14},{9,15},{10,... | collective-permute-start | bytes 393224 | tf_op jit(solution)/shard_map/ppermute | solution.py:49
  31.6 10.1 %conditional.6 = (bf16[512,128]{1,0:T(8,128)(2,1)S(1)}, bf16[512,128]{1,0:T(8,128)(2,1)S(1)}, bf16[512,128]{1,0:T(8,128)(2,1)S(1)}, bf16[512,128]{1,0:T(8,128)(2,1)S(1)}, f32[80,256]{1,0:T(8,128)S(1)}) conditional(s32[]{:T(128)} %convert_element_type.75, () %tuple.38, (bf16[512,128]{1,0:T(8,128)(2,1)S(1)}, s32[8]{0:T(128)S(4)}, s32[160]{0:T(256)S(4)}, ...), branch_computations={%region_5.6_spmd, %region_6.7_spmd} | conditional | flops 184320 | bytes 1879240 | solution.py:54
  32.4 0.8 %collective-permute-done.5 = f32[80,256]{1,0:T(8,128)S(1)} collective-permute-done((f32[80,256]{1,0:T(8,128)S(1)}, f32[80,256]{1,0:T(8,128)S(1)}, u32[]{:S(2)}, u32[]{:S(2)}) %collective-permute-start.5) | collective-permute-done | bytes 81952 | tf_op jit(solution)/shard_map/cond/branch_1_fun/ppermute | solution.py:49
  33.2 1.9 %collective-permute-start.6 = (bf16[80,256]{1,0:T(8,128)(2,1)S(1)}, bf16[80,256]{1,0:T(8,128)(2,1)S(1)}, u32[]{:S(2)}, u32[]{:S(2)}) collective-permute-start(bf16[80,256]{1,0:T(8,128)(2,1)S(1)} %get-tuple-element.147), channel_id=1, source_target_pairs={{0,8},{1,17},{2,10},{3,19},{4,12},{5,21},{6,14},{7,23},{8,0},{9,25... | collective-permute-start | bytes 122888 | tf_op jit(solution)/shard_map/cond/branch_1_fun/ppermute | solution.py:49
  35.1 2.5 %backward_0.1 = (bf16[512,128]{1,0:T(8,128)(2,1)S(1)}, bf16[512,128]{1,0:T(8,128)(2,1)S(1)}, bf16[512,128]{1,0:T(8,128)(2,1)S(1)}, bf16[512,128]{1,0:T(8,128)(2,1)S(1)}, bf16[16,128]{1,0:T(8,128)(2,1)S(1)}) custom-call(s32[8]{0:T(128)S(4)} %get-tuple-element.62.bounds_ref, s32[160]{0:T(256)S(4)} %get-tuple-element.63.row_ref, ...), custom_call_target="tpu_custom_call" | custom-call | bytes 1024 | tf_op jit(solution)/shard_map/cond/branch_1_fun/backward_0/pallas_call | solution.py:470
  37.6 1.5 %collective-permute-start.7 = (bf16[80,256]{1,0:T(8,128)(2,1)S(1)}, bf16[80,256]{1,0:T(8,128)(2,1)S(1)}, u32[]{:S(2)}, u32[]{:S(2)}) collective-permute-start(bf16[80,256]{1,0:T(8,128)(2,1)S(1)} %fusion), channel_id=1, source_target_pairs={{0,16},{1,9},{2,18},{3,11},{4,20},{5,13},{6,22},{7,15},{8,24},{9,1... | collective-permute-start | bytes 122888 | tf_op jit(solution)/shard_map/cond/branch_1_fun/ppermute | solution.py:49
  39.2 2.5 %collective-permute-done.7 = bf16[80,256]{1,0:T(8,128)(2,1)S(1)} collective-permute-done((bf16[80,256]{1,0:T(8,128)(2,1)S(1)}, bf16[80,256]{1,0:T(8,128)(2,1)S(1)}, u32[]{:S(2)}, u32[]{:S(2)}) %collective-permute-start.7) | collective-permute-done | bytes 40992 | tf_op jit(solution)/shard_map/cond/branch_1_fun/ppermute | solution.py:49
  42.0 2.1 %collective-permute-start.14 = (bf16[80,256]{1,0:T(8,128)(2,1)S(1)}, bf16[80,256]{1,0:T(8,128)(2,1)S(1)}, u32[]{:S(2)}, u32[]{:S(2)}) collective-permute-start(bf16[80,256]{1,0:T(8,128)(2,1)S(1)} %convert_element_type.77), channel_id=1, source_target_pairs={{0,2},{1,3},{2,0},{3,1},{4,6},{5,7},{6,4},{7,5},{8,10},{9,11},{10,... | collective-permute-start | bytes 122888 | tf_op jit(solution)/shard_map/ppermute | solution.py:49
  44.1 3.6 %backward_1_2_3.1 = (f32[512,128]{1,0:T(8,128)S(1)}, bf16[512,128]{1,0:T(8,128)(2,1)S(1)}, bf16[512,128]{1,0:T(8,128)(2,1)S(1)}, bf16[512,128]{1,0:T(8,128)(2,1)S(1)}) custom-call(s32[8]{0:T(128)S(4)} %get-tuple-element.117.bounds_ref, s32[160]{0:T(256)S(4)} %get-tuple-element.118.row_ref, s32[160]{0:T(256)S(4)} %get-tuple-element.119.col_ref, ...), custom_call_target="tpu_custom_call" | custom-call | bytes 1024 | tf_op jit(solution)/shard_map/backward_1_2_3/pallas_call | solution.py:470
  47.8 1.4 %collective-permute-start.19 = (bf16[512,128]{1,0:T(8,128)(2,1)S(1)}, bf16[512,128]{1,0:T(8,128)(2,1)S(1)}, u32[]{:S(2)}, u32[]{:S(2)}) collective-permute-start(bf16[512,128]{1,0:T(8,128)(2,1)S(1)} %get-tuple-element.142), channel_id=1, source_target_pairs={{0,8},{1,17},{2,10},{3,19},{4,12},{5,21},{6,14},{7,23},{8,0},{9,25... | collective-permute-start | bytes 393224 | tf_op jit(solution)/shard_map/ppermute | solution.py:49
  49.9 1.4 %collective-permute-start.21 = (bf16[512,128]{1,0:T(8,128)(2,1)S(1)}, bf16[512,128]{1,0:T(8,128)(2,1)S(1)}, u32[]{:S(2)}, u32[]{:S(2)}) collective-permute-start(bf16[512,128]{1,0:T(8,128)(2,1)S(1)} %get-tuple-element.144), channel_id=1, source_target_pairs={{0,24},{1,25},{2,26},{3,27},{4,28},{5,29},{6,30},{7,31},{8,16},{9,... | collective-permute-start | bytes 393224 | tf_op jit(solution)/shard_map/ppermute | solution.py:49
  51.4 6.8 %conditional.7 = (f32[128,256]{1,0:T(8,128)S(1)}, f32[256]{0:T(256)S(1)}, bf16[512,256]{1,0:T(8,128)(2,1)S(1)}) conditional(s32[]{:T(128)} %convert_element_type.75, () %tuple.37, (s32[]{:T(128)}, bf16[80,256]{1,0:T(8,128)(2,1)S(1)}, f32[80,256]{1,0:T(8,128)S(1)}, bf16[512,256]{1,0:T(8,128)(2,1)S(1)}) %tuple.43), branch_computations={%region_7.8_spmd, %region_8.9_spmd} | conditional | flops 262145 | bytes 1231986 | solution.py:54
  51.4 2.9 %collective-permute-start.2 = (bf16[80,256]{1,0:T(8,128)(2,1)S(1)}, bf16[80,256]{1,0:T(8,128)(2,1)S(1)}, u32[]{:S(2)}, u32[]{:S(2)}) collective-permute-start(bf16[80,256]{1,0:T(8,128)(2,1)S(1)} %fusion.1), channel_id=1, source_target_pairs={{0,4},{1,5},{2,6},{3,7},{4,0},{5,1},{6,2},{7,3},{8,12},{9,13},{10,... | collective-permute-start | bytes 122888 | tf_op jit(solution)/shard_map/cond/branch_1_fun/ppermute | solution.py:49
  54.3 2.5 %collective-permute-done.2 = bf16[80,256]{1,0:T(8,128)(2,1)S(1)} collective-permute-done((bf16[80,256]{1,0:T(8,128)(2,1)S(1)}, bf16[80,256]{1,0:T(8,128)(2,1)S(1)}, u32[]{:S(2)}, u32[]{:S(2)}) %collective-permute-start.2) | collective-permute-done | bytes 40992 | tf_op jit(solution)/shard_map/cond/branch_1_fun/ppermute | solution.py:49
  56.9 1.2 %collective-permute-done.3 = f32[64,256]{1,0:T(8,128)S(1)} collective-permute-done((f32[64,256]{1,0:T(8,128)S(1)}, f32[64,256]{1,0:T(8,128)S(1)}, u32[]{:S(2)}, u32[]{:S(2)}) %collective-permute-start.3) | collective-permute-done | bytes 65568 | tf_op jit(solution)/shard_map/cond/branch_1_fun/ppermute | solution.py:49
  58.2 0.8 %multiply_convert_fusion = bf16[512,128]{1,0:T(8,128)(2,1)} fusion(f32[512,128]{1,0:T(8,128)S(1)} %get-tuple-element.116.earlier_ref.refs_5_, bf16[512,128]{1,0:T(8,128)(2,1)S(1)} %get-tuple-element.124, bf16[512,128]{1,0:T(8,128)(2,1)S(1)} %collective-permute-done.21, bf16[512,128]{1,0:T(8,128)(2,1)S(1)} %collective-permute-done.20, ...), kind=kLoop, calls=%fused_computation.10 | loop fusion | flops 655360 | bytes 1179648 | tf_op jit(solution)/shard_map/convert_element_type | solution.py:548
  (66 shorter events, 6.4 us)
Async XLA Ops:
  1.6 9.5 %collective-permute-start.10 = (bf16[512,128]{1,0:T(8,128)(2,1)S(1)}, bf16[512,128]{1,0:T(8,128)(2,1)S(1)}, u32[]{:S(2)}, u32[]{:S(2)}) collective-permute-start(bf16[512,128]{1,0:T(8,128)(2,1)S(1)} %get-tuple-element.120.earlier_ref.refs_0_.refs_4_), channel_id=1, source_target_pairs={{0,24},{1,25},{2,26},{3,27},{4,28},{5,29},{6,30},{7,31},{8,16},{9,... | collective-permute-start | bytes 393224 | tf_op jit(solution)/shard_map/ppermute | solution.py:49
  5.6 6.3 %collective-permute-start.9 = (bf16[512,128]{1,0:T(8,128)(2,1)S(1)}, bf16[512,128]{1,0:T(8,128)(2,1)S(1)}, u32[]{:S(2)}, u32[]{:S(2)}) collective-permute-start(bf16[512,128]{1,0:T(8,128)(2,1)S(1)} %get-tuple-element.120.earlier_ref.refs_0_.refs_4_), channel_id=1, source_target_pairs={{0,16},{1,9},{2,18},{3,11},{4,20},{5,13},{6,22},{7,15},{8,24},{9,1... | collective-permute-start | bytes 393224 | tf_op jit(solution)/shard_map/ppermute | solution.py:49
  6.1 6.0 %collective-permute-start.8 = (bf16[512,128]{1,0:T(8,128)(2,1)S(1)}, bf16[512,128]{1,0:T(8,128)(2,1)S(1)}, u32[]{:S(2)}, u32[]{:S(2)}) collective-permute-start(bf16[512,128]{1,0:T(8,128)(2,1)S(1)} %get-tuple-element.120.earlier_ref.refs_0_.refs_4_), channel_id=1, source_target_pairs={{0,8},{1,17},{2,10},{3,19},{4,12},{5,21},{6,14},{7,23},{8,0},{9,25... | collective-permute-start | bytes 393224 | tf_op jit(solution)/shard_map/ppermute | solution.py:49
  12.5 11.7 %collective-permute-start.13 = (bf16[512,128]{1,0:T(8,128)(2,1)S(1)}, bf16[512,128]{1,0:T(8,128)(2,1)S(1)}, u32[]{:S(2)}, u32[]{:S(2)}) collective-permute-start(bf16[512,128]{1,0:T(8,128)(2,1)S(1)} %forward_3.1.earlier_ref), channel_id=1, source_target_pairs={{0,5},{1,4},{2,7},{3,6},{4,1},{5,0},{6,3},{7,2},{8,13},{9,12},{10,... | collective-permute-start | bytes 393224 | tf_op jit(solution)/shard_map/ppermute | solution.py:49
  16.1 11.7 %copy-start = (bf16[512,256]{1,0:T(8,128)(2,1)S(1)}, bf16[512,256]{1,0:T(8,128)(2,1)}, u32[]{:S(2)}) copy-start(bf16[512,256]{1,0:T(8,128)(2,1)} %refs_8_.1) | copy-start | bytes 786436
  16.1 11.6 %copy-start.1 = (bf16[128,256]{1,0:T(8,128)(2,1)S(1)}, bf16[128,256]{1,0:T(8,128)(2,1)}, u32[]{:S(2)}) copy-start(bf16[128,256]{1,0:T(8,128)(2,1)} %refs_6_.1) | copy-start | bytes 196612
  16.1 11.6 %copy-start.2 = (f32[256]{0:T(256)S(1)}, f32[256]{0:T(256)}, u32[]{:S(2)}) copy-start(f32[256]{0:T(256)} %param.24) | copy-start | bytes 3076
  16.1 1.8 %collective-permute-start = (bf16[1024,128]{1,0:T(8,128)(2,1)S(1)}, bf16[1024,128]{1,0:T(8,128)(2,1)S(1)}, u32[]{:S(2)}, u32[]{:S(2)}) collective-permute-start(bf16[1024,128]{1,0:T(8,128)(2,1)S(1)} %get-tuple-element.50), channel_id=1, source_target_pairs={{0,1},{1,0},{2,3},{3,2},{4,5},{5,4},{6,7},{7,6},{8,9},{9,8},{10,11... | collective-permute-start | bytes 786440 | tf_op jit(solution)/shard_map/cond/branch_1_fun/ppermute | solution.py:49
  18.0 8.2 %collective-permute-start.12 = (bf16[512,128]{1,0:T(8,128)(2,1)S(1)}, bf16[512,128]{1,0:T(8,128)(2,1)S(1)}, u32[]{:S(2)}, u32[]{:S(2)}) collective-permute-start(bf16[512,128]{1,0:T(8,128)(2,1)S(1)} %get-tuple-element.123), channel_id=1, source_target_pairs={{0,6},{1,7},{2,4},{3,5},{4,2},{5,3},{6,0},{7,1},{8,14},{9,15},{10,... | collective-permute-start | bytes 393224 | tf_op jit(solution)/shard_map/ppermute | solution.py:49
  19.4 8.3 %collective-permute-start.11 = (bf16[512,128]{1,0:T(8,128)(2,1)S(1)}, bf16[512,128]{1,0:T(8,128)(2,1)S(1)}, u32[]{:S(2)}, u32[]{:S(2)}) collective-permute-start(bf16[512,128]{1,0:T(8,128)(2,1)S(1)} %get-tuple-element.122), channel_id=1, source_target_pairs={{0,2},{1,3},{2,0},{3,1},{4,6},{5,7},{6,4},{7,5},{8,10},{9,11},{10,... | collective-permute-start | bytes 393224 | tf_op jit(solution)/shard_map/ppermute | solution.py:49
  22.7 1.4 %collective-permute-start.1 = (bf16[512,128]{1,0:T(8,128)(2,1)S(1)}, bf16[512,128]{1,0:T(8,128)(2,1)S(1)}, u32[]{:S(2)}, u32[]{:S(2)}) collective-permute-start(bf16[512,128]{1,0:T(8,128)(2,1)S(1)} %get-tuple-element.61), channel_id=1, source_target_pairs={{0,1},{1,0},{2,3},{3,2},{4,5},{5,4},{6,7},{7,6},{8,9},{9,8},{10,11... | collective-permute-start | bytes 393224 | tf_op jit(solution)/shard_map/cond/branch_1_fun/ppermute | solution.py:49
  28.2 13.5 %collective-permute-start.17 = (bf16[512,128]{1,0:T(8,128)(2,1)S(1)}, bf16[512,128]{1,0:T(8,128)(2,1)S(1)}, u32[]{:S(2)}, u32[]{:S(2)}) collective-permute-start(bf16[512,128]{1,0:T(8,128)(2,1)S(1)} %get-tuple-element.124), channel_id=1, source_target_pairs={{0,5},{1,4},{2,7},{3,6},{4,1},{5,0},{6,3},{7,2},{8,13},{9,12},{10,... | collective-permute-start | bytes 393224 | tf_op jit(solution)/shard_map/ppermute | solution.py:49
  30.3 11.5 %collective-permute-start.16 = (bf16[512,128]{1,0:T(8,128)(2,1)S(1)}, bf16[512,128]{1,0:T(8,128)(2,1)S(1)}, u32[]{:S(2)}, u32[]{:S(2)}) collective-permute-start(bf16[512,128]{1,0:T(8,128)(2,1)S(1)} %get-tuple-element.124), channel_id=1, source_target_pairs={{0,6},{1,7},{2,4},{3,5},{4,2},{5,3},{6,0},{7,1},{8,14},{9,15},{10,... | collective-permute-start | bytes 393224 | tf_op jit(solution)/shard_map/ppermute | solution.py:49
  31.5 10.4 %collective-permute-start.15 = (bf16[512,128]{1,0:T(8,128)(2,1)S(1)}, bf16[512,128]{1,0:T(8,128)(2,1)S(1)}, u32[]{:S(2)}, u32[]{:S(2)}) collective-permute-start(bf16[512,128]{1,0:T(8,128)(2,1)S(1)} %get-tuple-element.124), channel_id=1, source_target_pairs={{0,2},{1,3},{2,0},{3,1},{4,6},{5,7},{6,4},{7,5},{8,10},{9,11},{10,... | collective-permute-start | bytes 393224 | tf_op jit(solution)/shard_map/ppermute | solution.py:49
  31.9 1.3 %collective-permute-start.5 = (f32[80,256]{1,0:T(8,128)S(1)}, f32[80,256]{1,0:T(8,128)S(1)}, u32[]{:S(2)}, u32[]{:S(2)}) collective-permute-start(f32[80,256]{1,0:T(8,128)S(1)} %get-tuple-element.75), channel_id=1, source_target_pairs={{0,1},{1,0},{2,3},{3,2},{4,5},{5,4},{6,7},{7,6},{8,9},{9,8},{10,11... | collective-permute-start | bytes 245768 | tf_op jit(solution)/shard_map/cond/branch_1_fun/ppermute | solution.py:49
  32.1 3.0 %collective-permute-start.4 = (bf16[512,128]{1,0:T(8,128)(2,1)S(1)}, bf16[512,128]{1,0:T(8,128)(2,1)S(1)}, u32[]{:S(2)}, u32[]{:S(2)}) collective-permute-start(bf16[512,128]{1,0:T(8,128)(2,1)S(1)} %get-tuple-element.66.refs_0_), channel_id=1, source_target_pairs={{0,1},{1,0},{2,3},{3,2},{4,5},{5,4},{6,7},{7,6},{8,9},{9,8},{10,11... | collective-permute-start | bytes 393224 | tf_op jit(solution)/shard_map/cond/branch_1_fun/ppermute | solution.py:49
  33.2 4.4 %collective-permute-start.6 = (bf16[80,256]{1,0:T(8,128)(2,1)S(1)}, bf16[80,256]{1,0:T(8,128)(2,1)S(1)}, u32[]{:S(2)}, u32[]{:S(2)}) collective-permute-start(bf16[80,256]{1,0:T(8,128)(2,1)S(1)} %get-tuple-element.147), channel_id=1, source_target_pairs={{0,8},{1,17},{2,10},{3,19},{4,12},{5,21},{6,14},{7,23},{8,0},{9,25... | collective-permute-start | bytes 122888 | tf_op jit(solution)/shard_map/cond/branch_1_fun/ppermute | solution.py:49
  37.6 4.1 %collective-permute-start.7 = (bf16[80,256]{1,0:T(8,128)(2,1)S(1)}, bf16[80,256]{1,0:T(8,128)(2,1)S(1)}, u32[]{:S(2)}, u32[]{:S(2)}) collective-permute-start(bf16[80,256]{1,0:T(8,128)(2,1)S(1)} %fusion), channel_id=1, source_target_pairs={{0,16},{1,9},{2,18},{3,11},{4,20},{5,13},{6,22},{7,15},{8,24},{9,1... | collective-permute-start | bytes 122888 | tf_op jit(solution)/shard_map/cond/branch_1_fun/ppermute | solution.py:49
  41.9 2.2 %collective-permute-start.18 = (bf16[1024,128]{1,0:T(8,128)(2,1)S(1)}, bf16[1024,128]{1,0:T(8,128)(2,1)S(1)}, u32[]{:S(2)}, u32[]{:S(2)}) collective-permute-start(bf16[1024,128]{1,0:T(8,128)(2,1)S(1)} %constant_dynamic-update-slice_fusion.refs_0_), channel_id=1, source_target_pairs={{0,1},{1,0},{2,3},{3,2},{4,5},{5,4},{6,7},{7,6},{8,9},{9,8},{10,11... | collective-permute-start | bytes 786440 | tf_op jit(solution)/shard_map/ppermute | solution.py:49
  42.0 5.8 %collective-permute-start.14 = (bf16[80,256]{1,0:T(8,128)(2,1)S(1)}, bf16[80,256]{1,0:T(8,128)(2,1)S(1)}, u32[]{:S(2)}, u32[]{:S(2)}) collective-permute-start(bf16[80,256]{1,0:T(8,128)(2,1)S(1)} %convert_element_type.77), channel_id=1, source_target_pairs={{0,2},{1,3},{2,0},{3,1},{4,6},{5,7},{6,4},{7,5},{8,10},{9,11},{10,... | collective-permute-start | bytes 122888 | tf_op jit(solution)/shard_map/ppermute | solution.py:49
  47.8 10.4 %collective-permute-start.19 = (bf16[512,128]{1,0:T(8,128)(2,1)S(1)}, bf16[512,128]{1,0:T(8,128)(2,1)S(1)}, u32[]{:S(2)}, u32[]{:S(2)}) collective-permute-start(bf16[512,128]{1,0:T(8,128)(2,1)S(1)} %get-tuple-element.142), channel_id=1, source_target_pairs={{0,8},{1,17},{2,10},{3,19},{4,12},{5,21},{6,14},{7,23},{8,0},{9,25... | collective-permute-start | bytes 393224 | tf_op jit(solution)/shard_map/ppermute | solution.py:49
  49.2 9.0 %collective-permute-start.20 = (bf16[512,128]{1,0:T(8,128)(2,1)S(1)}, bf16[512,128]{1,0:T(8,128)(2,1)S(1)}, u32[]{:S(2)}, u32[]{:S(2)}) collective-permute-start(bf16[512,128]{1,0:T(8,128)(2,1)S(1)} %get-tuple-element.143), channel_id=1, source_target_pairs={{0,16},{1,9},{2,18},{3,11},{4,20},{5,13},{6,22},{7,15},{8,24},{9,1... | collective-permute-start | bytes 393224 | tf_op jit(solution)/shard_map/ppermute | solution.py:49
  49.9 8.3 %collective-permute-start.21 = (bf16[512,128]{1,0:T(8,128)(2,1)S(1)}, bf16[512,128]{1,0:T(8,128)(2,1)S(1)}, u32[]{:S(2)}, u32[]{:S(2)}) collective-permute-start(bf16[512,128]{1,0:T(8,128)(2,1)S(1)} %get-tuple-element.144), channel_id=1, source_target_pairs={{0,24},{1,25},{2,26},{3,27},{4,28},{5,29},{6,30},{7,31},{8,16},{9,... | collective-permute-start | bytes 393224 | tf_op jit(solution)/shard_map/ppermute | solution.py:49
  51.4 5.4 %collective-permute-start.2 = (bf16[80,256]{1,0:T(8,128)(2,1)S(1)}, bf16[80,256]{1,0:T(8,128)(2,1)S(1)}, u32[]{:S(2)}, u32[]{:S(2)}) collective-permute-start(bf16[80,256]{1,0:T(8,128)(2,1)S(1)} %fusion.1), channel_id=1, source_target_pairs={{0,4},{1,5},{2,6},{3,7},{4,0},{5,1},{6,2},{7,3},{8,12},{9,13},{10,... | collective-permute-start | bytes 122888 | tf_op jit(solution)/shard_map/cond/branch_1_fun/ppermute | solution.py:49
  56.8 1.3 %collective-permute-start.3 = (f32[64,256]{1,0:T(8,128)S(1)}, f32[64,256]{1,0:T(8,128)S(1)}, u32[]{:S(2)}, u32[]{:S(2)}) collective-permute-start(f32[64,256]{1,0:T(8,128)S(1)} %slice.24), channel_id=1, source_target_pairs={{0,1},{1,0},{2,3},{3,2},{4,5},{5,4},{6,7},{7,6},{8,9},{9,8},{10,11... | collective-permute-start | bytes 196616 | tf_op jit(solution)/shard_map/cond/branch_1_fun/ppermute | solution.py:49
  58.1 0.8 %copy-start.3 = (bf16[512,256]{1,0:T(8,128)(2,1)}, bf16[512,256]{1,0:T(8,128)(2,1)S(1)}, u32[]{:S(2)}) copy-start(bf16[512,256]{1,0:T(8,128)(2,1)S(1)} %get-tuple-element.112) | copy-start | bytes 786436
  58.2 0.8 %copy-start.4 = (f32[128,256]{1,0:T(8,128)}, f32[128,256]{1,0:T(8,128)S(1)}, u32[]{:S(2)}) copy-start(f32[128,256]{1,0:T(8,128)S(1)} %get-tuple-element.114) | copy-start | bytes 393220
  58.2 0.8 %copy-start.5 = (f32[256]{0:T(256)}, f32[256]{0:T(256)S(1)}, u32[]{:S(2)}) copy-start(f32[256]{0:T(256)S(1)} %get-tuple-element.115) | copy-start | bytes 3076
